TPU v7x, 256 devices: a whole 4x4x8 slice. The times are simulated.
256 devices in a mesh: store: 16 (over z_lo, x), group: 16 (over y, z_hi, core).
Axes of the slice: x: 4, y: 4, z: 8 (z_hi: 2, z_lo: 4; z = z_hi * 4 + z_lo), core: 2. Of those that a mesh axis runs over, the one named last changes fastest.
Arguments:
- activations: bfloat16 [1024, 16, 64, 256], P('group', 'store'), may hold values from -6 to 6
- out_grads: bfloat16 [1024, 16, 64, 256], P('group', 'store'), may hold values from -6 to 6
- stored: bfloat16 [12288, 16, 4096], P('group', 'store'), may hold values from -0.0019989014 to 0.0019989014
- lengths: int32 [1024], P('group'), may hold values from 64 to 256, as said below
- store_ids: int32 [12288], P('group'), may hold values from 0 to 767, as said below
Outputs:
- scores: float32 [1024, 12288], P('store', 'group')
Inputs may be any that keep to these rules, and one draw needn't show every extreme that they name: `lengths`: one query pair has all 256 slots live. `store_ids`: each aligned block of 768 entries is a permutation of 0 to 767.
All inputs are finite; a program needn't handle non-finite values.
Results may differ from a plain program's by a relative error of at most 0.0029.
Values may be sent and summed in bfloat16 or wider, within the bound.
No kernel may reach another device: no remote copies, remote signals or barrier semaphores. Data moves between devices by JAX's collectives and lax.ppermute only.
A program may use at most 64 MiB of HBM per device.

v0:
```python
import jax
import jax.numpy as jnp
from jax import lax
from jax.sharding import PartitionSpec as P


def on_device(activations, out_grads, stored, lengths, store_ids):
    pairs, layers, width, slots = activations.shape
    positions = jnp.arange(slots, dtype=jnp.int32)
    live = positions[None, :] < lengths[:, None]
    masked = jnp.where(live[:, None, None, :], activations, jnp.zeros((), activations.dtype))
    query_grad = jnp.einsum(
        "plit,pljt->plij", out_grads, masked, preferred_element_type=jnp.float32
    )
    query_grad = query_grad.astype(jnp.bfloat16).reshape(pairs, layers * width * width)
    stored_flat = stored.reshape(stored.shape[0], layers * width * width)
    partial_scores = lax.dot_general(
        lax.all_gather(query_grad, "group", axis=0, tiled=True),
        stored_flat,
        (((1,), (1,)), ((), ())),
        preferred_element_type=jnp.float32,
    )
    summed = lax.psum_scatter(partial_scores, "store", scatter_dimension=0, tiled=True)
    return jnp.take(summed, store_ids, axis=1)


def solution(mesh):
    in_specs = (
        P("group", "store", None, None),
        P("group", "store", None, None),
        P("group", "store", None),
        P("group"),
        P("group"),
    )
    out_specs = P("store", "group")
    return jax.shard_map(
        on_device, mesh=mesh, in_specs=in_specs, out_specs=out_specs, check_vma=False
    )
```

profile of v0, /device:TPU:8, one launch (start us, length us, event | category | flops | bytes accessed | tf_op | source)
XLA Modules:
  0.0 234.6 jit_solution(15591833989646386707)
XLA Ops:
  6.5 0.0 copy-start
  6.5 0.0 all-gather.2.cloned.1.call-start
  6.5 0.9 iota_compare_fusion
  7.4 0.7 copy-done
  8.1 3.3 %fusion.12 = bf16[64,64,64]{1,2,0:T(8,128)(2,1)} fusion(bf16[64,1,64,256]{3,2,1,0:T(8,128)(2,1)S(1)} %copy-done, bf16[64,1,64,256]{3,2,1,0:T(8,128)(2,1)} %param.5, pred[64,256]{1,0:T(8,128)(4,1)S(1)} %iota_compare_fusion), kind=kOutput, calls=%fused_computation.9 | convolution fusion | flops 135528448 | bytes 4734976 | tf_op jit(solution)/shard_map/plit,pljt->plij/dot_general | solution.py:12
  11.4 1.6 copy.8
  13.0 1.7 reshape.41
  14.7 0.0 all-gather.2.cloned.1.call-update
  14.7 0.0 reduce-scatter.2.cloned.1.call-start
  14.7 110.0 %all-gather.2.cloned.1.call-done = bf16[1024,4096]{1,0:T(8,128)(2,1)} async-done(((bf16[64,4096]{1,0:T(8,128)(2,1)}), bf16[1024,4096]{1,0:T(8,128)(2,1)}) %all-gather.2.cloned.1.call-update) | async-done | bytes 8388624 | tf_op jit(solution)/shard_map/all_gather | solution.py:18
  124.7 12.1 %fusion = f32[1024,768]{1,0:T(8,128)} fusion(bf16[1024,4096]{1,0:T(8,128)(2,1)} %all-gather.2.cloned.1.call-done, bf16[768,1,4096]{2,0,1:T(8,128)(2,1)} %param.7), kind=kOutput, calls=%fused_computation.1 | convolution fusion | flops 6442450944 | bytes 17825792 | tf_op jit(solution)/shard_map/dot_general | solution.py:17
  136.8 0.0 copy-start.1
  136.8 0.0 reduce-scatter.2.cloned.1.call-update
  136.8 0.7 copy-done.1
  137.5 86.5 %reduce-scatter.2.cloned.1.call-done = f32[64,768]{1,0:T(8,128)} async-done(((f32[1024,768]{1,0:T(8,128)}), f32[64,768]{1,0:T(8,128)}) %reduce-scatter.2.cloned.1.call-update) | async-done | bytes 196624 | tf_op jit(solution)/shard_map/reduce_scatter | solution.py:23
  224.1 1.1 copy.9
  225.2 1.6 gather_fusion
  226.8 0.2 select_bitcast_fusion
  226.9 0.8 copy.10
  (3 shorter events, 0.0 us)
Async XLA Ops:
  6.5 1.6 copy-start
  6.5 118.2 %all-gather.2.cloned.1.call-start = ((), (), s32[]{:S(2)}) async-start(), calls=%async_computation.1 | async-start | bytes 8912896 | tf_op jit(solution)/shard_map/all_gather | solution.py:18
  14.7 209.4 %reduce-scatter.2.cloned.1.call-start = ((), (), s32[]{:S(2)}) async-start(), calls=%async_computation.2 | async-start | bytes 3342336 | tf_op jit(solution)/shard_map/reduce_scatter | solution.py:23
  136.8 0.7 copy-start.1
Sparse Core Ops, SparseCore 0:
  14.8 109.8 all-gather.1
  137.0 87.0 reduce-scatter.1
where the time goes:
time: 235 us
  waiting for transfers between devices  197 us (84%)
  matrix products  15.4 us (7%)
  between operations  13.4 us (6%)
  local copies, waits for them, and re-layouts  8.13 us (3%)
    all_gather x1, waiting for transfers between devices, on_device(): lax.all_gather(query_grad, 'group', axis=0, tiled=True)  110 us
    reduce_scatter x1, waiting for transfers between devices, on_device(): lax.psum_scatter(partial_scores, 'store', scatter_dimension=0, tiled=True)  86.5 us
    dot_general x1, matrix products, on_device(): lax.dot_general(lax.all_gather(query_grad, 'group', axis=0, tiled=True),...  12.1 us
  transfers between devices with their start and end apart: 2, of which 2 were waited for; matrix products, arithmetic and copies ran while one was open for 0% of the time, Pallas kernels for 0%

commit v1 on v0

v1 whole, which is shorter than its diff:
```python
import functools

import jax
import jax.numpy as jnp
from jax import lax
from jax.experimental import pallas as pl
from jax.experimental.pallas import tpu as pltpu
from jax.sharding import PartitionSpec as P

CHUNKS = 2
PAIRS = 64
ROWS = PAIRS // CHUNKS
WIDTH = 64
SLOTS = 256
FEATURES = WIDTH * WIDTH
HELD = 768
STEP_PAIRS = 8
PITCH = 72
COLS = 256
F32 = jnp.float32
BF16 = jnp.bfloat16


def node(x, z_lo, y, z_hi, core):
    return (z_lo % 4) * 4 + x % 4, ((y % 4) * 2 + z_hi % 2) * 2 + core % 2


def group_pairs(move):
    pairs = []
    for y in range(4):
        for z_hi in range(2):
            for core in range(2):
                dst = move(y, z_hi, core)
                if dst is not None:
                    pairs.append((node(0, 0, y, z_hi, core)[1], node(0, 0, *dst)[1]))
    return pairs


def place():
    store, group = lax.axis_index("store"), lax.axis_index("group")
    return store % 4, store // 4, group // 4, (group // 2) % 2, group % 2


def grad_kernel(chunk, *refs):
    lengths_hbm, acts_hbm, grads_hbm, *earlier = refs[: 3 + chunk]
    out_ref, *whole = refs[3 + chunk : -5]
    acts_ref, grads_ref, lengths_ref, wide_ref, sems = refs[-5:]
    first = chunk * ROWS

    def copies(n):
        src, dst = pl.ds(first + n * STEP_PAIRS, STEP_PAIRS), pl.ds(n * STEP_PAIRS, STEP_PAIRS)
        return (
            pltpu.make_async_copy(acts_hbm.at[src, 0], acts_ref.at[dst], sems.at[2 * n]),
            pltpu.make_async_copy(grads_hbm.at[src, 0], grads_ref.at[dst], sems.at[2 * n + 1]),
        )

    steps = ROWS // STEP_PAIRS
    lengths_copy = pltpu.make_async_copy(lengths_hbm, lengths_ref, sems.at[2 * steps])
    lengths_copy.start()
    for n in range(steps):
        for copy in copies(n):
            copy.start()
    lengths_copy.wait()
    slot = lax.broadcasted_iota(jnp.int32, (WIDTH, SLOTS), 1)
    for n in range(steps):
        for copy in copies(n):
            copy.wait()
        for p in range(n * STEP_PAIRS, (n + 1) * STEP_PAIRS):
            acts = acts_ref[p]
            acts = jnp.where(slot < lengths_ref[first + p], acts, jnp.zeros_like(acts))
            wide_ref[pl.ds(p * PITCH, WIDTH), :] = lax.dot_general(
                grads_ref[p],
                jnp.concatenate([acts, acts], axis=0),
                (((1,), (1,)), ((), ())),
                preferred_element_type=F32,
            )
    low = lax.broadcasted_iota(jnp.int32, (ROWS, 128), 1) < WIDTH
    for c in range(FEATURES // 128):
        even = wide_ref[pl.ds(2 * c, ROWS, stride=PITCH), :]
        odd = wide_ref[pl.ds(2 * c + 1, ROWS, stride=PITCH), :]
        out_ref[:, c * 128 : (c + 1) * 128] = jnp.where(low, even, odd).astype(BF16)
    for whole_ref in whole:
        for n, piece in enumerate((*earlier, out_ref)):
            whole_ref[n * ROWS : (n + 1) * ROWS, :] = piece[...]


def query_grads(lengths, activations, out_grads, earlier):
    chunk = len(earlier)
    last = chunk == CHUNKS - 1
    hbm = pl.BlockSpec(memory_space=pltpu.HBM)
    return pl.pallas_call(
        functools.partial(grad_kernel, chunk),
        out_shape=[jax.ShapeDtypeStruct((ROWS, FEATURES), BF16)]
        + [jax.ShapeDtypeStruct((PAIRS, FEATURES), BF16)] * last,
        in_specs=[hbm] * 3 + [pl.BlockSpec(memory_space=pltpu.VMEM)] * chunk,
        scratch_shapes=[
            pltpu.VMEM((ROWS, WIDTH, SLOTS), BF16),
            pltpu.VMEM((ROWS, WIDTH, SLOTS), BF16),
            pltpu.SMEM((PAIRS,), jnp.int32),
            pltpu.VMEM((ROWS * PITCH, 128), F32),
            pltpu.SemaphoreType.DMA((2 * (ROWS // STEP_PAIRS) + 1,)),
        ],
        compiler_params=pltpu.CompilerParams(vmem_limit_bytes=16 << 20),
        cost_estimate=pl.CostEstimate(
            flops=chunk * 8 * FEATURES * SLOTS * PAIRS * ROWS, bytes_accessed=0, transcendentals=0
        ),
        name="query_grads",
    )(lengths, activations, out_grads, *earlier)


def score_kernel(own_ref, *refs):
    blocks, (mine_ref, other_ref), outs = refs[:4], refs[4:6], refs[6:]
    step = pl.program_id(0)
    x, _, y, z_hi, core = place()

    def part(weights_ref, rel_core, tile):
        got = lax.dot_general(
            jnp.concatenate(
                [own_ref[...].reshape(4 * ROWS, FEATURES)] + [b[...] for b in blocks], axis=0
            ),
            weights_ref[...],
            (((1,), (1,)), ((), ())),
            preferred_element_type=F32,
        ).astype(BF16)
        for rel_z in range(2):
            to_x = 2 * ((z_hi + rel_z) % 2) + core
            away = (to_x - x + 4) % 4
            if rel_core == 0:
                buf = jnp.where(away == 0, 3, jnp.where(away == 1, 1, jnp.where(away == 2, 0, 2)))
            else:
                buf = jnp.where(away == 0, 2, jnp.where(away == 1, 0, jnp.where(away == 2, 1, 3)))
            for b in range(4):

                @pl.when(buf == b)
                def _():
                    cols = slice(tile * COLS, (tile + 1) * COLS)
                    if rel_z == 0:
                        outs[b][:, cols] = got[: 4 * ROWS]
                    else:
                        for j, dy in enumerate((0, 3, 1, 2)):
                            row = pl.multiple_of(((y + dy) % 4) * ROWS, ROWS)
                            at = (4 + j) * ROWS
                            outs[b][pl.ds(row, ROWS), cols] = got[at : at + ROWS]

    tiles = HELD // COLS
    for s in range(2 * tiles):

        @pl.when(step == s)
        def _():
            part(mine_ref if s < tiles else other_ref, s // tiles, s % tiles)


def partial_scores(own, fars, mine, other, chunk):
    tiles = HELD // COLS
    whole = pl.BlockSpec((ROWS, FEATURES), lambda i: (0, 0))
    out = pl.BlockSpec((4 * ROWS, HELD), lambda i: (0, 0))
    return pl.pallas_call(
        score_kernel,
        out_shape=[jax.ShapeDtypeStruct((4 * ROWS, HELD), BF16)] * 4,
        grid=(2 * tiles,),
        in_specs=[pl.BlockSpec((4, ROWS, FEATURES), lambda i: (0, chunk, 0))]
        + [whole] * 4
        + [
            pl.BlockSpec((COLS, FEATURES), lambda i: (jnp.minimum(i, tiles - 1), 0)),
            pl.BlockSpec((COLS, FEATURES), lambda i: (jnp.maximum(i - tiles, 0), 0)),
        ],
        out_specs=[out] * 4,
        compiler_params=pltpu.CompilerParams(vmem_limit_bytes=24 << 20),
        cost_estimate=pl.CostEstimate(
            flops=2 * 8 * ROWS * FEATURES * 2 * HELD,
            bytes_accessed=2 * FEATURES * (2 * HELD + 8 * ROWS),
            transcendentals=0,
        ),
        name="partial_scores",
    )(own, *fars, mine, other)


def cross_sum_kernel(a_ref, b_ref, c_ref, d_ref, own_ref, keep_ref, *outs):
    x, z_lo, _, _, core = place()
    match = (x % 2) == core
    for k in range(4):
        rows = pl.ds(pl.multiple_of(((z_lo + k) % 4) * ROWS, ROWS), ROWS)
        last = jnp.where(match, own_ref[rows, :].astype(F32), d_ref[rows, :].astype(F32))
        total = a_ref[rows, :].astype(F32) + b_ref[rows, :].astype(F32)
        total = total + (c_ref[rows, :].astype(F32) + last)
        if k == 0:
            keep_ref[...] = total
        else:
            outs[k - 1][...] = total.astype(BF16)


def cross_sum(*parts):
    return pl.pallas_call(
        cross_sum_kernel,
        out_shape=[jax.ShapeDtypeStruct((ROWS, HELD), F32)]
        + [jax.ShapeDtypeStruct((ROWS, HELD), BF16)] * 3,
        compiler_params=pltpu.CompilerParams(vmem_limit_bytes=16 << 20),
        name="cross_sum",
    )(*parts)


def final_kernel(*refs):
    pick_ref, out_ref = refs[-2:]
    totals = []
    for n in range(CHUNKS):
        keep, first, second, third = refs[4 * n : 4 * n + 4]
        total = keep[...] + first[...].astype(F32)
        totals.append(total + (second[...].astype(F32) + third[...].astype(F32)))
    total = jnp.concatenate(totals, axis=0)
    high = total.astype(BF16)
    rest = total - high.astype(F32)
    middle = rest.astype(BF16)
    low = (rest - middle.astype(F32)).astype(BF16)
    picked = lax.dot_general(
        jnp.concatenate([high, middle, low], axis=0),
        pick_ref[...],
        (((1,), (0,)), ((), ())),
        preferred_element_type=F32,
    )
    out_ref[...] = picked[:PAIRS] + (picked[PAIRS : 2 * PAIRS] + picked[2 * PAIRS :])


def final_sum(parts, pick):
    return pl.pallas_call(
        final_kernel,
        out_shape=jax.ShapeDtypeStruct((PAIRS, HELD), F32),
        compiler_params=pltpu.CompilerParams(vmem_limit_bytes=16 << 20),
        name="final_sum",
    )(*parts, pick)


def store_pairs(move):
    pairs = []
    for z_lo in range(4):
        for x in range(4):
            pairs.append((node(x, z_lo, 0, 0, 0)[0], node(*move(x, z_lo), 0, 0, 0)[0]))
    return pairs


def all_pairs(move):
    pairs = []
    for z_lo in range(4):
        for x in range(4):
            for y in range(4):
                for z_hi in range(2):
                    for core in range(2):
                        dst = move(x, core)
                        if dst is None:
                            continue
                        s, g = node(x, z_lo, y, z_hi, core)
                        t, h = node(dst[0], z_lo, y, z_hi, dst[1])
                        pairs.append((s * 16 + g, t * 16 + h))
    return pairs


def along(value, move):
    return lax.ppermute(value, "group", group_pairs(move))


def fence_kernel(*refs):
    pass


def after(value, *others):
    hold = pl.BlockSpec(memory_space=pl.ANY)
    return pl.pallas_call(
        fence_kernel,
        out_shape=jax.ShapeDtypeStruct(value.shape, value.dtype),
        in_specs=[hold] * (1 + len(others)),
        out_specs=hold,
        input_output_aliases={0: 0},
        compiler_params=pltpu.CompilerParams(vmem_limit_bytes=1 << 20),
        name="fence",
    )(value, *others)


def far_blocks(value, earlier):
    far = along(value, lambda y, z, c: (y, z + 1, c))
    if earlier:
        far = after(far, *earlier)
    above = along(far, lambda y, z, c: (y - 1, z, c))
    below = along(far, lambda y, z, c: (y + 1, z, c))
    opposite = along(above, lambda y, z, c: (y - 1, z, c))
    return [far, below, above, opposite]


def own_blocks(value):
    groups = [[(y * 2 + z) * 2 + c for y in range(4)] for z in range(2) for c in range(2)]
    got = lax.all_gather(value, "group", axis=0, tiled=True, axis_index_groups=groups)
    return pltpu.with_memory_space_constraint(got.reshape(4, PAIRS, FEATURES), pltpu.HBM)


def over_x(bufs):
    def match(x, core):
        return x % 2 == core

    moves = (
        lambda x, c: (x + 2, c) if match(x, c) else (x + 1, 1 - c),
        lambda x, c: (x + 2, 1 - c) if match(x, c) else (x + 1, c),
        lambda x, c: (x, 1 - c) if match(x, c) else (x - 1, c),
        lambda x, c: None if match(x, c) else (x - 1, 1 - c),
    )
    return [lax.ppermute(b, ("store", "group"), all_pairs(m)) for b, m in zip(bufs, moves)]


def on_device(activations, out_grads, stored, lengths, store_ids):
    stored = stored.reshape(HELD, FEATURES)
    other = lax.ppermute(stored, "group", group_pairs(lambda y, z, c: (y, z, 1 - c)))
    pick = (store_ids[None, :] == jnp.arange(HELD, dtype=jnp.int32)[:, None]).astype(BF16)
    inputs = [
        pltpu.with_memory_space_constraint(v, pltpu.HBM) for v in (lengths, activations, out_grads)
    ]
    (a,) = query_grads(*inputs, ())
    b, both = query_grads(*inputs, (a,))
    own = own_blocks(both)
    parts = []
    far_a = far_blocks(a, ())
    far_b = far_blocks(b, far_a[1:])
    for n, fars in enumerate([far_a, far_b]):
        bufs = partial_scores(own, fars, stored, other, n)
        keep, *sends = cross_sum(*over_x(bufs), bufs[3])
        parts.append(keep)
        for k, send in enumerate(sends, 1):
            parts.append(lax.ppermute(send, "store", store_pairs(lambda x, z: (x, z + k))))
    return final_sum(parts, pick)


def solution(mesh):
    in_specs = (
        P("group", "store", None, None),
        P("group", "store", None, None),
        P("group", "store", None),
        P("group"),
        P("group"),
    )
    out_specs = P("store", "group")
    return jax.shard_map(
        on_device, mesh=mesh, in_specs=in_specs, out_specs=out_specs, check_vma=False
    )
```

time: 235 us -> 126 us (0.54)
  the two profiles are of different devices: /device:TPU:8 before, /device:TPU:32 now
where the time goes in v1:
time: 126 us
  starting transfers between devices  44.7 us (35%)
  waiting for transfers between devices  41.4 us (33%)
  Pallas kernels  23.1 us (18%)
  between operations  13.5 us (11%)
  local copies, waits for them, and re-layouts  2.79 us (2%)
    ppermute x8, waiting for transfers between devices, along(): return lax.ppermute(value, 'group', group_pairs(move))  33.3 us
    ppermute x8, starting transfers between devices, along(): return lax.ppermute(value, 'group', group_pairs(move))  23.7 us
    pallas_call x2, Pallas kernels, partial_scores(): pl.pallas_call(score_kernel, out_shape=[jax.ShapeDtypeStruct((4 * ROWS, H...  15.9 us
    ppermute x8, starting transfers between devices, over_x(): lax.ppermute(b, ('store', 'group'), all_pairs(m))  10.8 us
    ppermute x6, starting transfers between devices, on_device(): lax.ppermute(send, 'store', store_pairs(lambda x, z: (x, z + k)))  10.3 us
    pallas_call x2, Pallas kernels, query_grads(): pl.pallas_call(functools.partial(grad_kernel, chunk), out_shape=[jax.Shap...  5.84 us
    ppermute x8, waiting for transfers between devices, over_x(): lax.ppermute(b, ('store', 'group'), all_pairs(m))  4.47 us
    ppermute x6, waiting for transfers between devices, on_device(): lax.ppermute(send, 'store', store_pairs(lambda x, z: (x, z + k)))  3.65 us
  transfers between devices with their start and end apart: 24, of which 11 were waited for; matrix products, arithmetic and copies ran while one was open for 0% of the time, Pallas kernels for 17%

profile of v1, /device:TPU:32, one launch (start us, length us, event | category | flops | bytes accessed | tf_op | source)
XLA Modules:
  0.0 125.9 jit_solution(1027522312616905308)
XLA Ops:
  6.5 2.5 %query_grads.2.refs_3_ = bf16[32,4096]{1,0:T(8,128)(2,1)S(1)} custom-call(s32[64]{0:T(128)} %refs_0_.3, bf16[64,1,64,256]{3,2,1,0:T(8,128)(2,1)} %refs_1_.3, bf16[64,1,64,256]{3,2,1,0:T(8,128)(2,1)} %refs_2_.3), custom_call_target="tpu_custom_call" | custom-call | tf_op jit(solution)/shard_map/query_grads/pallas_call | solution.py:91
  9.0 3.3 %query_grads.3 = (bf16[32,4096]{1,0:T(8,128)(2,1)S(1)}, bf16[64,4096]{1,0:T(8,128)(2,1)}) custom-call(s32[64]{0:T(128)} %refs_0_.3, bf16[64,1,64,256]{3,2,1,0:T(8,128)(2,1)} %refs_1_.3, bf16[64,1,64,256]{3,2,1,0:T(8,128)(2,1)} %refs_2_.3, bf16[32,4096]{1,0:T(8,128)(2,1)S(1)} %query_grads.2.refs_3_), custom_call_target="tpu_custom_call" | custom-call | flops 17179869184 | tf_op jit(solution)/shard_map/query_grads/pallas_call | solution.py:91
  12.4 6.4 %collective-permute-start = (bf16[32,4096]{1,0:T(8,128)(2,1)S(1)}, bf16[32,4096]{1,0:T(8,128)(2,1)S(1)}, u32[]{:S(2)}, u32[]{:S(2)}) collective-permute-start(bf16[32,4096]{1,0:T(8,128)(2,1)S(1)} %query_grads.2.refs_3_), channel_id=1, source_target_pairs={{0,2},{1,3},{2,0},{3,1},{4,6},{5,7},{6,4},{7,5},{8,10},{9,11},{10,... | collective-permute-start | bytes 786440 | tf_op jit(solution)/shard_map/ppermute | solution.py:257
  18.8 12.7 %collective-permute-done.refs_0_ = bf16[32,4096]{1,0:T(8,128)(2,1)S(1)} collective-permute-done((bf16[32,4096]{1,0:T(8,128)(2,1)S(1)}, bf16[32,4096]{1,0:T(8,128)(2,1)S(1)}, u32[]{:S(2)}, u32[]{:S(2)}) %collective-permute-start) | collective-permute-done | bytes 262176 | tf_op jit(solution)/shard_map/ppermute | solution.py:257
  31.5 3.0 %collective-permute-start.2 = (bf16[32,4096]{1,0:T(8,128)(2,1)S(1)}, bf16[32,4096]{1,0:T(8,128)(2,1)S(1)}, u32[]{:S(2)}, u32[]{:S(2)}) collective-permute-start(bf16[32,4096]{1,0:T(8,128)(2,1)S(1)} %collective-permute-done.refs_0_), channel_id=1, source_target_pairs={{0,12},{1,13},{2,14},{3,15},{4,0},{5,1},{6,2},{7,3},{8,4},{9,5},{1... | collective-permute-start | bytes 786440 | tf_op jit(solution)/shard_map/ppermute | solution.py:257
  34.5 5.6 %collective-permute-start.12 = (bf16[32,4096]{1,0:T(8,128)(2,1)S(1)}, bf16[32,4096]{1,0:T(8,128)(2,1)S(1)}, u32[]{:S(2)}, u32[]{:S(2)}) collective-permute-start(bf16[32,4096]{1,0:T(8,128)(2,1)S(1)} %get-tuple-element.32), channel_id=1, source_target_pairs={{0,2},{1,3},{2,0},{3,1},{4,6},{5,7},{6,4},{7,5},{8,10},{9,11},{10,... | collective-permute-start | bytes 786440 | tf_op jit(solution)/shard_map/ppermute | solution.py:257
  40.1 6.2 %collective-permute-done.2.refs_2_ = bf16[32,4096]{1,0:T(8,128)(2,1)S(1)} collective-permute-done((bf16[32,4096]{1,0:T(8,128)(2,1)S(1)}, bf16[32,4096]{1,0:T(8,128)(2,1)S(1)}, u32[]{:S(2)}, u32[]{:S(2)}) %collective-permute-start.2) | collective-permute-done | bytes 262176 | tf_op jit(solution)/shard_map/ppermute | solution.py:257
  46.2 3.7 %collective-permute-start.3 = (bf16[32,4096]{1,0:T(8,128)(2,1)S(1)}, bf16[32,4096]{1,0:T(8,128)(2,1)S(1)}, u32[]{:S(2)}, u32[]{:S(2)}) collective-permute-start(bf16[32,4096]{1,0:T(8,128)(2,1)S(1)} %collective-permute-done.2.refs_2_), channel_id=1, source_target_pairs={{0,12},{1,13},{2,14},{3,15},{4,0},{5,1},{6,2},{7,3},{8,4},{9,5},{1... | collective-permute-start | bytes 786440 | tf_op jit(solution)/shard_map/ppermute | solution.py:257
  50.2 3.7 %collective-permute-done.1.refs_1_ = bf16[32,4096]{1,0:T(8,128)(2,1)S(1)} collective-permute-done((bf16[32,4096]{1,0:T(8,128)(2,1)S(1)}, bf16[32,4096]{1,0:T(8,128)(2,1)S(1)}, u32[]{:S(2)}, u32[]{:S(2)}) %collective-permute-start.1) | collective-permute-done | bytes 262176 | tf_op jit(solution)/shard_map/ppermute | solution.py:257
  54.0 4.7 %collective-permute-done.3.refs_3_ = bf16[32,4096]{1,0:T(8,128)(2,1)S(1)} collective-permute-done((bf16[32,4096]{1,0:T(8,128)(2,1)S(1)}, bf16[32,4096]{1,0:T(8,128)(2,1)S(1)}, u32[]{:S(2)}, u32[]{:S(2)}) %collective-permute-start.3) | collective-permute-done | bytes 262176 | tf_op jit(solution)/shard_map/ppermute | solution.py:257
  58.6 1.8 %collective-permute-start.14 = (bf16[32,4096]{1,0:T(8,128)(2,1)S(1)}, bf16[32,4096]{1,0:T(8,128)(2,1)S(1)}, u32[]{:S(2)}, u32[]{:S(2)}) collective-permute-start(bf16[32,4096]{1,0:T(8,128)(2,1)S(1)} %fence.1.refs_0_), channel_id=1, source_target_pairs={{0,12},{1,13},{2,14},{3,15},{4,0},{5,1},{6,2},{7,3},{8,4},{9,5},{1... | collective-permute-start | bytes 786440 | tf_op jit(solution)/shard_map/ppermute | solution.py:257
  60.7 5.7 %collective-permute-done.14.refs_2_ = bf16[32,4096]{1,0:T(8,128)(2,1)S(1)} collective-permute-done((bf16[32,4096]{1,0:T(8,128)(2,1)S(1)}, bf16[32,4096]{1,0:T(8,128)(2,1)S(1)}, u32[]{:S(2)}, u32[]{:S(2)}) %collective-permute-start.14) | collective-permute-done | bytes 262176 | tf_op jit(solution)/shard_map/ppermute | solution.py:257
  66.4 3.0 %collective-permute-start.15 = (bf16[32,4096]{1,0:T(8,128)(2,1)S(1)}, bf16[32,4096]{1,0:T(8,128)(2,1)S(1)}, u32[]{:S(2)}, u32[]{:S(2)}) collective-permute-start(bf16[32,4096]{1,0:T(8,128)(2,1)S(1)} %collective-permute-done.14.refs_2_), channel_id=1, source_target_pairs={{0,12},{1,13},{2,14},{3,15},{4,0},{5,1},{6,2},{7,3},{8,4},{9,5},{1... | collective-permute-start | bytes 786440 | tf_op jit(solution)/shard_map/ppermute | solution.py:257
  69.4 2.8 %copy-done = bf16[768,1,4096]{2,0,1:T(8,128)(2,1)S(1)} copy-done((bf16[768,1,4096]{2,0,1:T(8,128)(2,1)S(1)}, bf16[768,1,4096]{2,0,1:T(8,128)(2,1)}, u32[]{:S(2)}) %copy-start) | copy-done | bytes 6291480
  72.2 7.9 %partial_scores.2 = (bf16[128,768]{1,0:T(8,128)(2,1)S(1)}, bf16[128,768]{1,0:T(8,128)(2,1)S(1)}, bf16[128,768]{1,0:T(8,128)(2,1)S(1)}, bf16[128,768]{1,0:T(8,128)(2,1)S(1)}) custom-call(bf16[4,64,4096]{2,1,0:T(8,128)(2,1)} %bitcast.5, bf16[32,4096]{1,0:T(8,128)(2,1)S(1)} %collective-permute-done.refs_0_, ...), custom_call_target="tpu_custom_call" | custom-call | flops 3221225472 | bytes 14680064 | tf_op jit(solution)/shard_map/partial_scores/pallas_call | solution.py:157
  80.1 3.2 %collective-permute-start.5 = (bf16[128,768]{1,0:T(8,128)(2,1)S(1)}, bf16[128,768]{1,0:T(8,128)(2,1)S(1)}, u32[]{:S(2)}, u32[]{:S(2)}) collective-permute-start(bf16[128,768]{1,0:T(8,128)(2,1)S(1)} %get-tuple-element.24), channel_id=1, source_target_pairs={{0,32},{1,16},{2,34},{3,18},{4,36},{5,20},{6,38},{7,22},{8,40},{9,... | collective-permute-start | bytes 589832 | tf_op jit(solution)/shard_map/ppermute | solution.py:303
  83.3 0.9 collective-permute-start.6
  84.2 0.8 collective-permute-start.8
  85.0 7.9 %partial_scores.3 = (bf16[128,768]{1,0:T(8,128)(2,1)S(1)}, bf16[128,768]{1,0:T(8,128)(2,1)S(1)}, bf16[128,768]{1,0:T(8,128)(2,1)S(1)}, bf16[128,768]{1,0:T(8,128)(2,1)S(1)}) custom-call(bf16[4,64,4096]{2,1,0:T(8,128)(2,1)} %bitcast.6, bf16[32,4096]{1,0:T(8,128)(2,1)S(1)} %fence.1.refs_0_, bf16[32,4096]{1,0:T(8,128)(2,1)S(1)} %collective-permute-done.13.refs_1_, ...), custom_call_target="tpu_custom_call" | custom-call | flops 3221225472 | bytes 14680064 | tf_op jit(solution)/shard_map/partial_scores/pallas_call | solution.py:157
  93.0 0.9 collective-permute-start.16
  93.9 4.3 %collective-permute-start.17 = (bf16[128,768]{1,0:T(8,128)(2,1)S(1)}, bf16[128,768]{1,0:T(8,128)(2,1)S(1)}, u32[]{:S(2)}, u32[]{:S(2)}) collective-permute-start(bf16[128,768]{1,0:T(8,128)(2,1)S(1)} %get-tuple-element.34), channel_id=1, source_target_pairs={{0,33},{1,17},{2,35},{3,19},{4,37},{5,21},{6,39},{7,23},{8,41},{9,... | collective-permute-start | bytes 589832 | tf_op jit(solution)/shard_map/ppermute | solution.py:303
  98.2 0.7 collective-permute-start.19
  99.1 1.5 %collective-permute-start.9 = (bf16[32,768]{1,0:T(8,128)(2,1)S(1)}, bf16[32,768]{1,0:T(8,128)(2,1)S(1)}, u32[]{:S(2)}, u32[]{:S(2)}) collective-permute-start(bf16[32,768]{1,0:T(8,128)(2,1)S(1)} %get-tuple-element.29), channel_id=1, source_target_pairs={{0,64},{16,80},{32,96},{48,112},{64,128},{80,144},{96,160},{112,17... | collective-permute-start | bytes 147464 | tf_op jit(solution)/shard_map/ppermute | solution.py:324
  100.5 0.6 collective-permute-done.16.a_ref
  101.1 2.5 %collective-permute-start.10 = (bf16[32,768]{1,0:T(8,128)(2,1)S(1)}, bf16[32,768]{1,0:T(8,128)(2,1)S(1)}, u32[]{:S(2)}, u32[]{:S(2)}) collective-permute-start(bf16[32,768]{1,0:T(8,128)(2,1)S(1)} %get-tuple-element.30), channel_id=1, source_target_pairs={{0,128},{16,144},{32,160},{48,176},{64,192},{80,208},{96,224},{112... | collective-permute-start | bytes 147464 | tf_op jit(solution)/shard_map/ppermute | solution.py:324
  103.6 3.9 %collective-permute-done.17.b_ref = bf16[128,768]{1,0:T(8,128)(2,1)S(1)} collective-permute-done((bf16[128,768]{1,0:T(8,128)(2,1)S(1)}, bf16[128,768]{1,0:T(8,128)(2,1)S(1)}, u32[]{:S(2)}, u32[]{:S(2)}) %collective-permute-start.17) | collective-permute-done | bytes 196640 | tf_op jit(solution)/shard_map/ppermute | solution.py:303
  107.7 2.0 %collective-permute-start.20 = (bf16[32,768]{1,0:T(8,128)(2,1)S(1)}, bf16[32,768]{1,0:T(8,128)(2,1)S(1)}, u32[]{:S(2)}, u32[]{:S(2)}) collective-permute-start(bf16[32,768]{1,0:T(8,128)(2,1)S(1)} %get-tuple-element.38), channel_id=1, source_target_pairs={{0,64},{16,80},{32,96},{48,112},{64,128},{80,144},{96,160},{112,17... | collective-permute-start | bytes 147464 | tf_op jit(solution)/shard_map/ppermute | solution.py:324
  109.7 4.2 %collective-permute-start.21 = (bf16[32,768]{1,0:T(8,128)(2,1)S(1)}, bf16[32,768]{1,0:T(8,128)(2,1)S(1)}, u32[]{:S(2)}, u32[]{:S(2)}) collective-permute-start(bf16[32,768]{1,0:T(8,128)(2,1)S(1)} %get-tuple-element.39), channel_id=1, source_target_pairs={{0,128},{16,144},{32,160},{48,176},{64,192},{80,208},{96,224},{112... | collective-permute-start | bytes 147464 | tf_op jit(solution)/shard_map/ppermute | solution.py:324
  113.9 0.4 fusion.refs_8_
  114.6 1.9 %collective-permute-done.21.refs_6_ = bf16[32,768]{1,0:T(8,128)(2,1)S(1)} collective-permute-done((bf16[32,768]{1,0:T(8,128)(2,1)S(1)}, bf16[32,768]{1,0:T(8,128)(2,1)S(1)}, u32[]{:S(2)}, u32[]{:S(2)}) %collective-permute-start.21) | collective-permute-done | bytes 49184 | tf_op jit(solution)/shard_map/ppermute | solution.py:324
  116.5 1.5 %collective-permute-done.22.refs_7_ = bf16[32,768]{1,0:T(8,128)(2,1)S(1)} collective-permute-done((bf16[32,768]{1,0:T(8,128)(2,1)S(1)}, bf16[32,768]{1,0:T(8,128)(2,1)S(1)}, u32[]{:S(2)}, u32[]{:S(2)}) %collective-permute-start.22) | collective-permute-done | bytes 49184 | tf_op jit(solution)/shard_map/ppermute | solution.py:324
  118.0 1.1 final_sum.1
  (30 shorter events, 1.3 us)
Async XLA Ops:
  6.5 62.8 %all-gather.2.cloned.1.call-start = ((), (), s32[]{:S(2)}) async-start(), calls=%async_computation | async-start | bytes 2621440 | tf_op jit(solution)/shard_map/all_gather | solution.py:289
  6.5 62.8 %collective-permute-start.4 = (bf16[768,4096]{1,0:T(8,128)(2,1)}, bf16[768,4096]{1,0:T(8,128)(2,1)}, u32[]{:S(2)}, u32[]{:S(2)}) collective-permute-start(bf16[768,4096]{1,0:T(8,128)(2,1)} %bitcast.2), channel_id=1, source_target_pairs={{0,1},{1,0},{2,3},{3,2},{4,5},{5,4},{6,7},{7,6},{8,9},{9,8},{10,11... | collective-permute-start | bytes 18874376 | tf_op jit(solution)/shard_map/ppermute | solution.py:308
  12.4 19.0 %collective-permute-start = (bf16[32,4096]{1,0:T(8,128)(2,1)S(1)}, bf16[32,4096]{1,0:T(8,128)(2,1)S(1)}, u32[]{:S(2)}, u32[]{:S(2)}) collective-permute-start(bf16[32,4096]{1,0:T(8,128)(2,1)S(1)} %query_grads.2.refs_3_), channel_id=1, source_target_pairs={{0,2},{1,3},{2,0},{3,1},{4,6},{5,7},{6,4},{7,5},{8,10},{9,11},{10,... | collective-permute-start | bytes 786440 | tf_op jit(solution)/shard_map/ppermute | solution.py:257
  31.5 14.8 %collective-permute-start.2 = (bf16[32,4096]{1,0:T(8,128)(2,1)S(1)}, bf16[32,4096]{1,0:T(8,128)(2,1)S(1)}, u32[]{:S(2)}, u32[]{:S(2)}) collective-permute-start(bf16[32,4096]{1,0:T(8,128)(2,1)S(1)} %collective-permute-done.refs_0_), channel_id=1, source_target_pairs={{0,12},{1,13},{2,14},{3,15},{4,0},{5,1},{6,2},{7,3},{8,4},{9,5},{1... | collective-permute-start | bytes 786440 | tf_op jit(solution)/shard_map/ppermute | solution.py:257
  34.5 15.7 %collective-permute-start.12 = (bf16[32,4096]{1,0:T(8,128)(2,1)S(1)}, bf16[32,4096]{1,0:T(8,128)(2,1)S(1)}, u32[]{:S(2)}, u32[]{:S(2)}) collective-permute-start(bf16[32,4096]{1,0:T(8,128)(2,1)S(1)} %get-tuple-element.32), channel_id=1, source_target_pairs={{0,2},{1,3},{2,0},{3,1},{4,6},{5,7},{6,4},{7,5},{8,10},{9,11},{10,... | collective-permute-start | bytes 786440 | tf_op jit(solution)/shard_map/ppermute | solution.py:257
  40.1 13.9 %collective-permute-start.1 = (bf16[32,4096]{1,0:T(8,128)(2,1)S(1)}, bf16[32,4096]{1,0:T(8,128)(2,1)S(1)}, u32[]{:S(2)}, u32[]{:S(2)}) collective-permute-start(bf16[32,4096]{1,0:T(8,128)(2,1)S(1)} %collective-permute-done.refs_0_), channel_id=1, source_target_pairs={{0,4},{1,5},{2,6},{3,7},{4,8},{5,9},{6,10},{7,11},{8,12},{9,13},{1... | collective-permute-start | bytes 786440 | tf_op jit(solution)/shard_map/ppermute | solution.py:257
  46.2 12.4 %collective-permute-start.3 = (bf16[32,4096]{1,0:T(8,128)(2,1)S(1)}, bf16[32,4096]{1,0:T(8,128)(2,1)S(1)}, u32[]{:S(2)}, u32[]{:S(2)}) collective-permute-start(bf16[32,4096]{1,0:T(8,128)(2,1)S(1)} %collective-permute-done.2.refs_2_), channel_id=1, source_target_pairs={{0,12},{1,13},{2,14},{3,15},{4,0},{5,1},{6,2},{7,3},{8,4},{9,5},{1... | collective-permute-start | bytes 786440 | tf_op jit(solution)/shard_map/ppermute | solution.py:257
  58.6 7.8 %collective-permute-start.14 = (bf16[32,4096]{1,0:T(8,128)(2,1)S(1)}, bf16[32,4096]{1,0:T(8,128)(2,1)S(1)}, u32[]{:S(2)}, u32[]{:S(2)}) collective-permute-start(bf16[32,4096]{1,0:T(8,128)(2,1)S(1)} %fence.1.refs_0_), channel_id=1, source_target_pairs={{0,12},{1,13},{2,14},{3,15},{4,0},{5,1},{6,2},{7,3},{8,4},{9,5},{1... | collective-permute-start | bytes 786440 | tf_op jit(solution)/shard_map/ppermute | solution.py:257
  60.4 23.8 %collective-permute-start.13 = (bf16[32,4096]{1,0:T(8,128)(2,1)S(1)}, bf16[32,4096]{1,0:T(8,128)(2,1)S(1)}, u32[]{:S(2)}, u32[]{:S(2)}) collective-permute-start(bf16[32,4096]{1,0:T(8,128)(2,1)S(1)} %fence.1.refs_0_), channel_id=1, source_target_pairs={{0,4},{1,5},{2,6},{3,7},{4,8},{5,9},{6,10},{7,11},{8,12},{9,13},{1... | collective-permute-start | bytes 786440 | tf_op jit(solution)/shard_map/ppermute | solution.py:257
  66.4 18.7 %collective-permute-start.15 = (bf16[32,4096]{1,0:T(8,128)(2,1)S(1)}, bf16[32,4096]{1,0:T(8,128)(2,1)S(1)}, u32[]{:S(2)}, u32[]{:S(2)}) collective-permute-start(bf16[32,4096]{1,0:T(8,128)(2,1)S(1)} %collective-permute-done.14.refs_2_), channel_id=1, source_target_pairs={{0,12},{1,13},{2,14},{3,15},{4,0},{5,1},{6,2},{7,3},{8,4},{9,5},{1... | collective-permute-start | bytes 786440 | tf_op jit(solution)/shard_map/ppermute | solution.py:257
  69.4 2.8 %copy-start = (bf16[768,1,4096]{2,0,1:T(8,128)(2,1)S(1)}, bf16[768,1,4096]{2,0,1:T(8,128)(2,1)}, u32[]{:S(2)}) copy-start(bf16[768,1,4096]{2,0,1:T(8,128)(2,1)} %param.7) | copy-start | bytes 18874372
  80.1 13.8 %collective-permute-start.5 = (bf16[128,768]{1,0:T(8,128)(2,1)S(1)}, bf16[128,768]{1,0:T(8,128)(2,1)S(1)}, u32[]{:S(2)}, u32[]{:S(2)}) collective-permute-start(bf16[128,768]{1,0:T(8,128)(2,1)S(1)} %get-tuple-element.24), channel_id=1, source_target_pairs={{0,32},{1,16},{2,34},{3,18},{4,36},{5,20},{6,38},{7,22},{8,40},{9,... | collective-permute-start | bytes 589832 | tf_op jit(solution)/shard_map/ppermute | solution.py:303
  83.3 14.9 %collective-permute-start.6 = (bf16[128,768]{1,0:T(8,128)(2,1)S(1)}, bf16[128,768]{1,0:T(8,128)(2,1)S(1)}, u32[]{:S(2)}, u32[]{:S(2)}) collective-permute-start(bf16[128,768]{1,0:T(8,128)(2,1)S(1)} %get-tuple-element.25), channel_id=1, source_target_pairs={{0,33},{1,17},{2,35},{3,19},{4,37},{5,21},{6,39},{7,23},{8,41},{9,... | collective-permute-start | bytes 589832 | tf_op jit(solution)/shard_map/ppermute | solution.py:303
  84.2 14.0 %collective-permute-start.7 = (bf16[128,768]{1,0:T(8,128)(2,1)S(1)}, bf16[128,768]{1,0:T(8,128)(2,1)S(1)}, u32[]{:S(2)}, u32[]{:S(2)}) collective-permute-start(bf16[128,768]{1,0:T(8,128)(2,1)S(1)} %get-tuple-element.26), channel_id=1, source_target_pairs={{0,1},{1,49},{2,3},{3,51},{4,5},{5,53},{6,7},{7,55},{8,9},{9,57},{... | collective-permute-start | bytes 589832 | tf_op jit(solution)/shard_map/ppermute | solution.py:303
  84.2 29.7 %copy-start.1 = (s32[768]{0:T(1024)S(1)}, s32[768]{0:T(1024)}, u32[]{:S(2)}) copy-start(s32[768]{0:T(1024)} %param.9) | copy-start | bytes 9220
  84.2 14.7 %collective-permute-start.8 = (bf16[128,768]{1,0:T(8,128)(2,1)S(1)}, bf16[128,768]{1,0:T(8,128)(2,1)S(1)}, u32[]{:S(2)}, u32[]{:S(2)}) collective-permute-start(bf16[128,768]{1,0:T(8,128)(2,1)S(1)} %get-tuple-element.27.own_ref), channel_id=1, source_target_pairs={{1,48},{3,50},{5,52},{7,54},{9,56},{11,58},{13,60},{15,62},{16,1},... | collective-permute-start | bytes 589832 | tf_op jit(solution)/shard_map/ppermute | solution.py:303
  93.0 8.1 %collective-permute-start.16 = (bf16[128,768]{1,0:T(8,128)(2,1)S(1)}, bf16[128,768]{1,0:T(8,128)(2,1)S(1)}, u32[]{:S(2)}, u32[]{:S(2)}) collective-permute-start(bf16[128,768]{1,0:T(8,128)(2,1)S(1)} %get-tuple-element.33), channel_id=1, source_target_pairs={{0,32},{1,16},{2,34},{3,18},{4,36},{5,20},{6,38},{7,22},{8,40},{9,... | collective-permute-start | bytes 589832 | tf_op jit(solution)/shard_map/ppermute | solution.py:303
  93.9 13.5 %collective-permute-start.17 = (bf16[128,768]{1,0:T(8,128)(2,1)S(1)}, bf16[128,768]{1,0:T(8,128)(2,1)S(1)}, u32[]{:S(2)}, u32[]{:S(2)}) collective-permute-start(bf16[128,768]{1,0:T(8,128)(2,1)S(1)} %get-tuple-element.34), channel_id=1, source_target_pairs={{0,33},{1,17},{2,35},{3,19},{4,37},{5,21},{6,39},{7,23},{8,41},{9,... | collective-permute-start | bytes 589832 | tf_op jit(solution)/shard_map/ppermute | solution.py:303
  98.2 9.4 %collective-permute-start.18 = (bf16[128,768]{1,0:T(8,128)(2,1)S(1)}, bf16[128,768]{1,0:T(8,128)(2,1)S(1)}, u32[]{:S(2)}, u32[]{:S(2)}) collective-permute-start(bf16[128,768]{1,0:T(8,128)(2,1)S(1)} %get-tuple-element.35), channel_id=1, source_target_pairs={{0,1},{1,49},{2,3},{3,51},{4,5},{5,53},{6,7},{7,55},{8,9},{9,57},{... | collective-permute-start | bytes 589832 | tf_op jit(solution)/shard_map/ppermute | solution.py:303
  98.2 9.4 %collective-permute-start.19 = (bf16[128,768]{1,0:T(8,128)(2,1)S(1)}, bf16[128,768]{1,0:T(8,128)(2,1)S(1)}, u32[]{:S(2)}, u32[]{:S(2)}) collective-permute-start(bf16[128,768]{1,0:T(8,128)(2,1)S(1)} %get-tuple-element.36.own_ref), channel_id=1, source_target_pairs={{1,48},{3,50},{5,52},{7,54},{9,56},{11,58},{13,60},{15,62},{16,1},... | collective-permute-start | bytes 589832 | tf_op jit(solution)/shard_map/ppermute | solution.py:303
  99.1 14.9 %collective-permute-start.9 = (bf16[32,768]{1,0:T(8,128)(2,1)S(1)}, bf16[32,768]{1,0:T(8,128)(2,1)S(1)}, u32[]{:S(2)}, u32[]{:S(2)}) collective-permute-start(bf16[32,768]{1,0:T(8,128)(2,1)S(1)} %get-tuple-element.29), channel_id=1, source_target_pairs={{0,64},{16,80},{32,96},{48,112},{64,128},{80,144},{96,160},{112,17... | collective-permute-start | bytes 147464 | tf_op jit(solution)/shard_map/ppermute | solution.py:324
  101.1 13.2 %collective-permute-start.10 = (bf16[32,768]{1,0:T(8,128)(2,1)S(1)}, bf16[32,768]{1,0:T(8,128)(2,1)S(1)}, u32[]{:S(2)}, u32[]{:S(2)}) collective-permute-start(bf16[32,768]{1,0:T(8,128)(2,1)S(1)} %get-tuple-element.30), channel_id=1, source_target_pairs={{0,128},{16,144},{32,160},{48,176},{64,192},{80,208},{96,224},{112... | collective-permute-start | bytes 147464 | tf_op jit(solution)/shard_map/ppermute | solution.py:324
  107.4 6.9 %collective-permute-start.11 = (bf16[32,768]{1,0:T(8,128)(2,1)S(1)}, bf16[32,768]{1,0:T(8,128)(2,1)S(1)}, u32[]{:S(2)}, u32[]{:S(2)}) collective-permute-start(bf16[32,768]{1,0:T(8,128)(2,1)S(1)} %get-tuple-element.31), channel_id=1, source_target_pairs={{0,192},{16,208},{32,224},{48,240},{64,0},{80,16},{96,32},{112,48}... | collective-permute-start | bytes 147464 | tf_op jit(solution)/shard_map/ppermute | solution.py:324
  107.7 6.9 %collective-permute-start.20 = (bf16[32,768]{1,0:T(8,128)(2,1)S(1)}, bf16[32,768]{1,0:T(8,128)(2,1)S(1)}, u32[]{:S(2)}, u32[]{:S(2)}) collective-permute-start(bf16[32,768]{1,0:T(8,128)(2,1)S(1)} %get-tuple-element.38), channel_id=1, source_target_pairs={{0,64},{16,80},{32,96},{48,112},{64,128},{80,144},{96,160},{112,17... | collective-permute-start | bytes 147464 | tf_op jit(solution)/shard_map/ppermute | solution.py:324
  109.7 6.8 %collective-permute-start.21 = (bf16[32,768]{1,0:T(8,128)(2,1)S(1)}, bf16[32,768]{1,0:T(8,128)(2,1)S(1)}, u32[]{:S(2)}, u32[]{:S(2)}) collective-permute-start(bf16[32,768]{1,0:T(8,128)(2,1)S(1)} %get-tuple-element.39), channel_id=1, source_target_pairs={{0,128},{16,144},{32,160},{48,176},{64,192},{80,208},{96,224},{112... | collective-permute-start | bytes 147464 | tf_op jit(solution)/shard_map/ppermute | solution.py:324
  113.9 4.1 %collective-permute-start.22 = (bf16[32,768]{1,0:T(8,128)(2,1)S(1)}, bf16[32,768]{1,0:T(8,128)(2,1)S(1)}, u32[]{:S(2)}, u32[]{:S(2)}) collective-permute-start(bf16[32,768]{1,0:T(8,128)(2,1)S(1)} %get-tuple-element.40), channel_id=1, source_target_pairs={{0,192},{16,208},{32,224},{48,240},{64,0},{80,16},{96,32},{112,48}... | collective-permute-start | bytes 147464 | tf_op jit(solution)/shard_map/ppermute | solution.py:324
Sparse Core Ops, SparseCore 0:
  12.5 45.3 all-gather.1

commit v2 on v1

--- a/solution.py
+++ b/solution.py
@@ -41,12 +41,7 @@
     return store % 4, store // 4, group // 4, (group // 2) % 2, group % 2
 
 
-def grad_kernel(chunk, *refs):
-    lengths_hbm, acts_hbm, grads_hbm, *earlier = refs[: 3 + chunk]
-    out_ref, *whole = refs[3 + chunk : -5]
-    acts_ref, grads_ref, lengths_ref, wide_ref, sems = refs[-5:]
-    first = chunk * ROWS
-
+def grad_kernel(first, lengths_hbm, acts_hbm, grads_hbm, out_ref, acts_ref, grads_ref, lengths_ref, wide_ref, sems):
     def copies(n):
         src, dst = pl.ds(first + n * STEP_PAIRS, STEP_PAIRS), pl.ds(n * STEP_PAIRS, STEP_PAIRS)
         return (
@@ -79,20 +74,14 @@
         even = wide_ref[pl.ds(2 * c, ROWS, stride=PITCH), :]
         odd = wide_ref[pl.ds(2 * c + 1, ROWS, stride=PITCH), :]
         out_ref[:, c * 128 : (c + 1) * 128] = jnp.where(low, even, odd).astype(BF16)
-    for whole_ref in whole:
-        for n, piece in enumerate((*earlier, out_ref)):
-            whole_ref[n * ROWS : (n + 1) * ROWS, :] = piece[...]
-
-
-def query_grads(lengths, activations, out_grads, earlier):
-    chunk = len(earlier)
-    last = chunk == CHUNKS - 1
+
+
+def query_grads(lengths, activations, out_grads, chunk):
     hbm = pl.BlockSpec(memory_space=pltpu.HBM)
     return pl.pallas_call(
-        functools.partial(grad_kernel, chunk),
-        out_shape=[jax.ShapeDtypeStruct((ROWS, FEATURES), BF16)]
-        + [jax.ShapeDtypeStruct((PAIRS, FEATURES), BF16)] * last,
-        in_specs=[hbm] * 3 + [pl.BlockSpec(memory_space=pltpu.VMEM)] * chunk,
+        functools.partial(grad_kernel, chunk * ROWS),
+        out_shape=jax.ShapeDtypeStruct((ROWS, FEATURES), BF16),
+        in_specs=[hbm] * 3,
         scratch_shapes=[
             pltpu.VMEM((ROWS, WIDTH, SLOTS), BF16),
             pltpu.VMEM((ROWS, WIDTH, SLOTS), BF16),
@@ -101,23 +90,30 @@
             pltpu.SemaphoreType.DMA((2 * (ROWS // STEP_PAIRS) + 1,)),
         ],
         compiler_params=pltpu.CompilerParams(vmem_limit_bytes=16 << 20),
-        cost_estimate=pl.CostEstimate(
-            flops=chunk * 8 * FEATURES * SLOTS * PAIRS * ROWS, bytes_accessed=0, transcendentals=0
-        ),
         name="query_grads",
-    )(lengths, activations, out_grads, *earlier)
-
-
-def score_kernel(own_ref, *refs):
-    blocks, (mine_ref, other_ref), outs = refs[:4], refs[4:6], refs[6:]
+    )(lengths, activations, out_grads)
+
+
+def score_kernel(*refs):
+    blocks, (mine_ref, other_ref), outs = refs[:8], refs[8:10], refs[10:14]
+    rows_ref, sem = refs[14:]
     step = pl.program_id(0)
     x, _, y, z_hi, core = place()
 
+    @pl.when(step == 0)
+    def _():
+        copies = [
+            pltpu.make_async_copy(block, rows_ref.at[pl.ds(i * ROWS, ROWS)], sem.at[i])
+            for i, block in enumerate(blocks)
+        ]
+        for copy in copies:
+            copy.start()
+        for copy in copies:
+            copy.wait()
+
     def part(weights_ref, rel_core, tile):
         got = lax.dot_general(
-            jnp.concatenate(
-                [own_ref[...].reshape(4 * ROWS, FEATURES)] + [b[...] for b in blocks], axis=0
-            ),
+            rows_ref[...],
             weights_ref[...],
             (((1,), (1,)), ((), ())),
             preferred_element_type=F32,
@@ -133,14 +129,10 @@
 
                 @pl.when(buf == b)
                 def _():
-                    cols = slice(tile * COLS, (tile + 1) * COLS)
-                    if rel_z == 0:
-                        outs[b][:, cols] = got[: 4 * ROWS]
-                    else:
-                        for j, dy in enumerate((0, 3, 1, 2)):
-                            row = pl.multiple_of(((y + dy) % 4) * ROWS, ROWS)
-                            at = (4 + j) * ROWS
-                            outs[b][pl.ds(row, ROWS), cols] = got[at : at + ROWS]
+                    for j, dy in enumerate((0, 3, 1, 2)):
+                        row = pl.multiple_of(((y + dy) % 4) * ROWS, ROWS)
+                        at = (rel_z * 4 + j) * ROWS
+                        outs[b][pl.ds(row, ROWS), tile * COLS : (tile + 1) * COLS] = got[at : at + ROWS]
 
     tiles = HELD // COLS
     for s in range(2 * tiles):
@@ -150,29 +142,27 @@
             part(mine_ref if s < tiles else other_ref, s // tiles, s % tiles)
 
 
-def partial_scores(own, fars, mine, other, chunk):
+def partial_scores(blocks, mine, other):
     tiles = HELD // COLS
-    whole = pl.BlockSpec((ROWS, FEATURES), lambda i: (0, 0))
     out = pl.BlockSpec((4 * ROWS, HELD), lambda i: (0, 0))
     return pl.pallas_call(
         score_kernel,
         out_shape=[jax.ShapeDtypeStruct((4 * ROWS, HELD), BF16)] * 4,
         grid=(2 * tiles,),
-        in_specs=[pl.BlockSpec((4, ROWS, FEATURES), lambda i: (0, chunk, 0))]
-        + [whole] * 4
+        in_specs=[pl.BlockSpec(memory_space=pl.ANY)] * 8
         + [
             pl.BlockSpec((COLS, FEATURES), lambda i: (jnp.minimum(i, tiles - 1), 0)),
             pl.BlockSpec((COLS, FEATURES), lambda i: (jnp.maximum(i - tiles, 0), 0)),
         ],
         out_specs=[out] * 4,
-        compiler_params=pltpu.CompilerParams(vmem_limit_bytes=24 << 20),
-        cost_estimate=pl.CostEstimate(
-            flops=2 * 8 * ROWS * FEATURES * 2 * HELD,
-            bytes_accessed=2 * FEATURES * (2 * HELD + 8 * ROWS),
-            transcendentals=0,
-        ),
+        scratch_shapes=[
+            pltpu.VMEM((8 * ROWS, FEATURES), BF16),
+            pltpu.SemaphoreType.DMA((8,)),
+        ],
+        compiler_params=pltpu.CompilerParams(vmem_limit_bytes=18 << 20),
+        cost_estimate=pl.CostEstimate(flops=1, bytes_accessed=1, transcendentals=0),
         name="partial_scores",
-    )(own, *fars, mine, other)
+    )(*blocks, mine, other)
 
 
 def cross_sum_kernel(a_ref, b_ref, c_ref, d_ref, own_ref, keep_ref, *outs):
@@ -261,33 +251,49 @@
     pass
 
 
-def after(value, *others):
+def after(values, *others):
     hold = pl.BlockSpec(memory_space=pl.ANY)
     return pl.pallas_call(
         fence_kernel,
-        out_shape=jax.ShapeDtypeStruct(value.shape, value.dtype),
-        in_specs=[hold] * (1 + len(others)),
-        out_specs=hold,
-        input_output_aliases={0: 0},
+        out_shape=[jax.ShapeDtypeStruct(v.shape, v.dtype) for v in values],
+        in_specs=[hold] * (len(values) + len(others)),
+        out_specs=[hold] * len(values),
+        input_output_aliases={i: i for i in range(len(values))},
         compiler_params=pltpu.CompilerParams(vmem_limit_bytes=1 << 20),
         name="fence",
-    )(value, *others)
-
-
-def far_blocks(value, earlier):
-    far = along(value, lambda y, z, c: (y, z + 1, c))
-    if earlier:
-        far = after(far, *earlier)
-    above = along(far, lambda y, z, c: (y - 1, z, c))
-    below = along(far, lambda y, z, c: (y + 1, z, c))
-    opposite = along(above, lambda y, z, c: (y - 1, z, c))
-    return [far, below, above, opposite]
-
-
-def own_blocks(value):
-    groups = [[(y * 2 + z) * 2 + c for y in range(4)] for z in range(2) for c in range(2)]
-    got = lax.all_gather(value, "group", axis=0, tiled=True, axis_index_groups=groups)
-    return pltpu.with_memory_space_constraint(got.reshape(4, PAIRS, FEATURES), pltpu.HBM)
+    )(*values, *others)
+
+
+def up(value):
+    return along(value, lambda y, z, c: (y + 1, z, c))
+
+
+def down(value):
+    return along(value, lambda y, z, c: (y - 1, z, c))
+
+
+def beyond(value):
+    return along(value, lambda y, z, c: (y, z + 1, c))
+
+
+def gather_blocks(a, b, other):
+    far_a = beyond(a)
+    a_below, a_above = up(a), down(a)
+    (b,) = after((b,), other)
+    far_b = beyond(b)
+    b_below, b_above = up(b), down(b)
+    far_a, a_below = after((far_a, a_below), a_above, b_below, b_above)
+    far_a_above, far_a_below = down(far_a), up(far_a)
+    a_opposite = up(a_below)
+    far_a_opposite = down(far_a_above)
+    far_b, b_below = after((far_b, b_below), a_opposite, far_a_opposite, far_a_below)
+    b_opposite = up(b_below)
+    far_b_above, far_b_below = down(far_b), up(far_b)
+    far_b_opposite = down(far_b_above)
+    return (
+        [a, a_below, a_above, a_opposite, far_a, far_a_below, far_a_above, far_a_opposite],
+        [b, b_below, b_above, b_opposite, far_b, far_b_below, far_b_above, far_b_opposite],
+    )
 
 
 def over_x(bufs):
@@ -310,15 +316,16 @@
     inputs = [
         pltpu.with_memory_space_constraint(v, pltpu.HBM) for v in (lengths, activations, out_grads)
     ]
-    (a,) = query_grads(*inputs, ())
-    b, both = query_grads(*inputs, (a,))
-    own = own_blocks(both)
-    parts = []
-    far_a = far_blocks(a, ())
-    far_b = far_blocks(b, far_a[1:])
-    for n, fars in enumerate([far_a, far_b]):
-        bufs = partial_scores(own, fars, stored, other, n)
-        keep, *sends = cross_sum(*over_x(bufs), bufs[3])
+    a, b = (query_grads(*inputs, n) for n in range(CHUNKS))
+    parts, got = [], ()
+    a_blocks, b_blocks = gather_blocks(a, b, other)
+    for blocks in (a_blocks, b_blocks):
+        blocks[-1:] = after(blocks[-1:], *got) if got else blocks[-1:]
+        bufs = list(partial_scores(blocks, stored, other))
+        if not got:
+            bufs[1:2] = after(bufs[1:2], b_blocks[3], b_blocks[5])
+        got = over_x(bufs)
+        keep, *sends = cross_sum(*got, bufs[3])
         parts.append(keep)
         for k, send in enumerate(sends, 1):
             parts.append(lax.ppermute(send, "store", store_pairs(lambda x, z: (x, z + k))))

time: 126 us -> 99 us (0.79)
  between operations: 13.5 us -> 0.16 us
  waiting for transfers between devices: 41.4 us -> 34.1 us
  Pallas kernels: 23.1 us -> 17.4 us
  local copies, waits for them, and re-layouts: 2.79 us -> 0.02 us
  starting transfers between devices: 44.7 us -> 46.8 us
    ppermute x8 -> x14, waiting for transfers between devices: 33.3 us -> 20.6 us  [along(): return lax.ppermute(value, 'group', group_pairs(move))]
    ppermute x8, waiting for transfers between devices: 4.47 us -> 10.9 us  [over_x(): lax.ppermute(b, ('store', 'group'), all_pairs(m))]
    pallas_call x2, Pallas kernels: 15.9 us -> 10.9 us  [partial_scores(): pl.pallas_call(score_kernel, out_shape=[jax.ShapeDtypeStruct((4 * ROWS, H...]
    ppermute x6, starting transfers between devices: 10.3 us -> 5.82 us  [on_device(): lax.ppermute(send, 'store', store_pairs(lambda x, z: (x, z + k)))]
    ppermute x8 -> x14, starting transfers between devices: 23.7 us -> 27.1 us  [along(): return lax.ppermute(value, 'group', group_pairs(move))]
    ppermute x8, starting transfers between devices: 10.8 us -> 13.9 us  [over_x(): lax.ppermute(b, ('store', 'group'), all_pairs(m))]
    unnamed x4 -> x6, local copies, waits for them, and re-layouts: 2.79 us -> 0.02 us
    pallas_call x3 -> x7, Pallas kernels: 5.84 us -> 5.13 us  [the longest x2 5.12 us: query_grads(): pl.pallas_call(functools.partial(grad_kernel, chunk * ROWS), out_shape=ja...]
  transfers between devices with their start and end apart: 24 -> 29, of which waited for: 11 -> 13; matrix products, arithmetic and copies ran while one was open for 0% -> 0% of each run, Pallas kernels for 17% -> 11%
where the time goes in v2:
time: 99 us; the launch traced here: 98.9 us
  starting transfers between devices  46.8 us (47%)
  waiting for transfers between devices  34.1 us (34%)
  Pallas kernels  17.4 us (18%)
    ppermute x14, starting transfers between devices, along(): return lax.ppermute(value, 'group', group_pairs(move))  27.1 us
    ppermute x14, waiting for transfers between devices, along(): return lax.ppermute(value, 'group', group_pairs(move))  20.6 us
    ppermute x8, starting transfers between devices, over_x(): lax.ppermute(b, ('store', 'group'), all_pairs(m))  13.9 us
    pallas_call x2, Pallas kernels, partial_scores(): pl.pallas_call(score_kernel, out_shape=[jax.ShapeDtypeStruct((4 * ROWS, H...  10.9 us
    ppermute x8, waiting for transfers between devices, over_x(): lax.ppermute(b, ('store', 'group'), all_pairs(m))  10.9 us
    ppermute x6, starting transfers between devices, on_device(): lax.ppermute(send, 'store', store_pairs(lambda x, z: (x, z + k)))  5.82 us
    pallas_call x2, Pallas kernels, query_grads(): pl.pallas_call(functools.partial(grad_kernel, chunk * ROWS), out_shape=ja...  5.12 us
    ppermute x6, waiting for transfers between devices, on_device(): lax.ppermute(send, 'store', store_pairs(lambda x, z: (x, z + k)))  2.67 us
  transfers between devices with their start and end apart: 29, of which 13 were waited for; matrix products, arithmetic and copies ran while one was open for 0% of the time, Pallas kernels for 11%

profile of v2, /device:TPU:32, one launch (start us, length us, event | category | flops | bytes accessed | tf_op | source)
XLA Modules:
  0.0 98.9 jit_solution(14489959732415765488)
XLA Ops:
  0.0 2.5 %query_grads.2.refs_0_ = bf16[32,4096]{1,0:T(8,128)(2,1)S(1)} custom-call(s32[64]{0:T(128)} %lengths_hbm.3, bf16[64,1,64,256]{3,2,1,0:T(8,128)(2,1)} %acts_hbm.3, bf16[64,1,64,256]{3,2,1,0:T(8,128)(2,1)} %grads_hbm.3), custom_call_target="tpu_custom_call" | custom-call | tf_op jit(solution)/shard_map/query_grads/pallas_call | solution.py:81
  2.5 6.3 %collective-permute-start = (bf16[32,4096]{1,0:T(8,128)(2,1)S(1)}, bf16[32,4096]{1,0:T(8,128)(2,1)S(1)}, u32[]{:S(2)}, u32[]{:S(2)}) collective-permute-start(bf16[32,4096]{1,0:T(8,128)(2,1)S(1)} %query_grads.2.refs_0_), channel_id=1, source_target_pairs={{0,2},{1,3},{2,0},{3,1},{4,6},{5,7},{6,4},{7,5},{8,10},{9,11},{10,... | collective-permute-start | bytes 786440 | tf_op jit(solution)/shard_map/ppermute | solution.py:247
  8.9 1.6 %collective-permute-start.1 = (bf16[32,4096]{1,0:T(8,128)(2,1)S(1)}, bf16[32,4096]{1,0:T(8,128)(2,1)S(1)}, u32[]{:S(2)}, u32[]{:S(2)}) collective-permute-start(bf16[32,4096]{1,0:T(8,128)(2,1)S(1)} %query_grads.2.refs_0_), channel_id=1, source_target_pairs={{0,4},{1,5},{2,6},{3,7},{4,8},{5,9},{6,10},{7,11},{8,12},{9,13},{1... | collective-permute-start | bytes 786440 | tf_op jit(solution)/shard_map/ppermute | solution.py:247
  10.4 1.7 %collective-permute-start.2 = (bf16[32,4096]{1,0:T(8,128)(2,1)S(1)}, bf16[32,4096]{1,0:T(8,128)(2,1)S(1)}, u32[]{:S(2)}, u32[]{:S(2)}) collective-permute-start(bf16[32,4096]{1,0:T(8,128)(2,1)S(1)} %query_grads.2.refs_0_), channel_id=1, source_target_pairs={{0,12},{1,13},{2,14},{3,15},{4,0},{5,1},{6,2},{7,3},{8,4},{9,5},{1... | collective-permute-start | bytes 786440 | tf_op jit(solution)/shard_map/ppermute | solution.py:247
  12.1 2.6 %query_grads.3.refs_0_ = bf16[32,4096]{1,0:T(8,128)(2,1)S(1)} custom-call(s32[64]{0:T(128)} %lengths_hbm.3, bf16[64,1,64,256]{3,2,1,0:T(8,128)(2,1)} %acts_hbm.3, bf16[64,1,64,256]{3,2,1,0:T(8,128)(2,1)} %grads_hbm.3), custom_call_target="tpu_custom_call" | custom-call | tf_op jit(solution)/shard_map/query_grads/pallas_call | solution.py:81
  15.2 2.9 %collective-permute-start.5 = (bf16[32,4096]{1,0:T(8,128)(2,1)S(1)}, bf16[32,4096]{1,0:T(8,128)(2,1)S(1)}, u32[]{:S(2)}, u32[]{:S(2)}) collective-permute-start(bf16[32,4096]{1,0:T(8,128)(2,1)S(1)} %fence.5.refs_0_), channel_id=1, source_target_pairs={{0,12},{1,13},{2,14},{3,15},{4,0},{5,1},{6,2},{7,3},{8,4},{9,5},{1... | collective-permute-start | bytes 786440 | tf_op jit(solution)/shard_map/ppermute | solution.py:247
  18.1 3.5 %collective-permute-done.refs_0_ = bf16[32,4096]{1,0:T(8,128)(2,1)S(1)} collective-permute-done((bf16[32,4096]{1,0:T(8,128)(2,1)S(1)}, bf16[32,4096]{1,0:T(8,128)(2,1)S(1)}, u32[]{:S(2)}, u32[]{:S(2)}) %collective-permute-start) | collective-permute-done | bytes 262176 | tf_op jit(solution)/shard_map/ppermute | solution.py:247
  21.6 2.6 %collective-permute-done.4.refs_3_.refs_1_ = bf16[32,4096]{1,0:T(8,128)(2,1)S(1)} collective-permute-done((bf16[32,4096]{1,0:T(8,128)(2,1)S(1)}, bf16[32,4096]{1,0:T(8,128)(2,1)S(1)}, u32[]{:S(2)}, u32[]{:S(2)}) %collective-permute-start.4) | collective-permute-done | bytes 262176 | tf_op jit(solution)/shard_map/ppermute | solution.py:247
  24.2 2.9 %collective-permute-start.8 = (bf16[32,4096]{1,0:T(8,128)(2,1)S(1)}, bf16[32,4096]{1,0:T(8,128)(2,1)S(1)}, u32[]{:S(2)}, u32[]{:S(2)}) collective-permute-start(bf16[32,4096]{1,0:T(8,128)(2,1)S(1)} %get-tuple-element.26.refs_4_), channel_id=1, source_target_pairs={{0,12},{1,13},{2,14},{3,15},{4,0},{5,1},{6,2},{7,3},{8,4},{9,5},{1... | collective-permute-start | bytes 786440 | tf_op jit(solution)/shard_map/ppermute | solution.py:247
  27.2 3.1 %collective-permute-start.11 = (bf16[32,4096]{1,0:T(8,128)(2,1)S(1)}, bf16[32,4096]{1,0:T(8,128)(2,1)S(1)}, u32[]{:S(2)}, u32[]{:S(2)}) collective-permute-start(bf16[32,4096]{1,0:T(8,128)(2,1)S(1)} %fence.5.refs_0_), channel_id=1, source_target_pairs={{0,2},{1,3},{2,0},{3,1},{4,6},{5,7},{6,4},{7,5},{8,10},{9,11},{10,... | collective-permute-start | bytes 786440 | tf_op jit(solution)/shard_map/ppermute | solution.py:247
  30.8 0.8 collective-permute-done.8.refs_6_
  31.6 3.7 %collective-permute-start.9 = (bf16[32,4096]{1,0:T(8,128)(2,1)S(1)}, bf16[32,4096]{1,0:T(8,128)(2,1)S(1)}, u32[]{:S(2)}, u32[]{:S(2)}) collective-permute-start(bf16[32,4096]{1,0:T(8,128)(2,1)S(1)} %collective-permute-done.8.refs_6_), channel_id=1, source_target_pairs={{0,12},{1,13},{2,14},{3,15},{4,0},{5,1},{6,2},{7,3},{8,4},{9,5},{1... | collective-permute-start | bytes 786440 | tf_op jit(solution)/shard_map/ppermute | solution.py:247
  35.3 8.0 %collective-permute-done.11.refs_0_ = bf16[32,4096]{1,0:T(8,128)(2,1)S(1)} collective-permute-done((bf16[32,4096]{1,0:T(8,128)(2,1)S(1)}, bf16[32,4096]{1,0:T(8,128)(2,1)S(1)}, u32[]{:S(2)}, u32[]{:S(2)}) %collective-permute-start.11) | collective-permute-done | bytes 262176 | tf_op jit(solution)/shard_map/ppermute | solution.py:247
  43.4 1.1 %collective-permute-done.6.refs_3_.refs_2_ = bf16[32,4096]{1,0:T(8,128)(2,1)S(1)} collective-permute-done((bf16[32,4096]{1,0:T(8,128)(2,1)S(1)}, bf16[32,4096]{1,0:T(8,128)(2,1)S(1)}, u32[]{:S(2)}, u32[]{:S(2)}) %collective-permute-start.6) | collective-permute-done | bytes 262176 | tf_op jit(solution)/shard_map/ppermute | solution.py:247
  44.6 2.0 %collective-permute-start.12 = (bf16[32,4096]{1,0:T(8,128)(2,1)S(1)}, bf16[32,4096]{1,0:T(8,128)(2,1)S(1)}, u32[]{:S(2)}, u32[]{:S(2)}) collective-permute-start(bf16[32,4096]{1,0:T(8,128)(2,1)S(1)} %get-tuple-element.29.refs_1_), channel_id=1, source_target_pairs={{0,4},{1,5},{2,6},{3,7},{4,8},{5,9},{6,10},{7,11},{8,12},{9,13},{1... | collective-permute-start | bytes 786440 | tf_op jit(solution)/shard_map/ppermute | solution.py:247
  46.6 4.4 %collective-permute-done.20.refs_6_ = bf16[32,4096]{1,0:T(8,128)(2,1)S(1)} collective-permute-done((bf16[32,4096]{1,0:T(8,128)(2,1)S(1)}, bf16[32,4096]{1,0:T(8,128)(2,1)S(1)}, u32[]{:S(2)}, u32[]{:S(2)}) %collective-permute-start.20) | collective-permute-done | bytes 262176 | tf_op jit(solution)/shard_map/ppermute | solution.py:247
  51.1 1.8 %collective-permute-start.21 = (bf16[32,4096]{1,0:T(8,128)(2,1)S(1)}, bf16[32,4096]{1,0:T(8,128)(2,1)S(1)}, u32[]{:S(2)}, u32[]{:S(2)}) collective-permute-start(bf16[32,4096]{1,0:T(8,128)(2,1)S(1)} %collective-permute-done.20.refs_6_), channel_id=1, source_target_pairs={{0,12},{1,13},{2,14},{3,15},{4,0},{5,1},{6,2},{7,3},{8,4},{9,5},{1... | collective-permute-start | bytes 786440 | tf_op jit(solution)/shard_map/ppermute | solution.py:247
  52.9 5.4 %partial_scores.2 = (bf16[128,768]{1,0:T(8,128)(2,1)S(1)}, bf16[128,768]{1,0:T(8,128)(2,1)S(1)}, bf16[128,768]{1,0:T(8,128)(2,1)S(1)}, bf16[128,768]{1,0:T(8,128)(2,1)S(1)}) custom-call(bf16[32,4096]{1,0:T(8,128)(2,1)S(1)} %query_grads.2.refs_0_, bf16[32,4096]{1,0:T(8,128)(2,1)S(1)} %get-tuple-element.25.refs_1_, ...), custom_call_target="tpu_custom_call" | custom-call | flops 1 | bytes 1 | tf_op jit(solution)/shard_map/partial_scores/pallas_call | solution.py:148
  58.3 3.0 %collective-permute-start.10 = (bf16[128,768]{1,0:T(8,128)(2,1)S(1)}, bf16[128,768]{1,0:T(8,128)(2,1)S(1)}, u32[]{:S(2)}, u32[]{:S(2)}) collective-permute-start(bf16[128,768]{1,0:T(8,128)(2,1)S(1)} %get-tuple-element.27), channel_id=1, source_target_pairs={{0,32},{1,16},{2,34},{3,18},{4,36},{5,20},{6,38},{7,22},{8,40},{9,... | collective-permute-start | bytes 589832 | tf_op jit(solution)/shard_map/ppermute | solution.py:309
  62.0 5.1 %collective-permute-start.14 = (bf16[128,768]{1,0:T(8,128)(2,1)S(1)}, bf16[128,768]{1,0:T(8,128)(2,1)S(1)}, u32[]{:S(2)}, u32[]{:S(2)}) collective-permute-start(bf16[128,768]{1,0:T(8,128)(2,1)S(1)} %fence.8), channel_id=1, source_target_pairs={{0,33},{1,17},{2,35},{3,19},{4,37},{5,21},{6,39},{7,23},{8,41},{9,... | collective-permute-start | bytes 589832 | tf_op jit(solution)/shard_map/ppermute | solution.py:309
  67.7 2.6 %collective-permute-done.14.b_ref.refs_2_ = bf16[128,768]{1,0:T(8,128)(2,1)S(1)} collective-permute-done((bf16[128,768]{1,0:T(8,128)(2,1)S(1)}, bf16[128,768]{1,0:T(8,128)(2,1)S(1)}, u32[]{:S(2)}, u32[]{:S(2)}) %collective-permute-start.14) | collective-permute-done | bytes 196640 | tf_op jit(solution)/shard_map/ppermute | solution.py:309
  70.4 5.4 %partial_scores.3 = (bf16[128,768]{1,0:T(8,128)(2,1)S(1)}, bf16[128,768]{1,0:T(8,128)(2,1)S(1)}, bf16[128,768]{1,0:T(8,128)(2,1)S(1)}, bf16[128,768]{1,0:T(8,128)(2,1)S(1)}) custom-call(bf16[32,4096]{1,0:T(8,128)(2,1)S(1)} %fence.5.refs_0_, bf16[32,4096]{1,0:T(8,128)(2,1)S(1)} %get-tuple-element.29.refs_1_, ...), custom_call_target="tpu_custom_call" | custom-call | flops 1 | bytes 1 | tf_op jit(solution)/shard_map/partial_scores/pallas_call | solution.py:148
  75.8 1.9 %collective-permute-start.22 = (bf16[128,768]{1,0:T(8,128)(2,1)S(1)}, bf16[128,768]{1,0:T(8,128)(2,1)S(1)}, u32[]{:S(2)}, u32[]{:S(2)}) collective-permute-start(bf16[128,768]{1,0:T(8,128)(2,1)S(1)} %get-tuple-element.37), channel_id=1, source_target_pairs={{0,32},{1,16},{2,34},{3,18},{4,36},{5,20},{6,38},{7,22},{8,40},{9,... | collective-permute-start | bytes 589832 | tf_op jit(solution)/shard_map/ppermute | solution.py:309
  77.7 2.5 %collective-permute-start.23 = (bf16[128,768]{1,0:T(8,128)(2,1)S(1)}, bf16[128,768]{1,0:T(8,128)(2,1)S(1)}, u32[]{:S(2)}, u32[]{:S(2)}) collective-permute-start(bf16[128,768]{1,0:T(8,128)(2,1)S(1)} %get-tuple-element.38), channel_id=1, source_target_pairs={{0,33},{1,17},{2,35},{3,19},{4,37},{5,21},{6,39},{7,23},{8,41},{9,... | collective-permute-start | bytes 589832 | tf_op jit(solution)/shard_map/ppermute | solution.py:309
  81.0 1.2 %collective-permute-start.17 = (bf16[32,768]{1,0:T(8,128)(2,1)S(1)}, bf16[32,768]{1,0:T(8,128)(2,1)S(1)}, u32[]{:S(2)}, u32[]{:S(2)}) collective-permute-start(bf16[32,768]{1,0:T(8,128)(2,1)S(1)} %get-tuple-element.34), channel_id=1, source_target_pairs={{0,64},{16,80},{32,96},{48,112},{64,128},{80,144},{96,160},{112,17... | collective-permute-start | bytes 147464 | tf_op jit(solution)/shard_map/ppermute | solution.py:331
  82.2 2.5 %collective-permute-done.22.a_ref = bf16[128,768]{1,0:T(8,128)(2,1)S(1)} collective-permute-done((bf16[128,768]{1,0:T(8,128)(2,1)S(1)}, bf16[128,768]{1,0:T(8,128)(2,1)S(1)}, u32[]{:S(2)}, u32[]{:S(2)}) %collective-permute-start.22) | collective-permute-done | bytes 196640 | tf_op jit(solution)/shard_map/ppermute | solution.py:309
  84.8 5.1 %collective-permute-done.23.b_ref = bf16[128,768]{1,0:T(8,128)(2,1)S(1)} collective-permute-done((bf16[128,768]{1,0:T(8,128)(2,1)S(1)}, bf16[128,768]{1,0:T(8,128)(2,1)S(1)}, u32[]{:S(2)}, u32[]{:S(2)}) %collective-permute-start.23) | collective-permute-done | bytes 196640 | tf_op jit(solution)/shard_map/ppermute | solution.py:309
  90.1 2.1 %collective-permute-start.26 = (bf16[32,768]{1,0:T(8,128)(2,1)S(1)}, bf16[32,768]{1,0:T(8,128)(2,1)S(1)}, u32[]{:S(2)}, u32[]{:S(2)}) collective-permute-start(bf16[32,768]{1,0:T(8,128)(2,1)S(1)} %get-tuple-element.42), channel_id=1, source_target_pairs={{0,64},{16,80},{32,96},{48,112},{64,128},{80,144},{96,160},{112,17... | collective-permute-start | bytes 147464 | tf_op jit(solution)/shard_map/ppermute | solution.py:331
  92.1 0.8 collective-permute-start.27
  93.0 1.7 %collective-permute-start.28 = (bf16[32,768]{1,0:T(8,128)(2,1)S(1)}, bf16[32,768]{1,0:T(8,128)(2,1)S(1)}, u32[]{:S(2)}, u32[]{:S(2)}) collective-permute-start(bf16[32,768]{1,0:T(8,128)(2,1)S(1)} %get-tuple-element.44), channel_id=1, source_target_pairs={{0,192},{16,208},{32,224},{48,240},{64,0},{80,16},{96,32},{112,48}... | collective-permute-start | bytes 147464 | tf_op jit(solution)/shard_map/ppermute | solution.py:331
  95.8 1.4 %collective-permute-done.27.refs_6_ = bf16[32,768]{1,0:T(8,128)(2,1)S(1)} collective-permute-done((bf16[32,768]{1,0:T(8,128)(2,1)S(1)}, bf16[32,768]{1,0:T(8,128)(2,1)S(1)}, u32[]{:S(2)}, u32[]{:S(2)}) %collective-permute-start.27) | collective-permute-done | bytes 49184 | tf_op jit(solution)/shard_map/ppermute | solution.py:331
  97.8 1.1 %final_sum.1 = f32[64,768]{1,0:T(8,128)} custom-call(f32[32,768]{1,0:T(8,128)S(1)} %get-tuple-element.33.refs_0_, bf16[32,768]{1,0:T(8,128)(2,1)S(1)} %collective-permute-done.17.refs_1_, bf16[32,768]{1,0:T(8,128)(2,1)S(1)} %collective-permute-done.18.refs_2_, bf16[32,768]{1,0:T(8,128)(2,1)S(1)} %collective-permute-done.19.refs_3_, ...), custom_call_target="tpu_custom_call" | custom-call | tf_op jit(solution)/shard_map/final_sum/pallas_call | solution.py:214
  (46 shorter events, 5.0 us)
Async XLA Ops:
  0.0 14.8 %collective-permute-start.3 = (bf16[768,4096]{1,0:T(8,128)(2,1)}, bf16[768,4096]{1,0:T(8,128)(2,1)S(1)}, u32[]{:S(2)}, u32[]{:S(2)}) collective-permute-start(bf16[768,4096]{1,0:T(8,128)(2,1)} %bitcast.1), channel_id=1, source_target_pairs={{0,1},{1,0},{2,3},{3,2},{4,5},{5,4},{6,7},{7,6},{8,9},{9,8},{10,11... | collective-permute-start | bytes 18874376 | tf_op jit(solution)/shard_map/ppermute | solution.py:314
  2.5 19.1 %collective-permute-start = (bf16[32,4096]{1,0:T(8,128)(2,1)S(1)}, bf16[32,4096]{1,0:T(8,128)(2,1)S(1)}, u32[]{:S(2)}, u32[]{:S(2)}) collective-permute-start(bf16[32,4096]{1,0:T(8,128)(2,1)S(1)} %query_grads.2.refs_0_), channel_id=1, source_target_pairs={{0,2},{1,3},{2,0},{3,1},{4,6},{5,7},{6,4},{7,5},{8,10},{9,11},{10,... | collective-permute-start | bytes 786440 | tf_op jit(solution)/shard_map/ppermute | solution.py:247
  8.9 12.7 %collective-permute-start.1 = (bf16[32,4096]{1,0:T(8,128)(2,1)S(1)}, bf16[32,4096]{1,0:T(8,128)(2,1)S(1)}, u32[]{:S(2)}, u32[]{:S(2)}) collective-permute-start(bf16[32,4096]{1,0:T(8,128)(2,1)S(1)} %query_grads.2.refs_0_), channel_id=1, source_target_pairs={{0,4},{1,5},{2,6},{3,7},{4,8},{5,9},{6,10},{7,11},{8,12},{9,13},{1... | collective-permute-start | bytes 786440 | tf_op jit(solution)/shard_map/ppermute | solution.py:247
  10.4 11.1 %collective-permute-start.2 = (bf16[32,4096]{1,0:T(8,128)(2,1)S(1)}, bf16[32,4096]{1,0:T(8,128)(2,1)S(1)}, u32[]{:S(2)}, u32[]{:S(2)}) collective-permute-start(bf16[32,4096]{1,0:T(8,128)(2,1)S(1)} %query_grads.2.refs_0_), channel_id=1, source_target_pairs={{0,12},{1,13},{2,14},{3,15},{4,0},{5,1},{6,2},{7,3},{8,4},{9,5},{1... | collective-permute-start | bytes 786440 | tf_op jit(solution)/shard_map/ppermute | solution.py:247
  12.1 40.8 %slice-start = ((s8[6291456]{0:T(1024)(128)(4,1)}), s8[4194304]{0:T(1024)(128)(4,1)S(1)}, s32[]{:S(2)}) async-start(s8[6291456]{0:T(1024)(128)(4,1)} %bitcast.2), calls=%async_computation | async-start | bytes 8388608
  14.7 38.1 %slice-start.1 = ((s8[6291456]{0:T(1024)(128)(4,1)}), s8[2097152]{0:T(1024)(128)(4,1)S(1)}, s32[]{:S(2)}) async-start(s8[6291456]{0:T(1024)(128)(4,1)} %bitcast.2), calls=%async_computation.1 | async-start | bytes 4194304
  14.8 9.4 %collective-permute-start.4 = (bf16[32,4096]{1,0:T(8,128)(2,1)S(1)}, bf16[32,4096]{1,0:T(8,128)(2,1)S(1)}, u32[]{:S(2)}, u32[]{:S(2)}) collective-permute-start(bf16[32,4096]{1,0:T(8,128)(2,1)S(1)} %fence.5.refs_0_), channel_id=1, source_target_pairs={{0,4},{1,5},{2,6},{3,7},{4,8},{5,9},{6,10},{7,11},{8,12},{9,13},{1... | collective-permute-start | bytes 786440 | tf_op jit(solution)/shard_map/ppermute | solution.py:247
  15.2 9.0 %collective-permute-start.5 = (bf16[32,4096]{1,0:T(8,128)(2,1)S(1)}, bf16[32,4096]{1,0:T(8,128)(2,1)S(1)}, u32[]{:S(2)}, u32[]{:S(2)}) collective-permute-start(bf16[32,4096]{1,0:T(8,128)(2,1)S(1)} %fence.5.refs_0_), channel_id=1, source_target_pairs={{0,12},{1,13},{2,14},{3,15},{4,0},{5,1},{6,2},{7,3},{8,4},{9,5},{1... | collective-permute-start | bytes 786440 | tf_op jit(solution)/shard_map/ppermute | solution.py:247
  24.2 7.4 %collective-permute-start.8 = (bf16[32,4096]{1,0:T(8,128)(2,1)S(1)}, bf16[32,4096]{1,0:T(8,128)(2,1)S(1)}, u32[]{:S(2)}, u32[]{:S(2)}) collective-permute-start(bf16[32,4096]{1,0:T(8,128)(2,1)S(1)} %get-tuple-element.26.refs_4_), channel_id=1, source_target_pairs={{0,12},{1,13},{2,14},{3,15},{4,0},{5,1},{6,2},{7,3},{8,4},{9,5},{1... | collective-permute-start | bytes 786440 | tf_op jit(solution)/shard_map/ppermute | solution.py:247
  27.2 16.2 %collective-permute-start.11 = (bf16[32,4096]{1,0:T(8,128)(2,1)S(1)}, bf16[32,4096]{1,0:T(8,128)(2,1)S(1)}, u32[]{:S(2)}, u32[]{:S(2)}) collective-permute-start(bf16[32,4096]{1,0:T(8,128)(2,1)S(1)} %fence.5.refs_0_), channel_id=1, source_target_pairs={{0,2},{1,3},{2,0},{3,1},{4,6},{5,7},{6,4},{7,5},{8,10},{9,11},{10,... | collective-permute-start | bytes 786440 | tf_op jit(solution)/shard_map/ppermute | solution.py:247
  30.3 14.2 %collective-permute-start.7 = (bf16[32,4096]{1,0:T(8,128)(2,1)S(1)}, bf16[32,4096]{1,0:T(8,128)(2,1)S(1)}, u32[]{:S(2)}, u32[]{:S(2)}) collective-permute-start(bf16[32,4096]{1,0:T(8,128)(2,1)S(1)} %get-tuple-element.26.refs_4_), channel_id=1, source_target_pairs={{0,4},{1,5},{2,6},{3,7},{4,8},{5,9},{6,10},{7,11},{8,12},{9,13},{1... | collective-permute-start | bytes 786440 | tf_op jit(solution)/shard_map/ppermute | solution.py:247
  30.3 14.2 %collective-permute-start.6 = (bf16[32,4096]{1,0:T(8,128)(2,1)S(1)}, bf16[32,4096]{1,0:T(8,128)(2,1)S(1)}, u32[]{:S(2)}, u32[]{:S(2)}) collective-permute-start(bf16[32,4096]{1,0:T(8,128)(2,1)S(1)} %get-tuple-element.25.refs_1_), channel_id=1, source_target_pairs={{0,4},{1,5},{2,6},{3,7},{4,8},{5,9},{6,10},{7,11},{8,12},{9,13},{1... | collective-permute-start | bytes 786440 | tf_op jit(solution)/shard_map/ppermute | solution.py:247
  31.6 12.9 %collective-permute-start.9 = (bf16[32,4096]{1,0:T(8,128)(2,1)S(1)}, bf16[32,4096]{1,0:T(8,128)(2,1)S(1)}, u32[]{:S(2)}, u32[]{:S(2)}) collective-permute-start(bf16[32,4096]{1,0:T(8,128)(2,1)S(1)} %collective-permute-done.8.refs_6_), channel_id=1, source_target_pairs={{0,12},{1,13},{2,14},{3,15},{4,0},{5,1},{6,2},{7,3},{8,4},{9,5},{1... | collective-permute-start | bytes 786440 | tf_op jit(solution)/shard_map/ppermute | solution.py:247
  44.5 6.6 %collective-permute-start.20 = (bf16[32,4096]{1,0:T(8,128)(2,1)S(1)}, bf16[32,4096]{1,0:T(8,128)(2,1)S(1)}, u32[]{:S(2)}, u32[]{:S(2)}) collective-permute-start(bf16[32,4096]{1,0:T(8,128)(2,1)S(1)} %get-tuple-element.30.refs_4_), channel_id=1, source_target_pairs={{0,12},{1,13},{2,14},{3,15},{4,0},{5,1},{6,2},{7,3},{8,4},{9,5},{1... | collective-permute-start | bytes 786440 | tf_op jit(solution)/shard_map/ppermute | solution.py:247
  44.6 16.8 %collective-permute-start.12 = (bf16[32,4096]{1,0:T(8,128)(2,1)S(1)}, bf16[32,4096]{1,0:T(8,128)(2,1)S(1)}, u32[]{:S(2)}, u32[]{:S(2)}) collective-permute-start(bf16[32,4096]{1,0:T(8,128)(2,1)S(1)} %get-tuple-element.29.refs_1_), channel_id=1, source_target_pairs={{0,4},{1,5},{2,6},{3,7},{4,8},{5,9},{6,10},{7,11},{8,12},{9,13},{1... | collective-permute-start | bytes 786440 | tf_op jit(solution)/shard_map/ppermute | solution.py:247
  46.6 15.4 %collective-permute-start.13 = (bf16[32,4096]{1,0:T(8,128)(2,1)S(1)}, bf16[32,4096]{1,0:T(8,128)(2,1)S(1)}, u32[]{:S(2)}, u32[]{:S(2)}) collective-permute-start(bf16[32,4096]{1,0:T(8,128)(2,1)S(1)} %get-tuple-element.30.refs_4_), channel_id=1, source_target_pairs={{0,4},{1,5},{2,6},{3,7},{4,8},{5,9},{6,10},{7,11},{8,12},{9,13},{1... | collective-permute-start | bytes 786440 | tf_op jit(solution)/shard_map/ppermute | solution.py:247
  51.1 19.3 %collective-permute-start.21 = (bf16[32,4096]{1,0:T(8,128)(2,1)S(1)}, bf16[32,4096]{1,0:T(8,128)(2,1)S(1)}, u32[]{:S(2)}, u32[]{:S(2)}) collective-permute-start(bf16[32,4096]{1,0:T(8,128)(2,1)S(1)} %collective-permute-done.20.refs_6_), channel_id=1, source_target_pairs={{0,12},{1,13},{2,14},{3,15},{4,0},{5,1},{6,2},{7,3},{8,4},{9,5},{1... | collective-permute-start | bytes 786440 | tf_op jit(solution)/shard_map/ppermute | solution.py:247
  58.3 9.4 %collective-permute-start.10 = (bf16[128,768]{1,0:T(8,128)(2,1)S(1)}, bf16[128,768]{1,0:T(8,128)(2,1)S(1)}, u32[]{:S(2)}, u32[]{:S(2)}) collective-permute-start(bf16[128,768]{1,0:T(8,128)(2,1)S(1)} %get-tuple-element.27), channel_id=1, source_target_pairs={{0,32},{1,16},{2,34},{3,18},{4,36},{5,20},{6,38},{7,22},{8,40},{9,... | collective-permute-start | bytes 589832 | tf_op jit(solution)/shard_map/ppermute | solution.py:309
  61.4 6.4 %collective-permute-start.15 = (bf16[128,768]{1,0:T(8,128)(2,1)S(1)}, bf16[128,768]{1,0:T(8,128)(2,1)S(1)}, u32[]{:S(2)}, u32[]{:S(2)}) collective-permute-start(bf16[128,768]{1,0:T(8,128)(2,1)S(1)} %get-tuple-element.31), channel_id=1, source_target_pairs={{0,1},{1,49},{2,3},{3,51},{4,5},{5,53},{6,7},{7,55},{8,9},{9,57},{... | collective-permute-start | bytes 589832 | tf_op jit(solution)/shard_map/ppermute | solution.py:309
  61.4 6.4 %collective-permute-start.16 = (bf16[128,768]{1,0:T(8,128)(2,1)S(1)}, bf16[128,768]{1,0:T(8,128)(2,1)S(1)}, u32[]{:S(2)}, u32[]{:S(2)}) collective-permute-start(bf16[128,768]{1,0:T(8,128)(2,1)S(1)} %get-tuple-element.32.own_ref), channel_id=1, source_target_pairs={{1,48},{3,50},{5,52},{7,54},{9,56},{11,58},{13,60},{15,62},{16,1},... | collective-permute-start | bytes 589832 | tf_op jit(solution)/shard_map/ppermute | solution.py:309
  62.0 8.3 %collective-permute-start.14 = (bf16[128,768]{1,0:T(8,128)(2,1)S(1)}, bf16[128,768]{1,0:T(8,128)(2,1)S(1)}, u32[]{:S(2)}, u32[]{:S(2)}) collective-permute-start(bf16[128,768]{1,0:T(8,128)(2,1)S(1)} %fence.8), channel_id=1, source_target_pairs={{0,33},{1,17},{2,35},{3,19},{4,37},{5,21},{6,39},{7,23},{8,41},{9,... | collective-permute-start | bytes 589832 | tf_op jit(solution)/shard_map/ppermute | solution.py:309
  70.4 24.3 %copy-start = (s32[768]{0:T(1024)S(1)}, s32[768]{0:T(1024)}, u32[]{:S(2)}) copy-start(s32[768]{0:T(1024)} %param.9) | copy-start | bytes 9220
  75.8 8.9 %collective-permute-start.22 = (bf16[128,768]{1,0:T(8,128)(2,1)S(1)}, bf16[128,768]{1,0:T(8,128)(2,1)S(1)}, u32[]{:S(2)}, u32[]{:S(2)}) collective-permute-start(bf16[128,768]{1,0:T(8,128)(2,1)S(1)} %get-tuple-element.37), channel_id=1, source_target_pairs={{0,32},{1,16},{2,34},{3,18},{4,36},{5,20},{6,38},{7,22},{8,40},{9,... | collective-permute-start | bytes 589832 | tf_op jit(solution)/shard_map/ppermute | solution.py:309
  77.7 12.2 %collective-permute-start.23 = (bf16[128,768]{1,0:T(8,128)(2,1)S(1)}, bf16[128,768]{1,0:T(8,128)(2,1)S(1)}, u32[]{:S(2)}, u32[]{:S(2)}) collective-permute-start(bf16[128,768]{1,0:T(8,128)(2,1)S(1)} %get-tuple-element.38), channel_id=1, source_target_pairs={{0,33},{1,17},{2,35},{3,19},{4,37},{5,21},{6,39},{7,23},{8,41},{9,... | collective-permute-start | bytes 589832 | tf_op jit(solution)/shard_map/ppermute | solution.py:309
  80.2 9.7 %collective-permute-start.24 = (bf16[128,768]{1,0:T(8,128)(2,1)S(1)}, bf16[128,768]{1,0:T(8,128)(2,1)S(1)}, u32[]{:S(2)}, u32[]{:S(2)}) collective-permute-start(bf16[128,768]{1,0:T(8,128)(2,1)S(1)} %get-tuple-element.39), channel_id=1, source_target_pairs={{0,1},{1,49},{2,3},{3,51},{4,5},{5,53},{6,7},{7,55},{8,9},{9,57},{... | collective-permute-start | bytes 589832 | tf_op jit(solution)/shard_map/ppermute | solution.py:309
  80.2 9.7 %collective-permute-start.25 = (bf16[128,768]{1,0:T(8,128)(2,1)S(1)}, bf16[128,768]{1,0:T(8,128)(2,1)S(1)}, u32[]{:S(2)}, u32[]{:S(2)}) collective-permute-start(bf16[128,768]{1,0:T(8,128)(2,1)S(1)} %get-tuple-element.40.own_ref), channel_id=1, source_target_pairs={{1,48},{3,50},{5,52},{7,54},{9,56},{11,58},{13,60},{15,62},{16,1},... | collective-permute-start | bytes 589832 | tf_op jit(solution)/shard_map/ppermute | solution.py:309
  81.0 11.9 %collective-permute-start.17 = (bf16[32,768]{1,0:T(8,128)(2,1)S(1)}, bf16[32,768]{1,0:T(8,128)(2,1)S(1)}, u32[]{:S(2)}, u32[]{:S(2)}) collective-permute-start(bf16[32,768]{1,0:T(8,128)(2,1)S(1)} %get-tuple-element.34), channel_id=1, source_target_pairs={{0,64},{16,80},{32,96},{48,112},{64,128},{80,144},{96,160},{112,17... | collective-permute-start | bytes 147464 | tf_op jit(solution)/shard_map/ppermute | solution.py:331
  84.8 10.4 %collective-permute-start.18 = (bf16[32,768]{1,0:T(8,128)(2,1)S(1)}, bf16[32,768]{1,0:T(8,128)(2,1)S(1)}, u32[]{:S(2)}, u32[]{:S(2)}) collective-permute-start(bf16[32,768]{1,0:T(8,128)(2,1)S(1)} %get-tuple-element.35), channel_id=1, source_target_pairs={{0,128},{16,144},{32,160},{48,176},{64,192},{80,208},{96,224},{112... | collective-permute-start | bytes 147464 | tf_op jit(solution)/shard_map/ppermute | solution.py:331
  89.9 5.9 %collective-permute-start.19 = (bf16[32,768]{1,0:T(8,128)(2,1)S(1)}, bf16[32,768]{1,0:T(8,128)(2,1)S(1)}, u32[]{:S(2)}, u32[]{:S(2)}) collective-permute-start(bf16[32,768]{1,0:T(8,128)(2,1)S(1)} %get-tuple-element.36), channel_id=1, source_target_pairs={{0,192},{16,208},{32,224},{48,240},{64,0},{80,16},{96,32},{112,48}... | collective-permute-start | bytes 147464 | tf_op jit(solution)/shard_map/ppermute | solution.py:331
  90.1 5.7 %collective-permute-start.26 = (bf16[32,768]{1,0:T(8,128)(2,1)S(1)}, bf16[32,768]{1,0:T(8,128)(2,1)S(1)}, u32[]{:S(2)}, u32[]{:S(2)}) collective-permute-start(bf16[32,768]{1,0:T(8,128)(2,1)S(1)} %get-tuple-element.42), channel_id=1, source_target_pairs={{0,64},{16,80},{32,96},{48,112},{64,128},{80,144},{96,160},{112,17... | collective-permute-start | bytes 147464 | tf_op jit(solution)/shard_map/ppermute | solution.py:331
  92.1 5.1 %collective-permute-start.27 = (bf16[32,768]{1,0:T(8,128)(2,1)S(1)}, bf16[32,768]{1,0:T(8,128)(2,1)S(1)}, u32[]{:S(2)}, u32[]{:S(2)}) collective-permute-start(bf16[32,768]{1,0:T(8,128)(2,1)S(1)} %get-tuple-element.43), channel_id=1, source_target_pairs={{0,128},{16,144},{32,160},{48,176},{64,192},{80,208},{96,224},{112... | collective-permute-start | bytes 147464 | tf_op jit(solution)/shard_map/ppermute | solution.py:331
  93.0 4.8 %collective-permute-start.28 = (bf16[32,768]{1,0:T(8,128)(2,1)S(1)}, bf16[32,768]{1,0:T(8,128)(2,1)S(1)}, u32[]{:S(2)}, u32[]{:S(2)}) collective-permute-start(bf16[32,768]{1,0:T(8,128)(2,1)S(1)} %get-tuple-element.44), channel_id=1, source_target_pairs={{0,192},{16,208},{32,224},{48,240},{64,0},{80,16},{96,32},{112,48}... | collective-permute-start | bytes 147464 | tf_op jit(solution)/shard_map/ppermute | solution.py:331

commit v3 on v2

--- a/solution.py
+++ b/solution.py
@@ -95,71 +95,44 @@
 
 
 def score_kernel(*refs):
-    blocks, (mine_ref, other_ref), outs = refs[:8], refs[8:10], refs[10:14]
-    rows_ref, sem = refs[14:]
-    step = pl.program_id(0)
+    blocks, held, outs, rows_ref = refs[:8], refs[8:10], refs[10:14], refs[14]
     x, _, y, z_hi, core = place()
-
-    @pl.when(step == 0)
-    def _():
-        copies = [
-            pltpu.make_async_copy(block, rows_ref.at[pl.ds(i * ROWS, ROWS)], sem.at[i])
-            for i, block in enumerate(blocks)
-        ]
-        for copy in copies:
-            copy.start()
-        for copy in copies:
-            copy.wait()
-
-    def part(weights_ref, rel_core, tile):
-        got = lax.dot_general(
-            rows_ref[...],
-            weights_ref[...],
-            (((1,), (1,)), ((), ())),
-            preferred_element_type=F32,
-        ).astype(BF16)
-        for rel_z in range(2):
-            to_x = 2 * ((z_hi + rel_z) % 2) + core
-            away = (to_x - x + 4) % 4
-            if rel_core == 0:
-                buf = jnp.where(away == 0, 3, jnp.where(away == 1, 1, jnp.where(away == 2, 0, 2)))
-            else:
-                buf = jnp.where(away == 0, 2, jnp.where(away == 1, 0, jnp.where(away == 2, 1, 3)))
-            for b in range(4):
-
-                @pl.when(buf == b)
-                def _():
-                    for j, dy in enumerate((0, 3, 1, 2)):
-                        row = pl.multiple_of(((y + dy) % 4) * ROWS, ROWS)
-                        at = (rel_z * 4 + j) * ROWS
-                        outs[b][pl.ds(row, ROWS), tile * COLS : (tile + 1) * COLS] = got[at : at + ROWS]
-
-    tiles = HELD // COLS
-    for s in range(2 * tiles):
-
-        @pl.when(step == s)
-        def _():
-            part(mine_ref if s < tiles else other_ref, s // tiles, s % tiles)
+    for i, block in enumerate(blocks):
+        rows_ref[i * ROWS : (i + 1) * ROWS, :] = block[...]
+    for rel_core in range(2):
+        for tile in range(HELD // COLS):
+            cols = slice(tile * COLS, (tile + 1) * COLS)
+            got = lax.dot_general(
+                rows_ref[...],
+                held[rel_core][cols, :],
+                (((1,), (1,)), ((), ())),
+                preferred_element_type=F32,
+            ).astype(BF16)
+            for rel_z in range(2):
+                to_x = 2 * ((z_hi + rel_z) % 2) + core
+                away = (to_x - x + 4) % 4
+                if rel_core == 0:
+                    buf = jnp.where(away == 0, 3, jnp.where(away == 1, 1, jnp.where(away == 2, 0, 2)))
+                else:
+                    buf = jnp.where(away == 0, 2, jnp.where(away == 1, 0, jnp.where(away == 2, 1, 3)))
+                for b in range(4):
+
+                    @pl.when(buf == b)
+                    def _():
+                        for j, dy in enumerate((0, 3, 1, 2)):
+                            row = pl.multiple_of(((y + dy) % 4) * ROWS, ROWS)
+                            at = (rel_z * 4 + j) * ROWS
+                            outs[b][pl.ds(row, ROWS), cols] = got[at : at + ROWS]
 
 
 def partial_scores(blocks, mine, other):
-    tiles = HELD // COLS
-    out = pl.BlockSpec((4 * ROWS, HELD), lambda i: (0, 0))
     return pl.pallas_call(
         score_kernel,
         out_shape=[jax.ShapeDtypeStruct((4 * ROWS, HELD), BF16)] * 4,
-        grid=(2 * tiles,),
-        in_specs=[pl.BlockSpec(memory_space=pl.ANY)] * 8
-        + [
-            pl.BlockSpec((COLS, FEATURES), lambda i: (jnp.minimum(i, tiles - 1), 0)),
-            pl.BlockSpec((COLS, FEATURES), lambda i: (jnp.maximum(i - tiles, 0), 0)),
-        ],
-        out_specs=[out] * 4,
-        scratch_shapes=[
-            pltpu.VMEM((8 * ROWS, FEATURES), BF16),
-            pltpu.SemaphoreType.DMA((8,)),
-        ],
-        compiler_params=pltpu.CompilerParams(vmem_limit_bytes=18 << 20),
+        in_specs=[pl.BlockSpec(memory_space=pltpu.VMEM)] * 10,
+        out_specs=[pl.BlockSpec(memory_space=pltpu.VMEM)] * 4,
+        scratch_shapes=[pltpu.VMEM((8 * ROWS, FEATURES), BF16)],
+        compiler_params=pltpu.CompilerParams(vmem_limit_bytes=24 << 20),
         cost_estimate=pl.CostEstimate(flops=1, bytes_accessed=1, transcendentals=0),
         name="partial_scores",
     )(*blocks, mine, other)
@@ -276,24 +249,26 @@
     return along(value, lambda y, z, c: (y, z + 1, c))
 
 
-def gather_blocks(a, b, other):
+def first_scores(a, b, stored, other):
     far_a = beyond(a)
     a_below, a_above = up(a), down(a)
     (b,) = after((b,), other)
     far_b = beyond(b)
     b_below, b_above = up(b), down(b)
     far_a, a_below = after((far_a, a_below), a_above, b_below, b_above)
+    a_opposite = up(a_below)
     far_a_above, far_a_below = down(far_a), up(far_a)
-    a_opposite = up(a_below)
     far_a_opposite = down(far_a_above)
     far_b, b_below = after((far_b, b_below), a_opposite, far_a_opposite, far_a_below)
     b_opposite = up(b_below)
     far_b_above, far_b_below = down(far_b), up(far_b)
+    a_blocks = [a, a_below, a_above, a_opposite, far_a, far_a_below, far_a_above, far_a_opposite]
+    a_bufs = list(partial_scores(a_blocks, stored, other))
+    (far_b_above,) = after((far_b_above,), a_bufs[3])
     far_b_opposite = down(far_b_above)
-    return (
-        [a, a_below, a_above, a_opposite, far_a, far_a_below, far_a_above, far_a_opposite],
-        [b, b_below, b_above, b_opposite, far_b, far_b_below, far_b_above, far_b_opposite],
-    )
+    a_bufs[0:1] = after(a_bufs[0:1], b_opposite, far_b_below)
+    b_blocks = [b, b_below, b_above, b_opposite, far_b, far_b_below, far_b_above, far_b_opposite]
+    return a_bufs, b_blocks
 
 
 def over_x(bufs):
@@ -317,14 +292,13 @@
         pltpu.with_memory_space_constraint(v, pltpu.HBM) for v in (lengths, activations, out_grads)
     ]
     a, b = (query_grads(*inputs, n) for n in range(CHUNKS))
-    parts, got = [], ()
-    a_blocks, b_blocks = gather_blocks(a, b, other)
-    for blocks in (a_blocks, b_blocks):
-        blocks[-1:] = after(blocks[-1:], *got) if got else blocks[-1:]
-        bufs = list(partial_scores(blocks, stored, other))
-        if not got:
-            bufs[1:2] = after(bufs[1:2], b_blocks[3], b_blocks[5])
-        got = over_x(bufs)
+    a_bufs, b_blocks = first_scores(a, b, stored, other)
+    a_got = over_x(a_bufs)
+    b_bufs = list(partial_scores(b_blocks, stored, other))
+    b_bufs[:3] = after(b_bufs[:3], *a_got)
+    b_got = over_x(b_bufs)
+    parts = []
+    for got, bufs in ((a_got, a_bufs), (b_got, b_bufs)):
         keep, *sends = cross_sum(*got, bufs[3])
         parts.append(keep)
         for k, send in enumerate(sends, 1):

time: 99 us -> 95.7 us (0.967)
  waiting for transfers between devices: 34.1 us -> 27.8 us
  Pallas kernels: 17.4 us -> 22.3 us
  starting transfers between devices: 46.8 us -> 44.9 us
    pallas_call x2, Pallas kernels: 10.9 us -> 15.7 us  [partial_scores(): pl.pallas_call(score_kernel, out_shape=[jax.ShapeDtypeStruct((4 * ROWS, H...]
    ppermute x14, waiting for transfers between devices: 20.6 us -> 16.1 us  [along(): return lax.ppermute(value, 'group', group_pairs(move))]
    ppermute x8, starting transfers between devices: 13.9 us -> 11 us  [over_x(): lax.ppermute(b, ('store', 'group'), all_pairs(m))]
    ppermute x8, waiting for transfers between devices: 10.9 us -> 8.43 us  [over_x(): lax.ppermute(b, ('store', 'group'), all_pairs(m))]
    ppermute x14, starting transfers between devices: 27.1 us -> 28.6 us  [along(): return lax.ppermute(value, 'group', group_pairs(move))]
  transfers between devices with their start and end apart: 29 -> 29, of which waited for: 13 -> 10; matrix products, arithmetic and copies ran while one was open for 0% -> 0% of each run, Pallas kernels for 11% -> 22%
where the time goes in v3:
time: 95.7 us; the launch traced here: 95.6 us
  starting transfers between devices  44.9 us (47%)
  waiting for transfers between devices  27.8 us (29%)
  Pallas kernels  22.3 us (23%)
    ppermute x14, starting transfers between devices, along(): return lax.ppermute(value, 'group', group_pairs(move))  28.6 us
    ppermute x14, waiting for transfers between devices, along(): return lax.ppermute(value, 'group', group_pairs(move))  16.1 us
    pallas_call x2, Pallas kernels, partial_scores(): pl.pallas_call(score_kernel, out_shape=[jax.ShapeDtypeStruct((4 * ROWS, H...  15.7 us
    ppermute x8, starting transfers between devices, over_x(): lax.ppermute(b, ('store', 'group'), all_pairs(m))  11 us
    ppermute x8, waiting for transfers between devices, over_x(): lax.ppermute(b, ('store', 'group'), all_pairs(m))  8.43 us
    ppermute x6, starting transfers between devices, on_device(): lax.ppermute(send, 'store', store_pairs(lambda x, z: (x, z + k)))  5.34 us
    pallas_call x2, Pallas kernels, query_grads(): pl.pallas_call(functools.partial(grad_kernel, chunk * ROWS), out_shape=ja...  5.12 us
    ppermute x6, waiting for transfers between devices, on_device(): lax.ppermute(send, 'store', store_pairs(lambda x, z: (x, z + k)))  3.2 us
  transfers between devices with their start and end apart: 29, of which 10 were waited for; matrix products, arithmetic and copies ran while one was open for 0% of the time, Pallas kernels for 22%

profile of v3, /device:TPU:32, one launch (start us, length us, event | category | flops | bytes accessed | tf_op | source)
XLA Modules:
  0.0 95.6 jit_solution(7508735859070020898)
XLA Ops:
  0.0 2.5 %query_grads.2.refs_0_ = bf16[32,4096]{1,0:T(8,128)(2,1)S(1)} custom-call(s32[64]{0:T(128)} %lengths_hbm.3, bf16[64,1,64,256]{3,2,1,0:T(8,128)(2,1)} %acts_hbm.3, bf16[64,1,64,256]{3,2,1,0:T(8,128)(2,1)} %grads_hbm.3), custom_call_target="tpu_custom_call" | custom-call | tf_op jit(solution)/shard_map/query_grads/pallas_call | solution.py:81
  2.5 6.3 %collective-permute-start = (bf16[32,4096]{1,0:T(8,128)(2,1)S(1)}, bf16[32,4096]{1,0:T(8,128)(2,1)S(1)}, u32[]{:S(2)}, u32[]{:S(2)}) collective-permute-start(bf16[32,4096]{1,0:T(8,128)(2,1)S(1)} %query_grads.2.refs_0_), channel_id=1, source_target_pairs={{0,2},{1,3},{2,0},{3,1},{4,6},{5,7},{6,4},{7,5},{8,10},{9,11},{10,... | collective-permute-start | bytes 786440 | tf_op jit(solution)/shard_map/ppermute | solution.py:220
  8.9 1.6 %collective-permute-start.1 = (bf16[32,4096]{1,0:T(8,128)(2,1)S(1)}, bf16[32,4096]{1,0:T(8,128)(2,1)S(1)}, u32[]{:S(2)}, u32[]{:S(2)}) collective-permute-start(bf16[32,4096]{1,0:T(8,128)(2,1)S(1)} %query_grads.2.refs_0_), channel_id=1, source_target_pairs={{0,4},{1,5},{2,6},{3,7},{4,8},{5,9},{6,10},{7,11},{8,12},{9,13},{1... | collective-permute-start | bytes 786440 | tf_op jit(solution)/shard_map/ppermute | solution.py:220
  10.4 1.7 %collective-permute-start.2 = (bf16[32,4096]{1,0:T(8,128)(2,1)S(1)}, bf16[32,4096]{1,0:T(8,128)(2,1)S(1)}, u32[]{:S(2)}, u32[]{:S(2)}) collective-permute-start(bf16[32,4096]{1,0:T(8,128)(2,1)S(1)} %query_grads.2.refs_0_), channel_id=1, source_target_pairs={{0,12},{1,13},{2,14},{3,15},{4,0},{5,1},{6,2},{7,3},{8,4},{9,5},{1... | collective-permute-start | bytes 786440 | tf_op jit(solution)/shard_map/ppermute | solution.py:220
  12.1 2.6 %query_grads.3.refs_0_ = bf16[32,4096]{1,0:T(8,128)(2,1)S(1)} custom-call(s32[64]{0:T(128)} %lengths_hbm.3, bf16[64,1,64,256]{3,2,1,0:T(8,128)(2,1)} %acts_hbm.3, bf16[64,1,64,256]{3,2,1,0:T(8,128)(2,1)} %grads_hbm.3), custom_call_target="tpu_custom_call" | custom-call | tf_op jit(solution)/shard_map/query_grads/pallas_call | solution.py:81
  15.2 2.9 %collective-permute-start.5 = (bf16[32,4096]{1,0:T(8,128)(2,1)S(1)}, bf16[32,4096]{1,0:T(8,128)(2,1)S(1)}, u32[]{:S(2)}, u32[]{:S(2)}) collective-permute-start(bf16[32,4096]{1,0:T(8,128)(2,1)S(1)} %fence.6.refs_0_), channel_id=1, source_target_pairs={{0,12},{1,13},{2,14},{3,15},{4,0},{5,1},{6,2},{7,3},{8,4},{9,5},{1... | collective-permute-start | bytes 786440 | tf_op jit(solution)/shard_map/ppermute | solution.py:220
  18.1 3.5 %collective-permute-done.refs_0_ = bf16[32,4096]{1,0:T(8,128)(2,1)S(1)} collective-permute-done((bf16[32,4096]{1,0:T(8,128)(2,1)S(1)}, bf16[32,4096]{1,0:T(8,128)(2,1)S(1)}, u32[]{:S(2)}, u32[]{:S(2)}) %collective-permute-start) | collective-permute-done | bytes 262176 | tf_op jit(solution)/shard_map/ppermute | solution.py:220
  21.6 2.6 %collective-permute-done.4.refs_3_.refs_1_ = bf16[32,4096]{1,0:T(8,128)(2,1)S(1)} collective-permute-done((bf16[32,4096]{1,0:T(8,128)(2,1)S(1)}, bf16[32,4096]{1,0:T(8,128)(2,1)S(1)}, u32[]{:S(2)}, u32[]{:S(2)}) %collective-permute-start.4) | collective-permute-done | bytes 262176 | tf_op jit(solution)/shard_map/ppermute | solution.py:220
  24.2 2.9 %collective-permute-start.8 = (bf16[32,4096]{1,0:T(8,128)(2,1)S(1)}, bf16[32,4096]{1,0:T(8,128)(2,1)S(1)}, u32[]{:S(2)}, u32[]{:S(2)}) collective-permute-start(bf16[32,4096]{1,0:T(8,128)(2,1)S(1)} %get-tuple-element.29.refs_4_), channel_id=1, source_target_pairs={{0,12},{1,13},{2,14},{3,15},{4,0},{5,1},{6,2},{7,3},{8,4},{9,5},{1... | collective-permute-start | bytes 786440 | tf_op jit(solution)/shard_map/ppermute | solution.py:220
  27.2 3.1 %collective-permute-start.10 = (bf16[32,4096]{1,0:T(8,128)(2,1)S(1)}, bf16[32,4096]{1,0:T(8,128)(2,1)S(1)}, u32[]{:S(2)}, u32[]{:S(2)}) collective-permute-start(bf16[32,4096]{1,0:T(8,128)(2,1)S(1)} %fence.6.refs_0_), channel_id=1, source_target_pairs={{0,2},{1,3},{2,0},{3,1},{4,6},{5,7},{6,4},{7,5},{8,10},{9,11},{10,... | collective-permute-start | bytes 786440 | tf_op jit(solution)/shard_map/ppermute | solution.py:220
  30.8 0.8 collective-permute-done.8.refs_6_
  31.6 3.7 %collective-permute-start.9 = (bf16[32,4096]{1,0:T(8,128)(2,1)S(1)}, bf16[32,4096]{1,0:T(8,128)(2,1)S(1)}, u32[]{:S(2)}, u32[]{:S(2)}) collective-permute-start(bf16[32,4096]{1,0:T(8,128)(2,1)S(1)} %collective-permute-done.8.refs_6_), channel_id=1, source_target_pairs={{0,12},{1,13},{2,14},{3,15},{4,0},{5,1},{6,2},{7,3},{8,4},{9,5},{1... | collective-permute-start | bytes 786440 | tf_op jit(solution)/shard_map/ppermute | solution.py:220
  35.3 8.0 %collective-permute-done.10.refs_0_ = bf16[32,4096]{1,0:T(8,128)(2,1)S(1)} collective-permute-done((bf16[32,4096]{1,0:T(8,128)(2,1)S(1)}, bf16[32,4096]{1,0:T(8,128)(2,1)S(1)}, u32[]{:S(2)}, u32[]{:S(2)}) %collective-permute-start.10) | collective-permute-done | bytes 262176 | tf_op jit(solution)/shard_map/ppermute | solution.py:220
  43.4 1.1 %collective-permute-done.6.refs_3_.refs_2_ = bf16[32,4096]{1,0:T(8,128)(2,1)S(1)} collective-permute-done((bf16[32,4096]{1,0:T(8,128)(2,1)S(1)}, bf16[32,4096]{1,0:T(8,128)(2,1)S(1)}, u32[]{:S(2)}, u32[]{:S(2)}) %collective-permute-start.6) | collective-permute-done | bytes 262176 | tf_op jit(solution)/shard_map/ppermute | solution.py:220
  44.6 2.0 %collective-permute-start.11 = (bf16[32,4096]{1,0:T(8,128)(2,1)S(1)}, bf16[32,4096]{1,0:T(8,128)(2,1)S(1)}, u32[]{:S(2)}, u32[]{:S(2)}) collective-permute-start(bf16[32,4096]{1,0:T(8,128)(2,1)S(1)} %get-tuple-element.31.refs_1_), channel_id=1, source_target_pairs={{0,4},{1,5},{2,6},{3,7},{4,8},{5,9},{6,10},{7,11},{8,12},{9,13},{1... | collective-permute-start | bytes 786440 | tf_op jit(solution)/shard_map/ppermute | solution.py:220
  46.6 7.9 %partial_scores.2 = (bf16[128,768]{1,0:T(8,128)(2,1)S(1)}, bf16[128,768]{1,0:T(8,128)(2,1)S(1)}, bf16[128,768]{1,0:T(8,128)(2,1)S(1)}, bf16[128,768]{1,0:T(8,128)(2,1)S(1)}) custom-call(bf16[32,4096]{1,0:T(8,128)(2,1)S(1)} %query_grads.2.refs_0_, bf16[32,4096]{1,0:T(8,128)(2,1)S(1)} %get-tuple-element.28.refs_1_, ...), custom_call_target="tpu_custom_call" | custom-call | flops 1 | bytes 1 | tf_op jit(solution)/shard_map/partial_scores/pallas_call | solution.py:129
  54.5 3.3 %collective-permute-start.21 = (bf16[32,4096]{1,0:T(8,128)(2,1)S(1)}, bf16[32,4096]{1,0:T(8,128)(2,1)S(1)}, u32[]{:S(2)}, u32[]{:S(2)}) collective-permute-start(bf16[32,4096]{1,0:T(8,128)(2,1)S(1)} %fence.10.refs_6_), channel_id=1, source_target_pairs={{0,12},{1,13},{2,14},{3,15},{4,0},{5,1},{6,2},{7,3},{8,4},{9,5},{1... | collective-permute-start | bytes 786440 | tf_op jit(solution)/shard_map/ppermute | solution.py:220
  58.5 4.6 %collective-permute-start.14 = (bf16[128,768]{1,0:T(8,128)(2,1)S(1)}, bf16[128,768]{1,0:T(8,128)(2,1)S(1)}, u32[]{:S(2)}, u32[]{:S(2)}) collective-permute-start(bf16[128,768]{1,0:T(8,128)(2,1)S(1)} %get-tuple-element.33), channel_id=1, source_target_pairs={{0,33},{1,17},{2,35},{3,19},{4,37},{5,21},{6,39},{7,23},{8,41},{9,... | collective-permute-start | bytes 589832 | tf_op jit(solution)/shard_map/ppermute | solution.py:284
  63.1 2.7 %collective-permute-start.13 = (bf16[128,768]{1,0:T(8,128)(2,1)S(1)}, bf16[128,768]{1,0:T(8,128)(2,1)S(1)}, u32[]{:S(2)}, u32[]{:S(2)}) collective-permute-start(bf16[128,768]{1,0:T(8,128)(2,1)S(1)} %fence.9), channel_id=1, source_target_pairs={{0,32},{1,16},{2,34},{3,18},{4,36},{5,20},{6,38},{7,22},{8,40},{9,... | collective-permute-start | bytes 589832 | tf_op jit(solution)/shard_map/ppermute | solution.py:284
  65.8 7.9 %partial_scores.3 = (bf16[128,768]{1,0:T(8,128)(2,1)S(1)}, bf16[128,768]{1,0:T(8,128)(2,1)S(1)}, bf16[128,768]{1,0:T(8,128)(2,1)S(1)}, bf16[128,768]{1,0:T(8,128)(2,1)S(1)}) custom-call(bf16[32,4096]{1,0:T(8,128)(2,1)S(1)} %fence.6.refs_0_, bf16[32,4096]{1,0:T(8,128)(2,1)S(1)} %get-tuple-element.31.refs_1_, ...), custom_call_target="tpu_custom_call" | custom-call | flops 1 | bytes 1 | tf_op jit(solution)/shard_map/partial_scores/pallas_call | solution.py:129
  73.8 1.6 %collective-permute-start.22 = (bf16[128,768]{1,0:T(8,128)(2,1)S(1)}, bf16[128,768]{1,0:T(8,128)(2,1)S(1)}, u32[]{:S(2)}, u32[]{:S(2)}) collective-permute-start(bf16[128,768]{1,0:T(8,128)(2,1)S(1)} %get-tuple-element.43), channel_id=1, source_target_pairs={{0,32},{1,16},{2,34},{3,18},{4,36},{5,20},{6,38},{7,22},{8,40},{9,... | collective-permute-start | bytes 589832 | tf_op jit(solution)/shard_map/ppermute | solution.py:284
  75.4 0.7 collective-permute-start.23
  76.1 0.7 collective-permute-start.25
  76.9 0.9 collective-permute-start.17
  77.9 5.6 %collective-permute-done.22.a_ref = bf16[128,768]{1,0:T(8,128)(2,1)S(1)} collective-permute-done((bf16[128,768]{1,0:T(8,128)(2,1)S(1)}, bf16[128,768]{1,0:T(8,128)(2,1)S(1)}, u32[]{:S(2)}, u32[]{:S(2)}) %collective-permute-start.22) | collective-permute-done | bytes 196640 | tf_op jit(solution)/shard_map/ppermute | solution.py:284
  83.4 2.9 %collective-permute-done.23.b_ref = bf16[128,768]{1,0:T(8,128)(2,1)S(1)} collective-permute-done((bf16[128,768]{1,0:T(8,128)(2,1)S(1)}, bf16[128,768]{1,0:T(8,128)(2,1)S(1)}, u32[]{:S(2)}, u32[]{:S(2)}) %collective-permute-start.23) | collective-permute-done | bytes 196640 | tf_op jit(solution)/shard_map/ppermute | solution.py:284
  86.4 2.1 %collective-permute-start.26 = (bf16[32,768]{1,0:T(8,128)(2,1)S(1)}, bf16[32,768]{1,0:T(8,128)(2,1)S(1)}, u32[]{:S(2)}, u32[]{:S(2)}) collective-permute-start(bf16[32,768]{1,0:T(8,128)(2,1)S(1)} %get-tuple-element.48), channel_id=1, source_target_pairs={{0,64},{16,80},{32,96},{48,112},{64,128},{80,144},{96,160},{112,17... | collective-permute-start | bytes 147464 | tf_op jit(solution)/shard_map/ppermute | solution.py:305
  88.5 1.9 %collective-permute-start.27 = (bf16[32,768]{1,0:T(8,128)(2,1)S(1)}, bf16[32,768]{1,0:T(8,128)(2,1)S(1)}, u32[]{:S(2)}, u32[]{:S(2)}) collective-permute-start(bf16[32,768]{1,0:T(8,128)(2,1)S(1)} %get-tuple-element.49), channel_id=1, source_target_pairs={{0,128},{16,144},{32,160},{48,176},{64,192},{80,208},{96,224},{112... | collective-permute-start | bytes 147464 | tf_op jit(solution)/shard_map/ppermute | solution.py:305
  91.3 0.7 collective-permute-done.19.refs_3_
  92.0 1.6 %collective-permute-done.27.refs_6_ = bf16[32,768]{1,0:T(8,128)(2,1)S(1)} collective-permute-done((bf16[32,768]{1,0:T(8,128)(2,1)S(1)}, bf16[32,768]{1,0:T(8,128)(2,1)S(1)}, u32[]{:S(2)}, u32[]{:S(2)}) %collective-permute-start.27) | collective-permute-done | bytes 49184 | tf_op jit(solution)/shard_map/ppermute | solution.py:305
  93.5 1.0 %collective-permute-done.28.refs_7_ = bf16[32,768]{1,0:T(8,128)(2,1)S(1)} collective-permute-done((bf16[32,768]{1,0:T(8,128)(2,1)S(1)}, bf16[32,768]{1,0:T(8,128)(2,1)S(1)}, u32[]{:S(2)}, u32[]{:S(2)}) %collective-permute-start.28) | collective-permute-done | bytes 49184 | tf_op jit(solution)/shard_map/ppermute | solution.py:305
  94.5 1.1 %final_sum.1 = f32[64,768]{1,0:T(8,128)} custom-call(f32[32,768]{1,0:T(8,128)S(1)} %get-tuple-element.36.refs_0_, bf16[32,768]{1,0:T(8,128)(2,1)S(1)} %collective-permute-done.17.refs_1_, bf16[32,768]{1,0:T(8,128)(2,1)S(1)} %collective-permute-done.18.refs_2_, bf16[32,768]{1,0:T(8,128)(2,1)S(1)} %collective-permute-done.19.refs_3_, ...), custom_call_target="tpu_custom_call" | custom-call | tf_op jit(solution)/shard_map/final_sum/pallas_call | solution.py:187
  (47 shorter events, 3.1 us)
Async XLA Ops:
  0.0 14.8 %collective-permute-start.3 = (bf16[768,4096]{1,0:T(8,128)(2,1)}, bf16[768,4096]{1,0:T(8,128)(2,1)S(1)}, u32[]{:S(2)}, u32[]{:S(2)}) collective-permute-start(bf16[768,4096]{1,0:T(8,128)(2,1)} %bitcast.1), channel_id=1, source_target_pairs={{0,1},{1,0},{2,3},{3,2},{4,5},{5,4},{6,7},{7,6},{8,9},{9,8},{10,11... | collective-permute-start | bytes 18874376 | tf_op jit(solution)/shard_map/ppermute | solution.py:289
  2.5 19.1 %collective-permute-start = (bf16[32,4096]{1,0:T(8,128)(2,1)S(1)}, bf16[32,4096]{1,0:T(8,128)(2,1)S(1)}, u32[]{:S(2)}, u32[]{:S(2)}) collective-permute-start(bf16[32,4096]{1,0:T(8,128)(2,1)S(1)} %query_grads.2.refs_0_), channel_id=1, source_target_pairs={{0,2},{1,3},{2,0},{3,1},{4,6},{5,7},{6,4},{7,5},{8,10},{9,11},{10,... | collective-permute-start | bytes 786440 | tf_op jit(solution)/shard_map/ppermute | solution.py:220
  8.9 12.7 %collective-permute-start.1 = (bf16[32,4096]{1,0:T(8,128)(2,1)S(1)}, bf16[32,4096]{1,0:T(8,128)(2,1)S(1)}, u32[]{:S(2)}, u32[]{:S(2)}) collective-permute-start(bf16[32,4096]{1,0:T(8,128)(2,1)S(1)} %query_grads.2.refs_0_), channel_id=1, source_target_pairs={{0,4},{1,5},{2,6},{3,7},{4,8},{5,9},{6,10},{7,11},{8,12},{9,13},{1... | collective-permute-start | bytes 786440 | tf_op jit(solution)/shard_map/ppermute | solution.py:220
  10.4 11.1 %collective-permute-start.2 = (bf16[32,4096]{1,0:T(8,128)(2,1)S(1)}, bf16[32,4096]{1,0:T(8,128)(2,1)S(1)}, u32[]{:S(2)}, u32[]{:S(2)}) collective-permute-start(bf16[32,4096]{1,0:T(8,128)(2,1)S(1)} %query_grads.2.refs_0_), channel_id=1, source_target_pairs={{0,12},{1,13},{2,14},{3,15},{4,0},{5,1},{6,2},{7,3},{8,4},{9,5},{1... | collective-permute-start | bytes 786440 | tf_op jit(solution)/shard_map/ppermute | solution.py:220
  12.1 34.5 %slice-start = ((s8[6291456]{0:T(1024)(128)(4,1)}), s8[4194304]{0:T(1024)(128)(4,1)S(1)}, s32[]{:S(2)}) async-start(s8[6291456]{0:T(1024)(128)(4,1)} %bitcast.2), calls=%async_computation | async-start | bytes 8388608
  14.7 31.9 %slice-start.1 = ((s8[6291456]{0:T(1024)(128)(4,1)}), s8[2097152]{0:T(1024)(128)(4,1)S(1)}, s32[]{:S(2)}) async-start(s8[6291456]{0:T(1024)(128)(4,1)} %bitcast.2), calls=%async_computation.1 | async-start | bytes 4194304
  14.8 9.4 %collective-permute-start.4 = (bf16[32,4096]{1,0:T(8,128)(2,1)S(1)}, bf16[32,4096]{1,0:T(8,128)(2,1)S(1)}, u32[]{:S(2)}, u32[]{:S(2)}) collective-permute-start(bf16[32,4096]{1,0:T(8,128)(2,1)S(1)} %fence.6.refs_0_), channel_id=1, source_target_pairs={{0,4},{1,5},{2,6},{3,7},{4,8},{5,9},{6,10},{7,11},{8,12},{9,13},{1... | collective-permute-start | bytes 786440 | tf_op jit(solution)/shard_map/ppermute | solution.py:220
  15.2 9.0 %collective-permute-start.5 = (bf16[32,4096]{1,0:T(8,128)(2,1)S(1)}, bf16[32,4096]{1,0:T(8,128)(2,1)S(1)}, u32[]{:S(2)}, u32[]{:S(2)}) collective-permute-start(bf16[32,4096]{1,0:T(8,128)(2,1)S(1)} %fence.6.refs_0_), channel_id=1, source_target_pairs={{0,12},{1,13},{2,14},{3,15},{4,0},{5,1},{6,2},{7,3},{8,4},{9,5},{1... | collective-permute-start | bytes 786440 | tf_op jit(solution)/shard_map/ppermute | solution.py:220
  24.2 7.4 %collective-permute-start.8 = (bf16[32,4096]{1,0:T(8,128)(2,1)S(1)}, bf16[32,4096]{1,0:T(8,128)(2,1)S(1)}, u32[]{:S(2)}, u32[]{:S(2)}) collective-permute-start(bf16[32,4096]{1,0:T(8,128)(2,1)S(1)} %get-tuple-element.29.refs_4_), channel_id=1, source_target_pairs={{0,12},{1,13},{2,14},{3,15},{4,0},{5,1},{6,2},{7,3},{8,4},{9,5},{1... | collective-permute-start | bytes 786440 | tf_op jit(solution)/shard_map/ppermute | solution.py:220
  27.2 16.2 %collective-permute-start.10 = (bf16[32,4096]{1,0:T(8,128)(2,1)S(1)}, bf16[32,4096]{1,0:T(8,128)(2,1)S(1)}, u32[]{:S(2)}, u32[]{:S(2)}) collective-permute-start(bf16[32,4096]{1,0:T(8,128)(2,1)S(1)} %fence.6.refs_0_), channel_id=1, source_target_pairs={{0,2},{1,3},{2,0},{3,1},{4,6},{5,7},{6,4},{7,5},{8,10},{9,11},{10,... | collective-permute-start | bytes 786440 | tf_op jit(solution)/shard_map/ppermute | solution.py:220
  30.3 14.2 %collective-permute-start.7 = (bf16[32,4096]{1,0:T(8,128)(2,1)S(1)}, bf16[32,4096]{1,0:T(8,128)(2,1)S(1)}, u32[]{:S(2)}, u32[]{:S(2)}) collective-permute-start(bf16[32,4096]{1,0:T(8,128)(2,1)S(1)} %get-tuple-element.29.refs_4_), channel_id=1, source_target_pairs={{0,4},{1,5},{2,6},{3,7},{4,8},{5,9},{6,10},{7,11},{8,12},{9,13},{1... | collective-permute-start | bytes 786440 | tf_op jit(solution)/shard_map/ppermute | solution.py:220
  30.3 14.2 %collective-permute-start.6 = (bf16[32,4096]{1,0:T(8,128)(2,1)S(1)}, bf16[32,4096]{1,0:T(8,128)(2,1)S(1)}, u32[]{:S(2)}, u32[]{:S(2)}) collective-permute-start(bf16[32,4096]{1,0:T(8,128)(2,1)S(1)} %get-tuple-element.28.refs_1_), channel_id=1, source_target_pairs={{0,4},{1,5},{2,6},{3,7},{4,8},{5,9},{6,10},{7,11},{8,12},{9,13},{1... | collective-permute-start | bytes 786440 | tf_op jit(solution)/shard_map/ppermute | solution.py:220
  31.6 12.9 %collective-permute-start.9 = (bf16[32,4096]{1,0:T(8,128)(2,1)S(1)}, bf16[32,4096]{1,0:T(8,128)(2,1)S(1)}, u32[]{:S(2)}, u32[]{:S(2)}) collective-permute-start(bf16[32,4096]{1,0:T(8,128)(2,1)S(1)} %collective-permute-done.8.refs_6_), channel_id=1, source_target_pairs={{0,12},{1,13},{2,14},{3,15},{4,0},{5,1},{6,2},{7,3},{8,4},{9,5},{1... | collective-permute-start | bytes 786440 | tf_op jit(solution)/shard_map/ppermute | solution.py:220
  44.5 10.0 %collective-permute-start.20 = (bf16[32,4096]{1,0:T(8,128)(2,1)S(1)}, bf16[32,4096]{1,0:T(8,128)(2,1)S(1)}, u32[]{:S(2)}, u32[]{:S(2)}) collective-permute-start(bf16[32,4096]{1,0:T(8,128)(2,1)S(1)} %get-tuple-element.32.refs_4_), channel_id=1, source_target_pairs={{0,12},{1,13},{2,14},{3,15},{4,0},{5,1},{6,2},{7,3},{8,4},{9,5},{1... | collective-permute-start | bytes 786440 | tf_op jit(solution)/shard_map/ppermute | solution.py:220
  44.6 18.5 %collective-permute-start.11 = (bf16[32,4096]{1,0:T(8,128)(2,1)S(1)}, bf16[32,4096]{1,0:T(8,128)(2,1)S(1)}, u32[]{:S(2)}, u32[]{:S(2)}) collective-permute-start(bf16[32,4096]{1,0:T(8,128)(2,1)S(1)} %get-tuple-element.31.refs_1_), channel_id=1, source_target_pairs={{0,4},{1,5},{2,6},{3,7},{4,8},{5,9},{6,10},{7,11},{8,12},{9,13},{1... | collective-permute-start | bytes 786440 | tf_op jit(solution)/shard_map/ppermute | solution.py:220
  46.6 16.5 %collective-permute-start.12 = (bf16[32,4096]{1,0:T(8,128)(2,1)S(1)}, bf16[32,4096]{1,0:T(8,128)(2,1)S(1)}, u32[]{:S(2)}, u32[]{:S(2)}) collective-permute-start(bf16[32,4096]{1,0:T(8,128)(2,1)S(1)} %get-tuple-element.32.refs_4_), channel_id=1, source_target_pairs={{0,4},{1,5},{2,6},{3,7},{4,8},{5,9},{6,10},{7,11},{8,12},{9,13},{1... | collective-permute-start | bytes 786440 | tf_op jit(solution)/shard_map/ppermute | solution.py:220
  54.5 11.3 %collective-permute-start.21 = (bf16[32,4096]{1,0:T(8,128)(2,1)S(1)}, bf16[32,4096]{1,0:T(8,128)(2,1)S(1)}, u32[]{:S(2)}, u32[]{:S(2)}) collective-permute-start(bf16[32,4096]{1,0:T(8,128)(2,1)S(1)} %fence.10.refs_6_), channel_id=1, source_target_pairs={{0,12},{1,13},{2,14},{3,15},{4,0},{5,1},{6,2},{7,3},{8,4},{9,5},{1... | collective-permute-start | bytes 786440 | tf_op jit(solution)/shard_map/ppermute | solution.py:220
  57.8 15.9 %collective-permute-start.16 = (bf16[128,768]{1,0:T(8,128)(2,1)S(1)}, bf16[128,768]{1,0:T(8,128)(2,1)S(1)}, u32[]{:S(2)}, u32[]{:S(2)}) collective-permute-start(bf16[128,768]{1,0:T(8,128)(2,1)S(1)} %get-tuple-element.35.own_ref.refs_1_), channel_id=1, source_target_pairs={{1,48},{3,50},{5,52},{7,54},{9,56},{11,58},{13,60},{15,62},{16,1},... | collective-permute-start | bytes 589832 | tf_op jit(solution)/shard_map/ppermute | solution.py:284
  58.5 15.2 %collective-permute-start.14 = (bf16[128,768]{1,0:T(8,128)(2,1)S(1)}, bf16[128,768]{1,0:T(8,128)(2,1)S(1)}, u32[]{:S(2)}, u32[]{:S(2)}) collective-permute-start(bf16[128,768]{1,0:T(8,128)(2,1)S(1)} %get-tuple-element.33), channel_id=1, source_target_pairs={{0,33},{1,17},{2,35},{3,19},{4,37},{5,21},{6,39},{7,23},{8,41},{9,... | collective-permute-start | bytes 589832 | tf_op jit(solution)/shard_map/ppermute | solution.py:284
  63.1 10.6 %collective-permute-start.15 = (bf16[128,768]{1,0:T(8,128)(2,1)S(1)}, bf16[128,768]{1,0:T(8,128)(2,1)S(1)}, u32[]{:S(2)}, u32[]{:S(2)}) collective-permute-start(bf16[128,768]{1,0:T(8,128)(2,1)S(1)} %get-tuple-element.34), channel_id=1, source_target_pairs={{0,1},{1,49},{2,3},{3,51},{4,5},{5,53},{6,7},{7,55},{8,9},{9,57},{... | collective-permute-start | bytes 589832 | tf_op jit(solution)/shard_map/ppermute | solution.py:284
  63.1 10.6 %collective-permute-start.13 = (bf16[128,768]{1,0:T(8,128)(2,1)S(1)}, bf16[128,768]{1,0:T(8,128)(2,1)S(1)}, u32[]{:S(2)}, u32[]{:S(2)}) collective-permute-start(bf16[128,768]{1,0:T(8,128)(2,1)S(1)} %fence.9), channel_id=1, source_target_pairs={{0,32},{1,16},{2,34},{3,18},{4,36},{5,20},{6,38},{7,22},{8,40},{9,... | collective-permute-start | bytes 589832 | tf_op jit(solution)/shard_map/ppermute | solution.py:284
  73.7 17.1 %copy-start = (s32[768]{0:T(1024)S(1)}, s32[768]{0:T(1024)}, u32[]{:S(2)}) copy-start(s32[768]{0:T(1024)} %param.9) | copy-start | bytes 9220
  73.8 9.6 %collective-permute-start.22 = (bf16[128,768]{1,0:T(8,128)(2,1)S(1)}, bf16[128,768]{1,0:T(8,128)(2,1)S(1)}, u32[]{:S(2)}, u32[]{:S(2)}) collective-permute-start(bf16[128,768]{1,0:T(8,128)(2,1)S(1)} %get-tuple-element.43), channel_id=1, source_target_pairs={{0,32},{1,16},{2,34},{3,18},{4,36},{5,20},{6,38},{7,22},{8,40},{9,... | collective-permute-start | bytes 589832 | tf_op jit(solution)/shard_map/ppermute | solution.py:284
  75.4 10.9 %collective-permute-start.23 = (bf16[128,768]{1,0:T(8,128)(2,1)S(1)}, bf16[128,768]{1,0:T(8,128)(2,1)S(1)}, u32[]{:S(2)}, u32[]{:S(2)}) collective-permute-start(bf16[128,768]{1,0:T(8,128)(2,1)S(1)} %get-tuple-element.44), channel_id=1, source_target_pairs={{0,33},{1,17},{2,35},{3,19},{4,37},{5,21},{6,39},{7,23},{8,41},{9,... | collective-permute-start | bytes 589832 | tf_op jit(solution)/shard_map/ppermute | solution.py:284
  76.1 10.2 %collective-permute-start.24 = (bf16[128,768]{1,0:T(8,128)(2,1)S(1)}, bf16[128,768]{1,0:T(8,128)(2,1)S(1)}, u32[]{:S(2)}, u32[]{:S(2)}) collective-permute-start(bf16[128,768]{1,0:T(8,128)(2,1)S(1)} %get-tuple-element.45), channel_id=1, source_target_pairs={{0,1},{1,49},{2,3},{3,51},{4,5},{5,53},{6,7},{7,55},{8,9},{9,57},{... | collective-permute-start | bytes 589832 | tf_op jit(solution)/shard_map/ppermute | solution.py:284
  76.1 10.2 %collective-permute-start.25 = (bf16[128,768]{1,0:T(8,128)(2,1)S(1)}, bf16[128,768]{1,0:T(8,128)(2,1)S(1)}, u32[]{:S(2)}, u32[]{:S(2)}) collective-permute-start(bf16[128,768]{1,0:T(8,128)(2,1)S(1)} %get-tuple-element.46.own_ref), channel_id=1, source_target_pairs={{1,48},{3,50},{5,52},{7,54},{9,56},{11,58},{13,60},{15,62},{16,1},... | collective-permute-start | bytes 589832 | tf_op jit(solution)/shard_map/ppermute | solution.py:284
  76.9 13.5 %collective-permute-start.17 = (bf16[32,768]{1,0:T(8,128)(2,1)S(1)}, bf16[32,768]{1,0:T(8,128)(2,1)S(1)}, u32[]{:S(2)}, u32[]{:S(2)}) collective-permute-start(bf16[32,768]{1,0:T(8,128)(2,1)S(1)} %get-tuple-element.37), channel_id=1, source_target_pairs={{0,64},{16,80},{32,96},{48,112},{64,128},{80,144},{96,160},{112,17... | collective-permute-start | bytes 147464 | tf_op jit(solution)/shard_map/ppermute | solution.py:305
  83.4 7.9 %collective-permute-start.18 = (bf16[32,768]{1,0:T(8,128)(2,1)S(1)}, bf16[32,768]{1,0:T(8,128)(2,1)S(1)}, u32[]{:S(2)}, u32[]{:S(2)}) collective-permute-start(bf16[32,768]{1,0:T(8,128)(2,1)S(1)} %get-tuple-element.38), channel_id=1, source_target_pairs={{0,128},{16,144},{32,160},{48,176},{64,192},{80,208},{96,224},{112... | collective-permute-start | bytes 147464 | tf_op jit(solution)/shard_map/ppermute | solution.py:305
  86.3 5.7 %collective-permute-start.19 = (bf16[32,768]{1,0:T(8,128)(2,1)S(1)}, bf16[32,768]{1,0:T(8,128)(2,1)S(1)}, u32[]{:S(2)}, u32[]{:S(2)}) collective-permute-start(bf16[32,768]{1,0:T(8,128)(2,1)S(1)} %get-tuple-element.39), channel_id=1, source_target_pairs={{0,192},{16,208},{32,224},{48,240},{64,0},{80,16},{96,32},{112,48}... | collective-permute-start | bytes 147464 | tf_op jit(solution)/shard_map/ppermute | solution.py:305
  86.4 5.5 %collective-permute-start.26 = (bf16[32,768]{1,0:T(8,128)(2,1)S(1)}, bf16[32,768]{1,0:T(8,128)(2,1)S(1)}, u32[]{:S(2)}, u32[]{:S(2)}) collective-permute-start(bf16[32,768]{1,0:T(8,128)(2,1)S(1)} %get-tuple-element.48), channel_id=1, source_target_pairs={{0,64},{16,80},{32,96},{48,112},{64,128},{80,144},{96,160},{112,17... | collective-permute-start | bytes 147464 | tf_op jit(solution)/shard_map/ppermute | solution.py:305
  88.5 5.0 %collective-permute-start.27 = (bf16[32,768]{1,0:T(8,128)(2,1)S(1)}, bf16[32,768]{1,0:T(8,128)(2,1)S(1)}, u32[]{:S(2)}, u32[]{:S(2)}) collective-permute-start(bf16[32,768]{1,0:T(8,128)(2,1)S(1)} %get-tuple-element.49), channel_id=1, source_target_pairs={{0,128},{16,144},{32,160},{48,176},{64,192},{80,208},{96,224},{112... | collective-permute-start | bytes 147464 | tf_op jit(solution)/shard_map/ppermute | solution.py:305
  90.4 4.1 %collective-permute-start.28 = (bf16[32,768]{1,0:T(8,128)(2,1)S(1)}, bf16[32,768]{1,0:T(8,128)(2,1)S(1)}, u32[]{:S(2)}, u32[]{:S(2)}) collective-permute-start(bf16[32,768]{1,0:T(8,128)(2,1)S(1)} %get-tuple-element.50), channel_id=1, source_target_pairs={{0,192},{16,208},{32,224},{48,240},{64,0},{80,16},{96,32},{112,48}... | collective-permute-start | bytes 147464 | tf_op jit(solution)/shard_map/ppermute | solution.py:305

commit v4 on v3

--- a/solution.py
+++ b/solution.py
@@ -16,7 +16,7 @@
 HELD = 768
 STEP_PAIRS = 8
 PITCH = 72
-COLS = 256
+DEPTH = 512
 F32 = jnp.float32
 BF16 = jnp.bfloat16
 
@@ -95,81 +95,86 @@
 
 
 def score_kernel(*refs):
-    blocks, held, outs, rows_ref = refs[:8], refs[8:10], refs[10:14], refs[14]
+    blocks, held, outs, (rows_ref, total_ref) = refs[:8], refs[8:10], refs[10:14], refs[14:]
     x, _, y, z_hi, core = place()
     for i, block in enumerate(blocks):
-        rows_ref[i * ROWS : (i + 1) * ROWS, :] = block[...]
+        to_z = (y + (0, 3, 1, 2)[i % 4]) % 4
+        row = pl.multiple_of((i // 4) * 4 * ROWS + to_z * ROWS, ROWS)
+        rows_ref[pl.ds(row, ROWS), :] = block[...]
     for rel_core in range(2):
-        for tile in range(HELD // COLS):
-            cols = slice(tile * COLS, (tile + 1) * COLS)
+        for k in range(0, FEATURES, DEPTH):
             got = lax.dot_general(
-                rows_ref[...],
-                held[rel_core][cols, :],
+                held[rel_core][:, k : k + DEPTH],
+                rows_ref[:, k : k + DEPTH],
                 (((1,), (1,)), ((), ())),
                 preferred_element_type=F32,
-            ).astype(BF16)
-            for rel_z in range(2):
-                to_x = 2 * ((z_hi + rel_z) % 2) + core
-                away = (to_x - x + 4) % 4
-                if rel_core == 0:
-                    buf = jnp.where(away == 0, 3, jnp.where(away == 1, 1, jnp.where(away == 2, 0, 2)))
-                else:
-                    buf = jnp.where(away == 0, 2, jnp.where(away == 1, 0, jnp.where(away == 2, 1, 3)))
-                for b in range(4):
-
-                    @pl.when(buf == b)
-                    def _():
-                        for j, dy in enumerate((0, 3, 1, 2)):
-                            row = pl.multiple_of(((y + dy) % 4) * ROWS, ROWS)
-                            at = (rel_z * 4 + j) * ROWS
-                            outs[b][pl.ds(row, ROWS), cols] = got[at : at + ROWS]
+            )
+            total_ref[...] = got if k == 0 else total_ref[...] + got
+        for rel_z in range(2):
+            to_x = 2 * ((z_hi + rel_z) % 2) + core
+            away = (to_x - x + 4) % 4
+            if rel_core == 0:
+                buf = jnp.where(away == 0, 3, jnp.where(away == 1, 1, jnp.where(away == 2, 0, 2)))
+            else:
+                buf = jnp.where(away == 0, 2, jnp.where(away == 1, 0, jnp.where(away == 2, 1, 3)))
+            for b in range(4):
+
+                @pl.when(buf == b)
+                def _():
+                    cols = slice(rel_z * 4 * ROWS, (rel_z + 1) * 4 * ROWS)
+                    outs[b][...] = total_ref[:, cols].astype(BF16)
 
 
 def partial_scores(blocks, mine, other):
     return pl.pallas_call(
         score_kernel,
-        out_shape=[jax.ShapeDtypeStruct((4 * ROWS, HELD), BF16)] * 4,
+        out_shape=[jax.ShapeDtypeStruct((HELD, 4 * ROWS), BF16)] * 4,
         in_specs=[pl.BlockSpec(memory_space=pltpu.VMEM)] * 10,
         out_specs=[pl.BlockSpec(memory_space=pltpu.VMEM)] * 4,
-        scratch_shapes=[pltpu.VMEM((8 * ROWS, FEATURES), BF16)],
+        scratch_shapes=[
+            pltpu.VMEM((8 * ROWS, FEATURES), BF16),
+            pltpu.VMEM((HELD, 8 * ROWS), F32),
+        ],
         compiler_params=pltpu.CompilerParams(vmem_limit_bytes=24 << 20),
         cost_estimate=pl.CostEstimate(flops=1, bytes_accessed=1, transcendentals=0),
         name="partial_scores",
     )(*blocks, mine, other)
 
 
-def cross_sum_kernel(a_ref, b_ref, c_ref, d_ref, own_ref, keep_ref, *outs):
+def cross_sum_kernel(*refs):
+    keep_ref, *outs, turned_ref = refs[5 * CHUNKS :]
     x, z_lo, _, _, core = place()
     match = (x % 2) == core
-    for k in range(4):
-        rows = pl.ds(pl.multiple_of(((z_lo + k) % 4) * ROWS, ROWS), ROWS)
-        last = jnp.where(match, own_ref[rows, :].astype(F32), d_ref[rows, :].astype(F32))
-        total = a_ref[rows, :].astype(F32) + b_ref[rows, :].astype(F32)
-        total = total + (c_ref[rows, :].astype(F32) + last)
-        if k == 0:
-            keep_ref[...] = total
-        else:
-            outs[k - 1][...] = total.astype(BF16)
-
-
-def cross_sum(*parts):
+    for n in range(CHUNKS):
+        a_ref, b_ref, c_ref, d_ref, own_ref = refs[5 * n : 5 * n + 5]
+        last = jnp.where(match, own_ref[...].astype(F32), d_ref[...].astype(F32))
+        total = a_ref[...].astype(F32) + b_ref[...].astype(F32)
+        total = total + (c_ref[...].astype(F32) + last)
+        turned_ref[...] = total.T
+        for k in range(4):
+            rows = pl.ds(pl.multiple_of(((z_lo + k) % 4) * ROWS, ROWS), ROWS)
+            part = turned_ref[rows, :]
+            at = slice(n * ROWS, (n + 1) * ROWS)
+            if k == 0:
+                keep_ref[at, :] = part
+            else:
+                outs[k - 1][at, :] = part.astype(BF16)
+
+
+def cross_sum(parts):
     return pl.pallas_call(
         cross_sum_kernel,
-        out_shape=[jax.ShapeDtypeStruct((ROWS, HELD), F32)]
-        + [jax.ShapeDtypeStruct((ROWS, HELD), BF16)] * 3,
+        out_shape=[jax.ShapeDtypeStruct((PAIRS, HELD), F32)]
+        + [jax.ShapeDtypeStruct((PAIRS, HELD), BF16)] * 3,
+        scratch_shapes=[pltpu.VMEM((4 * ROWS, HELD), F32)],
         compiler_params=pltpu.CompilerParams(vmem_limit_bytes=16 << 20),
         name="cross_sum",
     )(*parts)
 
 
-def final_kernel(*refs):
-    pick_ref, out_ref = refs[-2:]
-    totals = []
-    for n in range(CHUNKS):
-        keep, first, second, third = refs[4 * n : 4 * n + 4]
-        total = keep[...] + first[...].astype(F32)
-        totals.append(total + (second[...].astype(F32) + third[...].astype(F32)))
-    total = jnp.concatenate(totals, axis=0)
+def final_kernel(keep_ref, first_ref, second_ref, third_ref, pick_ref, out_ref):
+    total = keep_ref[...] + first_ref[...].astype(F32)
+    total = total + (second_ref[...].astype(F32) + third_ref[...].astype(F32))
     high = total.astype(BF16)
     rest = total - high.astype(F32)
     middle = rest.astype(BF16)
@@ -297,12 +302,10 @@
     b_bufs = list(partial_scores(b_blocks, stored, other))
     b_bufs[:3] = after(b_bufs[:3], *a_got)
     b_got = over_x(b_bufs)
-    parts = []
-    for got, bufs in ((a_got, a_bufs), (b_got, b_bufs)):
-        keep, *sends = cross_sum(*got, bufs[3])
-        parts.append(keep)
-        for k, send in enumerate(sends, 1):
-            parts.append(lax.ppermute(send, "store", store_pairs(lambda x, z: (x, z + k))))
+    keep, *sends = cross_sum([*a_got, a_bufs[3], *b_got, b_bufs[3]])
+    parts = [keep]
+    for k, send in enumerate(sends, 1):
+        parts.append(lax.ppermute(send, "store", store_pairs(lambda x, z: (x, z + k))))
     return final_sum(parts, pick)
 
 

time: 95.7 us -> 96.9 us (1.013)
  waiting for transfers between devices: 27.8 us -> 33.7 us
  starting transfers between devices: 44.9 us -> 41.7 us
  Pallas kernels: 22.3 us -> 20.9 us
    ppermute x6 -> x3, waiting for transfers between devices: 3.2 us -> 7.12 us  [on_device(): lax.ppermute(send, 'store', store_pairs(lambda x, z: (x, z + k)))]
    ppermute x6 -> x3, starting transfers between devices: 5.34 us -> 2.62 us  [on_device(): lax.ppermute(send, 'store', store_pairs(lambda x, z: (x, z + k)))]
    ppermute x8, waiting for transfers between devices: 8.43 us -> 10.4 us  [over_x(): lax.ppermute(b, ('store', 'group'), all_pairs(m))]
    pallas_call x4 -> x3, Pallas kernels: 16 us -> 14.6 us  [the longest x2 14.3 us: partial_scores(): pl.pallas_call(score_kernel, out_shape=[jax.ShapeDtypeStruct((HELD, 4 * R...]
  transfers between devices with their start and end apart: 29 -> 26, of which waited for: 10 -> 11; matrix products, arithmetic and copies ran while one was open for 0% -> 0% of each run, Pallas kernels for 22% -> 20%
where the time goes in v4:
time: 96.9 us; the launch traced here: 96.8 us
  starting transfers between devices  41.7 us (43%)
  waiting for transfers between devices  33.7 us (35%)
  Pallas kernels  20.9 us (22%)
    ppermute x14, starting transfers between devices, along(): return lax.ppermute(value, 'group', group_pairs(move))  28.6 us
    ppermute x14, waiting for transfers between devices, along(): return lax.ppermute(value, 'group', group_pairs(move))  16.1 us
    pallas_call x2, Pallas kernels, partial_scores(): pl.pallas_call(score_kernel, out_shape=[jax.ShapeDtypeStruct((HELD, 4 * R...  14.3 us
    ppermute x8, starting transfers between devices, over_x(): lax.ppermute(b, ('store', 'group'), all_pairs(m))  10.5 us
    ppermute x8, waiting for transfers between devices, over_x(): lax.ppermute(b, ('store', 'group'), all_pairs(m))  10.4 us
    ppermute x3, waiting for transfers between devices, on_device(): lax.ppermute(send, 'store', store_pairs(lambda x, z: (x, z + k)))  7.12 us
    pallas_call x2, Pallas kernels, query_grads(): pl.pallas_call(functools.partial(grad_kernel, chunk * ROWS), out_shape=ja...  5.12 us
    ppermute x3, starting transfers between devices, on_device(): lax.ppermute(send, 'store', store_pairs(lambda x, z: (x, z + k)))  2.62 us
  transfers between devices with their start and end apart: 26, of which 11 were waited for; matrix products, arithmetic and copies ran while one was open for 0% of the time, Pallas kernels for 20%

profile of v4, /device:TPU:32, one launch (start us, length us, event | category | flops | bytes accessed | tf_op | source)
XLA Modules:
  0.0 96.8 jit_solution(12079438433087716618)
XLA Ops:
  0.0 2.5 %query_grads.2.refs_0_ = bf16[32,4096]{1,0:T(8,128)(2,1)S(1)} custom-call(s32[64]{0:T(128)} %lengths_hbm.3, bf16[64,1,64,256]{3,2,1,0:T(8,128)(2,1)} %acts_hbm.3, bf16[64,1,64,256]{3,2,1,0:T(8,128)(2,1)} %grads_hbm.3), custom_call_target="tpu_custom_call" | custom-call | tf_op jit(solution)/shard_map/query_grads/pallas_call | solution.py:81
  2.5 6.3 %collective-permute-start = (bf16[32,4096]{1,0:T(8,128)(2,1)S(1)}, bf16[32,4096]{1,0:T(8,128)(2,1)S(1)}, u32[]{:S(2)}, u32[]{:S(2)}) collective-permute-start(bf16[32,4096]{1,0:T(8,128)(2,1)S(1)} %query_grads.2.refs_0_), channel_id=1, source_target_pairs={{0,2},{1,3},{2,0},{3,1},{4,6},{5,7},{6,4},{7,5},{8,10},{9,11},{10,... | collective-permute-start | bytes 786440 | tf_op jit(solution)/shard_map/ppermute | solution.py:225
  8.9 1.6 %collective-permute-start.1 = (bf16[32,4096]{1,0:T(8,128)(2,1)S(1)}, bf16[32,4096]{1,0:T(8,128)(2,1)S(1)}, u32[]{:S(2)}, u32[]{:S(2)}) collective-permute-start(bf16[32,4096]{1,0:T(8,128)(2,1)S(1)} %query_grads.2.refs_0_), channel_id=1, source_target_pairs={{0,4},{1,5},{2,6},{3,7},{4,8},{5,9},{6,10},{7,11},{8,12},{9,13},{1... | collective-permute-start | bytes 786440 | tf_op jit(solution)/shard_map/ppermute | solution.py:225
  10.4 1.7 %collective-permute-start.2 = (bf16[32,4096]{1,0:T(8,128)(2,1)S(1)}, bf16[32,4096]{1,0:T(8,128)(2,1)S(1)}, u32[]{:S(2)}, u32[]{:S(2)}) collective-permute-start(bf16[32,4096]{1,0:T(8,128)(2,1)S(1)} %query_grads.2.refs_0_), channel_id=1, source_target_pairs={{0,12},{1,13},{2,14},{3,15},{4,0},{5,1},{6,2},{7,3},{8,4},{9,5},{1... | collective-permute-start | bytes 786440 | tf_op jit(solution)/shard_map/ppermute | solution.py:225
  12.1 2.6 %query_grads.3.refs_0_ = bf16[32,4096]{1,0:T(8,128)(2,1)S(1)} custom-call(s32[64]{0:T(128)} %lengths_hbm.3, bf16[64,1,64,256]{3,2,1,0:T(8,128)(2,1)} %acts_hbm.3, bf16[64,1,64,256]{3,2,1,0:T(8,128)(2,1)} %grads_hbm.3), custom_call_target="tpu_custom_call" | custom-call | tf_op jit(solution)/shard_map/query_grads/pallas_call | solution.py:81
  15.2 2.9 %collective-permute-start.5 = (bf16[32,4096]{1,0:T(8,128)(2,1)S(1)}, bf16[32,4096]{1,0:T(8,128)(2,1)S(1)}, u32[]{:S(2)}, u32[]{:S(2)}) collective-permute-start(bf16[32,4096]{1,0:T(8,128)(2,1)S(1)} %fence.6.refs_0_), channel_id=1, source_target_pairs={{0,12},{1,13},{2,14},{3,15},{4,0},{5,1},{6,2},{7,3},{8,4},{9,5},{1... | collective-permute-start | bytes 786440 | tf_op jit(solution)/shard_map/ppermute | solution.py:225
  18.1 3.5 %collective-permute-done.refs_0_ = bf16[32,4096]{1,0:T(8,128)(2,1)S(1)} collective-permute-done((bf16[32,4096]{1,0:T(8,128)(2,1)S(1)}, bf16[32,4096]{1,0:T(8,128)(2,1)S(1)}, u32[]{:S(2)}, u32[]{:S(2)}) %collective-permute-start) | collective-permute-done | bytes 262176 | tf_op jit(solution)/shard_map/ppermute | solution.py:225
  21.6 2.6 %collective-permute-done.4.refs_3_.refs_1_ = bf16[32,4096]{1,0:T(8,128)(2,1)S(1)} collective-permute-done((bf16[32,4096]{1,0:T(8,128)(2,1)S(1)}, bf16[32,4096]{1,0:T(8,128)(2,1)S(1)}, u32[]{:S(2)}, u32[]{:S(2)}) %collective-permute-start.4) | collective-permute-done | bytes 262176 | tf_op jit(solution)/shard_map/ppermute | solution.py:225
  24.2 2.9 %collective-permute-start.8 = (bf16[32,4096]{1,0:T(8,128)(2,1)S(1)}, bf16[32,4096]{1,0:T(8,128)(2,1)S(1)}, u32[]{:S(2)}, u32[]{:S(2)}) collective-permute-start(bf16[32,4096]{1,0:T(8,128)(2,1)S(1)} %get-tuple-element.25.refs_4_), channel_id=1, source_target_pairs={{0,12},{1,13},{2,14},{3,15},{4,0},{5,1},{6,2},{7,3},{8,4},{9,5},{1... | collective-permute-start | bytes 786440 | tf_op jit(solution)/shard_map/ppermute | solution.py:225
  27.2 3.1 %collective-permute-start.10 = (bf16[32,4096]{1,0:T(8,128)(2,1)S(1)}, bf16[32,4096]{1,0:T(8,128)(2,1)S(1)}, u32[]{:S(2)}, u32[]{:S(2)}) collective-permute-start(bf16[32,4096]{1,0:T(8,128)(2,1)S(1)} %fence.6.refs_0_), channel_id=1, source_target_pairs={{0,2},{1,3},{2,0},{3,1},{4,6},{5,7},{6,4},{7,5},{8,10},{9,11},{10,... | collective-permute-start | bytes 786440 | tf_op jit(solution)/shard_map/ppermute | solution.py:225
  30.8 0.8 collective-permute-done.8.refs_6_
  31.6 3.7 %collective-permute-start.9 = (bf16[32,4096]{1,0:T(8,128)(2,1)S(1)}, bf16[32,4096]{1,0:T(8,128)(2,1)S(1)}, u32[]{:S(2)}, u32[]{:S(2)}) collective-permute-start(bf16[32,4096]{1,0:T(8,128)(2,1)S(1)} %collective-permute-done.8.refs_6_), channel_id=1, source_target_pairs={{0,12},{1,13},{2,14},{3,15},{4,0},{5,1},{6,2},{7,3},{8,4},{9,5},{1... | collective-permute-start | bytes 786440 | tf_op jit(solution)/shard_map/ppermute | solution.py:225
  35.3 8.0 %collective-permute-done.10.refs_0_ = bf16[32,4096]{1,0:T(8,128)(2,1)S(1)} collective-permute-done((bf16[32,4096]{1,0:T(8,128)(2,1)S(1)}, bf16[32,4096]{1,0:T(8,128)(2,1)S(1)}, u32[]{:S(2)}, u32[]{:S(2)}) %collective-permute-start.10) | collective-permute-done | bytes 262176 | tf_op jit(solution)/shard_map/ppermute | solution.py:225
  43.4 1.1 %collective-permute-done.6.refs_3_.refs_2_ = bf16[32,4096]{1,0:T(8,128)(2,1)S(1)} collective-permute-done((bf16[32,4096]{1,0:T(8,128)(2,1)S(1)}, bf16[32,4096]{1,0:T(8,128)(2,1)S(1)}, u32[]{:S(2)}, u32[]{:S(2)}) %collective-permute-start.6) | collective-permute-done | bytes 262176 | tf_op jit(solution)/shard_map/ppermute | solution.py:225
  44.6 2.0 %collective-permute-start.11 = (bf16[32,4096]{1,0:T(8,128)(2,1)S(1)}, bf16[32,4096]{1,0:T(8,128)(2,1)S(1)}, u32[]{:S(2)}, u32[]{:S(2)}) collective-permute-start(bf16[32,4096]{1,0:T(8,128)(2,1)S(1)} %get-tuple-element.27.refs_1_), channel_id=1, source_target_pairs={{0,4},{1,5},{2,6},{3,7},{4,8},{5,9},{6,10},{7,11},{8,12},{9,13},{1... | collective-permute-start | bytes 786440 | tf_op jit(solution)/shard_map/ppermute | solution.py:225
  46.6 7.2 %partial_scores.2 = (bf16[768,128]{1,0:T(8,128)(2,1)S(1)}, bf16[768,128]{1,0:T(8,128)(2,1)S(1)}, bf16[768,128]{1,0:T(8,128)(2,1)S(1)}, bf16[768,128]{1,0:T(8,128)(2,1)S(1)}) custom-call(bf16[32,4096]{1,0:T(8,128)(2,1)S(1)} %query_grads.2.refs_0_, bf16[32,4096]{1,0:T(8,128)(2,1)S(1)} %get-tuple-element.24.refs_1_, ...), custom_call_target="tpu_custom_call" | custom-call | flops 1 | bytes 1 | tf_op jit(solution)/shard_map/partial_scores/pallas_call | solution.py:129
  53.8 3.3 %collective-permute-start.18 = (bf16[32,4096]{1,0:T(8,128)(2,1)S(1)}, bf16[32,4096]{1,0:T(8,128)(2,1)S(1)}, u32[]{:S(2)}, u32[]{:S(2)}) collective-permute-start(bf16[32,4096]{1,0:T(8,128)(2,1)S(1)} %fence.10.refs_6_), channel_id=1, source_target_pairs={{0,12},{1,13},{2,14},{3,15},{4,0},{5,1},{6,2},{7,3},{8,4},{9,5},{1... | collective-permute-start | bytes 786440 | tf_op jit(solution)/shard_map/ppermute | solution.py:225
  57.1 0.7 collective-permute-start.16
  57.8 4.6 %collective-permute-start.14 = (bf16[768,128]{1,0:T(8,128)(2,1)S(1)}, bf16[768,128]{1,0:T(8,128)(2,1)S(1)}, u32[]{:S(2)}, u32[]{:S(2)}) collective-permute-start(bf16[768,128]{1,0:T(8,128)(2,1)S(1)} %get-tuple-element.29), channel_id=1, source_target_pairs={{0,33},{1,17},{2,35},{3,19},{4,37},{5,21},{6,39},{7,23},{8,41},{9,... | collective-permute-start | bytes 589832 | tf_op jit(solution)/shard_map/ppermute | solution.py:289
  62.4 2.7 %collective-permute-start.13 = (bf16[768,128]{1,0:T(8,128)(2,1)S(1)}, bf16[768,128]{1,0:T(8,128)(2,1)S(1)}, u32[]{:S(2)}, u32[]{:S(2)}) collective-permute-start(bf16[768,128]{1,0:T(8,128)(2,1)S(1)} %fence.9), channel_id=1, source_target_pairs={{0,32},{1,16},{2,34},{3,18},{4,36},{5,20},{6,38},{7,22},{8,40},{9,... | collective-permute-start | bytes 589832 | tf_op jit(solution)/shard_map/ppermute | solution.py:289
  65.1 7.2 %partial_scores.3 = (bf16[768,128]{1,0:T(8,128)(2,1)S(1)}, bf16[768,128]{1,0:T(8,128)(2,1)S(1)}, bf16[768,128]{1,0:T(8,128)(2,1)S(1)}, bf16[768,128]{1,0:T(8,128)(2,1)S(1)}) custom-call(bf16[32,4096]{1,0:T(8,128)(2,1)S(1)} %fence.6.refs_0_, bf16[32,4096]{1,0:T(8,128)(2,1)S(1)} %get-tuple-element.27.refs_1_, ...), custom_call_target="tpu_custom_call" | custom-call | flops 1 | bytes 1 | tf_op jit(solution)/shard_map/partial_scores/pallas_call | solution.py:129
  72.9 1.8 %collective-permute-start.19 = (bf16[768,128]{1,0:T(8,128)(2,1)S(1)}, bf16[768,128]{1,0:T(8,128)(2,1)S(1)}, u32[]{:S(2)}, u32[]{:S(2)}) collective-permute-start(bf16[768,128]{1,0:T(8,128)(2,1)S(1)} %get-tuple-element.35), channel_id=1, source_target_pairs={{0,32},{1,16},{2,34},{3,18},{4,36},{5,20},{6,38},{7,22},{8,40},{9,... | collective-permute-start | bytes 589832 | tf_op jit(solution)/shard_map/ppermute | solution.py:289
  74.7 0.7 collective-permute-start.22
  75.4 6.7 %collective-permute-done.19.refs_5_ = bf16[768,128]{1,0:T(8,128)(2,1)S(1)} collective-permute-done((bf16[768,128]{1,0:T(8,128)(2,1)S(1)}, bf16[768,128]{1,0:T(8,128)(2,1)S(1)}, u32[]{:S(2)}, u32[]{:S(2)}) %collective-permute-start.19) | collective-permute-done | bytes 196640 | tf_op jit(solution)/shard_map/ppermute | solution.py:289
  82.1 3.1 %collective-permute-done.20.refs_6_ = bf16[768,128]{1,0:T(8,128)(2,1)S(1)} collective-permute-done((bf16[768,128]{1,0:T(8,128)(2,1)S(1)}, bf16[768,128]{1,0:T(8,128)(2,1)S(1)}, u32[]{:S(2)}, u32[]{:S(2)}) %collective-permute-start.20) | collective-permute-done | bytes 196640 | tf_op jit(solution)/shard_map/ppermute | solution.py:289
  85.5 1.1 %collective-permute-start.23 = (bf16[64,768]{1,0:T(8,128)(2,1)S(1)}, bf16[64,768]{1,0:T(8,128)(2,1)S(1)}, u32[]{:S(2)}, u32[]{:S(2)}) collective-permute-start(bf16[64,768]{1,0:T(8,128)(2,1)S(1)} %get-tuple-element.40), channel_id=1, source_target_pairs={{0,64},{16,80},{32,96},{48,112},{64,128},{80,144},{96,160},{112,17... | collective-permute-start | bytes 294920 | tf_op jit(solution)/shard_map/ppermute | solution.py:308
  86.6 0.8 collective-permute-start.24
  87.4 0.8 collective-permute-start.25
  88.6 4.5 %collective-permute-done.23.first_ref = bf16[64,768]{1,0:T(8,128)(2,1)S(1)} collective-permute-done((bf16[64,768]{1,0:T(8,128)(2,1)S(1)}, bf16[64,768]{1,0:T(8,128)(2,1)S(1)}, u32[]{:S(2)}, u32[]{:S(2)}) %collective-permute-start.23) | collective-permute-done | bytes 98336 | tf_op jit(solution)/shard_map/ppermute | solution.py:308
  93.1 1.0 %collective-permute-done.24.second_ref = bf16[64,768]{1,0:T(8,128)(2,1)S(1)} collective-permute-done((bf16[64,768]{1,0:T(8,128)(2,1)S(1)}, bf16[64,768]{1,0:T(8,128)(2,1)S(1)}, u32[]{:S(2)}, u32[]{:S(2)}) %collective-permute-start.24) | collective-permute-done | bytes 98336 | tf_op jit(solution)/shard_map/ppermute | solution.py:308
  94.1 1.6 %collective-permute-done.25.third_ref = bf16[64,768]{1,0:T(8,128)(2,1)S(1)} collective-permute-done((bf16[64,768]{1,0:T(8,128)(2,1)S(1)}, bf16[64,768]{1,0:T(8,128)(2,1)S(1)}, u32[]{:S(2)}, u32[]{:S(2)}) %collective-permute-start.25) | collective-permute-done | bytes 98336 | tf_op jit(solution)/shard_map/ppermute | solution.py:308
  95.7 1.1 %final_sum.1 = f32[64,768]{1,0:T(8,128)} custom-call(f32[64,768]{1,0:T(8,128)S(1)} %get-tuple-element.39.keep_ref, bf16[64,768]{1,0:T(8,128)(2,1)S(1)} %collective-permute-done.23.first_ref, bf16[64,768]{1,0:T(8,128)(2,1)S(1)} %collective-permute-done.24.second_ref, bf16[64,768]{1,0:T(8,128)(2,1)S(1)} %collective-permute-done.25.third_ref, ...), custom_call_target="tpu_custom_call" | custom-call | tf_op jit(solution)/shard_map/final_sum/pallas_call | solution.py:192
  (40 shorter events, 2.5 us)
Async XLA Ops:
  0.0 14.8 %collective-permute-start.3 = (bf16[768,4096]{1,0:T(8,128)(2,1)}, bf16[768,4096]{1,0:T(8,128)(2,1)S(1)}, u32[]{:S(2)}, u32[]{:S(2)}) collective-permute-start(bf16[768,4096]{1,0:T(8,128)(2,1)} %bitcast.1), channel_id=1, source_target_pairs={{0,1},{1,0},{2,3},{3,2},{4,5},{5,4},{6,7},{7,6},{8,9},{9,8},{10,11... | collective-permute-start | bytes 18874376 | tf_op jit(solution)/shard_map/ppermute | solution.py:294
  2.5 19.1 %collective-permute-start = (bf16[32,4096]{1,0:T(8,128)(2,1)S(1)}, bf16[32,4096]{1,0:T(8,128)(2,1)S(1)}, u32[]{:S(2)}, u32[]{:S(2)}) collective-permute-start(bf16[32,4096]{1,0:T(8,128)(2,1)S(1)} %query_grads.2.refs_0_), channel_id=1, source_target_pairs={{0,2},{1,3},{2,0},{3,1},{4,6},{5,7},{6,4},{7,5},{8,10},{9,11},{10,... | collective-permute-start | bytes 786440 | tf_op jit(solution)/shard_map/ppermute | solution.py:225
  8.9 12.7 %collective-permute-start.1 = (bf16[32,4096]{1,0:T(8,128)(2,1)S(1)}, bf16[32,4096]{1,0:T(8,128)(2,1)S(1)}, u32[]{:S(2)}, u32[]{:S(2)}) collective-permute-start(bf16[32,4096]{1,0:T(8,128)(2,1)S(1)} %query_grads.2.refs_0_), channel_id=1, source_target_pairs={{0,4},{1,5},{2,6},{3,7},{4,8},{5,9},{6,10},{7,11},{8,12},{9,13},{1... | collective-permute-start | bytes 786440 | tf_op jit(solution)/shard_map/ppermute | solution.py:225
  10.4 11.1 %collective-permute-start.2 = (bf16[32,4096]{1,0:T(8,128)(2,1)S(1)}, bf16[32,4096]{1,0:T(8,128)(2,1)S(1)}, u32[]{:S(2)}, u32[]{:S(2)}) collective-permute-start(bf16[32,4096]{1,0:T(8,128)(2,1)S(1)} %query_grads.2.refs_0_), channel_id=1, source_target_pairs={{0,12},{1,13},{2,14},{3,15},{4,0},{5,1},{6,2},{7,3},{8,4},{9,5},{1... | collective-permute-start | bytes 786440 | tf_op jit(solution)/shard_map/ppermute | solution.py:225
  12.1 34.5 %slice-start = ((s8[6291456]{0:T(1024)(128)(4,1)}), s8[4194304]{0:T(1024)(128)(4,1)S(1)}, s32[]{:S(2)}) async-start(s8[6291456]{0:T(1024)(128)(4,1)} %bitcast.2), calls=%async_computation | async-start | bytes 8388608
  14.7 31.9 %slice-start.1 = ((s8[6291456]{0:T(1024)(128)(4,1)}), s8[2097152]{0:T(1024)(128)(4,1)S(1)}, s32[]{:S(2)}) async-start(s8[6291456]{0:T(1024)(128)(4,1)} %bitcast.2), calls=%async_computation.1 | async-start | bytes 4194304
  14.8 9.4 %collective-permute-start.4 = (bf16[32,4096]{1,0:T(8,128)(2,1)S(1)}, bf16[32,4096]{1,0:T(8,128)(2,1)S(1)}, u32[]{:S(2)}, u32[]{:S(2)}) collective-permute-start(bf16[32,4096]{1,0:T(8,128)(2,1)S(1)} %fence.6.refs_0_), channel_id=1, source_target_pairs={{0,4},{1,5},{2,6},{3,7},{4,8},{5,9},{6,10},{7,11},{8,12},{9,13},{1... | collective-permute-start | bytes 786440 | tf_op jit(solution)/shard_map/ppermute | solution.py:225
  15.2 9.0 %collective-permute-start.5 = (bf16[32,4096]{1,0:T(8,128)(2,1)S(1)}, bf16[32,4096]{1,0:T(8,128)(2,1)S(1)}, u32[]{:S(2)}, u32[]{:S(2)}) collective-permute-start(bf16[32,4096]{1,0:T(8,128)(2,1)S(1)} %fence.6.refs_0_), channel_id=1, source_target_pairs={{0,12},{1,13},{2,14},{3,15},{4,0},{5,1},{6,2},{7,3},{8,4},{9,5},{1... | collective-permute-start | bytes 786440 | tf_op jit(solution)/shard_map/ppermute | solution.py:225
  24.2 7.4 %collective-permute-start.8 = (bf16[32,4096]{1,0:T(8,128)(2,1)S(1)}, bf16[32,4096]{1,0:T(8,128)(2,1)S(1)}, u32[]{:S(2)}, u32[]{:S(2)}) collective-permute-start(bf16[32,4096]{1,0:T(8,128)(2,1)S(1)} %get-tuple-element.25.refs_4_), channel_id=1, source_target_pairs={{0,12},{1,13},{2,14},{3,15},{4,0},{5,1},{6,2},{7,3},{8,4},{9,5},{1... | collective-permute-start | bytes 786440 | tf_op jit(solution)/shard_map/ppermute | solution.py:225
  27.2 16.2 %collective-permute-start.10 = (bf16[32,4096]{1,0:T(8,128)(2,1)S(1)}, bf16[32,4096]{1,0:T(8,128)(2,1)S(1)}, u32[]{:S(2)}, u32[]{:S(2)}) collective-permute-start(bf16[32,4096]{1,0:T(8,128)(2,1)S(1)} %fence.6.refs_0_), channel_id=1, source_target_pairs={{0,2},{1,3},{2,0},{3,1},{4,6},{5,7},{6,4},{7,5},{8,10},{9,11},{10,... | collective-permute-start | bytes 786440 | tf_op jit(solution)/shard_map/ppermute | solution.py:225
  30.3 14.2 %collective-permute-start.7 = (bf16[32,4096]{1,0:T(8,128)(2,1)S(1)}, bf16[32,4096]{1,0:T(8,128)(2,1)S(1)}, u32[]{:S(2)}, u32[]{:S(2)}) collective-permute-start(bf16[32,4096]{1,0:T(8,128)(2,1)S(1)} %get-tuple-element.25.refs_4_), channel_id=1, source_target_pairs={{0,4},{1,5},{2,6},{3,7},{4,8},{5,9},{6,10},{7,11},{8,12},{9,13},{1... | collective-permute-start | bytes 786440 | tf_op jit(solution)/shard_map/ppermute | solution.py:225
  30.3 14.2 %collective-permute-start.6 = (bf16[32,4096]{1,0:T(8,128)(2,1)S(1)}, bf16[32,4096]{1,0:T(8,128)(2,1)S(1)}, u32[]{:S(2)}, u32[]{:S(2)}) collective-permute-start(bf16[32,4096]{1,0:T(8,128)(2,1)S(1)} %get-tuple-element.24.refs_1_), channel_id=1, source_target_pairs={{0,4},{1,5},{2,6},{3,7},{4,8},{5,9},{6,10},{7,11},{8,12},{9,13},{1... | collective-permute-start | bytes 786440 | tf_op jit(solution)/shard_map/ppermute | solution.py:225
  31.6 12.9 %collective-permute-start.9 = (bf16[32,4096]{1,0:T(8,128)(2,1)S(1)}, bf16[32,4096]{1,0:T(8,128)(2,1)S(1)}, u32[]{:S(2)}, u32[]{:S(2)}) collective-permute-start(bf16[32,4096]{1,0:T(8,128)(2,1)S(1)} %collective-permute-done.8.refs_6_), channel_id=1, source_target_pairs={{0,12},{1,13},{2,14},{3,15},{4,0},{5,1},{6,2},{7,3},{8,4},{9,5},{1... | collective-permute-start | bytes 786440 | tf_op jit(solution)/shard_map/ppermute | solution.py:225
  44.5 9.3 %collective-permute-start.17 = (bf16[32,4096]{1,0:T(8,128)(2,1)S(1)}, bf16[32,4096]{1,0:T(8,128)(2,1)S(1)}, u32[]{:S(2)}, u32[]{:S(2)}) collective-permute-start(bf16[32,4096]{1,0:T(8,128)(2,1)S(1)} %get-tuple-element.28.refs_4_), channel_id=1, source_target_pairs={{0,12},{1,13},{2,14},{3,15},{4,0},{5,1},{6,2},{7,3},{8,4},{9,5},{1... | collective-permute-start | bytes 786440 | tf_op jit(solution)/shard_map/ppermute | solution.py:225
  44.6 17.8 %collective-permute-start.11 = (bf16[32,4096]{1,0:T(8,128)(2,1)S(1)}, bf16[32,4096]{1,0:T(8,128)(2,1)S(1)}, u32[]{:S(2)}, u32[]{:S(2)}) collective-permute-start(bf16[32,4096]{1,0:T(8,128)(2,1)S(1)} %get-tuple-element.27.refs_1_), channel_id=1, source_target_pairs={{0,4},{1,5},{2,6},{3,7},{4,8},{5,9},{6,10},{7,11},{8,12},{9,13},{1... | collective-permute-start | bytes 786440 | tf_op jit(solution)/shard_map/ppermute | solution.py:225
  46.6 15.8 %collective-permute-start.12 = (bf16[32,4096]{1,0:T(8,128)(2,1)S(1)}, bf16[32,4096]{1,0:T(8,128)(2,1)S(1)}, u32[]{:S(2)}, u32[]{:S(2)}) collective-permute-start(bf16[32,4096]{1,0:T(8,128)(2,1)S(1)} %get-tuple-element.28.refs_4_), channel_id=1, source_target_pairs={{0,4},{1,5},{2,6},{3,7},{4,8},{5,9},{6,10},{7,11},{8,12},{9,13},{1... | collective-permute-start | bytes 786440 | tf_op jit(solution)/shard_map/ppermute | solution.py:225
  53.8 11.3 %collective-permute-start.18 = (bf16[32,4096]{1,0:T(8,128)(2,1)S(1)}, bf16[32,4096]{1,0:T(8,128)(2,1)S(1)}, u32[]{:S(2)}, u32[]{:S(2)}) collective-permute-start(bf16[32,4096]{1,0:T(8,128)(2,1)S(1)} %fence.10.refs_6_), channel_id=1, source_target_pairs={{0,12},{1,13},{2,14},{3,15},{4,0},{5,1},{6,2},{7,3},{8,4},{9,5},{1... | collective-permute-start | bytes 786440 | tf_op jit(solution)/shard_map/ppermute | solution.py:225
  57.1 15.2 %collective-permute-start.16 = (bf16[768,128]{1,0:T(8,128)(2,1)S(1)}, bf16[768,128]{1,0:T(8,128)(2,1)S(1)}, u32[]{:S(2)}, u32[]{:S(2)}) collective-permute-start(bf16[768,128]{1,0:T(8,128)(2,1)S(1)} %get-tuple-element.31.refs_1_.refs_4_), channel_id=1, source_target_pairs={{1,48},{3,50},{5,52},{7,54},{9,56},{11,58},{13,60},{15,62},{16,1},... | collective-permute-start | bytes 589832 | tf_op jit(solution)/shard_map/ppermute | solution.py:289
  57.8 14.5 %collective-permute-start.14 = (bf16[768,128]{1,0:T(8,128)(2,1)S(1)}, bf16[768,128]{1,0:T(8,128)(2,1)S(1)}, u32[]{:S(2)}, u32[]{:S(2)}) collective-permute-start(bf16[768,128]{1,0:T(8,128)(2,1)S(1)} %get-tuple-element.29), channel_id=1, source_target_pairs={{0,33},{1,17},{2,35},{3,19},{4,37},{5,21},{6,39},{7,23},{8,41},{9,... | collective-permute-start | bytes 589832 | tf_op jit(solution)/shard_map/ppermute | solution.py:289
  62.4 9.9 %collective-permute-start.15 = (bf16[768,128]{1,0:T(8,128)(2,1)S(1)}, bf16[768,128]{1,0:T(8,128)(2,1)S(1)}, u32[]{:S(2)}, u32[]{:S(2)}) collective-permute-start(bf16[768,128]{1,0:T(8,128)(2,1)S(1)} %get-tuple-element.30), channel_id=1, source_target_pairs={{0,1},{1,49},{2,3},{3,51},{4,5},{5,53},{6,7},{7,55},{8,9},{9,57},{... | collective-permute-start | bytes 589832 | tf_op jit(solution)/shard_map/ppermute | solution.py:289
  62.4 10.5 %collective-permute-start.13 = (bf16[768,128]{1,0:T(8,128)(2,1)S(1)}, bf16[768,128]{1,0:T(8,128)(2,1)S(1)}, u32[]{:S(2)}, u32[]{:S(2)}) collective-permute-start(bf16[768,128]{1,0:T(8,128)(2,1)S(1)} %fence.9), channel_id=1, source_target_pairs={{0,32},{1,16},{2,34},{3,18},{4,36},{5,20},{6,38},{7,22},{8,40},{9,... | collective-permute-start | bytes 589832 | tf_op jit(solution)/shard_map/ppermute | solution.py:289
  72.3 15.9 %copy-start = (s32[768]{0:T(1024)S(1)}, s32[768]{0:T(1024)}, u32[]{:S(2)}) copy-start(s32[768]{0:T(1024)} %param.9) | copy-start | bytes 9220
  72.9 9.2 %collective-permute-start.19 = (bf16[768,128]{1,0:T(8,128)(2,1)S(1)}, bf16[768,128]{1,0:T(8,128)(2,1)S(1)}, u32[]{:S(2)}, u32[]{:S(2)}) collective-permute-start(bf16[768,128]{1,0:T(8,128)(2,1)S(1)} %get-tuple-element.35), channel_id=1, source_target_pairs={{0,32},{1,16},{2,34},{3,18},{4,36},{5,20},{6,38},{7,22},{8,40},{9,... | collective-permute-start | bytes 589832 | tf_op jit(solution)/shard_map/ppermute | solution.py:289
  74.7 10.5 %collective-permute-start.20 = (bf16[768,128]{1,0:T(8,128)(2,1)S(1)}, bf16[768,128]{1,0:T(8,128)(2,1)S(1)}, u32[]{:S(2)}, u32[]{:S(2)}) collective-permute-start(bf16[768,128]{1,0:T(8,128)(2,1)S(1)} %get-tuple-element.36), channel_id=1, source_target_pairs={{0,33},{1,17},{2,35},{3,19},{4,37},{5,21},{6,39},{7,23},{8,41},{9,... | collective-permute-start | bytes 589832 | tf_op jit(solution)/shard_map/ppermute | solution.py:289
  74.7 10.5 %collective-permute-start.21 = (bf16[768,128]{1,0:T(8,128)(2,1)S(1)}, bf16[768,128]{1,0:T(8,128)(2,1)S(1)}, u32[]{:S(2)}, u32[]{:S(2)}) collective-permute-start(bf16[768,128]{1,0:T(8,128)(2,1)S(1)} %get-tuple-element.37), channel_id=1, source_target_pairs={{0,1},{1,49},{2,3},{3,51},{4,5},{5,53},{6,7},{7,55},{8,9},{9,57},{... | collective-permute-start | bytes 589832 | tf_op jit(solution)/shard_map/ppermute | solution.py:289
  74.7 10.5 %collective-permute-start.22 = (bf16[768,128]{1,0:T(8,128)(2,1)S(1)}, bf16[768,128]{1,0:T(8,128)(2,1)S(1)}, u32[]{:S(2)}, u32[]{:S(2)}) collective-permute-start(bf16[768,128]{1,0:T(8,128)(2,1)S(1)} %get-tuple-element.38.refs_9_), channel_id=1, source_target_pairs={{1,48},{3,50},{5,52},{7,54},{9,56},{11,58},{13,60},{15,62},{16,1},... | collective-permute-start | bytes 589832 | tf_op jit(solution)/shard_map/ppermute | solution.py:289
  85.5 7.5 %collective-permute-start.23 = (bf16[64,768]{1,0:T(8,128)(2,1)S(1)}, bf16[64,768]{1,0:T(8,128)(2,1)S(1)}, u32[]{:S(2)}, u32[]{:S(2)}) collective-permute-start(bf16[64,768]{1,0:T(8,128)(2,1)S(1)} %get-tuple-element.40), channel_id=1, source_target_pairs={{0,64},{16,80},{32,96},{48,112},{64,128},{80,144},{96,160},{112,17... | collective-permute-start | bytes 294920 | tf_op jit(solution)/shard_map/ppermute | solution.py:308
  86.6 7.5 %collective-permute-start.24 = (bf16[64,768]{1,0:T(8,128)(2,1)S(1)}, bf16[64,768]{1,0:T(8,128)(2,1)S(1)}, u32[]{:S(2)}, u32[]{:S(2)}) collective-permute-start(bf16[64,768]{1,0:T(8,128)(2,1)S(1)} %get-tuple-element.41), channel_id=1, source_target_pairs={{0,128},{16,144},{32,160},{48,176},{64,192},{80,208},{96,224},{112... | collective-permute-start | bytes 294920 | tf_op jit(solution)/shard_map/ppermute | solution.py:308
  87.4 8.3 %collective-permute-start.25 = (bf16[64,768]{1,0:T(8,128)(2,1)S(1)}, bf16[64,768]{1,0:T(8,128)(2,1)S(1)}, u32[]{:S(2)}, u32[]{:S(2)}) collective-permute-start(bf16[64,768]{1,0:T(8,128)(2,1)S(1)} %get-tuple-element.42), channel_id=1, source_target_pairs={{0,192},{16,208},{32,224},{48,240},{64,0},{80,16},{96,32},{112,48}... | collective-permute-start | bytes 294920 | tf_op jit(solution)/shard_map/ppermute | solution.py:308

commit v5 on v2

--- a/solution.py
+++ b/solution.py
@@ -122,9 +122,9 @@
             to_x = 2 * ((z_hi + rel_z) % 2) + core
             away = (to_x - x + 4) % 4
             if rel_core == 0:
-                buf = jnp.where(away == 0, 3, jnp.where(away == 1, 1, jnp.where(away == 2, 0, 2)))
+                buf = jnp.where(away == 0, 1, jnp.where(away == 1, 3, jnp.where(away == 2, 2, 0)))
             else:
-                buf = jnp.where(away == 0, 2, jnp.where(away == 1, 0, jnp.where(away == 2, 1, 3)))
+                buf = jnp.where(away == 0, 0, jnp.where(away == 1, 2, jnp.where(away == 2, 3, 1)))
             for b in range(4):
 
                 @pl.when(buf == b)
@@ -165,7 +165,7 @@
     )(*blocks, mine, other)
 
 
-def cross_sum_kernel(a_ref, b_ref, c_ref, d_ref, own_ref, keep_ref, *outs):
+def cross_sum_kernel(c_ref, d_ref, a_ref, b_ref, own_ref, keep_ref, *outs):
     x, z_lo, _, _, core = place()
     match = (x % 2) == core
     for k in range(4):
@@ -276,24 +276,26 @@
     return along(value, lambda y, z, c: (y, z + 1, c))
 
 
-def gather_blocks(a, b, other):
+def first_scores(a, b, stored, other):
     far_a = beyond(a)
     a_below, a_above = up(a), down(a)
     (b,) = after((b,), other)
     far_b = beyond(b)
     b_below, b_above = up(b), down(b)
     far_a, a_below = after((far_a, a_below), a_above, b_below, b_above)
+    a_opposite = up(a_below)
     far_a_above, far_a_below = down(far_a), up(far_a)
-    a_opposite = up(a_below)
+    far_a_above, far_b = after((far_a_above, far_b))
     far_a_opposite = down(far_a_above)
-    far_b, b_below = after((far_b, b_below), a_opposite, far_a_opposite, far_a_below)
+    far_b_above, far_b_below = down(far_b), up(far_b)
     b_opposite = up(b_below)
-    far_b_above, far_b_below = down(far_b), up(far_b)
+    a_blocks = [a, a_below, a_above, a_opposite, far_a, far_a_below, far_a_above, far_a_opposite]
+    a_bufs = list(partial_scores(a_blocks, stored, other))
+    (far_b_above,) = after((far_b_above,), a_bufs[1])
     far_b_opposite = down(far_b_above)
-    return (
-        [a, a_below, a_above, a_opposite, far_a, far_a_below, far_a_above, far_a_opposite],
-        [b, b_below, b_above, b_opposite, far_b, far_b_below, far_b_above, far_b_opposite],
-    )
+    a_bufs[3:] = after(a_bufs[3:], b_opposite, far_b_below)
+    b_blocks = [b, b_below, b_above, b_opposite, far_b, far_b_below, far_b_above, far_b_opposite]
+    return a_bufs, b_blocks
 
 
 def over_x(bufs):
@@ -301,10 +303,10 @@
         return x % 2 == core
 
     moves = (
+        lambda x, c: (x, 1 - c) if match(x, c) else (x - 1, c),
+        lambda x, c: None if match(x, c) else (x - 1, 1 - c),
         lambda x, c: (x + 2, c) if match(x, c) else (x + 1, 1 - c),
         lambda x, c: (x + 2, 1 - c) if match(x, c) else (x + 1, c),
-        lambda x, c: (x, 1 - c) if match(x, c) else (x - 1, c),
-        lambda x, c: None if match(x, c) else (x - 1, 1 - c),
     )
     return [lax.ppermute(b, ("store", "group"), all_pairs(m)) for b, m in zip(bufs, moves)]
 
@@ -317,15 +319,14 @@
         pltpu.with_memory_space_constraint(v, pltpu.HBM) for v in (lengths, activations, out_grads)
     ]
     a, b = (query_grads(*inputs, n) for n in range(CHUNKS))
-    parts, got = [], ()
-    a_blocks, b_blocks = gather_blocks(a, b, other)
-    for blocks in (a_blocks, b_blocks):
-        blocks[-1:] = after(blocks[-1:], *got) if got else blocks[-1:]
-        bufs = list(partial_scores(blocks, stored, other))
-        if not got:
-            bufs[1:2] = after(bufs[1:2], b_blocks[3], b_blocks[5])
-        got = over_x(bufs)
-        keep, *sends = cross_sum(*got, bufs[3])
+    a_bufs, b_blocks = first_scores(a, b, stored, other)
+    a_got = over_x(a_bufs)
+    b_bufs = list(partial_scores(b_blocks, stored, other))
+    b_bufs = after(b_bufs, *a_got)
+    b_got = over_x(b_bufs)
+    parts = []
+    for got, bufs in ((a_got, a_bufs), (b_got, b_bufs)):
+        keep, *sends = cross_sum(*got, bufs[1])
         parts.append(keep)
         for k, send in enumerate(sends, 1):
             parts.append(lax.ppermute(send, "store", store_pairs(lambda x, z: (x, z + k))))

time: 99 us -> 96.2 us (0.972)
  waiting for transfers between devices: 34.1 us -> 27.9 us
  starting transfers between devices: 46.8 us -> 50.1 us
    ppermute x6, starting transfers between devices: 5.82 us -> 12.9 us  [on_device(): lax.ppermute(send, 'store', store_pairs(lambda x, z: (x, z + k)))]
    ppermute x8, waiting for transfers between devices: 10.9 us -> 5.76 us  [over_x(): lax.ppermute(b, ('store', 'group'), all_pairs(m))]
    ppermute x14, starting transfers between devices: 27.1 us -> 23.3 us  [along(): return lax.ppermute(value, 'group', group_pairs(move))]
    ppermute x14, waiting for transfers between devices: 20.6 us -> 18.5 us  [along(): return lax.ppermute(value, 'group', group_pairs(move))]
  transfers between devices with their start and end apart: 29 -> 29, of which waited for: 13 -> 10; matrix products, arithmetic and copies ran while one was open for 0% -> 0% of each run, Pallas kernels for 11% -> 17%
where the time goes in v5:
time: 96.2 us; the launch traced here: 96 us
  starting transfers between devices  50.1 us (52%)
  waiting for transfers between devices  27.9 us (29%)
  Pallas kernels  17.3 us (18%)
    ppermute x14, starting transfers between devices, along(): return lax.ppermute(value, 'group', group_pairs(move))  23.3 us
    ppermute x14, waiting for transfers between devices, along(): return lax.ppermute(value, 'group', group_pairs(move))  18.5 us
    ppermute x8, starting transfers between devices, over_x(): lax.ppermute(b, ('store', 'group'), all_pairs(m))  14 us
    ppermute x6, starting transfers between devices, on_device(): lax.ppermute(send, 'store', store_pairs(lambda x, z: (x, z + k)))  12.9 us
    pallas_call x2, Pallas kernels, partial_scores(): pl.pallas_call(score_kernel, out_shape=[jax.ShapeDtypeStruct((4 * ROWS, H...  10.9 us
    ppermute x8, waiting for transfers between devices, over_x(): lax.ppermute(b, ('store', 'group'), all_pairs(m))  5.76 us
    pallas_call x2, Pallas kernels, query_grads(): pl.pallas_call(functools.partial(grad_kernel, chunk * ROWS), out_shape=ja...  5.13 us
    ppermute x6, waiting for transfers between devices, on_device(): lax.ppermute(send, 'store', store_pairs(lambda x, z: (x, z + k)))  3.64 us
  transfers between devices with their start and end apart: 29, of which 10 were waited for; matrix products, arithmetic and copies ran while one was open for 0% of the time, Pallas kernels for 17%

profile of v5, /device:TPU:32, one launch (start us, length us, event | category | flops | bytes accessed | tf_op | source)
XLA Modules:
  0.0 96.0 jit_solution(15990261045935343952)
XLA Ops:
  0.0 2.5 %query_grads.2.refs_0_ = bf16[32,4096]{1,0:T(8,128)(2,1)S(1)} custom-call(s32[64]{0:T(128)} %lengths_hbm.3, bf16[64,1,64,256]{3,2,1,0:T(8,128)(2,1)} %acts_hbm.3, bf16[64,1,64,256]{3,2,1,0:T(8,128)(2,1)} %grads_hbm.3), custom_call_target="tpu_custom_call" | custom-call | tf_op jit(solution)/shard_map/query_grads/pallas_call | solution.py:81
  2.5 3.1 %collective-permute-start.2 = (bf16[32,4096]{1,0:T(8,128)(2,1)S(1)}, bf16[32,4096]{1,0:T(8,128)(2,1)S(1)}, u32[]{:S(2)}, u32[]{:S(2)}) collective-permute-start(bf16[32,4096]{1,0:T(8,128)(2,1)S(1)} %query_grads.2.refs_0_), channel_id=1, source_target_pairs={{0,12},{1,13},{2,14},{3,15},{4,0},{5,1},{6,2},{7,3},{8,4},{9,5},{1... | collective-permute-start | bytes 786440 | tf_op jit(solution)/shard_map/ppermute | solution.py:247
  5.6 6.3 %collective-permute-start = (bf16[32,4096]{1,0:T(8,128)(2,1)S(1)}, bf16[32,4096]{1,0:T(8,128)(2,1)S(1)}, u32[]{:S(2)}, u32[]{:S(2)}) collective-permute-start(bf16[32,4096]{1,0:T(8,128)(2,1)S(1)} %query_grads.2.refs_0_), channel_id=1, source_target_pairs={{0,2},{1,3},{2,0},{3,1},{4,6},{5,7},{6,4},{7,5},{8,10},{9,11},{10,... | collective-permute-start | bytes 786440 | tf_op jit(solution)/shard_map/ppermute | solution.py:247
  11.9 2.6 %query_grads.3.refs_0_ = bf16[32,4096]{1,0:T(8,128)(2,1)S(1)} custom-call(s32[64]{0:T(128)} %lengths_hbm.3, bf16[64,1,64,256]{3,2,1,0:T(8,128)(2,1)} %acts_hbm.3, bf16[64,1,64,256]{3,2,1,0:T(8,128)(2,1)} %grads_hbm.3), custom_call_target="tpu_custom_call" | custom-call | tf_op jit(solution)/shard_map/query_grads/pallas_call | solution.py:81
  14.5 0.7 collective-permute-start.4
  15.2 2.7 %collective-permute-start.5 = (bf16[32,4096]{1,0:T(8,128)(2,1)S(1)}, bf16[32,4096]{1,0:T(8,128)(2,1)S(1)}, u32[]{:S(2)}, u32[]{:S(2)}) collective-permute-start(bf16[32,4096]{1,0:T(8,128)(2,1)S(1)} %fence.6.refs_0_), channel_id=1, source_target_pairs={{0,12},{1,13},{2,14},{3,15},{4,0},{5,1},{6,2},{7,3},{8,4},{9,5},{1... | collective-permute-start | bytes 786440 | tf_op jit(solution)/shard_map/ppermute | solution.py:247
  18.0 1.9 %collective-permute-start.9 = (bf16[32,4096]{1,0:T(8,128)(2,1)S(1)}, bf16[32,4096]{1,0:T(8,128)(2,1)S(1)}, u32[]{:S(2)}, u32[]{:S(2)}) collective-permute-start(bf16[32,4096]{1,0:T(8,128)(2,1)S(1)} %fence.6.refs_0_), channel_id=1, source_target_pairs={{0,2},{1,3},{2,0},{3,1},{4,6},{5,7},{6,4},{7,5},{8,10},{9,11},{10,... | collective-permute-start | bytes 786440 | tf_op jit(solution)/shard_map/ppermute | solution.py:247
  19.9 4.7 %collective-permute-done.refs_0_ = bf16[32,4096]{1,0:T(8,128)(2,1)S(1)} collective-permute-done((bf16[32,4096]{1,0:T(8,128)(2,1)S(1)}, bf16[32,4096]{1,0:T(8,128)(2,1)S(1)}, u32[]{:S(2)}, u32[]{:S(2)}) %collective-permute-start) | collective-permute-done | bytes 262176 | tf_op jit(solution)/shard_map/ppermute | solution.py:247
  24.6 2.2 %collective-permute-done.4.refs_3_.refs_1_ = bf16[32,4096]{1,0:T(8,128)(2,1)S(1)} collective-permute-done((bf16[32,4096]{1,0:T(8,128)(2,1)S(1)}, bf16[32,4096]{1,0:T(8,128)(2,1)S(1)}, u32[]{:S(2)}, u32[]{:S(2)}) %collective-permute-start.4) | collective-permute-done | bytes 262176 | tf_op jit(solution)/shard_map/ppermute | solution.py:247
  27.1 1.8 %collective-permute-start.7 = (bf16[32,4096]{1,0:T(8,128)(2,1)S(1)}, bf16[32,4096]{1,0:T(8,128)(2,1)S(1)}, u32[]{:S(2)}, u32[]{:S(2)}) collective-permute-start(bf16[32,4096]{1,0:T(8,128)(2,1)S(1)} %get-tuple-element.30.refs_4_), channel_id=1, source_target_pairs={{0,4},{1,5},{2,6},{3,7},{4,8},{5,9},{6,10},{7,11},{8,12},{9,13},{1... | collective-permute-start | bytes 786440 | tf_op jit(solution)/shard_map/ppermute | solution.py:247
  28.9 6.3 %collective-permute-done.9.refs_1_ = bf16[32,4096]{1,0:T(8,128)(2,1)S(1)} collective-permute-done((bf16[32,4096]{1,0:T(8,128)(2,1)S(1)}, bf16[32,4096]{1,0:T(8,128)(2,1)S(1)}, u32[]{:S(2)}, u32[]{:S(2)}) %collective-permute-start.9) | collective-permute-done | bytes 262176 | tf_op jit(solution)/shard_map/ppermute | solution.py:247
  35.3 1.2 %collective-permute-start.10 = (bf16[32,4096]{1,0:T(8,128)(2,1)S(1)}, bf16[32,4096]{1,0:T(8,128)(2,1)S(1)}, u32[]{:S(2)}, u32[]{:S(2)}) collective-permute-start(bf16[32,4096]{1,0:T(8,128)(2,1)S(1)} %get-tuple-element.31.refs_6_), channel_id=1, source_target_pairs={{0,12},{1,13},{2,14},{3,15},{4,0},{5,1},{6,2},{7,3},{8,4},{9,5},{1... | collective-permute-start | bytes 786440 | tf_op jit(solution)/shard_map/ppermute | solution.py:247
  36.6 1.9 %collective-permute-start.14 = (bf16[32,4096]{1,0:T(8,128)(2,1)S(1)}, bf16[32,4096]{1,0:T(8,128)(2,1)S(1)}, u32[]{:S(2)}, u32[]{:S(2)}) collective-permute-start(bf16[32,4096]{1,0:T(8,128)(2,1)S(1)} %collective-permute-done.4.refs_3_.refs_1_), channel_id=1, source_target_pairs={{0,4},{1,5},{2,6},{3,7},{4,8},{5,9},{6,10},{7,11},{8,12},{9,13},{1... | collective-permute-start | bytes 786440 | tf_op jit(solution)/shard_map/ppermute | solution.py:247
  38.5 0.9 collective-permute-start.15
  39.4 3.8 %collective-permute-done.6.refs_3_ = bf16[32,4096]{1,0:T(8,128)(2,1)S(1)} collective-permute-done((bf16[32,4096]{1,0:T(8,128)(2,1)S(1)}, bf16[32,4096]{1,0:T(8,128)(2,1)S(1)}, u32[]{:S(2)}, u32[]{:S(2)}) %collective-permute-start.6) | collective-permute-done | bytes 262176 | tf_op jit(solution)/shard_map/ppermute | solution.py:247
  43.1 1.4 %collective-permute-done.10.refs_7_ = bf16[32,4096]{1,0:T(8,128)(2,1)S(1)} collective-permute-done((bf16[32,4096]{1,0:T(8,128)(2,1)S(1)}, bf16[32,4096]{1,0:T(8,128)(2,1)S(1)}, u32[]{:S(2)}, u32[]{:S(2)}) %collective-permute-start.10) | collective-permute-done | bytes 262176 | tf_op jit(solution)/shard_map/ppermute | solution.py:247
  44.5 5.4 %partial_scores.2 = (bf16[128,768]{1,0:T(8,128)(2,1)S(1)}, bf16[128,768]{1,0:T(8,128)(2,1)S(1)}, bf16[128,768]{1,0:T(8,128)(2,1)S(1)}, bf16[128,768]{1,0:T(8,128)(2,1)S(1)}) custom-call(bf16[32,4096]{1,0:T(8,128)(2,1)S(1)} %query_grads.2.refs_0_, bf16[32,4096]{1,0:T(8,128)(2,1)S(1)} %get-tuple-element.29.refs_1_, ...), custom_call_target="tpu_custom_call" | custom-call | flops 1 | bytes 1 | tf_op jit(solution)/shard_map/partial_scores/pallas_call | solution.py:148
  50.0 2.4 %collective-permute-start.21 = (bf16[32,4096]{1,0:T(8,128)(2,1)S(1)}, bf16[32,4096]{1,0:T(8,128)(2,1)S(1)}, u32[]{:S(2)}, u32[]{:S(2)}) collective-permute-start(bf16[32,4096]{1,0:T(8,128)(2,1)S(1)} %fence.10.refs_6_), channel_id=1, source_target_pairs={{0,12},{1,13},{2,14},{3,15},{4,0},{5,1},{6,2},{7,3},{8,4},{9,5},{1... | collective-permute-start | bytes 786440 | tf_op jit(solution)/shard_map/ppermute | solution.py:247
  53.1 4.6 %collective-permute-start.16 = (bf16[128,768]{1,0:T(8,128)(2,1)S(1)}, bf16[128,768]{1,0:T(8,128)(2,1)S(1)}, u32[]{:S(2)}, u32[]{:S(2)}) collective-permute-start(bf16[128,768]{1,0:T(8,128)(2,1)S(1)} %fence.9), channel_id=1, source_target_pairs={{0,33},{1,17},{2,35},{3,19},{4,37},{5,21},{6,39},{7,23},{8,41},{9,... | collective-permute-start | bytes 589832 | tf_op jit(solution)/shard_map/ppermute | solution.py:311
  57.7 2.8 %collective-permute-start.13 = (bf16[128,768]{1,0:T(8,128)(2,1)S(1)}, bf16[128,768]{1,0:T(8,128)(2,1)S(1)}, u32[]{:S(2)}, u32[]{:S(2)}) collective-permute-start(bf16[128,768]{1,0:T(8,128)(2,1)S(1)} %get-tuple-element.34), channel_id=1, source_target_pairs={{0,32},{1,16},{2,34},{3,18},{4,36},{5,20},{6,38},{7,22},{8,40},{9,... | collective-permute-start | bytes 589832 | tf_op jit(solution)/shard_map/ppermute | solution.py:311
  60.6 5.4 %partial_scores.3 = (bf16[128,768]{1,0:T(8,128)(2,1)S(1)}, bf16[128,768]{1,0:T(8,128)(2,1)S(1)}, bf16[128,768]{1,0:T(8,128)(2,1)S(1)}, bf16[128,768]{1,0:T(8,128)(2,1)S(1)}) custom-call(bf16[32,4096]{1,0:T(8,128)(2,1)S(1)} %fence.6.refs_0_, bf16[32,4096]{1,0:T(8,128)(2,1)S(1)} %collective-permute-done.4.refs_3_.refs_1_, ...), custom_call_target="tpu_custom_call" | custom-call | flops 1 | bytes 1 | tf_op jit(solution)/shard_map/partial_scores/pallas_call | solution.py:148
  66.1 2.4 %collective-permute-done.13.a_ref.refs_6_ = bf16[128,768]{1,0:T(8,128)(2,1)S(1)} collective-permute-done((bf16[128,768]{1,0:T(8,128)(2,1)S(1)}, bf16[128,768]{1,0:T(8,128)(2,1)S(1)}, u32[]{:S(2)}, u32[]{:S(2)}) %collective-permute-start.13) | collective-permute-done | bytes 196640 | tf_op jit(solution)/shard_map/ppermute | solution.py:311
  68.4 0.7 collective-permute-start.23
  69.1 1.9 %collective-permute-start.24 = (bf16[128,768]{1,0:T(8,128)(2,1)S(1)}, bf16[128,768]{1,0:T(8,128)(2,1)S(1)}, u32[]{:S(2)}, u32[]{:S(2)}) collective-permute-start(bf16[128,768]{1,0:T(8,128)(2,1)S(1)} %get-tuple-element.47), channel_id=1, source_target_pairs={{0,32},{1,16},{2,34},{3,18},{4,36},{5,20},{6,38},{7,22},{8,40},{9,... | collective-permute-start | bytes 589832 | tf_op jit(solution)/shard_map/ppermute | solution.py:311
  71.0 3.3 %collective-permute-start.25 = (bf16[128,768]{1,0:T(8,128)(2,1)S(1)}, bf16[128,768]{1,0:T(8,128)(2,1)S(1)}, u32[]{:S(2)}, u32[]{:S(2)}) collective-permute-start(bf16[128,768]{1,0:T(8,128)(2,1)S(1)} %get-tuple-element.48), channel_id=1, source_target_pairs={{0,33},{1,17},{2,35},{3,19},{4,37},{5,21},{6,39},{7,23},{8,41},{9,... | collective-permute-start | bytes 589832 | tf_op jit(solution)/shard_map/ppermute | solution.py:311
  74.7 1.4 %collective-permute-done.22.c_ref = bf16[128,768]{1,0:T(8,128)(2,1)S(1)} collective-permute-done((bf16[128,768]{1,0:T(8,128)(2,1)S(1)}, bf16[128,768]{1,0:T(8,128)(2,1)S(1)}, u32[]{:S(2)}, u32[]{:S(2)}) %collective-permute-start.22) | collective-permute-done | bytes 196640 | tf_op jit(solution)/shard_map/ppermute | solution.py:311
  76.0 5.5 %collective-permute-start.18 = (bf16[32,768]{1,0:T(8,128)(2,1)S(1)}, bf16[32,768]{1,0:T(8,128)(2,1)S(1)}, u32[]{:S(2)}, u32[]{:S(2)}) collective-permute-start(bf16[32,768]{1,0:T(8,128)(2,1)S(1)} %get-tuple-element.39), channel_id=1, source_target_pairs={{0,128},{16,144},{32,160},{48,176},{64,192},{80,208},{96,224},{112... | collective-permute-start | bytes 147464 | tf_op jit(solution)/shard_map/ppermute | solution.py:332
  81.6 2.0 %collective-permute-done.25.b_ref = bf16[128,768]{1,0:T(8,128)(2,1)S(1)} collective-permute-done((bf16[128,768]{1,0:T(8,128)(2,1)S(1)}, bf16[128,768]{1,0:T(8,128)(2,1)S(1)}, u32[]{:S(2)}, u32[]{:S(2)}) %collective-permute-start.25) | collective-permute-done | bytes 196640 | tf_op jit(solution)/shard_map/ppermute | solution.py:311
  83.9 6.9 %collective-permute-start.27 = (bf16[32,768]{1,0:T(8,128)(2,1)S(1)}, bf16[32,768]{1,0:T(8,128)(2,1)S(1)}, u32[]{:S(2)}, u32[]{:S(2)}) collective-permute-start(bf16[32,768]{1,0:T(8,128)(2,1)S(1)} %get-tuple-element.51), channel_id=1, source_target_pairs={{0,128},{16,144},{32,160},{48,176},{64,192},{80,208},{96,224},{112... | collective-permute-start | bytes 147464 | tf_op jit(solution)/shard_map/ppermute | solution.py:332
  91.3 2.2 %collective-permute-done.27.refs_6_ = bf16[32,768]{1,0:T(8,128)(2,1)S(1)} collective-permute-done((bf16[32,768]{1,0:T(8,128)(2,1)S(1)}, bf16[32,768]{1,0:T(8,128)(2,1)S(1)}, u32[]{:S(2)}, u32[]{:S(2)}) %collective-permute-start.27) | collective-permute-done | bytes 49184 | tf_op jit(solution)/shard_map/ppermute | solution.py:332
  93.6 1.4 %collective-permute-done.28.refs_7_ = bf16[32,768]{1,0:T(8,128)(2,1)S(1)} collective-permute-done((bf16[32,768]{1,0:T(8,128)(2,1)S(1)}, bf16[32,768]{1,0:T(8,128)(2,1)S(1)}, u32[]{:S(2)}, u32[]{:S(2)}) %collective-permute-start.28) | collective-permute-done | bytes 49184 | tf_op jit(solution)/shard_map/ppermute | solution.py:332
  95.0 1.1 %final_sum.1 = f32[64,768]{1,0:T(8,128)} custom-call(f32[32,768]{1,0:T(8,128)S(1)} %get-tuple-element.37.refs_0_, bf16[32,768]{1,0:T(8,128)(2,1)S(1)} %collective-permute-done.17.refs_1_, bf16[32,768]{1,0:T(8,128)(2,1)S(1)} %collective-permute-done.18.refs_2_, bf16[32,768]{1,0:T(8,128)(2,1)S(1)} %collective-permute-done.19.refs_3_, ...), custom_call_target="tpu_custom_call" | custom-call | tf_op jit(solution)/shard_map/final_sum/pallas_call | solution.py:214
  (47 shorter events, 2.2 us)
Async XLA Ops:
  0.0 14.5 %collective-permute-start.3 = (bf16[768,4096]{1,0:T(8,128)(2,1)}, bf16[768,4096]{1,0:T(8,128)(2,1)S(1)}, u32[]{:S(2)}, u32[]{:S(2)}) collective-permute-start(bf16[768,4096]{1,0:T(8,128)(2,1)} %bitcast.1), channel_id=1, source_target_pairs={{0,1},{1,0},{2,3},{3,2},{4,5},{5,4},{6,7},{7,6},{8,9},{9,8},{10,11... | collective-permute-start | bytes 18874376 | tf_op jit(solution)/shard_map/ppermute | solution.py:316
  2.5 15.4 %collective-permute-start.2 = (bf16[32,4096]{1,0:T(8,128)(2,1)S(1)}, bf16[32,4096]{1,0:T(8,128)(2,1)S(1)}, u32[]{:S(2)}, u32[]{:S(2)}) collective-permute-start(bf16[32,4096]{1,0:T(8,128)(2,1)S(1)} %query_grads.2.refs_0_), channel_id=1, source_target_pairs={{0,12},{1,13},{2,14},{3,15},{4,0},{5,1},{6,2},{7,3},{8,4},{9,5},{1... | collective-permute-start | bytes 786440 | tf_op jit(solution)/shard_map/ppermute | solution.py:247
  5.6 19.1 %collective-permute-start = (bf16[32,4096]{1,0:T(8,128)(2,1)S(1)}, bf16[32,4096]{1,0:T(8,128)(2,1)S(1)}, u32[]{:S(2)}, u32[]{:S(2)}) collective-permute-start(bf16[32,4096]{1,0:T(8,128)(2,1)S(1)} %query_grads.2.refs_0_), channel_id=1, source_target_pairs={{0,2},{1,3},{2,0},{3,1},{4,6},{5,7},{6,4},{7,5},{8,10},{9,11},{10,... | collective-permute-start | bytes 786440 | tf_op jit(solution)/shard_map/ppermute | solution.py:247
  11.9 12.8 %collective-permute-start.1 = (bf16[32,4096]{1,0:T(8,128)(2,1)S(1)}, bf16[32,4096]{1,0:T(8,128)(2,1)S(1)}, u32[]{:S(2)}, u32[]{:S(2)}) collective-permute-start(bf16[32,4096]{1,0:T(8,128)(2,1)S(1)} %query_grads.2.refs_0_), channel_id=1, source_target_pairs={{0,4},{1,5},{2,6},{3,7},{4,8},{5,9},{6,10},{7,11},{8,12},{9,13},{1... | collective-permute-start | bytes 786440 | tf_op jit(solution)/shard_map/ppermute | solution.py:247
  11.9 32.7 %slice-start = ((s8[6291456]{0:T(1024)(128)(4,1)}), s8[4194304]{0:T(1024)(128)(4,1)S(1)}, s32[]{:S(2)}) async-start(s8[6291456]{0:T(1024)(128)(4,1)} %bitcast.2), calls=%async_computation | async-start | bytes 8388608
  14.5 30.0 %slice-start.1 = ((s8[6291456]{0:T(1024)(128)(4,1)}), s8[2097152]{0:T(1024)(128)(4,1)S(1)}, s32[]{:S(2)}) async-start(s8[6291456]{0:T(1024)(128)(4,1)} %bitcast.2), calls=%async_computation.1 | async-start | bytes 4194304
  14.5 12.3 %collective-permute-start.4 = (bf16[32,4096]{1,0:T(8,128)(2,1)S(1)}, bf16[32,4096]{1,0:T(8,128)(2,1)S(1)}, u32[]{:S(2)}, u32[]{:S(2)}) collective-permute-start(bf16[32,4096]{1,0:T(8,128)(2,1)S(1)} %fence.6.refs_0_), channel_id=1, source_target_pairs={{0,4},{1,5},{2,6},{3,7},{4,8},{5,9},{6,10},{7,11},{8,12},{9,13},{1... | collective-permute-start | bytes 786440 | tf_op jit(solution)/shard_map/ppermute | solution.py:247
  15.2 11.7 %collective-permute-start.5 = (bf16[32,4096]{1,0:T(8,128)(2,1)S(1)}, bf16[32,4096]{1,0:T(8,128)(2,1)S(1)}, u32[]{:S(2)}, u32[]{:S(2)}) collective-permute-start(bf16[32,4096]{1,0:T(8,128)(2,1)S(1)} %fence.6.refs_0_), channel_id=1, source_target_pairs={{0,12},{1,13},{2,14},{3,15},{4,0},{5,1},{6,2},{7,3},{8,4},{9,5},{1... | collective-permute-start | bytes 786440 | tf_op jit(solution)/shard_map/ppermute | solution.py:247
  18.0 17.3 %collective-permute-start.9 = (bf16[32,4096]{1,0:T(8,128)(2,1)S(1)}, bf16[32,4096]{1,0:T(8,128)(2,1)S(1)}, u32[]{:S(2)}, u32[]{:S(2)}) collective-permute-start(bf16[32,4096]{1,0:T(8,128)(2,1)S(1)} %fence.6.refs_0_), channel_id=1, source_target_pairs={{0,2},{1,3},{2,0},{3,1},{4,6},{5,7},{6,4},{7,5},{8,10},{9,11},{10,... | collective-permute-start | bytes 786440 | tf_op jit(solution)/shard_map/ppermute | solution.py:247
  26.9 8.4 %collective-permute-start.8 = (bf16[32,4096]{1,0:T(8,128)(2,1)S(1)}, bf16[32,4096]{1,0:T(8,128)(2,1)S(1)}, u32[]{:S(2)}, u32[]{:S(2)}) collective-permute-start(bf16[32,4096]{1,0:T(8,128)(2,1)S(1)} %get-tuple-element.30.refs_4_), channel_id=1, source_target_pairs={{0,12},{1,13},{2,14},{3,15},{4,0},{5,1},{6,2},{7,3},{8,4},{9,5},{1... | collective-permute-start | bytes 786440 | tf_op jit(solution)/shard_map/ppermute | solution.py:247
  27.1 11.4 %collective-permute-start.7 = (bf16[32,4096]{1,0:T(8,128)(2,1)S(1)}, bf16[32,4096]{1,0:T(8,128)(2,1)S(1)}, u32[]{:S(2)}, u32[]{:S(2)}) collective-permute-start(bf16[32,4096]{1,0:T(8,128)(2,1)S(1)} %get-tuple-element.30.refs_4_), channel_id=1, source_target_pairs={{0,4},{1,5},{2,6},{3,7},{4,8},{5,9},{6,10},{7,11},{8,12},{9,13},{1... | collective-permute-start | bytes 786440 | tf_op jit(solution)/shard_map/ppermute | solution.py:247
  28.9 14.2 %collective-permute-start.6 = (bf16[32,4096]{1,0:T(8,128)(2,1)S(1)}, bf16[32,4096]{1,0:T(8,128)(2,1)S(1)}, u32[]{:S(2)}, u32[]{:S(2)}) collective-permute-start(bf16[32,4096]{1,0:T(8,128)(2,1)S(1)} %get-tuple-element.29.refs_1_), channel_id=1, source_target_pairs={{0,4},{1,5},{2,6},{3,7},{4,8},{5,9},{6,10},{7,11},{8,12},{9,13},{1... | collective-permute-start | bytes 786440 | tf_op jit(solution)/shard_map/ppermute | solution.py:247
  35.3 9.2 %collective-permute-start.10 = (bf16[32,4096]{1,0:T(8,128)(2,1)S(1)}, bf16[32,4096]{1,0:T(8,128)(2,1)S(1)}, u32[]{:S(2)}, u32[]{:S(2)}) collective-permute-start(bf16[32,4096]{1,0:T(8,128)(2,1)S(1)} %get-tuple-element.31.refs_6_), channel_id=1, source_target_pairs={{0,12},{1,13},{2,14},{3,15},{4,0},{5,1},{6,2},{7,3},{8,4},{9,5},{1... | collective-permute-start | bytes 786440 | tf_op jit(solution)/shard_map/ppermute | solution.py:247
  36.4 13.5 %collective-permute-start.20 = (bf16[32,4096]{1,0:T(8,128)(2,1)S(1)}, bf16[32,4096]{1,0:T(8,128)(2,1)S(1)}, u32[]{:S(2)}, u32[]{:S(2)}) collective-permute-start(bf16[32,4096]{1,0:T(8,128)(2,1)S(1)} %get-tuple-element.36.refs_4_), channel_id=1, source_target_pairs={{0,12},{1,13},{2,14},{3,15},{4,0},{5,1},{6,2},{7,3},{8,4},{9,5},{1... | collective-permute-start | bytes 786440 | tf_op jit(solution)/shard_map/ppermute | solution.py:247
  36.6 16.5 %collective-permute-start.14 = (bf16[32,4096]{1,0:T(8,128)(2,1)S(1)}, bf16[32,4096]{1,0:T(8,128)(2,1)S(1)}, u32[]{:S(2)}, u32[]{:S(2)}) collective-permute-start(bf16[32,4096]{1,0:T(8,128)(2,1)S(1)} %collective-permute-done.4.refs_3_.refs_1_), channel_id=1, source_target_pairs={{0,4},{1,5},{2,6},{3,7},{4,8},{5,9},{6,10},{7,11},{8,12},{9,13},{1... | collective-permute-start | bytes 786440 | tf_op jit(solution)/shard_map/ppermute | solution.py:247
  38.5 14.7 %collective-permute-start.15 = (bf16[32,4096]{1,0:T(8,128)(2,1)S(1)}, bf16[32,4096]{1,0:T(8,128)(2,1)S(1)}, u32[]{:S(2)}, u32[]{:S(2)}) collective-permute-start(bf16[32,4096]{1,0:T(8,128)(2,1)S(1)} %get-tuple-element.36.refs_4_), channel_id=1, source_target_pairs={{0,4},{1,5},{2,6},{3,7},{4,8},{5,9},{6,10},{7,11},{8,12},{9,13},{1... | collective-permute-start | bytes 786440 | tf_op jit(solution)/shard_map/ppermute | solution.py:247
  50.0 10.6 %collective-permute-start.21 = (bf16[32,4096]{1,0:T(8,128)(2,1)S(1)}, bf16[32,4096]{1,0:T(8,128)(2,1)S(1)}, u32[]{:S(2)}, u32[]{:S(2)}) collective-permute-start(bf16[32,4096]{1,0:T(8,128)(2,1)S(1)} %fence.10.refs_6_), channel_id=1, source_target_pairs={{0,12},{1,13},{2,14},{3,15},{4,0},{5,1},{6,2},{7,3},{8,4},{9,5},{1... | collective-permute-start | bytes 786440 | tf_op jit(solution)/shard_map/ppermute | solution.py:247
  52.4 13.6 %collective-permute-start.12 = (bf16[128,768]{1,0:T(8,128)(2,1)S(1)}, bf16[128,768]{1,0:T(8,128)(2,1)S(1)}, u32[]{:S(2)}, u32[]{:S(2)}) collective-permute-start(bf16[128,768]{1,0:T(8,128)(2,1)S(1)} %get-tuple-element.33.own_ref.refs_1_), channel_id=1, source_target_pairs={{1,48},{3,50},{5,52},{7,54},{9,56},{11,58},{13,60},{15,62},{16,1},... | collective-permute-start | bytes 589832 | tf_op jit(solution)/shard_map/ppermute | solution.py:311
  53.1 12.9 %collective-permute-start.16 = (bf16[128,768]{1,0:T(8,128)(2,1)S(1)}, bf16[128,768]{1,0:T(8,128)(2,1)S(1)}, u32[]{:S(2)}, u32[]{:S(2)}) collective-permute-start(bf16[128,768]{1,0:T(8,128)(2,1)S(1)} %fence.9), channel_id=1, source_target_pairs={{0,33},{1,17},{2,35},{3,19},{4,37},{5,21},{6,39},{7,23},{8,41},{9,... | collective-permute-start | bytes 589832 | tf_op jit(solution)/shard_map/ppermute | solution.py:311
  57.7 8.3 %collective-permute-start.11 = (bf16[128,768]{1,0:T(8,128)(2,1)S(1)}, bf16[128,768]{1,0:T(8,128)(2,1)S(1)}, u32[]{:S(2)}, u32[]{:S(2)}) collective-permute-start(bf16[128,768]{1,0:T(8,128)(2,1)S(1)} %get-tuple-element.32), channel_id=1, source_target_pairs={{0,1},{1,49},{2,3},{3,51},{4,5},{5,53},{6,7},{7,55},{8,9},{9,57},{... | collective-permute-start | bytes 589832 | tf_op jit(solution)/shard_map/ppermute | solution.py:311
  57.7 10.7 %collective-permute-start.13 = (bf16[128,768]{1,0:T(8,128)(2,1)S(1)}, bf16[128,768]{1,0:T(8,128)(2,1)S(1)}, u32[]{:S(2)}, u32[]{:S(2)}) collective-permute-start(bf16[128,768]{1,0:T(8,128)(2,1)S(1)} %get-tuple-element.34), channel_id=1, source_target_pairs={{0,32},{1,16},{2,34},{3,18},{4,36},{5,20},{6,38},{7,22},{8,40},{9,... | collective-permute-start | bytes 589832 | tf_op jit(solution)/shard_map/ppermute | solution.py:311
  66.0 24.9 %copy-start = (s32[768]{0:T(1024)S(1)}, s32[768]{0:T(1024)}, u32[]{:S(2)}) copy-start(s32[768]{0:T(1024)} %param.9) | copy-start | bytes 9220
  68.4 7.6 %collective-permute-start.22 = (bf16[128,768]{1,0:T(8,128)(2,1)S(1)}, bf16[128,768]{1,0:T(8,128)(2,1)S(1)}, u32[]{:S(2)}, u32[]{:S(2)}) collective-permute-start(bf16[128,768]{1,0:T(8,128)(2,1)S(1)} %get-tuple-element.45), channel_id=1, source_target_pairs={{0,1},{1,49},{2,3},{3,51},{4,5},{5,53},{6,7},{7,55},{8,9},{9,57},{... | collective-permute-start | bytes 589832 | tf_op jit(solution)/shard_map/ppermute | solution.py:311
  68.4 13.2 %collective-permute-start.23 = (bf16[128,768]{1,0:T(8,128)(2,1)S(1)}, bf16[128,768]{1,0:T(8,128)(2,1)S(1)}, u32[]{:S(2)}, u32[]{:S(2)}) collective-permute-start(bf16[128,768]{1,0:T(8,128)(2,1)S(1)} %get-tuple-element.46.own_ref), channel_id=1, source_target_pairs={{1,48},{3,50},{5,52},{7,54},{9,56},{11,58},{13,60},{15,62},{16,1},... | collective-permute-start | bytes 589832 | tf_op jit(solution)/shard_map/ppermute | solution.py:311
  69.1 12.5 %collective-permute-start.24 = (bf16[128,768]{1,0:T(8,128)(2,1)S(1)}, bf16[128,768]{1,0:T(8,128)(2,1)S(1)}, u32[]{:S(2)}, u32[]{:S(2)}) collective-permute-start(bf16[128,768]{1,0:T(8,128)(2,1)S(1)} %get-tuple-element.47), channel_id=1, source_target_pairs={{0,32},{1,16},{2,34},{3,18},{4,36},{5,20},{6,38},{7,22},{8,40},{9,... | collective-permute-start | bytes 589832 | tf_op jit(solution)/shard_map/ppermute | solution.py:311
  71.0 12.6 %collective-permute-start.25 = (bf16[128,768]{1,0:T(8,128)(2,1)S(1)}, bf16[128,768]{1,0:T(8,128)(2,1)S(1)}, u32[]{:S(2)}, u32[]{:S(2)}) collective-permute-start(bf16[128,768]{1,0:T(8,128)(2,1)S(1)} %get-tuple-element.48), channel_id=1, source_target_pairs={{0,33},{1,17},{2,35},{3,19},{4,37},{5,21},{6,39},{7,23},{8,41},{9,... | collective-permute-start | bytes 589832 | tf_op jit(solution)/shard_map/ppermute | solution.py:311
  74.4 16.4 %collective-permute-start.17 = (bf16[32,768]{1,0:T(8,128)(2,1)S(1)}, bf16[32,768]{1,0:T(8,128)(2,1)S(1)}, u32[]{:S(2)}, u32[]{:S(2)}) collective-permute-start(bf16[32,768]{1,0:T(8,128)(2,1)S(1)} %get-tuple-element.38), channel_id=1, source_target_pairs={{0,64},{16,80},{32,96},{48,112},{64,128},{80,144},{96,160},{112,17... | collective-permute-start | bytes 147464 | tf_op jit(solution)/shard_map/ppermute | solution.py:332
  76.0 15.2 %collective-permute-start.18 = (bf16[32,768]{1,0:T(8,128)(2,1)S(1)}, bf16[32,768]{1,0:T(8,128)(2,1)S(1)}, u32[]{:S(2)}, u32[]{:S(2)}) collective-permute-start(bf16[32,768]{1,0:T(8,128)(2,1)S(1)} %get-tuple-element.39), channel_id=1, source_target_pairs={{0,128},{16,144},{32,160},{48,176},{64,192},{80,208},{96,224},{112... | collective-permute-start | bytes 147464 | tf_op jit(solution)/shard_map/ppermute | solution.py:332
  81.6 9.7 %collective-permute-start.19 = (bf16[32,768]{1,0:T(8,128)(2,1)S(1)}, bf16[32,768]{1,0:T(8,128)(2,1)S(1)}, u32[]{:S(2)}, u32[]{:S(2)}) collective-permute-start(bf16[32,768]{1,0:T(8,128)(2,1)S(1)} %get-tuple-element.40), channel_id=1, source_target_pairs={{0,192},{16,208},{32,224},{48,240},{64,0},{80,16},{96,32},{112,48}... | collective-permute-start | bytes 147464 | tf_op jit(solution)/shard_map/ppermute | solution.py:332
  83.7 7.6 %collective-permute-start.26 = (bf16[32,768]{1,0:T(8,128)(2,1)S(1)}, bf16[32,768]{1,0:T(8,128)(2,1)S(1)}, u32[]{:S(2)}, u32[]{:S(2)}) collective-permute-start(bf16[32,768]{1,0:T(8,128)(2,1)S(1)} %get-tuple-element.50), channel_id=1, source_target_pairs={{0,64},{16,80},{32,96},{48,112},{64,128},{80,144},{96,160},{112,17... | collective-permute-start | bytes 147464 | tf_op jit(solution)/shard_map/ppermute | solution.py:332
  83.9 9.6 %collective-permute-start.27 = (bf16[32,768]{1,0:T(8,128)(2,1)S(1)}, bf16[32,768]{1,0:T(8,128)(2,1)S(1)}, u32[]{:S(2)}, u32[]{:S(2)}) collective-permute-start(bf16[32,768]{1,0:T(8,128)(2,1)S(1)} %get-tuple-element.51), channel_id=1, source_target_pairs={{0,128},{16,144},{32,160},{48,176},{64,192},{80,208},{96,224},{112... | collective-permute-start | bytes 147464 | tf_op jit(solution)/shard_map/ppermute | solution.py:332
  90.9 4.1 %collective-permute-start.28 = (bf16[32,768]{1,0:T(8,128)(2,1)S(1)}, bf16[32,768]{1,0:T(8,128)(2,1)S(1)}, u32[]{:S(2)}, u32[]{:S(2)}) collective-permute-start(bf16[32,768]{1,0:T(8,128)(2,1)S(1)} %get-tuple-element.52), channel_id=1, source_target_pairs={{0,192},{16,208},{32,224},{48,240},{64,0},{80,16},{96,32},{112,48}... | collective-permute-start | bytes 147464 | tf_op jit(solution)/shard_map/ppermute | solution.py:332

commit v6 on v5

--- a/solution.py
+++ b/solution.py
@@ -165,14 +165,14 @@
     )(*blocks, mine, other)
 
 
-def cross_sum_kernel(c_ref, d_ref, a_ref, b_ref, own_ref, keep_ref, *outs):
+def cross_sum_kernel(b_ref, c_ref, a_ref, d_ref, own_ref, keep_ref, *outs):
     x, z_lo, _, _, core = place()
     match = (x % 2) == core
     for k in range(4):
         rows = pl.ds(pl.multiple_of(((z_lo + k) % 4) * ROWS, ROWS), ROWS)
-        last = jnp.where(match, own_ref[rows, :].astype(F32), d_ref[rows, :].astype(F32))
-        total = a_ref[rows, :].astype(F32) + b_ref[rows, :].astype(F32)
-        total = total + (c_ref[rows, :].astype(F32) + last)
+        near = own_ref[rows, :].astype(F32) + b_ref[rows, :].astype(F32)
+        last = jnp.where(match, near, d_ref[rows, :].astype(F32))
+        total = (a_ref[rows, :].astype(F32) + c_ref[rows, :].astype(F32)) + last
         if k == 0:
             keep_ref[...] = total
         else:
@@ -285,30 +285,47 @@
     far_a, a_below = after((far_a, a_below), a_above, b_below, b_above)
     a_opposite = up(a_below)
     far_a_above, far_a_below = down(far_a), up(far_a)
-    far_a_above, far_b = after((far_a_above, far_b))
     far_a_opposite = down(far_a_above)
+    far_b, b_below = after((far_b, b_below), a_opposite, far_a_opposite, far_a_below)
+    b_opposite = up(b_below)
     far_b_above, far_b_below = down(far_b), up(far_b)
-    b_opposite = up(b_below)
     a_blocks = [a, a_below, a_above, a_opposite, far_a, far_a_below, far_a_above, far_a_opposite]
     a_bufs = list(partial_scores(a_blocks, stored, other))
     (far_b_above,) = after((far_b_above,), a_bufs[1])
     far_b_opposite = down(far_b_above)
-    a_bufs[3:] = after(a_bufs[3:], b_opposite, far_b_below)
+    a_bufs[2:3] = after(a_bufs[2:3], b_opposite, far_b_below)
     b_blocks = [b, b_below, b_above, b_opposite, far_b, far_b_below, far_b_above, far_b_opposite]
     return a_bufs, b_blocks
 
 
+def join_kernel(send_ref, got_ref, out_ref):
+    x, _, _, _, core = place()
+    got = jnp.where((x % 2) == core, 0.0, got_ref[...].astype(F32))
+    out_ref[...] = (send_ref[...].astype(F32) + got).astype(BF16)
+
+
+def join(send, got):
+    return pl.pallas_call(
+        join_kernel,
+        out_shape=jax.ShapeDtypeStruct(send.shape, BF16),
+        compiler_params=pltpu.CompilerParams(vmem_limit_bytes=16 << 20),
+        name="join",
+    )(send, got)
+
+
 def over_x(bufs):
+    def send(value, move):
+        return lax.ppermute(value, ("store", "group"), all_pairs(move))
+
     def match(x, core):
         return x % 2 == core
 
-    moves = (
-        lambda x, c: (x, 1 - c) if match(x, c) else (x - 1, c),
-        lambda x, c: None if match(x, c) else (x - 1, 1 - c),
-        lambda x, c: (x + 2, c) if match(x, c) else (x + 1, 1 - c),
-        lambda x, c: (x + 2, 1 - c) if match(x, c) else (x + 1, c),
-    )
-    return [lax.ppermute(b, ("store", "group"), all_pairs(m)) for b, m in zip(bufs, moves)]
+    got_b = send(bufs[3], lambda x, c: (x - 1, c) if match(x, c) else (x + 1, c))
+    got_c = send(bufs[0], lambda x, c: (x, 1 - c) if match(x, c) else (x - 1, c))
+    got_a = send(bufs[2], lambda x, c: (x + 2, c) if match(x, c) else (x + 1, 1 - c))
+    joined = join(bufs[1], got_b)
+    got_d = send(joined, lambda x, c: None if match(x, c) else (x - 1, 1 - c))
+    return [got_b, got_c, got_a, got_d]
 
 
 def on_device(activations, out_grads, stored, lengths, store_ids):
@@ -322,7 +339,7 @@
     a_bufs, b_blocks = first_scores(a, b, stored, other)
     a_got = over_x(a_bufs)
     b_bufs = list(partial_scores(b_blocks, stored, other))
-    b_bufs = after(b_bufs, *a_got)
+    b_bufs = after(b_bufs, *a_got[:3])
     b_got = over_x(b_bufs)
     parts = []
     for got, bufs in ((a_got, a_bufs), (b_got, b_bufs)):

time: 96.2 us -> 91.9 us (0.955); the launches traced: 96 us -> 90.3 us
  starting transfers between devices: 50.1 us -> 44.3 us
    ppermute x6, starting transfers between devices: 12.9 us -> 3.65 us  [on_device(): lax.ppermute(send, 'store', store_pairs(lambda x, z: (x, z + k)))]
    ppermute x14, starting transfers between devices: 23.3 us -> 28.6 us  [along(): return lax.ppermute(value, 'group', group_pairs(move))]
    ppermute x14, waiting for transfers between devices: 18.5 us -> 16.3 us  [along(): return lax.ppermute(value, 'group', group_pairs(move))]
    ppermute x6, waiting for transfers between devices: 3.64 us -> 5.6 us  [on_device(): lax.ppermute(send, 'store', store_pairs(lambda x, z: (x, z + k)))]
    ppermute x8, starting transfers between devices: 14 us -> 12 us  [send(): return lax.ppermute(value, ('store', 'group'), all_pairs(move))]
  transfers between devices with their start and end apart: 29 -> 29, of which waited for: 10 -> 13; matrix products, arithmetic and copies ran while one was open for 0% -> 0% of each run, Pallas kernels for 17% -> 18%
where the time goes in v6:
time: 91.9 us; the launch traced here: 90.3 us
  starting transfers between devices  44.3 us (48%)
  waiting for transfers between devices  27.9 us (30%)
  Pallas kernels  17.6 us (19%)
    ppermute x14, starting transfers between devices, along(): return lax.ppermute(value, 'group', group_pairs(move))  28.6 us
    ppermute x14, waiting for transfers between devices, along(): return lax.ppermute(value, 'group', group_pairs(move))  16.3 us
    ppermute x8, starting transfers between devices, send(): return lax.ppermute(value, ('store', 'group'), all_pairs(move))  12 us
    pallas_call x2, Pallas kernels, partial_scores(): pl.pallas_call(score_kernel, out_shape=[jax.ShapeDtypeStruct((4 * ROWS, H...  10.9 us
    ppermute x8, waiting for transfers between devices, send(): return lax.ppermute(value, ('store', 'group'), all_pairs(move))  6.01 us
    ppermute x6, waiting for transfers between devices, on_device(): lax.ppermute(send, 'store', store_pairs(lambda x, z: (x, z + k)))  5.6 us
    pallas_call x2, Pallas kernels, query_grads(): pl.pallas_call(functools.partial(grad_kernel, chunk * ROWS), out_shape=ja...  5.12 us
    ppermute x6, starting transfers between devices, on_device(): lax.ppermute(send, 'store', store_pairs(lambda x, z: (x, z + k)))  3.65 us
  transfers between devices with their start and end apart: 29, of which 13 were waited for; matrix products, arithmetic and copies ran while one was open for 0% of the time, Pallas kernels for 18%

profile of v6, /device:TPU:32, one launch (start us, length us, event | category | flops | bytes accessed | tf_op | source)
XLA Modules:
  0.0 90.3 jit_solution(10149794459609776259)
XLA Ops:
  0.0 2.5 %query_grads.2.refs_0_ = bf16[32,4096]{1,0:T(8,128)(2,1)S(1)} custom-call(s32[64]{0:T(128)} %lengths_hbm.3, bf16[64,1,64,256]{3,2,1,0:T(8,128)(2,1)} %acts_hbm.3, bf16[64,1,64,256]{3,2,1,0:T(8,128)(2,1)} %grads_hbm.3), custom_call_target="tpu_custom_call" | custom-call | tf_op jit(solution)/shard_map/query_grads/pallas_call | solution.py:81
  2.5 6.3 %collective-permute-start = (bf16[32,4096]{1,0:T(8,128)(2,1)S(1)}, bf16[32,4096]{1,0:T(8,128)(2,1)S(1)}, u32[]{:S(2)}, u32[]{:S(2)}) collective-permute-start(bf16[32,4096]{1,0:T(8,128)(2,1)S(1)} %query_grads.2.refs_0_), channel_id=1, source_target_pairs={{0,2},{1,3},{2,0},{3,1},{4,6},{5,7},{6,4},{7,5},{8,10},{9,11},{10,... | collective-permute-start | bytes 786440 | tf_op jit(solution)/shard_map/ppermute | solution.py:247
  8.9 1.6 %collective-permute-start.1 = (bf16[32,4096]{1,0:T(8,128)(2,1)S(1)}, bf16[32,4096]{1,0:T(8,128)(2,1)S(1)}, u32[]{:S(2)}, u32[]{:S(2)}) collective-permute-start(bf16[32,4096]{1,0:T(8,128)(2,1)S(1)} %query_grads.2.refs_0_), channel_id=1, source_target_pairs={{0,4},{1,5},{2,6},{3,7},{4,8},{5,9},{6,10},{7,11},{8,12},{9,13},{1... | collective-permute-start | bytes 786440 | tf_op jit(solution)/shard_map/ppermute | solution.py:247
  10.4 1.7 %collective-permute-start.2 = (bf16[32,4096]{1,0:T(8,128)(2,1)S(1)}, bf16[32,4096]{1,0:T(8,128)(2,1)S(1)}, u32[]{:S(2)}, u32[]{:S(2)}) collective-permute-start(bf16[32,4096]{1,0:T(8,128)(2,1)S(1)} %query_grads.2.refs_0_), channel_id=1, source_target_pairs={{0,12},{1,13},{2,14},{3,15},{4,0},{5,1},{6,2},{7,3},{8,4},{9,5},{1... | collective-permute-start | bytes 786440 | tf_op jit(solution)/shard_map/ppermute | solution.py:247
  12.1 2.6 %query_grads.3.refs_0_ = bf16[32,4096]{1,0:T(8,128)(2,1)S(1)} custom-call(s32[64]{0:T(128)} %lengths_hbm.3, bf16[64,1,64,256]{3,2,1,0:T(8,128)(2,1)} %acts_hbm.3, bf16[64,1,64,256]{3,2,1,0:T(8,128)(2,1)} %grads_hbm.3), custom_call_target="tpu_custom_call" | custom-call | tf_op jit(solution)/shard_map/query_grads/pallas_call | solution.py:81
  15.2 2.9 %collective-permute-start.5 = (bf16[32,4096]{1,0:T(8,128)(2,1)S(1)}, bf16[32,4096]{1,0:T(8,128)(2,1)S(1)}, u32[]{:S(2)}, u32[]{:S(2)}) collective-permute-start(bf16[32,4096]{1,0:T(8,128)(2,1)S(1)} %fence.6.refs_0_), channel_id=1, source_target_pairs={{0,12},{1,13},{2,14},{3,15},{4,0},{5,1},{6,2},{7,3},{8,4},{9,5},{1... | collective-permute-start | bytes 786440 | tf_op jit(solution)/shard_map/ppermute | solution.py:247
  18.1 3.5 %collective-permute-done.refs_0_ = bf16[32,4096]{1,0:T(8,128)(2,1)S(1)} collective-permute-done((bf16[32,4096]{1,0:T(8,128)(2,1)S(1)}, bf16[32,4096]{1,0:T(8,128)(2,1)S(1)}, u32[]{:S(2)}, u32[]{:S(2)}) %collective-permute-start) | collective-permute-done | bytes 262176 | tf_op jit(solution)/shard_map/ppermute | solution.py:247
  21.6 2.6 %collective-permute-done.4.refs_3_.refs_1_ = bf16[32,4096]{1,0:T(8,128)(2,1)S(1)} collective-permute-done((bf16[32,4096]{1,0:T(8,128)(2,1)S(1)}, bf16[32,4096]{1,0:T(8,128)(2,1)S(1)}, u32[]{:S(2)}, u32[]{:S(2)}) %collective-permute-start.4) | collective-permute-done | bytes 262176 | tf_op jit(solution)/shard_map/ppermute | solution.py:247
  24.2 2.9 %collective-permute-start.8 = (bf16[32,4096]{1,0:T(8,128)(2,1)S(1)}, bf16[32,4096]{1,0:T(8,128)(2,1)S(1)}, u32[]{:S(2)}, u32[]{:S(2)}) collective-permute-start(bf16[32,4096]{1,0:T(8,128)(2,1)S(1)} %get-tuple-element.30.refs_4_), channel_id=1, source_target_pairs={{0,12},{1,13},{2,14},{3,15},{4,0},{5,1},{6,2},{7,3},{8,4},{9,5},{1... | collective-permute-start | bytes 786440 | tf_op jit(solution)/shard_map/ppermute | solution.py:247
  27.2 3.1 %collective-permute-start.12 = (bf16[32,4096]{1,0:T(8,128)(2,1)S(1)}, bf16[32,4096]{1,0:T(8,128)(2,1)S(1)}, u32[]{:S(2)}, u32[]{:S(2)}) collective-permute-start(bf16[32,4096]{1,0:T(8,128)(2,1)S(1)} %fence.6.refs_0_), channel_id=1, source_target_pairs={{0,2},{1,3},{2,0},{3,1},{4,6},{5,7},{6,4},{7,5},{8,10},{9,11},{10,... | collective-permute-start | bytes 786440 | tf_op jit(solution)/shard_map/ppermute | solution.py:247
  30.8 0.8 collective-permute-done.8.refs_6_
  31.6 3.7 %collective-permute-start.9 = (bf16[32,4096]{1,0:T(8,128)(2,1)S(1)}, bf16[32,4096]{1,0:T(8,128)(2,1)S(1)}, u32[]{:S(2)}, u32[]{:S(2)}) collective-permute-start(bf16[32,4096]{1,0:T(8,128)(2,1)S(1)} %collective-permute-done.8.refs_6_), channel_id=1, source_target_pairs={{0,12},{1,13},{2,14},{3,15},{4,0},{5,1},{6,2},{7,3},{8,4},{9,5},{1... | collective-permute-start | bytes 786440 | tf_op jit(solution)/shard_map/ppermute | solution.py:247
  35.3 8.0 %collective-permute-done.12.refs_0_ = bf16[32,4096]{1,0:T(8,128)(2,1)S(1)} collective-permute-done((bf16[32,4096]{1,0:T(8,128)(2,1)S(1)}, bf16[32,4096]{1,0:T(8,128)(2,1)S(1)}, u32[]{:S(2)}, u32[]{:S(2)}) %collective-permute-start.12) | collective-permute-done | bytes 262176 | tf_op jit(solution)/shard_map/ppermute | solution.py:247
  43.4 1.1 %collective-permute-done.6.refs_3_.refs_2_ = bf16[32,4096]{1,0:T(8,128)(2,1)S(1)} collective-permute-done((bf16[32,4096]{1,0:T(8,128)(2,1)S(1)}, bf16[32,4096]{1,0:T(8,128)(2,1)S(1)}, u32[]{:S(2)}, u32[]{:S(2)}) %collective-permute-start.6) | collective-permute-done | bytes 262176 | tf_op jit(solution)/shard_map/ppermute | solution.py:247
  44.6 2.0 %collective-permute-start.13 = (bf16[32,4096]{1,0:T(8,128)(2,1)S(1)}, bf16[32,4096]{1,0:T(8,128)(2,1)S(1)}, u32[]{:S(2)}, u32[]{:S(2)}) collective-permute-start(bf16[32,4096]{1,0:T(8,128)(2,1)S(1)} %get-tuple-element.34.refs_1_), channel_id=1, source_target_pairs={{0,4},{1,5},{2,6},{3,7},{4,8},{5,9},{6,10},{7,11},{8,12},{9,13},{1... | collective-permute-start | bytes 786440 | tf_op jit(solution)/shard_map/ppermute | solution.py:247
  46.6 5.5 %partial_scores.2 = (bf16[128,768]{1,0:T(8,128)(2,1)S(1)}, bf16[128,768]{1,0:T(8,128)(2,1)S(1)}, bf16[128,768]{1,0:T(8,128)(2,1)S(1)}, bf16[128,768]{1,0:T(8,128)(2,1)S(1)}) custom-call(bf16[32,4096]{1,0:T(8,128)(2,1)S(1)} %query_grads.2.refs_0_, bf16[32,4096]{1,0:T(8,128)(2,1)S(1)} %get-tuple-element.29.refs_1_, ...), custom_call_target="tpu_custom_call" | custom-call | flops 1 | bytes 1 | tf_op jit(solution)/shard_map/partial_scores/pallas_call | solution.py:148
  52.2 3.2 %collective-permute-start.21 = (bf16[32,4096]{1,0:T(8,128)(2,1)S(1)}, bf16[32,4096]{1,0:T(8,128)(2,1)S(1)}, u32[]{:S(2)}, u32[]{:S(2)}) collective-permute-start(bf16[32,4096]{1,0:T(8,128)(2,1)S(1)} %fence.10.refs_6_), channel_id=1, source_target_pairs={{0,12},{1,13},{2,14},{3,15},{4,0},{5,1},{6,2},{7,3},{8,4},{9,5},{1... | collective-permute-start | bytes 786440 | tf_op jit(solution)/shard_map/ppermute | solution.py:247
  55.4 2.7 %collective-permute-start.10 = (bf16[128,768]{1,0:T(8,128)(2,1)S(1)}, bf16[128,768]{1,0:T(8,128)(2,1)S(1)}, u32[]{:S(2)}, u32[]{:S(2)}) collective-permute-start(bf16[128,768]{1,0:T(8,128)(2,1)S(1)} %get-tuple-element.31), channel_id=1, source_target_pairs={{0,48},{1,17},{2,50},{3,19},{4,52},{5,21},{6,54},{7,23},{8,56},{9,... | collective-permute-start | bytes 589832 | tf_op jit(solution)/shard_map/ppermute | solution.py:318
  58.2 3.0 %collective-permute-start.15 = (bf16[128,768]{1,0:T(8,128)(2,1)S(1)}, bf16[128,768]{1,0:T(8,128)(2,1)S(1)}, u32[]{:S(2)}, u32[]{:S(2)}) collective-permute-start(bf16[128,768]{1,0:T(8,128)(2,1)S(1)} %fence.9), channel_id=1, source_target_pairs={{0,32},{1,16},{2,34},{3,18},{4,36},{5,20},{6,38},{7,22},{8,40},{9,... | collective-permute-start | bytes 589832 | tf_op jit(solution)/shard_map/ppermute | solution.py:318
  61.2 5.4 %partial_scores.3 = (bf16[128,768]{1,0:T(8,128)(2,1)S(1)}, bf16[128,768]{1,0:T(8,128)(2,1)S(1)}, bf16[128,768]{1,0:T(8,128)(2,1)S(1)}, bf16[128,768]{1,0:T(8,128)(2,1)S(1)}) custom-call(bf16[32,4096]{1,0:T(8,128)(2,1)S(1)} %fence.6.refs_0_, bf16[32,4096]{1,0:T(8,128)(2,1)S(1)} %get-tuple-element.34.refs_1_, ...), custom_call_target="tpu_custom_call" | custom-call | flops 1 | bytes 1 | tf_op jit(solution)/shard_map/partial_scores/pallas_call | solution.py:148
  66.6 0.8 collective-permute-done.15.a_ref.refs_6_
  68.7 4.4 %collective-permute-start.23 = (bf16[128,768]{1,0:T(8,128)(2,1)S(1)}, bf16[128,768]{1,0:T(8,128)(2,1)S(1)}, u32[]{:S(2)}, u32[]{:S(2)}) collective-permute-start(bf16[128,768]{1,0:T(8,128)(2,1)S(1)} %get-tuple-element.46), channel_id=1, source_target_pairs={{0,1},{1,49},{2,3},{3,51},{4,5},{5,53},{6,7},{7,55},{8,9},{9,57},{... | collective-permute-start | bytes 589832 | tf_op jit(solution)/shard_map/ppermute | solution.py:318
  73.3 1.1 %collective-permute-done.22.got_ref.b_ref = bf16[128,768]{1,0:T(8,128)(2,1)S(1)} collective-permute-done((bf16[128,768]{1,0:T(8,128)(2,1)S(1)}, bf16[128,768]{1,0:T(8,128)(2,1)S(1)}, u32[]{:S(2)}, u32[]{:S(2)}) %collective-permute-start.22) | collective-permute-done | bytes 196640 | tf_op jit(solution)/shard_map/ppermute | solution.py:318
  75.2 1.0 %collective-permute-start.17 = (bf16[32,768]{1,0:T(8,128)(2,1)S(1)}, bf16[32,768]{1,0:T(8,128)(2,1)S(1)}, u32[]{:S(2)}, u32[]{:S(2)}) collective-permute-start(bf16[32,768]{1,0:T(8,128)(2,1)S(1)} %get-tuple-element.38), channel_id=1, source_target_pairs={{0,64},{16,80},{32,96},{48,112},{64,128},{80,144},{96,160},{112,17... | collective-permute-start | bytes 147464 | tf_op jit(solution)/shard_map/ppermute | solution.py:349
  76.2 1.8 %collective-permute-done.23.c_ref = bf16[128,768]{1,0:T(8,128)(2,1)S(1)} collective-permute-done((bf16[128,768]{1,0:T(8,128)(2,1)S(1)}, bf16[128,768]{1,0:T(8,128)(2,1)S(1)}, u32[]{:S(2)}, u32[]{:S(2)}) %collective-permute-start.23) | collective-permute-done | bytes 196640 | tf_op jit(solution)/shard_map/ppermute | solution.py:318
  78.0 2.4 %collective-permute-done.24.a_ref = bf16[128,768]{1,0:T(8,128)(2,1)S(1)} collective-permute-done((bf16[128,768]{1,0:T(8,128)(2,1)S(1)}, bf16[128,768]{1,0:T(8,128)(2,1)S(1)}, u32[]{:S(2)}, u32[]{:S(2)}) %collective-permute-start.24) | collective-permute-done | bytes 196640 | tf_op jit(solution)/shard_map/ppermute | solution.py:318
  80.5 1.0 %collective-permute-start.26 = (bf16[32,768]{1,0:T(8,128)(2,1)S(1)}, bf16[32,768]{1,0:T(8,128)(2,1)S(1)}, u32[]{:S(2)}, u32[]{:S(2)}) collective-permute-start(bf16[32,768]{1,0:T(8,128)(2,1)S(1)} %get-tuple-element.50), channel_id=1, source_target_pairs={{0,64},{16,80},{32,96},{48,112},{64,128},{80,144},{96,160},{112,17... | collective-permute-start | bytes 147464 | tf_op jit(solution)/shard_map/ppermute | solution.py:349
  81.5 1.7 %collective-permute-start.27 = (bf16[32,768]{1,0:T(8,128)(2,1)S(1)}, bf16[32,768]{1,0:T(8,128)(2,1)S(1)}, u32[]{:S(2)}, u32[]{:S(2)}) collective-permute-start(bf16[32,768]{1,0:T(8,128)(2,1)S(1)} %get-tuple-element.51), channel_id=1, source_target_pairs={{0,128},{16,144},{32,160},{48,176},{64,192},{80,208},{96,224},{112... | collective-permute-start | bytes 147464 | tf_op jit(solution)/shard_map/ppermute | solution.py:349
  83.6 1.3 %collective-permute-done.26.refs_5_ = bf16[32,768]{1,0:T(8,128)(2,1)S(1)} collective-permute-done((bf16[32,768]{1,0:T(8,128)(2,1)S(1)}, bf16[32,768]{1,0:T(8,128)(2,1)S(1)}, u32[]{:S(2)}, u32[]{:S(2)}) %collective-permute-start.26) | collective-permute-done | bytes 49184 | tf_op jit(solution)/shard_map/ppermute | solution.py:349
  85.0 2.1 %collective-permute-done.27.refs_6_ = bf16[32,768]{1,0:T(8,128)(2,1)S(1)} collective-permute-done((bf16[32,768]{1,0:T(8,128)(2,1)S(1)}, bf16[32,768]{1,0:T(8,128)(2,1)S(1)}, u32[]{:S(2)}, u32[]{:S(2)}) %collective-permute-start.27) | collective-permute-done | bytes 49184 | tf_op jit(solution)/shard_map/ppermute | solution.py:349
  87.1 2.2 %collective-permute-done.28.refs_7_ = bf16[32,768]{1,0:T(8,128)(2,1)S(1)} collective-permute-done((bf16[32,768]{1,0:T(8,128)(2,1)S(1)}, bf16[32,768]{1,0:T(8,128)(2,1)S(1)}, u32[]{:S(2)}, u32[]{:S(2)}) %collective-permute-start.28) | collective-permute-done | bytes 49184 | tf_op jit(solution)/shard_map/ppermute | solution.py:349
  89.2 1.1 %final_sum.1 = f32[64,768]{1,0:T(8,128)} custom-call(f32[32,768]{1,0:T(8,128)S(1)} %get-tuple-element.37.refs_0_, bf16[32,768]{1,0:T(8,128)(2,1)S(1)} %collective-permute-done.17.refs_1_, bf16[32,768]{1,0:T(8,128)(2,1)S(1)} %collective-permute-done.18.refs_2_, bf16[32,768]{1,0:T(8,128)(2,1)S(1)} %collective-permute-done.19.refs_3_, ...), custom_call_target="tpu_custom_call" | custom-call | tf_op jit(solution)/shard_map/final_sum/pallas_call | solution.py:214
  (49 shorter events, 4.2 us)
Async XLA Ops:
  0.0 14.8 %collective-permute-start.3 = (bf16[768,4096]{1,0:T(8,128)(2,1)}, bf16[768,4096]{1,0:T(8,128)(2,1)S(1)}, u32[]{:S(2)}, u32[]{:S(2)}) collective-permute-start(bf16[768,4096]{1,0:T(8,128)(2,1)} %bitcast.1), channel_id=1, source_target_pairs={{0,1},{1,0},{2,3},{3,2},{4,5},{5,4},{6,7},{7,6},{8,9},{9,8},{10,11... | collective-permute-start | bytes 18874376 | tf_op jit(solution)/shard_map/ppermute | solution.py:333
  2.5 19.1 %collective-permute-start = (bf16[32,4096]{1,0:T(8,128)(2,1)S(1)}, bf16[32,4096]{1,0:T(8,128)(2,1)S(1)}, u32[]{:S(2)}, u32[]{:S(2)}) collective-permute-start(bf16[32,4096]{1,0:T(8,128)(2,1)S(1)} %query_grads.2.refs_0_), channel_id=1, source_target_pairs={{0,2},{1,3},{2,0},{3,1},{4,6},{5,7},{6,4},{7,5},{8,10},{9,11},{10,... | collective-permute-start | bytes 786440 | tf_op jit(solution)/shard_map/ppermute | solution.py:247
  8.9 12.7 %collective-permute-start.1 = (bf16[32,4096]{1,0:T(8,128)(2,1)S(1)}, bf16[32,4096]{1,0:T(8,128)(2,1)S(1)}, u32[]{:S(2)}, u32[]{:S(2)}) collective-permute-start(bf16[32,4096]{1,0:T(8,128)(2,1)S(1)} %query_grads.2.refs_0_), channel_id=1, source_target_pairs={{0,4},{1,5},{2,6},{3,7},{4,8},{5,9},{6,10},{7,11},{8,12},{9,13},{1... | collective-permute-start | bytes 786440 | tf_op jit(solution)/shard_map/ppermute | solution.py:247
  10.4 11.1 %collective-permute-start.2 = (bf16[32,4096]{1,0:T(8,128)(2,1)S(1)}, bf16[32,4096]{1,0:T(8,128)(2,1)S(1)}, u32[]{:S(2)}, u32[]{:S(2)}) collective-permute-start(bf16[32,4096]{1,0:T(8,128)(2,1)S(1)} %query_grads.2.refs_0_), channel_id=1, source_target_pairs={{0,12},{1,13},{2,14},{3,15},{4,0},{5,1},{6,2},{7,3},{8,4},{9,5},{1... | collective-permute-start | bytes 786440 | tf_op jit(solution)/shard_map/ppermute | solution.py:247
  12.1 34.5 %slice-start = ((s8[6291456]{0:T(1024)(128)(4,1)}), s8[4194304]{0:T(1024)(128)(4,1)S(1)}, s32[]{:S(2)}) async-start(s8[6291456]{0:T(1024)(128)(4,1)} %bitcast.2), calls=%async_computation | async-start | bytes 8388608
  14.7 31.9 %slice-start.1 = ((s8[6291456]{0:T(1024)(128)(4,1)}), s8[2097152]{0:T(1024)(128)(4,1)S(1)}, s32[]{:S(2)}) async-start(s8[6291456]{0:T(1024)(128)(4,1)} %bitcast.2), calls=%async_computation.1 | async-start | bytes 4194304
  14.8 9.4 %collective-permute-start.4 = (bf16[32,4096]{1,0:T(8,128)(2,1)S(1)}, bf16[32,4096]{1,0:T(8,128)(2,1)S(1)}, u32[]{:S(2)}, u32[]{:S(2)}) collective-permute-start(bf16[32,4096]{1,0:T(8,128)(2,1)S(1)} %fence.6.refs_0_), channel_id=1, source_target_pairs={{0,4},{1,5},{2,6},{3,7},{4,8},{5,9},{6,10},{7,11},{8,12},{9,13},{1... | collective-permute-start | bytes 786440 | tf_op jit(solution)/shard_map/ppermute | solution.py:247
  15.2 9.0 %collective-permute-start.5 = (bf16[32,4096]{1,0:T(8,128)(2,1)S(1)}, bf16[32,4096]{1,0:T(8,128)(2,1)S(1)}, u32[]{:S(2)}, u32[]{:S(2)}) collective-permute-start(bf16[32,4096]{1,0:T(8,128)(2,1)S(1)} %fence.6.refs_0_), channel_id=1, source_target_pairs={{0,12},{1,13},{2,14},{3,15},{4,0},{5,1},{6,2},{7,3},{8,4},{9,5},{1... | collective-permute-start | bytes 786440 | tf_op jit(solution)/shard_map/ppermute | solution.py:247
  24.2 7.4 %collective-permute-start.8 = (bf16[32,4096]{1,0:T(8,128)(2,1)S(1)}, bf16[32,4096]{1,0:T(8,128)(2,1)S(1)}, u32[]{:S(2)}, u32[]{:S(2)}) collective-permute-start(bf16[32,4096]{1,0:T(8,128)(2,1)S(1)} %get-tuple-element.30.refs_4_), channel_id=1, source_target_pairs={{0,12},{1,13},{2,14},{3,15},{4,0},{5,1},{6,2},{7,3},{8,4},{9,5},{1... | collective-permute-start | bytes 786440 | tf_op jit(solution)/shard_map/ppermute | solution.py:247
  27.2 16.2 %collective-permute-start.12 = (bf16[32,4096]{1,0:T(8,128)(2,1)S(1)}, bf16[32,4096]{1,0:T(8,128)(2,1)S(1)}, u32[]{:S(2)}, u32[]{:S(2)}) collective-permute-start(bf16[32,4096]{1,0:T(8,128)(2,1)S(1)} %fence.6.refs_0_), channel_id=1, source_target_pairs={{0,2},{1,3},{2,0},{3,1},{4,6},{5,7},{6,4},{7,5},{8,10},{9,11},{10,... | collective-permute-start | bytes 786440 | tf_op jit(solution)/shard_map/ppermute | solution.py:247
  30.3 14.2 %collective-permute-start.7 = (bf16[32,4096]{1,0:T(8,128)(2,1)S(1)}, bf16[32,4096]{1,0:T(8,128)(2,1)S(1)}, u32[]{:S(2)}, u32[]{:S(2)}) collective-permute-start(bf16[32,4096]{1,0:T(8,128)(2,1)S(1)} %get-tuple-element.30.refs_4_), channel_id=1, source_target_pairs={{0,4},{1,5},{2,6},{3,7},{4,8},{5,9},{6,10},{7,11},{8,12},{9,13},{1... | collective-permute-start | bytes 786440 | tf_op jit(solution)/shard_map/ppermute | solution.py:247
  30.3 14.2 %collective-permute-start.6 = (bf16[32,4096]{1,0:T(8,128)(2,1)S(1)}, bf16[32,4096]{1,0:T(8,128)(2,1)S(1)}, u32[]{:S(2)}, u32[]{:S(2)}) collective-permute-start(bf16[32,4096]{1,0:T(8,128)(2,1)S(1)} %get-tuple-element.29.refs_1_), channel_id=1, source_target_pairs={{0,4},{1,5},{2,6},{3,7},{4,8},{5,9},{6,10},{7,11},{8,12},{9,13},{1... | collective-permute-start | bytes 786440 | tf_op jit(solution)/shard_map/ppermute | solution.py:247
  31.6 12.9 %collective-permute-start.9 = (bf16[32,4096]{1,0:T(8,128)(2,1)S(1)}, bf16[32,4096]{1,0:T(8,128)(2,1)S(1)}, u32[]{:S(2)}, u32[]{:S(2)}) collective-permute-start(bf16[32,4096]{1,0:T(8,128)(2,1)S(1)} %collective-permute-done.8.refs_6_), channel_id=1, source_target_pairs={{0,12},{1,13},{2,14},{3,15},{4,0},{5,1},{6,2},{7,3},{8,4},{9,5},{1... | collective-permute-start | bytes 786440 | tf_op jit(solution)/shard_map/ppermute | solution.py:247
  44.5 7.6 %collective-permute-start.20 = (bf16[32,4096]{1,0:T(8,128)(2,1)S(1)}, bf16[32,4096]{1,0:T(8,128)(2,1)S(1)}, u32[]{:S(2)}, u32[]{:S(2)}) collective-permute-start(bf16[32,4096]{1,0:T(8,128)(2,1)S(1)} %get-tuple-element.35.refs_4_), channel_id=1, source_target_pairs={{0,12},{1,13},{2,14},{3,15},{4,0},{5,1},{6,2},{7,3},{8,4},{9,5},{1... | collective-permute-start | bytes 786440 | tf_op jit(solution)/shard_map/ppermute | solution.py:247
  44.6 13.5 %collective-permute-start.13 = (bf16[32,4096]{1,0:T(8,128)(2,1)S(1)}, bf16[32,4096]{1,0:T(8,128)(2,1)S(1)}, u32[]{:S(2)}, u32[]{:S(2)}) collective-permute-start(bf16[32,4096]{1,0:T(8,128)(2,1)S(1)} %get-tuple-element.34.refs_1_), channel_id=1, source_target_pairs={{0,4},{1,5},{2,6},{3,7},{4,8},{5,9},{6,10},{7,11},{8,12},{9,13},{1... | collective-permute-start | bytes 786440 | tf_op jit(solution)/shard_map/ppermute | solution.py:247
  46.6 11.6 %collective-permute-start.14 = (bf16[32,4096]{1,0:T(8,128)(2,1)S(1)}, bf16[32,4096]{1,0:T(8,128)(2,1)S(1)}, u32[]{:S(2)}, u32[]{:S(2)}) collective-permute-start(bf16[32,4096]{1,0:T(8,128)(2,1)S(1)} %get-tuple-element.35.refs_4_), channel_id=1, source_target_pairs={{0,4},{1,5},{2,6},{3,7},{4,8},{5,9},{6,10},{7,11},{8,12},{9,13},{1... | collective-permute-start | bytes 786440 | tf_op jit(solution)/shard_map/ppermute | solution.py:247
  52.2 9.0 %collective-permute-start.21 = (bf16[32,4096]{1,0:T(8,128)(2,1)S(1)}, bf16[32,4096]{1,0:T(8,128)(2,1)S(1)}, u32[]{:S(2)}, u32[]{:S(2)}) collective-permute-start(bf16[32,4096]{1,0:T(8,128)(2,1)S(1)} %fence.10.refs_6_), channel_id=1, source_target_pairs={{0,12},{1,13},{2,14},{3,15},{4,0},{5,1},{6,2},{7,3},{8,4},{9,5},{1... | collective-permute-start | bytes 786440 | tf_op jit(solution)/shard_map/ppermute | solution.py:247
  55.4 11.2 %collective-permute-start.10 = (bf16[128,768]{1,0:T(8,128)(2,1)S(1)}, bf16[128,768]{1,0:T(8,128)(2,1)S(1)}, u32[]{:S(2)}, u32[]{:S(2)}) collective-permute-start(bf16[128,768]{1,0:T(8,128)(2,1)S(1)} %get-tuple-element.31), channel_id=1, source_target_pairs={{0,48},{1,17},{2,50},{3,19},{4,52},{5,21},{6,54},{7,23},{8,56},{9,... | collective-permute-start | bytes 589832 | tf_op jit(solution)/shard_map/ppermute | solution.py:318
  58.1 8.6 %collective-permute-start.11 = (bf16[128,768]{1,0:T(8,128)(2,1)S(1)}, bf16[128,768]{1,0:T(8,128)(2,1)S(1)}, u32[]{:S(2)}, u32[]{:S(2)}) collective-permute-start(bf16[128,768]{1,0:T(8,128)(2,1)S(1)} %get-tuple-element.32), channel_id=1, source_target_pairs={{0,1},{1,49},{2,3},{3,51},{4,5},{5,53},{6,7},{7,55},{8,9},{9,57},{... | collective-permute-start | bytes 589832 | tf_op jit(solution)/shard_map/ppermute | solution.py:318
  58.2 9.2 %collective-permute-start.15 = (bf16[128,768]{1,0:T(8,128)(2,1)S(1)}, bf16[128,768]{1,0:T(8,128)(2,1)S(1)}, u32[]{:S(2)}, u32[]{:S(2)}) collective-permute-start(bf16[128,768]{1,0:T(8,128)(2,1)S(1)} %fence.9), channel_id=1, source_target_pairs={{0,32},{1,16},{2,34},{3,18},{4,36},{5,20},{6,38},{7,22},{8,40},{9,... | collective-permute-start | bytes 589832 | tf_op jit(solution)/shard_map/ppermute | solution.py:318
  66.6 16.6 %copy-start = (s32[768]{0:T(1024)S(1)}, s32[768]{0:T(1024)}, u32[]{:S(2)}) copy-start(s32[768]{0:T(1024)} %param.9) | copy-start | bytes 9220
  67.4 6.9 %collective-permute-start.22 = (bf16[128,768]{1,0:T(8,128)(2,1)S(1)}, bf16[128,768]{1,0:T(8,128)(2,1)S(1)}, u32[]{:S(2)}, u32[]{:S(2)}) collective-permute-start(bf16[128,768]{1,0:T(8,128)(2,1)S(1)} %get-tuple-element.45), channel_id=1, source_target_pairs={{0,48},{1,17},{2,50},{3,19},{4,52},{5,21},{6,54},{7,23},{8,56},{9,... | collective-permute-start | bytes 589832 | tf_op jit(solution)/shard_map/ppermute | solution.py:318
  68.0 7.1 %collective-permute-start.16 = (bf16[128,768]{1,0:T(8,128)(2,1)S(1)}, bf16[128,768]{1,0:T(8,128)(2,1)S(1)}, u32[]{:S(2)}, u32[]{:S(2)}) collective-permute-start(bf16[128,768]{1,0:T(8,128)(2,1)S(1)} %join.2), channel_id=1, source_target_pairs={{1,48},{3,50},{5,52},{7,54},{9,56},{11,58},{13,60},{15,62},{16,1},... | collective-permute-start | bytes 589832 | tf_op jit(solution)/shard_map/ppermute | solution.py:318
  68.7 9.3 %collective-permute-start.23 = (bf16[128,768]{1,0:T(8,128)(2,1)S(1)}, bf16[128,768]{1,0:T(8,128)(2,1)S(1)}, u32[]{:S(2)}, u32[]{:S(2)}) collective-permute-start(bf16[128,768]{1,0:T(8,128)(2,1)S(1)} %get-tuple-element.46), channel_id=1, source_target_pairs={{0,1},{1,49},{2,3},{3,51},{4,5},{5,53},{6,7},{7,55},{8,9},{9,57},{... | collective-permute-start | bytes 589832 | tf_op jit(solution)/shard_map/ppermute | solution.py:318
  73.1 7.3 %collective-permute-start.24 = (bf16[128,768]{1,0:T(8,128)(2,1)S(1)}, bf16[128,768]{1,0:T(8,128)(2,1)S(1)}, u32[]{:S(2)}, u32[]{:S(2)}) collective-permute-start(bf16[128,768]{1,0:T(8,128)(2,1)S(1)} %get-tuple-element.47), channel_id=1, source_target_pairs={{0,32},{1,16},{2,34},{3,18},{4,36},{5,20},{6,38},{7,22},{8,40},{9,... | collective-permute-start | bytes 589832 | tf_op jit(solution)/shard_map/ppermute | solution.py:318
  74.4 6.0 %collective-permute-start.25 = (bf16[128,768]{1,0:T(8,128)(2,1)S(1)}, bf16[128,768]{1,0:T(8,128)(2,1)S(1)}, u32[]{:S(2)}, u32[]{:S(2)}) collective-permute-start(bf16[128,768]{1,0:T(8,128)(2,1)S(1)} %join.3), channel_id=1, source_target_pairs={{1,48},{3,50},{5,52},{7,54},{9,56},{11,58},{13,60},{15,62},{16,1},... | collective-permute-start | bytes 589832 | tf_op jit(solution)/shard_map/ppermute | solution.py:318
  75.2 7.9 %collective-permute-start.17 = (bf16[32,768]{1,0:T(8,128)(2,1)S(1)}, bf16[32,768]{1,0:T(8,128)(2,1)S(1)}, u32[]{:S(2)}, u32[]{:S(2)}) collective-permute-start(bf16[32,768]{1,0:T(8,128)(2,1)S(1)} %get-tuple-element.38), channel_id=1, source_target_pairs={{0,64},{16,80},{32,96},{48,112},{64,128},{80,144},{96,160},{112,17... | collective-permute-start | bytes 147464 | tf_op jit(solution)/shard_map/ppermute | solution.py:349
  76.2 7.4 %collective-permute-start.18 = (bf16[32,768]{1,0:T(8,128)(2,1)S(1)}, bf16[32,768]{1,0:T(8,128)(2,1)S(1)}, u32[]{:S(2)}, u32[]{:S(2)}) collective-permute-start(bf16[32,768]{1,0:T(8,128)(2,1)S(1)} %get-tuple-element.39), channel_id=1, source_target_pairs={{0,128},{16,144},{32,160},{48,176},{64,192},{80,208},{96,224},{112... | collective-permute-start | bytes 147464 | tf_op jit(solution)/shard_map/ppermute | solution.py:349
  78.0 5.6 %collective-permute-start.19 = (bf16[32,768]{1,0:T(8,128)(2,1)S(1)}, bf16[32,768]{1,0:T(8,128)(2,1)S(1)}, u32[]{:S(2)}, u32[]{:S(2)}) collective-permute-start(bf16[32,768]{1,0:T(8,128)(2,1)S(1)} %get-tuple-element.40), channel_id=1, source_target_pairs={{0,192},{16,208},{32,224},{48,240},{64,0},{80,16},{96,32},{112,48}... | collective-permute-start | bytes 147464 | tf_op jit(solution)/shard_map/ppermute | solution.py:349
  80.5 4.5 %collective-permute-start.26 = (bf16[32,768]{1,0:T(8,128)(2,1)S(1)}, bf16[32,768]{1,0:T(8,128)(2,1)S(1)}, u32[]{:S(2)}, u32[]{:S(2)}) collective-permute-start(bf16[32,768]{1,0:T(8,128)(2,1)S(1)} %get-tuple-element.50), channel_id=1, source_target_pairs={{0,64},{16,80},{32,96},{48,112},{64,128},{80,144},{96,160},{112,17... | collective-permute-start | bytes 147464 | tf_op jit(solution)/shard_map/ppermute | solution.py:349
  81.5 5.6 %collective-permute-start.27 = (bf16[32,768]{1,0:T(8,128)(2,1)S(1)}, bf16[32,768]{1,0:T(8,128)(2,1)S(1)}, u32[]{:S(2)}, u32[]{:S(2)}) collective-permute-start(bf16[32,768]{1,0:T(8,128)(2,1)S(1)} %get-tuple-element.51), channel_id=1, source_target_pairs={{0,128},{16,144},{32,160},{48,176},{64,192},{80,208},{96,224},{112... | collective-permute-start | bytes 147464 | tf_op jit(solution)/shard_map/ppermute | solution.py:349
  83.2 6.0 %collective-permute-start.28 = (bf16[32,768]{1,0:T(8,128)(2,1)S(1)}, bf16[32,768]{1,0:T(8,128)(2,1)S(1)}, u32[]{:S(2)}, u32[]{:S(2)}) collective-permute-start(bf16[32,768]{1,0:T(8,128)(2,1)S(1)} %get-tuple-element.52), channel_id=1, source_target_pairs={{0,192},{16,208},{32,224},{48,240},{64,0},{80,16},{96,32},{112,48}... | collective-permute-start | bytes 147464 | tf_op jit(solution)/shard_map/ppermute | solution.py:349

commit v7 on v6

--- a/solution.py
+++ b/solution.py
@@ -96,7 +96,7 @@
 
 def score_kernel(*refs):
     blocks, (mine_ref, other_ref), outs = refs[:8], refs[8:10], refs[10:14]
-    rows_ref, sem = refs[14:]
+    rows_ref, cols_ref, sem = refs[14:]
     step = pl.program_id(0)
     x, _, y, z_hi, core = place()
 
@@ -110,14 +110,16 @@
             copy.start()
         for copy in copies:
             copy.wait()
+        for k in range(0, FEATURES, COLS):
+            cols_ref[k : k + COLS, :] = rows_ref[:, k : k + COLS].T
 
     def part(weights_ref, rel_core, tile):
         got = lax.dot_general(
-            rows_ref[...],
             weights_ref[...],
-            (((1,), (1,)), ((), ())),
+            cols_ref[...],
+            (((1,), (0,)), ((), ())),
             preferred_element_type=F32,
-        ).astype(BF16)
+        ).T.astype(BF16)
         for rel_z in range(2):
             to_x = 2 * ((z_hi + rel_z) % 2) + core
             away = (to_x - x + 4) % 4
@@ -157,9 +159,10 @@
         out_specs=[out] * 4,
         scratch_shapes=[
             pltpu.VMEM((8 * ROWS, FEATURES), BF16),
+            pltpu.VMEM((FEATURES, 8 * ROWS), BF16),
             pltpu.SemaphoreType.DMA((8,)),
         ],
-        compiler_params=pltpu.CompilerParams(vmem_limit_bytes=18 << 20),
+        compiler_params=pltpu.CompilerParams(vmem_limit_bytes=20 << 20),
         cost_estimate=pl.CostEstimate(flops=1, bytes_accessed=1, transcendentals=0),
         name="partial_scores",
     )(*blocks, mine, other)
@@ -293,7 +296,7 @@
     a_bufs = list(partial_scores(a_blocks, stored, other))
     (far_b_above,) = after((far_b_above,), a_bufs[1])
     far_b_opposite = down(far_b_above)
-    a_bufs[2:3] = after(a_bufs[2:3], b_opposite, far_b_below)
+    a_bufs[0:1] = after(a_bufs[0:1], b_opposite, far_b_below)
     b_blocks = [b, b_below, b_above, b_opposite, far_b, far_b_below, far_b_above, far_b_opposite]
     return a_bufs, b_blocks
 
@@ -339,7 +342,7 @@
     a_bufs, b_blocks = first_scores(a, b, stored, other)
     a_got = over_x(a_bufs)
     b_bufs = list(partial_scores(b_blocks, stored, other))
-    b_bufs = after(b_bufs, *a_got[:3])
+    b_bufs = after(b_bufs, *a_got)
     b_got = over_x(b_bufs)
     parts = []
     for got, bufs in ((a_got, a_bufs), (b_got, b_bufs)):

time: 91.9 us -> 96.1 us (1.046)
  starting transfers between devices: 44.3 us -> 49.8 us
  waiting for transfers between devices: 27.9 us -> 26.8 us
    ppermute x6, starting transfers between devices: 3.65 us -> 7.87 us  [on_device(): lax.ppermute(send, 'store', store_pairs(lambda x, z: (x, z + k)))]
    ppermute x6, waiting for transfers between devices: 5.6 us -> 3.98 us  [on_device(): lax.ppermute(send, 'store', store_pairs(lambda x, z: (x, z + k)))]
    ppermute x8, starting transfers between devices: 12 us -> 13.4 us  [send(): return lax.ppermute(value, ('store', 'group'), all_pairs(move))]
  transfers between devices with their start and end apart: 29 -> 29, of which waited for: 13 -> 10; matrix products, arithmetic and copies ran while one was open for 0% -> 0% of each run, Pallas kernels for 18% -> 18%
where the time goes in v7:
time: 96.1 us; the launch traced here: 95.4 us
  starting transfers between devices  49.8 us (52%)
  waiting for transfers between devices  26.8 us (28%)
  Pallas kernels  18.2 us (19%)
    ppermute x14, starting transfers between devices, along(): return lax.ppermute(value, 'group', group_pairs(move))  28.5 us
    ppermute x14, waiting for transfers between devices, along(): return lax.ppermute(value, 'group', group_pairs(move))  16.1 us
    ppermute x8, starting transfers between devices, send(): return lax.ppermute(value, ('store', 'group'), all_pairs(move))  13.4 us
    pallas_call x2, Pallas kernels, partial_scores(): pl.pallas_call(score_kernel, out_shape=[jax.ShapeDtypeStruct((4 * ROWS, H...  11.5 us
    ppermute x6, starting transfers between devices, on_device(): lax.ppermute(send, 'store', store_pairs(lambda x, z: (x, z + k)))  7.87 us
    ppermute x8, waiting for transfers between devices, send(): return lax.ppermute(value, ('store', 'group'), all_pairs(move))  6.68 us
    pallas_call x2, Pallas kernels, query_grads(): pl.pallas_call(functools.partial(grad_kernel, chunk * ROWS), out_shape=ja...  5.12 us
    ppermute x6, waiting for transfers between devices, on_device(): lax.ppermute(send, 'store', store_pairs(lambda x, z: (x, z + k)))  3.98 us
  transfers between devices with their start and end apart: 29, of which 10 were waited for; matrix products, arithmetic and copies ran while one was open for 0% of the time, Pallas kernels for 18%

profile of v7, /device:TPU:32, one launch (start us, length us, event | category | flops | bytes accessed | tf_op | source)
XLA Modules:
  0.0 95.4 jit_solution(3296146239432678661)
XLA Ops:
  0.0 2.5 %query_grads.2.refs_0_ = bf16[32,4096]{1,0:T(8,128)(2,1)S(1)} custom-call(s32[64]{0:T(128)} %lengths_hbm.3, bf16[64,1,64,256]{3,2,1,0:T(8,128)(2,1)} %acts_hbm.3, bf16[64,1,64,256]{3,2,1,0:T(8,128)(2,1)} %grads_hbm.3), custom_call_target="tpu_custom_call" | custom-call | tf_op jit(solution)/shard_map/query_grads/pallas_call | solution.py:81
  2.5 6.3 %collective-permute-start = (bf16[32,4096]{1,0:T(8,128)(2,1)S(1)}, bf16[32,4096]{1,0:T(8,128)(2,1)S(1)}, u32[]{:S(2)}, u32[]{:S(2)}) collective-permute-start(bf16[32,4096]{1,0:T(8,128)(2,1)S(1)} %query_grads.2.refs_0_), channel_id=1, source_target_pairs={{0,2},{1,3},{2,0},{3,1},{4,6},{5,7},{6,4},{7,5},{8,10},{9,11},{10,... | collective-permute-start | bytes 786440 | tf_op jit(solution)/shard_map/ppermute | solution.py:250
  8.9 1.6 %collective-permute-start.1 = (bf16[32,4096]{1,0:T(8,128)(2,1)S(1)}, bf16[32,4096]{1,0:T(8,128)(2,1)S(1)}, u32[]{:S(2)}, u32[]{:S(2)}) collective-permute-start(bf16[32,4096]{1,0:T(8,128)(2,1)S(1)} %query_grads.2.refs_0_), channel_id=1, source_target_pairs={{0,4},{1,5},{2,6},{3,7},{4,8},{5,9},{6,10},{7,11},{8,12},{9,13},{1... | collective-permute-start | bytes 786440 | tf_op jit(solution)/shard_map/ppermute | solution.py:250
  10.4 1.7 %collective-permute-start.2 = (bf16[32,4096]{1,0:T(8,128)(2,1)S(1)}, bf16[32,4096]{1,0:T(8,128)(2,1)S(1)}, u32[]{:S(2)}, u32[]{:S(2)}) collective-permute-start(bf16[32,4096]{1,0:T(8,128)(2,1)S(1)} %query_grads.2.refs_0_), channel_id=1, source_target_pairs={{0,12},{1,13},{2,14},{3,15},{4,0},{5,1},{6,2},{7,3},{8,4},{9,5},{1... | collective-permute-start | bytes 786440 | tf_op jit(solution)/shard_map/ppermute | solution.py:250
  12.1 2.6 %query_grads.3.refs_0_ = bf16[32,4096]{1,0:T(8,128)(2,1)S(1)} custom-call(s32[64]{0:T(128)} %lengths_hbm.3, bf16[64,1,64,256]{3,2,1,0:T(8,128)(2,1)} %acts_hbm.3, bf16[64,1,64,256]{3,2,1,0:T(8,128)(2,1)} %grads_hbm.3), custom_call_target="tpu_custom_call" | custom-call | tf_op jit(solution)/shard_map/query_grads/pallas_call | solution.py:81
  15.2 2.9 %collective-permute-start.5 = (bf16[32,4096]{1,0:T(8,128)(2,1)S(1)}, bf16[32,4096]{1,0:T(8,128)(2,1)S(1)}, u32[]{:S(2)}, u32[]{:S(2)}) collective-permute-start(bf16[32,4096]{1,0:T(8,128)(2,1)S(1)} %fence.6.refs_0_), channel_id=1, source_target_pairs={{0,12},{1,13},{2,14},{3,15},{4,0},{5,1},{6,2},{7,3},{8,4},{9,5},{1... | collective-permute-start | bytes 786440 | tf_op jit(solution)/shard_map/ppermute | solution.py:250
  18.1 3.5 %collective-permute-done.refs_0_ = bf16[32,4096]{1,0:T(8,128)(2,1)S(1)} collective-permute-done((bf16[32,4096]{1,0:T(8,128)(2,1)S(1)}, bf16[32,4096]{1,0:T(8,128)(2,1)S(1)}, u32[]{:S(2)}, u32[]{:S(2)}) %collective-permute-start) | collective-permute-done | bytes 262176 | tf_op jit(solution)/shard_map/ppermute | solution.py:250
  21.6 2.6 %collective-permute-done.4.refs_3_.refs_1_ = bf16[32,4096]{1,0:T(8,128)(2,1)S(1)} collective-permute-done((bf16[32,4096]{1,0:T(8,128)(2,1)S(1)}, bf16[32,4096]{1,0:T(8,128)(2,1)S(1)}, u32[]{:S(2)}, u32[]{:S(2)}) %collective-permute-start.4) | collective-permute-done | bytes 262176 | tf_op jit(solution)/shard_map/ppermute | solution.py:250
  24.2 2.9 %collective-permute-start.8 = (bf16[32,4096]{1,0:T(8,128)(2,1)S(1)}, bf16[32,4096]{1,0:T(8,128)(2,1)S(1)}, u32[]{:S(2)}, u32[]{:S(2)}) collective-permute-start(bf16[32,4096]{1,0:T(8,128)(2,1)S(1)} %get-tuple-element.30.refs_4_), channel_id=1, source_target_pairs={{0,12},{1,13},{2,14},{3,15},{4,0},{5,1},{6,2},{7,3},{8,4},{9,5},{1... | collective-permute-start | bytes 786440 | tf_op jit(solution)/shard_map/ppermute | solution.py:250
  27.2 3.1 %collective-permute-start.11 = (bf16[32,4096]{1,0:T(8,128)(2,1)S(1)}, bf16[32,4096]{1,0:T(8,128)(2,1)S(1)}, u32[]{:S(2)}, u32[]{:S(2)}) collective-permute-start(bf16[32,4096]{1,0:T(8,128)(2,1)S(1)} %fence.6.refs_0_), channel_id=1, source_target_pairs={{0,2},{1,3},{2,0},{3,1},{4,6},{5,7},{6,4},{7,5},{8,10},{9,11},{10,... | collective-permute-start | bytes 786440 | tf_op jit(solution)/shard_map/ppermute | solution.py:250
  30.8 0.8 collective-permute-done.8.refs_6_
  31.6 3.7 %collective-permute-start.9 = (bf16[32,4096]{1,0:T(8,128)(2,1)S(1)}, bf16[32,4096]{1,0:T(8,128)(2,1)S(1)}, u32[]{:S(2)}, u32[]{:S(2)}) collective-permute-start(bf16[32,4096]{1,0:T(8,128)(2,1)S(1)} %collective-permute-done.8.refs_6_), channel_id=1, source_target_pairs={{0,12},{1,13},{2,14},{3,15},{4,0},{5,1},{6,2},{7,3},{8,4},{9,5},{1... | collective-permute-start | bytes 786440 | tf_op jit(solution)/shard_map/ppermute | solution.py:250
  35.3 8.0 %collective-permute-done.11.refs_0_ = bf16[32,4096]{1,0:T(8,128)(2,1)S(1)} collective-permute-done((bf16[32,4096]{1,0:T(8,128)(2,1)S(1)}, bf16[32,4096]{1,0:T(8,128)(2,1)S(1)}, u32[]{:S(2)}, u32[]{:S(2)}) %collective-permute-start.11) | collective-permute-done | bytes 262176 | tf_op jit(solution)/shard_map/ppermute | solution.py:250
  43.4 1.1 %collective-permute-done.6.refs_3_.refs_2_ = bf16[32,4096]{1,0:T(8,128)(2,1)S(1)} collective-permute-done((bf16[32,4096]{1,0:T(8,128)(2,1)S(1)}, bf16[32,4096]{1,0:T(8,128)(2,1)S(1)}, u32[]{:S(2)}, u32[]{:S(2)}) %collective-permute-start.6) | collective-permute-done | bytes 262176 | tf_op jit(solution)/shard_map/ppermute | solution.py:250
  44.6 2.0 %collective-permute-start.12 = (bf16[32,4096]{1,0:T(8,128)(2,1)S(1)}, bf16[32,4096]{1,0:T(8,128)(2,1)S(1)}, u32[]{:S(2)}, u32[]{:S(2)}) collective-permute-start(bf16[32,4096]{1,0:T(8,128)(2,1)S(1)} %get-tuple-element.33.refs_1_), channel_id=1, source_target_pairs={{0,4},{1,5},{2,6},{3,7},{4,8},{5,9},{6,10},{7,11},{8,12},{9,13},{1... | collective-permute-start | bytes 786440 | tf_op jit(solution)/shard_map/ppermute | solution.py:250
  46.6 5.8 %partial_scores.2 = (bf16[128,768]{1,0:T(8,128)(2,1)S(1)}, bf16[128,768]{1,0:T(8,128)(2,1)S(1)}, bf16[128,768]{1,0:T(8,128)(2,1)S(1)}, bf16[128,768]{1,0:T(8,128)(2,1)S(1)}) custom-call(bf16[32,4096]{1,0:T(8,128)(2,1)S(1)} %query_grads.2.refs_0_, bf16[32,4096]{1,0:T(8,128)(2,1)S(1)} %get-tuple-element.29.refs_1_, ...), custom_call_target="tpu_custom_call" | custom-call | flops 1 | bytes 1 | tf_op jit(solution)/shard_map/partial_scores/pallas_call | solution.py:150
  52.4 2.8 %collective-permute-start.10 = (bf16[128,768]{1,0:T(8,128)(2,1)S(1)}, bf16[128,768]{1,0:T(8,128)(2,1)S(1)}, u32[]{:S(2)}, u32[]{:S(2)}) collective-permute-start(bf16[128,768]{1,0:T(8,128)(2,1)S(1)} %get-tuple-element.31), channel_id=1, source_target_pairs={{0,48},{1,17},{2,50},{3,19},{4,52},{5,21},{6,54},{7,23},{8,56},{9,... | collective-permute-start | bytes 589832 | tf_op jit(solution)/shard_map/ppermute | solution.py:321
  55.2 3.2 %collective-permute-start.21 = (bf16[32,4096]{1,0:T(8,128)(2,1)S(1)}, bf16[32,4096]{1,0:T(8,128)(2,1)S(1)}, u32[]{:S(2)}, u32[]{:S(2)}) collective-permute-start(bf16[32,4096]{1,0:T(8,128)(2,1)S(1)} %fence.10.refs_6_), channel_id=1, source_target_pairs={{0,12},{1,13},{2,14},{3,15},{4,0},{5,1},{6,2},{7,3},{8,4},{9,5},{1... | collective-permute-start | bytes 786440 | tf_op jit(solution)/shard_map/ppermute | solution.py:250
  58.4 0.9 collective-permute-start.15
  59.2 1.2 %collective-permute-done.10.got_ref.b_ref.refs_4_ = bf16[128,768]{1,0:T(8,128)(2,1)S(1)} collective-permute-done((bf16[128,768]{1,0:T(8,128)(2,1)S(1)}, bf16[128,768]{1,0:T(8,128)(2,1)S(1)}, u32[]{:S(2)}, u32[]{:S(2)}) %collective-permute-start.10) | collective-permute-done | bytes 196640 | tf_op jit(solution)/shard_map/ppermute | solution.py:321
  60.6 0.7 collective-permute-start.16
  61.3 5.4 %collective-permute-start.14 = (bf16[128,768]{1,0:T(8,128)(2,1)S(1)}, bf16[128,768]{1,0:T(8,128)(2,1)S(1)}, u32[]{:S(2)}, u32[]{:S(2)}) collective-permute-start(bf16[128,768]{1,0:T(8,128)(2,1)S(1)} %fence.9), channel_id=1, source_target_pairs={{0,1},{1,49},{2,3},{3,51},{4,5},{5,53},{6,7},{7,55},{8,9},{9,57},{... | collective-permute-start | bytes 589832 | tf_op jit(solution)/shard_map/ppermute | solution.py:321
  66.6 5.8 %partial_scores.3 = (bf16[128,768]{1,0:T(8,128)(2,1)S(1)}, bf16[128,768]{1,0:T(8,128)(2,1)S(1)}, bf16[128,768]{1,0:T(8,128)(2,1)S(1)}, bf16[128,768]{1,0:T(8,128)(2,1)S(1)}) custom-call(bf16[32,4096]{1,0:T(8,128)(2,1)S(1)} %fence.6.refs_0_, bf16[32,4096]{1,0:T(8,128)(2,1)S(1)} %get-tuple-element.33.refs_1_, ...), custom_call_target="tpu_custom_call" | custom-call | flops 1 | bytes 1 | tf_op jit(solution)/shard_map/partial_scores/pallas_call | solution.py:150
  72.7 2.9 %collective-permute-start.24 = (bf16[128,768]{1,0:T(8,128)(2,1)S(1)}, bf16[128,768]{1,0:T(8,128)(2,1)S(1)}, u32[]{:S(2)}, u32[]{:S(2)}) collective-permute-start(bf16[128,768]{1,0:T(8,128)(2,1)S(1)} %get-tuple-element.47), channel_id=1, source_target_pairs={{0,32},{1,16},{2,34},{3,18},{4,36},{5,20},{6,38},{7,22},{8,40},{9,... | collective-permute-start | bytes 589832 | tf_op jit(solution)/shard_map/ppermute | solution.py:321
  75.6 5.4 %collective-permute-done.22.got_ref.b_ref = bf16[128,768]{1,0:T(8,128)(2,1)S(1)} collective-permute-done((bf16[128,768]{1,0:T(8,128)(2,1)S(1)}, bf16[128,768]{1,0:T(8,128)(2,1)S(1)}, u32[]{:S(2)}, u32[]{:S(2)}) %collective-permute-start.22) | collective-permute-done | bytes 196640 | tf_op jit(solution)/shard_map/ppermute | solution.py:321
  81.9 1.0 %collective-permute-start.17 = (bf16[32,768]{1,0:T(8,128)(2,1)S(1)}, bf16[32,768]{1,0:T(8,128)(2,1)S(1)}, u32[]{:S(2)}, u32[]{:S(2)}) collective-permute-start(bf16[32,768]{1,0:T(8,128)(2,1)S(1)} %get-tuple-element.38), channel_id=1, source_target_pairs={{0,64},{16,80},{32,96},{48,112},{64,128},{80,144},{96,160},{112,17... | collective-permute-start | bytes 147464 | tf_op jit(solution)/shard_map/ppermute | solution.py:352
  83.0 1.6 %collective-permute-start.19 = (bf16[32,768]{1,0:T(8,128)(2,1)S(1)}, bf16[32,768]{1,0:T(8,128)(2,1)S(1)}, u32[]{:S(2)}, u32[]{:S(2)}) collective-permute-start(bf16[32,768]{1,0:T(8,128)(2,1)S(1)} %get-tuple-element.40), channel_id=1, source_target_pairs={{0,192},{16,208},{32,224},{48,240},{64,0},{80,16},{96,32},{112,48}... | collective-permute-start | bytes 147464 | tf_op jit(solution)/shard_map/ppermute | solution.py:352
  84.7 1.1 %collective-permute-start.26 = (bf16[32,768]{1,0:T(8,128)(2,1)S(1)}, bf16[32,768]{1,0:T(8,128)(2,1)S(1)}, u32[]{:S(2)}, u32[]{:S(2)}) collective-permute-start(bf16[32,768]{1,0:T(8,128)(2,1)S(1)} %get-tuple-element.50), channel_id=1, source_target_pairs={{0,64},{16,80},{32,96},{48,112},{64,128},{80,144},{96,160},{112,17... | collective-permute-start | bytes 147464 | tf_op jit(solution)/shard_map/ppermute | solution.py:352
  85.7 4.2 %collective-permute-start.27 = (bf16[32,768]{1,0:T(8,128)(2,1)S(1)}, bf16[32,768]{1,0:T(8,128)(2,1)S(1)}, u32[]{:S(2)}, u32[]{:S(2)}) collective-permute-start(bf16[32,768]{1,0:T(8,128)(2,1)S(1)} %get-tuple-element.51), channel_id=1, source_target_pairs={{0,128},{16,144},{32,160},{48,176},{64,192},{80,208},{96,224},{112... | collective-permute-start | bytes 147464 | tf_op jit(solution)/shard_map/ppermute | solution.py:352
  90.9 2.4 %collective-permute-done.27.refs_6_ = bf16[32,768]{1,0:T(8,128)(2,1)S(1)} collective-permute-done((bf16[32,768]{1,0:T(8,128)(2,1)S(1)}, bf16[32,768]{1,0:T(8,128)(2,1)S(1)}, u32[]{:S(2)}, u32[]{:S(2)}) %collective-permute-start.27) | collective-permute-done | bytes 49184 | tf_op jit(solution)/shard_map/ppermute | solution.py:352
  93.4 1.0 %collective-permute-done.28.refs_7_ = bf16[32,768]{1,0:T(8,128)(2,1)S(1)} collective-permute-done((bf16[32,768]{1,0:T(8,128)(2,1)S(1)}, bf16[32,768]{1,0:T(8,128)(2,1)S(1)}, u32[]{:S(2)}, u32[]{:S(2)}) %collective-permute-start.28) | collective-permute-done | bytes 49184 | tf_op jit(solution)/shard_map/ppermute | solution.py:352
  94.3 1.1 %final_sum.1 = f32[64,768]{1,0:T(8,128)} custom-call(f32[32,768]{1,0:T(8,128)S(1)} %get-tuple-element.37.refs_0_, bf16[32,768]{1,0:T(8,128)(2,1)S(1)} %collective-permute-done.17.refs_1_, bf16[32,768]{1,0:T(8,128)(2,1)S(1)} %collective-permute-done.18.refs_2_, bf16[32,768]{1,0:T(8,128)(2,1)S(1)} %collective-permute-done.19.refs_3_, ...), custom_call_target="tpu_custom_call" | custom-call | tf_op jit(solution)/shard_map/final_sum/pallas_call | solution.py:217
  (49 shorter events, 3.5 us)
Async XLA Ops:
  0.0 14.8 %collective-permute-start.3 = (bf16[768,4096]{1,0:T(8,128)(2,1)}, bf16[768,4096]{1,0:T(8,128)(2,1)S(1)}, u32[]{:S(2)}, u32[]{:S(2)}) collective-permute-start(bf16[768,4096]{1,0:T(8,128)(2,1)} %bitcast.1), channel_id=1, source_target_pairs={{0,1},{1,0},{2,3},{3,2},{4,5},{5,4},{6,7},{7,6},{8,9},{9,8},{10,11... | collective-permute-start | bytes 18874376 | tf_op jit(solution)/shard_map/ppermute | solution.py:336
  2.5 19.1 %collective-permute-start = (bf16[32,4096]{1,0:T(8,128)(2,1)S(1)}, bf16[32,4096]{1,0:T(8,128)(2,1)S(1)}, u32[]{:S(2)}, u32[]{:S(2)}) collective-permute-start(bf16[32,4096]{1,0:T(8,128)(2,1)S(1)} %query_grads.2.refs_0_), channel_id=1, source_target_pairs={{0,2},{1,3},{2,0},{3,1},{4,6},{5,7},{6,4},{7,5},{8,10},{9,11},{10,... | collective-permute-start | bytes 786440 | tf_op jit(solution)/shard_map/ppermute | solution.py:250
  8.9 12.7 %collective-permute-start.1 = (bf16[32,4096]{1,0:T(8,128)(2,1)S(1)}, bf16[32,4096]{1,0:T(8,128)(2,1)S(1)}, u32[]{:S(2)}, u32[]{:S(2)}) collective-permute-start(bf16[32,4096]{1,0:T(8,128)(2,1)S(1)} %query_grads.2.refs_0_), channel_id=1, source_target_pairs={{0,4},{1,5},{2,6},{3,7},{4,8},{5,9},{6,10},{7,11},{8,12},{9,13},{1... | collective-permute-start | bytes 786440 | tf_op jit(solution)/shard_map/ppermute | solution.py:250
  10.4 11.1 %collective-permute-start.2 = (bf16[32,4096]{1,0:T(8,128)(2,1)S(1)}, bf16[32,4096]{1,0:T(8,128)(2,1)S(1)}, u32[]{:S(2)}, u32[]{:S(2)}) collective-permute-start(bf16[32,4096]{1,0:T(8,128)(2,1)S(1)} %query_grads.2.refs_0_), channel_id=1, source_target_pairs={{0,12},{1,13},{2,14},{3,15},{4,0},{5,1},{6,2},{7,3},{8,4},{9,5},{1... | collective-permute-start | bytes 786440 | tf_op jit(solution)/shard_map/ppermute | solution.py:250
  12.1 34.5 %slice-start = ((s8[6291456]{0:T(1024)(128)(4,1)}), s8[4194304]{0:T(1024)(128)(4,1)S(1)}, s32[]{:S(2)}) async-start(s8[6291456]{0:T(1024)(128)(4,1)} %bitcast.2), calls=%async_computation | async-start | bytes 8388608
  14.7 31.9 %slice-start.1 = ((s8[6291456]{0:T(1024)(128)(4,1)}), s8[2097152]{0:T(1024)(128)(4,1)S(1)}, s32[]{:S(2)}) async-start(s8[6291456]{0:T(1024)(128)(4,1)} %bitcast.2), calls=%async_computation.1 | async-start | bytes 4194304
  14.8 9.4 %collective-permute-start.4 = (bf16[32,4096]{1,0:T(8,128)(2,1)S(1)}, bf16[32,4096]{1,0:T(8,128)(2,1)S(1)}, u32[]{:S(2)}, u32[]{:S(2)}) collective-permute-start(bf16[32,4096]{1,0:T(8,128)(2,1)S(1)} %fence.6.refs_0_), channel_id=1, source_target_pairs={{0,4},{1,5},{2,6},{3,7},{4,8},{5,9},{6,10},{7,11},{8,12},{9,13},{1... | collective-permute-start | bytes 786440 | tf_op jit(solution)/shard_map/ppermute | solution.py:250
  15.2 9.0 %collective-permute-start.5 = (bf16[32,4096]{1,0:T(8,128)(2,1)S(1)}, bf16[32,4096]{1,0:T(8,128)(2,1)S(1)}, u32[]{:S(2)}, u32[]{:S(2)}) collective-permute-start(bf16[32,4096]{1,0:T(8,128)(2,1)S(1)} %fence.6.refs_0_), channel_id=1, source_target_pairs={{0,12},{1,13},{2,14},{3,15},{4,0},{5,1},{6,2},{7,3},{8,4},{9,5},{1... | collective-permute-start | bytes 786440 | tf_op jit(solution)/shard_map/ppermute | solution.py:250
  24.2 7.4 %collective-permute-start.8 = (bf16[32,4096]{1,0:T(8,128)(2,1)S(1)}, bf16[32,4096]{1,0:T(8,128)(2,1)S(1)}, u32[]{:S(2)}, u32[]{:S(2)}) collective-permute-start(bf16[32,4096]{1,0:T(8,128)(2,1)S(1)} %get-tuple-element.30.refs_4_), channel_id=1, source_target_pairs={{0,12},{1,13},{2,14},{3,15},{4,0},{5,1},{6,2},{7,3},{8,4},{9,5},{1... | collective-permute-start | bytes 786440 | tf_op jit(solution)/shard_map/ppermute | solution.py:250
  27.2 16.2 %collective-permute-start.11 = (bf16[32,4096]{1,0:T(8,128)(2,1)S(1)}, bf16[32,4096]{1,0:T(8,128)(2,1)S(1)}, u32[]{:S(2)}, u32[]{:S(2)}) collective-permute-start(bf16[32,4096]{1,0:T(8,128)(2,1)S(1)} %fence.6.refs_0_), channel_id=1, source_target_pairs={{0,2},{1,3},{2,0},{3,1},{4,6},{5,7},{6,4},{7,5},{8,10},{9,11},{10,... | collective-permute-start | bytes 786440 | tf_op jit(solution)/shard_map/ppermute | solution.py:250
  30.3 14.2 %collective-permute-start.7 = (bf16[32,4096]{1,0:T(8,128)(2,1)S(1)}, bf16[32,4096]{1,0:T(8,128)(2,1)S(1)}, u32[]{:S(2)}, u32[]{:S(2)}) collective-permute-start(bf16[32,4096]{1,0:T(8,128)(2,1)S(1)} %get-tuple-element.30.refs_4_), channel_id=1, source_target_pairs={{0,4},{1,5},{2,6},{3,7},{4,8},{5,9},{6,10},{7,11},{8,12},{9,13},{1... | collective-permute-start | bytes 786440 | tf_op jit(solution)/shard_map/ppermute | solution.py:250
  30.3 14.2 %collective-permute-start.6 = (bf16[32,4096]{1,0:T(8,128)(2,1)S(1)}, bf16[32,4096]{1,0:T(8,128)(2,1)S(1)}, u32[]{:S(2)}, u32[]{:S(2)}) collective-permute-start(bf16[32,4096]{1,0:T(8,128)(2,1)S(1)} %get-tuple-element.29.refs_1_), channel_id=1, source_target_pairs={{0,4},{1,5},{2,6},{3,7},{4,8},{5,9},{6,10},{7,11},{8,12},{9,13},{1... | collective-permute-start | bytes 786440 | tf_op jit(solution)/shard_map/ppermute | solution.py:250
  31.6 12.9 %collective-permute-start.9 = (bf16[32,4096]{1,0:T(8,128)(2,1)S(1)}, bf16[32,4096]{1,0:T(8,128)(2,1)S(1)}, u32[]{:S(2)}, u32[]{:S(2)}) collective-permute-start(bf16[32,4096]{1,0:T(8,128)(2,1)S(1)} %collective-permute-done.8.refs_6_), channel_id=1, source_target_pairs={{0,12},{1,13},{2,14},{3,15},{4,0},{5,1},{6,2},{7,3},{8,4},{9,5},{1... | collective-permute-start | bytes 786440 | tf_op jit(solution)/shard_map/ppermute | solution.py:250
  44.5 10.7 %collective-permute-start.20 = (bf16[32,4096]{1,0:T(8,128)(2,1)S(1)}, bf16[32,4096]{1,0:T(8,128)(2,1)S(1)}, u32[]{:S(2)}, u32[]{:S(2)}) collective-permute-start(bf16[32,4096]{1,0:T(8,128)(2,1)S(1)} %get-tuple-element.34.refs_4_), channel_id=1, source_target_pairs={{0,12},{1,13},{2,14},{3,15},{4,0},{5,1},{6,2},{7,3},{8,4},{9,5},{1... | collective-permute-start | bytes 786440 | tf_op jit(solution)/shard_map/ppermute | solution.py:250
  44.6 16.7 %collective-permute-start.12 = (bf16[32,4096]{1,0:T(8,128)(2,1)S(1)}, bf16[32,4096]{1,0:T(8,128)(2,1)S(1)}, u32[]{:S(2)}, u32[]{:S(2)}) collective-permute-start(bf16[32,4096]{1,0:T(8,128)(2,1)S(1)} %get-tuple-element.33.refs_1_), channel_id=1, source_target_pairs={{0,4},{1,5},{2,6},{3,7},{4,8},{5,9},{6,10},{7,11},{8,12},{9,13},{1... | collective-permute-start | bytes 786440 | tf_op jit(solution)/shard_map/ppermute | solution.py:250
  46.6 14.7 %collective-permute-start.13 = (bf16[32,4096]{1,0:T(8,128)(2,1)S(1)}, bf16[32,4096]{1,0:T(8,128)(2,1)S(1)}, u32[]{:S(2)}, u32[]{:S(2)}) collective-permute-start(bf16[32,4096]{1,0:T(8,128)(2,1)S(1)} %get-tuple-element.34.refs_4_), channel_id=1, source_target_pairs={{0,4},{1,5},{2,6},{3,7},{4,8},{5,9},{6,10},{7,11},{8,12},{9,13},{1... | collective-permute-start | bytes 786440 | tf_op jit(solution)/shard_map/ppermute | solution.py:250
  52.4 8.0 %collective-permute-start.10 = (bf16[128,768]{1,0:T(8,128)(2,1)S(1)}, bf16[128,768]{1,0:T(8,128)(2,1)S(1)}, u32[]{:S(2)}, u32[]{:S(2)}) collective-permute-start(bf16[128,768]{1,0:T(8,128)(2,1)S(1)} %get-tuple-element.31), channel_id=1, source_target_pairs={{0,48},{1,17},{2,50},{3,19},{4,52},{5,21},{6,54},{7,23},{8,56},{9,... | collective-permute-start | bytes 589832 | tf_op jit(solution)/shard_map/ppermute | solution.py:321
  55.2 11.4 %collective-permute-start.21 = (bf16[32,4096]{1,0:T(8,128)(2,1)S(1)}, bf16[32,4096]{1,0:T(8,128)(2,1)S(1)}, u32[]{:S(2)}, u32[]{:S(2)}) collective-permute-start(bf16[32,4096]{1,0:T(8,128)(2,1)S(1)} %fence.10.refs_6_), channel_id=1, source_target_pairs={{0,12},{1,13},{2,14},{3,15},{4,0},{5,1},{6,2},{7,3},{8,4},{9,5},{1... | collective-permute-start | bytes 786440 | tf_op jit(solution)/shard_map/ppermute | solution.py:250
  58.4 14.1 %collective-permute-start.15 = (bf16[128,768]{1,0:T(8,128)(2,1)S(1)}, bf16[128,768]{1,0:T(8,128)(2,1)S(1)}, u32[]{:S(2)}, u32[]{:S(2)}) collective-permute-start(bf16[128,768]{1,0:T(8,128)(2,1)S(1)} %get-tuple-element.35), channel_id=1, source_target_pairs={{0,32},{1,16},{2,34},{3,18},{4,36},{5,20},{6,38},{7,22},{8,40},{9,... | collective-permute-start | bytes 589832 | tf_op jit(solution)/shard_map/ppermute | solution.py:321
  60.6 11.9 %collective-permute-start.16 = (bf16[128,768]{1,0:T(8,128)(2,1)S(1)}, bf16[128,768]{1,0:T(8,128)(2,1)S(1)}, u32[]{:S(2)}, u32[]{:S(2)}) collective-permute-start(bf16[128,768]{1,0:T(8,128)(2,1)S(1)} %join.2), channel_id=1, source_target_pairs={{1,48},{3,50},{5,52},{7,54},{9,56},{11,58},{13,60},{15,62},{16,1},... | collective-permute-start | bytes 589832 | tf_op jit(solution)/shard_map/ppermute | solution.py:321
  61.3 11.1 %collective-permute-start.14 = (bf16[128,768]{1,0:T(8,128)(2,1)S(1)}, bf16[128,768]{1,0:T(8,128)(2,1)S(1)}, u32[]{:S(2)}, u32[]{:S(2)}) collective-permute-start(bf16[128,768]{1,0:T(8,128)(2,1)S(1)} %fence.9), channel_id=1, source_target_pairs={{0,1},{1,49},{2,3},{3,51},{4,5},{5,53},{6,7},{7,55},{8,9},{9,57},{... | collective-permute-start | bytes 589832 | tf_op jit(solution)/shard_map/ppermute | solution.py:321
  72.4 17.5 %copy-start = (s32[768]{0:T(1024)S(1)}, s32[768]{0:T(1024)}, u32[]{:S(2)}) copy-start(s32[768]{0:T(1024)} %param.9) | copy-start | bytes 9220
  72.5 8.5 %collective-permute-start.22 = (bf16[128,768]{1,0:T(8,128)(2,1)S(1)}, bf16[128,768]{1,0:T(8,128)(2,1)S(1)}, u32[]{:S(2)}, u32[]{:S(2)}) collective-permute-start(bf16[128,768]{1,0:T(8,128)(2,1)S(1)} %get-tuple-element.45), channel_id=1, source_target_pairs={{0,48},{1,17},{2,50},{3,19},{4,52},{5,21},{6,54},{7,23},{8,56},{9,... | collective-permute-start | bytes 589832 | tf_op jit(solution)/shard_map/ppermute | solution.py:321
  72.6 10.4 %collective-permute-start.23 = (bf16[128,768]{1,0:T(8,128)(2,1)S(1)}, bf16[128,768]{1,0:T(8,128)(2,1)S(1)}, u32[]{:S(2)}, u32[]{:S(2)}) collective-permute-start(bf16[128,768]{1,0:T(8,128)(2,1)S(1)} %get-tuple-element.46), channel_id=1, source_target_pairs={{0,1},{1,49},{2,3},{3,51},{4,5},{5,53},{6,7},{7,55},{8,9},{9,57},{... | collective-permute-start | bytes 589832 | tf_op jit(solution)/shard_map/ppermute | solution.py:321
  72.7 11.8 %collective-permute-start.24 = (bf16[128,768]{1,0:T(8,128)(2,1)S(1)}, bf16[128,768]{1,0:T(8,128)(2,1)S(1)}, u32[]{:S(2)}, u32[]{:S(2)}) collective-permute-start(bf16[128,768]{1,0:T(8,128)(2,1)S(1)} %get-tuple-element.47), channel_id=1, source_target_pairs={{0,32},{1,16},{2,34},{3,18},{4,36},{5,20},{6,38},{7,22},{8,40},{9,... | collective-permute-start | bytes 589832 | tf_op jit(solution)/shard_map/ppermute | solution.py:321
  81.1 3.5 %collective-permute-start.25 = (bf16[128,768]{1,0:T(8,128)(2,1)S(1)}, bf16[128,768]{1,0:T(8,128)(2,1)S(1)}, u32[]{:S(2)}, u32[]{:S(2)}) collective-permute-start(bf16[128,768]{1,0:T(8,128)(2,1)S(1)} %join.3), channel_id=1, source_target_pairs={{1,48},{3,50},{5,52},{7,54},{9,56},{11,58},{13,60},{15,62},{16,1},... | collective-permute-start | bytes 589832 | tf_op jit(solution)/shard_map/ppermute | solution.py:321
  81.9 8.0 %collective-permute-start.17 = (bf16[32,768]{1,0:T(8,128)(2,1)S(1)}, bf16[32,768]{1,0:T(8,128)(2,1)S(1)}, u32[]{:S(2)}, u32[]{:S(2)}) collective-permute-start(bf16[32,768]{1,0:T(8,128)(2,1)S(1)} %get-tuple-element.38), channel_id=1, source_target_pairs={{0,64},{16,80},{32,96},{48,112},{64,128},{80,144},{96,160},{112,17... | collective-permute-start | bytes 147464 | tf_op jit(solution)/shard_map/ppermute | solution.py:352
  83.0 7.4 %collective-permute-start.18 = (bf16[32,768]{1,0:T(8,128)(2,1)S(1)}, bf16[32,768]{1,0:T(8,128)(2,1)S(1)}, u32[]{:S(2)}, u32[]{:S(2)}) collective-permute-start(bf16[32,768]{1,0:T(8,128)(2,1)S(1)} %get-tuple-element.39), channel_id=1, source_target_pairs={{0,128},{16,144},{32,160},{48,176},{64,192},{80,208},{96,224},{112... | collective-permute-start | bytes 147464 | tf_op jit(solution)/shard_map/ppermute | solution.py:352
  83.0 7.4 %collective-permute-start.19 = (bf16[32,768]{1,0:T(8,128)(2,1)S(1)}, bf16[32,768]{1,0:T(8,128)(2,1)S(1)}, u32[]{:S(2)}, u32[]{:S(2)}) collective-permute-start(bf16[32,768]{1,0:T(8,128)(2,1)S(1)} %get-tuple-element.40), channel_id=1, source_target_pairs={{0,192},{16,208},{32,224},{48,240},{64,0},{80,16},{96,32},{112,48}... | collective-permute-start | bytes 147464 | tf_op jit(solution)/shard_map/ppermute | solution.py:352
  84.7 6.3 %collective-permute-start.26 = (bf16[32,768]{1,0:T(8,128)(2,1)S(1)}, bf16[32,768]{1,0:T(8,128)(2,1)S(1)}, u32[]{:S(2)}, u32[]{:S(2)}) collective-permute-start(bf16[32,768]{1,0:T(8,128)(2,1)S(1)} %get-tuple-element.50), channel_id=1, source_target_pairs={{0,64},{16,80},{32,96},{48,112},{64,128},{80,144},{96,160},{112,17... | collective-permute-start | bytes 147464 | tf_op jit(solution)/shard_map/ppermute | solution.py:352
  85.7 7.6 %collective-permute-start.27 = (bf16[32,768]{1,0:T(8,128)(2,1)S(1)}, bf16[32,768]{1,0:T(8,128)(2,1)S(1)}, u32[]{:S(2)}, u32[]{:S(2)}) collective-permute-start(bf16[32,768]{1,0:T(8,128)(2,1)S(1)} %get-tuple-element.51), channel_id=1, source_target_pairs={{0,128},{16,144},{32,160},{48,176},{64,192},{80,208},{96,224},{112... | collective-permute-start | bytes 147464 | tf_op jit(solution)/shard_map/ppermute | solution.py:352
  89.9 4.4 %collective-permute-start.28 = (bf16[32,768]{1,0:T(8,128)(2,1)S(1)}, bf16[32,768]{1,0:T(8,128)(2,1)S(1)}, u32[]{:S(2)}, u32[]{:S(2)}) collective-permute-start(bf16[32,768]{1,0:T(8,128)(2,1)S(1)} %get-tuple-element.52), channel_id=1, source_target_pairs={{0,192},{16,208},{32,224},{48,240},{64,0},{80,16},{96,32},{112,48}... | collective-permute-start | bytes 147464 | tf_op jit(solution)/shard_map/ppermute | solution.py:352

commit v8 on v6

--- a/solution.py
+++ b/solution.py
@@ -282,18 +282,17 @@
     (b,) = after((b,), other)
     far_b = beyond(b)
     b_below, b_above = up(b), down(b)
-    far_a, a_below = after((far_a, a_below), a_above, b_below, b_above)
+    far_a, a_below, a_above = after((far_a, a_below, a_above), b_below, b_above)
     a_opposite = up(a_below)
     far_a_above, far_a_below = down(far_a), up(far_a)
     far_a_opposite = down(far_a_above)
-    far_b, b_below = after((far_b, b_below), a_opposite, far_a_opposite, far_a_below)
+    far_b, b_below = after((far_b, b_below), far_a_above, far_a_below)
     b_opposite = up(b_below)
     far_b_above, far_b_below = down(far_b), up(far_b)
     a_blocks = [a, a_below, a_above, a_opposite, far_a, far_a_below, far_a_above, far_a_opposite]
     a_bufs = list(partial_scores(a_blocks, stored, other))
     (far_b_above,) = after((far_b_above,), a_bufs[1])
     far_b_opposite = down(far_b_above)
-    a_bufs[2:3] = after(a_bufs[2:3], b_opposite, far_b_below)
     b_blocks = [b, b_below, b_above, b_opposite, far_b, far_b_below, far_b_above, far_b_opposite]
     return a_bufs, b_blocks
 

time: 91.9 us -> 89.6 us (0.975)
  waiting for transfers between devices: 27.9 us -> 25.7 us
    ppermute x8, starting transfers between devices: 12 us -> 10.2 us  [send(): return lax.ppermute(value, ('store', 'group'), all_pairs(move))]
    ppermute x6, starting transfers between devices: 3.65 us -> 5.36 us  [on_device(): lax.ppermute(send, 'store', store_pairs(lambda x, z: (x, z + k)))]
    ppermute x8, waiting for transfers between devices: 6.01 us -> 5.06 us  [send(): return lax.ppermute(value, ('store', 'group'), all_pairs(move))]
  transfers between devices with their start and end apart: 29 -> 29, of which waited for: 13 -> 13; matrix products, arithmetic and copies ran while one was open for 0% -> 0% of each run, Pallas kernels for 18% -> 19%
where the time goes in v8:
time: 89.6 us; the launch traced here: 88 us
  starting transfers between devices  44.1 us (49%)
  waiting for transfers between devices  25.7 us (29%)
  Pallas kernels  17.6 us (20%)
    ppermute x14, starting transfers between devices, along(): return lax.ppermute(value, 'group', group_pairs(move))  28.5 us
    ppermute x14, waiting for transfers between devices, along(): return lax.ppermute(value, 'group', group_pairs(move))  15.4 us
    pallas_call x2, Pallas kernels, partial_scores(): pl.pallas_call(score_kernel, out_shape=[jax.ShapeDtypeStruct((4 * ROWS, H...  10.9 us
    ppermute x8, starting transfers between devices, send(): return lax.ppermute(value, ('store', 'group'), all_pairs(move))  10.2 us
    ppermute x6, starting transfers between devices, on_device(): lax.ppermute(send, 'store', store_pairs(lambda x, z: (x, z + k)))  5.36 us
    ppermute x6, waiting for transfers between devices, on_device(): lax.ppermute(send, 'store', store_pairs(lambda x, z: (x, z + k)))  5.26 us
    pallas_call x2, Pallas kernels, query_grads(): pl.pallas_call(functools.partial(grad_kernel, chunk * ROWS), out_shape=ja...  5.12 us
    ppermute x8, waiting for transfers between devices, send(): return lax.ppermute(value, ('store', 'group'), all_pairs(move))  5.06 us
  transfers between devices with their start and end apart: 29, of which 13 were waited for; matrix products, arithmetic and copies ran while one was open for 0% of the time, Pallas kernels for 19%

profile of v8, /device:TPU:32, one launch (start us, length us, event | category | flops | bytes accessed | tf_op | source)
XLA Modules:
  0.0 88.0 jit_solution(238237354137219070)
XLA Ops:
  0.0 2.5 %query_grads.2.refs_0_ = bf16[32,4096]{1,0:T(8,128)(2,1)S(1)} custom-call(s32[64]{0:T(128)} %lengths_hbm.3, bf16[64,1,64,256]{3,2,1,0:T(8,128)(2,1)} %acts_hbm.3, bf16[64,1,64,256]{3,2,1,0:T(8,128)(2,1)} %grads_hbm.3), custom_call_target="tpu_custom_call" | custom-call | tf_op jit(solution)/shard_map/query_grads/pallas_call | solution.py:81
  2.5 6.3 %collective-permute-start = (bf16[32,4096]{1,0:T(8,128)(2,1)S(1)}, bf16[32,4096]{1,0:T(8,128)(2,1)S(1)}, u32[]{:S(2)}, u32[]{:S(2)}) collective-permute-start(bf16[32,4096]{1,0:T(8,128)(2,1)S(1)} %query_grads.2.refs_0_), channel_id=1, source_target_pairs={{0,2},{1,3},{2,0},{3,1},{4,6},{5,7},{6,4},{7,5},{8,10},{9,11},{10,... | collective-permute-start | bytes 786440 | tf_op jit(solution)/shard_map/ppermute | solution.py:247
  8.9 1.6 %collective-permute-start.1 = (bf16[32,4096]{1,0:T(8,128)(2,1)S(1)}, bf16[32,4096]{1,0:T(8,128)(2,1)S(1)}, u32[]{:S(2)}, u32[]{:S(2)}) collective-permute-start(bf16[32,4096]{1,0:T(8,128)(2,1)S(1)} %query_grads.2.refs_0_), channel_id=1, source_target_pairs={{0,4},{1,5},{2,6},{3,7},{4,8},{5,9},{6,10},{7,11},{8,12},{9,13},{1... | collective-permute-start | bytes 786440 | tf_op jit(solution)/shard_map/ppermute | solution.py:247
  10.4 1.7 %collective-permute-start.2 = (bf16[32,4096]{1,0:T(8,128)(2,1)S(1)}, bf16[32,4096]{1,0:T(8,128)(2,1)S(1)}, u32[]{:S(2)}, u32[]{:S(2)}) collective-permute-start(bf16[32,4096]{1,0:T(8,128)(2,1)S(1)} %query_grads.2.refs_0_), channel_id=1, source_target_pairs={{0,12},{1,13},{2,14},{3,15},{4,0},{5,1},{6,2},{7,3},{8,4},{9,5},{1... | collective-permute-start | bytes 786440 | tf_op jit(solution)/shard_map/ppermute | solution.py:247
  12.1 2.6 %query_grads.3.refs_0_ = bf16[32,4096]{1,0:T(8,128)(2,1)S(1)} custom-call(s32[64]{0:T(128)} %lengths_hbm.3, bf16[64,1,64,256]{3,2,1,0:T(8,128)(2,1)} %acts_hbm.3, bf16[64,1,64,256]{3,2,1,0:T(8,128)(2,1)} %grads_hbm.3), custom_call_target="tpu_custom_call" | custom-call | tf_op jit(solution)/shard_map/query_grads/pallas_call | solution.py:81
  15.2 2.9 %collective-permute-start.5 = (bf16[32,4096]{1,0:T(8,128)(2,1)S(1)}, bf16[32,4096]{1,0:T(8,128)(2,1)S(1)}, u32[]{:S(2)}, u32[]{:S(2)}) collective-permute-start(bf16[32,4096]{1,0:T(8,128)(2,1)S(1)} %fence.5.refs_0_), channel_id=1, source_target_pairs={{0,12},{1,13},{2,14},{3,15},{4,0},{5,1},{6,2},{7,3},{8,4},{9,5},{1... | collective-permute-start | bytes 786440 | tf_op jit(solution)/shard_map/ppermute | solution.py:247
  18.1 3.5 %collective-permute-done.refs_0_ = bf16[32,4096]{1,0:T(8,128)(2,1)S(1)} collective-permute-done((bf16[32,4096]{1,0:T(8,128)(2,1)S(1)}, bf16[32,4096]{1,0:T(8,128)(2,1)S(1)}, u32[]{:S(2)}, u32[]{:S(2)}) %collective-permute-start) | collective-permute-done | bytes 262176 | tf_op jit(solution)/shard_map/ppermute | solution.py:247
  21.6 2.6 %collective-permute-done.4.refs_3_.refs_1_ = bf16[32,4096]{1,0:T(8,128)(2,1)S(1)} collective-permute-done((bf16[32,4096]{1,0:T(8,128)(2,1)S(1)}, bf16[32,4096]{1,0:T(8,128)(2,1)S(1)}, u32[]{:S(2)}, u32[]{:S(2)}) %collective-permute-start.4) | collective-permute-done | bytes 262176 | tf_op jit(solution)/shard_map/ppermute | solution.py:247
  24.2 2.9 %collective-permute-start.8 = (bf16[32,4096]{1,0:T(8,128)(2,1)S(1)}, bf16[32,4096]{1,0:T(8,128)(2,1)S(1)}, u32[]{:S(2)}, u32[]{:S(2)}) collective-permute-start(bf16[32,4096]{1,0:T(8,128)(2,1)S(1)} %get-tuple-element.32.refs_4_), channel_id=1, source_target_pairs={{0,12},{1,13},{2,14},{3,15},{4,0},{5,1},{6,2},{7,3},{8,4},{9,5},{1... | collective-permute-start | bytes 786440 | tf_op jit(solution)/shard_map/ppermute | solution.py:247
  27.2 3.1 %collective-permute-start.17 = (bf16[32,4096]{1,0:T(8,128)(2,1)S(1)}, bf16[32,4096]{1,0:T(8,128)(2,1)S(1)}, u32[]{:S(2)}, u32[]{:S(2)}) collective-permute-start(bf16[32,4096]{1,0:T(8,128)(2,1)S(1)} %fence.5.refs_0_), channel_id=1, source_target_pairs={{0,2},{1,3},{2,0},{3,1},{4,6},{5,7},{6,4},{7,5},{8,10},{9,11},{10,... | collective-permute-start | bytes 786440 | tf_op jit(solution)/shard_map/ppermute | solution.py:247
  31.6 3.7 %collective-permute-start.9 = (bf16[32,4096]{1,0:T(8,128)(2,1)S(1)}, bf16[32,4096]{1,0:T(8,128)(2,1)S(1)}, u32[]{:S(2)}, u32[]{:S(2)}) collective-permute-start(bf16[32,4096]{1,0:T(8,128)(2,1)S(1)} %collective-permute-done.8.refs_6_.refs_2_), channel_id=1, source_target_pairs={{0,12},{1,13},{2,14},{3,15},{4,0},{5,1},{6,2},{7,3},{8,4},{9,5},{1... | collective-permute-start | bytes 786440 | tf_op jit(solution)/shard_map/ppermute | solution.py:247
  35.3 8.0 %collective-permute-done.17.refs_0_ = bf16[32,4096]{1,0:T(8,128)(2,1)S(1)} collective-permute-done((bf16[32,4096]{1,0:T(8,128)(2,1)S(1)}, bf16[32,4096]{1,0:T(8,128)(2,1)S(1)}, u32[]{:S(2)}, u32[]{:S(2)}) %collective-permute-start.17) | collective-permute-done | bytes 262176 | tf_op jit(solution)/shard_map/ppermute | solution.py:247
  43.4 0.9 %collective-permute-start.20 = (bf16[32,4096]{1,0:T(8,128)(2,1)S(1)}, bf16[32,4096]{1,0:T(8,128)(2,1)S(1)}, u32[]{:S(2)}, u32[]{:S(2)}) collective-permute-start(bf16[32,4096]{1,0:T(8,128)(2,1)S(1)} %get-tuple-element.42.refs_4_), channel_id=1, source_target_pairs={{0,12},{1,13},{2,14},{3,15},{4,0},{5,1},{6,2},{7,3},{8,4},{9,5},{1... | collective-permute-start | bytes 786440 | tf_op jit(solution)/shard_map/ppermute | solution.py:247
  44.3 1.1 %collective-permute-start.19 = (bf16[32,4096]{1,0:T(8,128)(2,1)S(1)}, bf16[32,4096]{1,0:T(8,128)(2,1)S(1)}, u32[]{:S(2)}, u32[]{:S(2)}) collective-permute-start(bf16[32,4096]{1,0:T(8,128)(2,1)S(1)} %get-tuple-element.42.refs_4_), channel_id=1, source_target_pairs={{0,4},{1,5},{2,6},{3,7},{4,8},{5,9},{6,10},{7,11},{8,12},{9,13},{1... | collective-permute-start | bytes 786440 | tf_op jit(solution)/shard_map/ppermute | solution.py:247
  45.5 5.5 %partial_scores.2 = (bf16[128,768]{1,0:T(8,128)(2,1)S(1)}, bf16[128,768]{1,0:T(8,128)(2,1)S(1)}, bf16[128,768]{1,0:T(8,128)(2,1)S(1)}, bf16[128,768]{1,0:T(8,128)(2,1)S(1)}) custom-call(bf16[32,4096]{1,0:T(8,128)(2,1)S(1)} %query_grads.2.refs_0_, bf16[32,4096]{1,0:T(8,128)(2,1)S(1)} %get-tuple-element.30.refs_1_, ...), custom_call_target="tpu_custom_call" | custom-call | flops 1 | bytes 1 | tf_op jit(solution)/shard_map/partial_scores/pallas_call | solution.py:148
  51.0 3.3 %collective-permute-start.21 = (bf16[32,4096]{1,0:T(8,128)(2,1)S(1)}, bf16[32,4096]{1,0:T(8,128)(2,1)S(1)}, u32[]{:S(2)}, u32[]{:S(2)}) collective-permute-start(bf16[32,4096]{1,0:T(8,128)(2,1)S(1)} %fence.8.refs_6_), channel_id=1, source_target_pairs={{0,12},{1,13},{2,14},{3,15},{4,0},{5,1},{6,2},{7,3},{8,4},{9,5},{1... | collective-permute-start | bytes 786440 | tf_op jit(solution)/shard_map/ppermute | solution.py:247
  54.3 2.7 %collective-permute-start.10 = (bf16[128,768]{1,0:T(8,128)(2,1)S(1)}, bf16[128,768]{1,0:T(8,128)(2,1)S(1)}, u32[]{:S(2)}, u32[]{:S(2)}) collective-permute-start(bf16[128,768]{1,0:T(8,128)(2,1)S(1)} %get-tuple-element.33), channel_id=1, source_target_pairs={{0,48},{1,17},{2,50},{3,19},{4,52},{5,21},{6,54},{7,23},{8,56},{9,... | collective-permute-start | bytes 589832 | tf_op jit(solution)/shard_map/ppermute | solution.py:317
  57.0 0.8 collective-permute-start.12
  58.2 5.4 %partial_scores.3 = (bf16[128,768]{1,0:T(8,128)(2,1)S(1)}, bf16[128,768]{1,0:T(8,128)(2,1)S(1)}, bf16[128,768]{1,0:T(8,128)(2,1)S(1)}, bf16[128,768]{1,0:T(8,128)(2,1)S(1)}) custom-call(bf16[32,4096]{1,0:T(8,128)(2,1)S(1)} %fence.5.refs_0_, bf16[32,4096]{1,0:T(8,128)(2,1)S(1)} %get-tuple-element.41.refs_1_, ...), custom_call_target="tpu_custom_call" | custom-call | flops 1 | bytes 1 | tf_op jit(solution)/shard_map/partial_scores/pallas_call | solution.py:148
  63.7 1.4 %collective-permute-done.12.a_ref.refs_6_ = bf16[128,768]{1,0:T(8,128)(2,1)S(1)} collective-permute-done((bf16[128,768]{1,0:T(8,128)(2,1)S(1)}, bf16[128,768]{1,0:T(8,128)(2,1)S(1)}, u32[]{:S(2)}, u32[]{:S(2)}) %collective-permute-start.12) | collective-permute-done | bytes 196640 | tf_op jit(solution)/shard_map/ppermute | solution.py:317
  65.1 1.3 %collective-permute-start.22 = (bf16[128,768]{1,0:T(8,128)(2,1)S(1)}, bf16[128,768]{1,0:T(8,128)(2,1)S(1)}, u32[]{:S(2)}, u32[]{:S(2)}) collective-permute-start(bf16[128,768]{1,0:T(8,128)(2,1)S(1)} %get-tuple-element.47), channel_id=1, source_target_pairs={{0,48},{1,17},{2,50},{3,19},{4,52},{5,21},{6,54},{7,23},{8,56},{9,... | collective-permute-start | bytes 589832 | tf_op jit(solution)/shard_map/ppermute | solution.py:317
  67.2 3.6 %collective-permute-start.23 = (bf16[128,768]{1,0:T(8,128)(2,1)S(1)}, bf16[128,768]{1,0:T(8,128)(2,1)S(1)}, u32[]{:S(2)}, u32[]{:S(2)}) collective-permute-start(bf16[128,768]{1,0:T(8,128)(2,1)S(1)} %get-tuple-element.48), channel_id=1, source_target_pairs={{0,1},{1,49},{2,3},{3,51},{4,5},{5,53},{6,7},{7,55},{8,9},{9,57},{... | collective-permute-start | bytes 589832 | tf_op jit(solution)/shard_map/ppermute | solution.py:317
  73.0 1.0 %collective-permute-start.14 = (bf16[32,768]{1,0:T(8,128)(2,1)S(1)}, bf16[32,768]{1,0:T(8,128)(2,1)S(1)}, u32[]{:S(2)}, u32[]{:S(2)}) collective-permute-start(bf16[32,768]{1,0:T(8,128)(2,1)S(1)} %get-tuple-element.38), channel_id=1, source_target_pairs={{0,64},{16,80},{32,96},{48,112},{64,128},{80,144},{96,160},{112,17... | collective-permute-start | bytes 147464 | tf_op jit(solution)/shard_map/ppermute | solution.py:348
  74.0 0.9 collective-permute-start.15
  74.9 1.5 %collective-permute-done.23.c_ref = bf16[128,768]{1,0:T(8,128)(2,1)S(1)} collective-permute-done((bf16[128,768]{1,0:T(8,128)(2,1)S(1)}, bf16[128,768]{1,0:T(8,128)(2,1)S(1)}, u32[]{:S(2)}, u32[]{:S(2)}) %collective-permute-start.23) | collective-permute-done | bytes 196640 | tf_op jit(solution)/shard_map/ppermute | solution.py:317
  76.9 1.2 %collective-permute-done.24.a_ref = bf16[128,768]{1,0:T(8,128)(2,1)S(1)} collective-permute-done((bf16[128,768]{1,0:T(8,128)(2,1)S(1)}, bf16[128,768]{1,0:T(8,128)(2,1)S(1)}, u32[]{:S(2)}, u32[]{:S(2)}) %collective-permute-start.24) | collective-permute-done | bytes 196640 | tf_op jit(solution)/shard_map/ppermute | solution.py:317
  78.2 1.0 %collective-permute-start.26 = (bf16[32,768]{1,0:T(8,128)(2,1)S(1)}, bf16[32,768]{1,0:T(8,128)(2,1)S(1)}, u32[]{:S(2)}, u32[]{:S(2)}) collective-permute-start(bf16[32,768]{1,0:T(8,128)(2,1)S(1)} %get-tuple-element.52), channel_id=1, source_target_pairs={{0,64},{16,80},{32,96},{48,112},{64,128},{80,144},{96,160},{112,17... | collective-permute-start | bytes 147464 | tf_op jit(solution)/shard_map/ppermute | solution.py:348
  79.3 2.0 %collective-permute-start.27 = (bf16[32,768]{1,0:T(8,128)(2,1)S(1)}, bf16[32,768]{1,0:T(8,128)(2,1)S(1)}, u32[]{:S(2)}, u32[]{:S(2)}) collective-permute-start(bf16[32,768]{1,0:T(8,128)(2,1)S(1)} %get-tuple-element.53), channel_id=1, source_target_pairs={{0,128},{16,144},{32,160},{48,176},{64,192},{80,208},{96,224},{112... | collective-permute-start | bytes 147464 | tf_op jit(solution)/shard_map/ppermute | solution.py:348
  81.7 1.1 %collective-permute-done.26.refs_5_ = bf16[32,768]{1,0:T(8,128)(2,1)S(1)} collective-permute-done((bf16[32,768]{1,0:T(8,128)(2,1)S(1)}, bf16[32,768]{1,0:T(8,128)(2,1)S(1)}, u32[]{:S(2)}, u32[]{:S(2)}) %collective-permute-start.26) | collective-permute-done | bytes 49184 | tf_op jit(solution)/shard_map/ppermute | solution.py:348
  82.8 2.0 %collective-permute-done.27.refs_6_ = bf16[32,768]{1,0:T(8,128)(2,1)S(1)} collective-permute-done((bf16[32,768]{1,0:T(8,128)(2,1)S(1)}, bf16[32,768]{1,0:T(8,128)(2,1)S(1)}, u32[]{:S(2)}, u32[]{:S(2)}) %collective-permute-start.27) | collective-permute-done | bytes 49184 | tf_op jit(solution)/shard_map/ppermute | solution.py:348
  84.9 2.1 %collective-permute-done.28.refs_7_ = bf16[32,768]{1,0:T(8,128)(2,1)S(1)} collective-permute-done((bf16[32,768]{1,0:T(8,128)(2,1)S(1)}, bf16[32,768]{1,0:T(8,128)(2,1)S(1)}, u32[]{:S(2)}, u32[]{:S(2)}) %collective-permute-start.28) | collective-permute-done | bytes 49184 | tf_op jit(solution)/shard_map/ppermute | solution.py:348
  86.9 1.1 %final_sum.1 = f32[64,768]{1,0:T(8,128)} custom-call(f32[32,768]{1,0:T(8,128)S(1)} %get-tuple-element.37.refs_0_, bf16[32,768]{1,0:T(8,128)(2,1)S(1)} %collective-permute-done.14.refs_1_, bf16[32,768]{1,0:T(8,128)(2,1)S(1)} %collective-permute-done.15.refs_2_, bf16[32,768]{1,0:T(8,128)(2,1)S(1)} %collective-permute-done.16.refs_3_, ...), custom_call_target="tpu_custom_call" | custom-call | tf_op jit(solution)/shard_map/final_sum/pallas_call | solution.py:214
  (48 shorter events, 6.2 us)
Async XLA Ops:
  0.0 14.8 %collective-permute-start.3 = (bf16[768,4096]{1,0:T(8,128)(2,1)}, bf16[768,4096]{1,0:T(8,128)(2,1)S(1)}, u32[]{:S(2)}, u32[]{:S(2)}) collective-permute-start(bf16[768,4096]{1,0:T(8,128)(2,1)} %bitcast.1), channel_id=1, source_target_pairs={{0,1},{1,0},{2,3},{3,2},{4,5},{5,4},{6,7},{7,6},{8,9},{9,8},{10,11... | collective-permute-start | bytes 18874376 | tf_op jit(solution)/shard_map/ppermute | solution.py:332
  2.5 19.1 %collective-permute-start = (bf16[32,4096]{1,0:T(8,128)(2,1)S(1)}, bf16[32,4096]{1,0:T(8,128)(2,1)S(1)}, u32[]{:S(2)}, u32[]{:S(2)}) collective-permute-start(bf16[32,4096]{1,0:T(8,128)(2,1)S(1)} %query_grads.2.refs_0_), channel_id=1, source_target_pairs={{0,2},{1,3},{2,0},{3,1},{4,6},{5,7},{6,4},{7,5},{8,10},{9,11},{10,... | collective-permute-start | bytes 786440 | tf_op jit(solution)/shard_map/ppermute | solution.py:247
  8.9 12.7 %collective-permute-start.1 = (bf16[32,4096]{1,0:T(8,128)(2,1)S(1)}, bf16[32,4096]{1,0:T(8,128)(2,1)S(1)}, u32[]{:S(2)}, u32[]{:S(2)}) collective-permute-start(bf16[32,4096]{1,0:T(8,128)(2,1)S(1)} %query_grads.2.refs_0_), channel_id=1, source_target_pairs={{0,4},{1,5},{2,6},{3,7},{4,8},{5,9},{6,10},{7,11},{8,12},{9,13},{1... | collective-permute-start | bytes 786440 | tf_op jit(solution)/shard_map/ppermute | solution.py:247
  10.4 11.1 %collective-permute-start.2 = (bf16[32,4096]{1,0:T(8,128)(2,1)S(1)}, bf16[32,4096]{1,0:T(8,128)(2,1)S(1)}, u32[]{:S(2)}, u32[]{:S(2)}) collective-permute-start(bf16[32,4096]{1,0:T(8,128)(2,1)S(1)} %query_grads.2.refs_0_), channel_id=1, source_target_pairs={{0,12},{1,13},{2,14},{3,15},{4,0},{5,1},{6,2},{7,3},{8,4},{9,5},{1... | collective-permute-start | bytes 786440 | tf_op jit(solution)/shard_map/ppermute | solution.py:247
  12.1 33.4 %slice-start = ((s8[6291456]{0:T(1024)(128)(4,1)}), s8[4194304]{0:T(1024)(128)(4,1)S(1)}, s32[]{:S(2)}) async-start(s8[6291456]{0:T(1024)(128)(4,1)} %bitcast.2), calls=%async_computation | async-start | bytes 8388608
  14.7 30.7 %slice-start.1 = ((s8[6291456]{0:T(1024)(128)(4,1)}), s8[2097152]{0:T(1024)(128)(4,1)S(1)}, s32[]{:S(2)}) async-start(s8[6291456]{0:T(1024)(128)(4,1)} %bitcast.2), calls=%async_computation.1 | async-start | bytes 4194304
  14.8 9.4 %collective-permute-start.4 = (bf16[32,4096]{1,0:T(8,128)(2,1)S(1)}, bf16[32,4096]{1,0:T(8,128)(2,1)S(1)}, u32[]{:S(2)}, u32[]{:S(2)}) collective-permute-start(bf16[32,4096]{1,0:T(8,128)(2,1)S(1)} %fence.5.refs_0_), channel_id=1, source_target_pairs={{0,4},{1,5},{2,6},{3,7},{4,8},{5,9},{6,10},{7,11},{8,12},{9,13},{1... | collective-permute-start | bytes 786440 | tf_op jit(solution)/shard_map/ppermute | solution.py:247
  15.2 9.0 %collective-permute-start.5 = (bf16[32,4096]{1,0:T(8,128)(2,1)S(1)}, bf16[32,4096]{1,0:T(8,128)(2,1)S(1)}, u32[]{:S(2)}, u32[]{:S(2)}) collective-permute-start(bf16[32,4096]{1,0:T(8,128)(2,1)S(1)} %fence.5.refs_0_), channel_id=1, source_target_pairs={{0,12},{1,13},{2,14},{3,15},{4,0},{5,1},{6,2},{7,3},{8,4},{9,5},{1... | collective-permute-start | bytes 786440 | tf_op jit(solution)/shard_map/ppermute | solution.py:247
  24.2 7.4 %collective-permute-start.8 = (bf16[32,4096]{1,0:T(8,128)(2,1)S(1)}, bf16[32,4096]{1,0:T(8,128)(2,1)S(1)}, u32[]{:S(2)}, u32[]{:S(2)}) collective-permute-start(bf16[32,4096]{1,0:T(8,128)(2,1)S(1)} %get-tuple-element.32.refs_4_), channel_id=1, source_target_pairs={{0,12},{1,13},{2,14},{3,15},{4,0},{5,1},{6,2},{7,3},{8,4},{9,5},{1... | collective-permute-start | bytes 786440 | tf_op jit(solution)/shard_map/ppermute | solution.py:247
  27.2 16.2 %collective-permute-start.17 = (bf16[32,4096]{1,0:T(8,128)(2,1)S(1)}, bf16[32,4096]{1,0:T(8,128)(2,1)S(1)}, u32[]{:S(2)}, u32[]{:S(2)}) collective-permute-start(bf16[32,4096]{1,0:T(8,128)(2,1)S(1)} %fence.5.refs_0_), channel_id=1, source_target_pairs={{0,2},{1,3},{2,0},{3,1},{4,6},{5,7},{6,4},{7,5},{8,10},{9,11},{10,... | collective-permute-start | bytes 786440 | tf_op jit(solution)/shard_map/ppermute | solution.py:247
  30.3 13.1 %collective-permute-start.7 = (bf16[32,4096]{1,0:T(8,128)(2,1)S(1)}, bf16[32,4096]{1,0:T(8,128)(2,1)S(1)}, u32[]{:S(2)}, u32[]{:S(2)}) collective-permute-start(bf16[32,4096]{1,0:T(8,128)(2,1)S(1)} %get-tuple-element.32.refs_4_), channel_id=1, source_target_pairs={{0,4},{1,5},{2,6},{3,7},{4,8},{5,9},{6,10},{7,11},{8,12},{9,13},{1... | collective-permute-start | bytes 786440 | tf_op jit(solution)/shard_map/ppermute | solution.py:247
  30.3 15.2 %collective-permute-start.6 = (bf16[32,4096]{1,0:T(8,128)(2,1)S(1)}, bf16[32,4096]{1,0:T(8,128)(2,1)S(1)}, u32[]{:S(2)}, u32[]{:S(2)}) collective-permute-start(bf16[32,4096]{1,0:T(8,128)(2,1)S(1)} %get-tuple-element.30.refs_1_), channel_id=1, source_target_pairs={{0,4},{1,5},{2,6},{3,7},{4,8},{5,9},{6,10},{7,11},{8,12},{9,13},{1... | collective-permute-start | bytes 786440 | tf_op jit(solution)/shard_map/ppermute | solution.py:247
  31.6 13.8 %collective-permute-start.9 = (bf16[32,4096]{1,0:T(8,128)(2,1)S(1)}, bf16[32,4096]{1,0:T(8,128)(2,1)S(1)}, u32[]{:S(2)}, u32[]{:S(2)}) collective-permute-start(bf16[32,4096]{1,0:T(8,128)(2,1)S(1)} %collective-permute-done.8.refs_6_.refs_2_), channel_id=1, source_target_pairs={{0,12},{1,13},{2,14},{3,15},{4,0},{5,1},{6,2},{7,3},{8,4},{9,5},{1... | collective-permute-start | bytes 786440 | tf_op jit(solution)/shard_map/ppermute | solution.py:247
  43.4 7.6 %collective-permute-start.20 = (bf16[32,4096]{1,0:T(8,128)(2,1)S(1)}, bf16[32,4096]{1,0:T(8,128)(2,1)S(1)}, u32[]{:S(2)}, u32[]{:S(2)}) collective-permute-start(bf16[32,4096]{1,0:T(8,128)(2,1)S(1)} %get-tuple-element.42.refs_4_), channel_id=1, source_target_pairs={{0,12},{1,13},{2,14},{3,15},{4,0},{5,1},{6,2},{7,3},{8,4},{9,5},{1... | collective-permute-start | bytes 786440 | tf_op jit(solution)/shard_map/ppermute | solution.py:247
  44.3 12.7 %collective-permute-start.19 = (bf16[32,4096]{1,0:T(8,128)(2,1)S(1)}, bf16[32,4096]{1,0:T(8,128)(2,1)S(1)}, u32[]{:S(2)}, u32[]{:S(2)}) collective-permute-start(bf16[32,4096]{1,0:T(8,128)(2,1)S(1)} %get-tuple-element.42.refs_4_), channel_id=1, source_target_pairs={{0,4},{1,5},{2,6},{3,7},{4,8},{5,9},{6,10},{7,11},{8,12},{9,13},{1... | collective-permute-start | bytes 786440 | tf_op jit(solution)/shard_map/ppermute | solution.py:247
  45.4 12.7 %collective-permute-start.18 = (bf16[32,4096]{1,0:T(8,128)(2,1)S(1)}, bf16[32,4096]{1,0:T(8,128)(2,1)S(1)}, u32[]{:S(2)}, u32[]{:S(2)}) collective-permute-start(bf16[32,4096]{1,0:T(8,128)(2,1)S(1)} %get-tuple-element.41.refs_1_), channel_id=1, source_target_pairs={{0,4},{1,5},{2,6},{3,7},{4,8},{5,9},{6,10},{7,11},{8,12},{9,13},{1... | collective-permute-start | bytes 786440 | tf_op jit(solution)/shard_map/ppermute | solution.py:247
  51.0 7.2 %collective-permute-start.21 = (bf16[32,4096]{1,0:T(8,128)(2,1)S(1)}, bf16[32,4096]{1,0:T(8,128)(2,1)S(1)}, u32[]{:S(2)}, u32[]{:S(2)}) collective-permute-start(bf16[32,4096]{1,0:T(8,128)(2,1)S(1)} %fence.8.refs_6_), channel_id=1, source_target_pairs={{0,12},{1,13},{2,14},{3,15},{4,0},{5,1},{6,2},{7,3},{8,4},{9,5},{1... | collective-permute-start | bytes 786440 | tf_op jit(solution)/shard_map/ppermute | solution.py:247
  54.3 9.4 %collective-permute-start.10 = (bf16[128,768]{1,0:T(8,128)(2,1)S(1)}, bf16[128,768]{1,0:T(8,128)(2,1)S(1)}, u32[]{:S(2)}, u32[]{:S(2)}) collective-permute-start(bf16[128,768]{1,0:T(8,128)(2,1)S(1)} %get-tuple-element.33), channel_id=1, source_target_pairs={{0,48},{1,17},{2,50},{3,19},{4,52},{5,21},{6,54},{7,23},{8,56},{9,... | collective-permute-start | bytes 589832 | tf_op jit(solution)/shard_map/ppermute | solution.py:317
  57.0 6.7 %collective-permute-start.11 = (bf16[128,768]{1,0:T(8,128)(2,1)S(1)}, bf16[128,768]{1,0:T(8,128)(2,1)S(1)}, u32[]{:S(2)}, u32[]{:S(2)}) collective-permute-start(bf16[128,768]{1,0:T(8,128)(2,1)S(1)} %get-tuple-element.34), channel_id=1, source_target_pairs={{0,1},{1,49},{2,3},{3,51},{4,5},{5,53},{6,7},{7,55},{8,9},{9,57},{... | collective-permute-start | bytes 589832 | tf_op jit(solution)/shard_map/ppermute | solution.py:317
  57.0 8.2 %collective-permute-start.12 = (bf16[128,768]{1,0:T(8,128)(2,1)S(1)}, bf16[128,768]{1,0:T(8,128)(2,1)S(1)}, u32[]{:S(2)}, u32[]{:S(2)}) collective-permute-start(bf16[128,768]{1,0:T(8,128)(2,1)S(1)} %get-tuple-element.35), channel_id=1, source_target_pairs={{0,32},{1,16},{2,34},{3,18},{4,36},{5,20},{6,38},{7,22},{8,40},{9,... | collective-permute-start | bytes 589832 | tf_op jit(solution)/shard_map/ppermute | solution.py:317
  63.7 17.6 %copy-start = (s32[768]{0:T(1024)S(1)}, s32[768]{0:T(1024)}, u32[]{:S(2)}) copy-start(s32[768]{0:T(1024)} %param.9) | copy-start | bytes 9220
  65.1 6.9 %collective-permute-start.22 = (bf16[128,768]{1,0:T(8,128)(2,1)S(1)}, bf16[128,768]{1,0:T(8,128)(2,1)S(1)}, u32[]{:S(2)}, u32[]{:S(2)}) collective-permute-start(bf16[128,768]{1,0:T(8,128)(2,1)S(1)} %get-tuple-element.47), channel_id=1, source_target_pairs={{0,48},{1,17},{2,50},{3,19},{4,52},{5,21},{6,54},{7,23},{8,56},{9,... | collective-permute-start | bytes 589832 | tf_op jit(solution)/shard_map/ppermute | solution.py:317
  66.6 6.2 %collective-permute-start.13 = (bf16[128,768]{1,0:T(8,128)(2,1)S(1)}, bf16[128,768]{1,0:T(8,128)(2,1)S(1)}, u32[]{:S(2)}, u32[]{:S(2)}) collective-permute-start(bf16[128,768]{1,0:T(8,128)(2,1)S(1)} %join.2), channel_id=1, source_target_pairs={{1,48},{3,50},{5,52},{7,54},{9,56},{11,58},{13,60},{15,62},{16,1},... | collective-permute-start | bytes 589832 | tf_op jit(solution)/shard_map/ppermute | solution.py:317
  67.2 9.2 %collective-permute-start.23 = (bf16[128,768]{1,0:T(8,128)(2,1)S(1)}, bf16[128,768]{1,0:T(8,128)(2,1)S(1)}, u32[]{:S(2)}, u32[]{:S(2)}) collective-permute-start(bf16[128,768]{1,0:T(8,128)(2,1)S(1)} %get-tuple-element.48), channel_id=1, source_target_pairs={{0,1},{1,49},{2,3},{3,51},{4,5},{5,53},{6,7},{7,55},{8,9},{9,57},{... | collective-permute-start | bytes 589832 | tf_op jit(solution)/shard_map/ppermute | solution.py:317
  70.8 7.3 %collective-permute-start.24 = (bf16[128,768]{1,0:T(8,128)(2,1)S(1)}, bf16[128,768]{1,0:T(8,128)(2,1)S(1)}, u32[]{:S(2)}, u32[]{:S(2)}) collective-permute-start(bf16[128,768]{1,0:T(8,128)(2,1)S(1)} %get-tuple-element.49), channel_id=1, source_target_pairs={{0,32},{1,16},{2,34},{3,18},{4,36},{5,20},{6,38},{7,22},{8,40},{9,... | collective-permute-start | bytes 589832 | tf_op jit(solution)/shard_map/ppermute | solution.py:317
  72.1 6.0 %collective-permute-start.25 = (bf16[128,768]{1,0:T(8,128)(2,1)S(1)}, bf16[128,768]{1,0:T(8,128)(2,1)S(1)}, u32[]{:S(2)}, u32[]{:S(2)}) collective-permute-start(bf16[128,768]{1,0:T(8,128)(2,1)S(1)} %join.3), channel_id=1, source_target_pairs={{1,48},{3,50},{5,52},{7,54},{9,56},{11,58},{13,60},{15,62},{16,1},... | collective-permute-start | bytes 589832 | tf_op jit(solution)/shard_map/ppermute | solution.py:317
  73.0 8.3 %collective-permute-start.14 = (bf16[32,768]{1,0:T(8,128)(2,1)S(1)}, bf16[32,768]{1,0:T(8,128)(2,1)S(1)}, u32[]{:S(2)}, u32[]{:S(2)}) collective-permute-start(bf16[32,768]{1,0:T(8,128)(2,1)S(1)} %get-tuple-element.38), channel_id=1, source_target_pairs={{0,64},{16,80},{32,96},{48,112},{64,128},{80,144},{96,160},{112,17... | collective-permute-start | bytes 147464 | tf_op jit(solution)/shard_map/ppermute | solution.py:348
  74.0 7.7 %collective-permute-start.15 = (bf16[32,768]{1,0:T(8,128)(2,1)S(1)}, bf16[32,768]{1,0:T(8,128)(2,1)S(1)}, u32[]{:S(2)}, u32[]{:S(2)}) collective-permute-start(bf16[32,768]{1,0:T(8,128)(2,1)S(1)} %get-tuple-element.39), channel_id=1, source_target_pairs={{0,128},{16,144},{32,160},{48,176},{64,192},{80,208},{96,224},{112... | collective-permute-start | bytes 147464 | tf_op jit(solution)/shard_map/ppermute | solution.py:348
  76.4 5.3 %collective-permute-start.16 = (bf16[32,768]{1,0:T(8,128)(2,1)S(1)}, bf16[32,768]{1,0:T(8,128)(2,1)S(1)}, u32[]{:S(2)}, u32[]{:S(2)}) collective-permute-start(bf16[32,768]{1,0:T(8,128)(2,1)S(1)} %get-tuple-element.40), channel_id=1, source_target_pairs={{0,192},{16,208},{32,224},{48,240},{64,0},{80,16},{96,32},{112,48}... | collective-permute-start | bytes 147464 | tf_op jit(solution)/shard_map/ppermute | solution.py:348
  78.2 4.6 %collective-permute-start.26 = (bf16[32,768]{1,0:T(8,128)(2,1)S(1)}, bf16[32,768]{1,0:T(8,128)(2,1)S(1)}, u32[]{:S(2)}, u32[]{:S(2)}) collective-permute-start(bf16[32,768]{1,0:T(8,128)(2,1)S(1)} %get-tuple-element.52), channel_id=1, source_target_pairs={{0,64},{16,80},{32,96},{48,112},{64,128},{80,144},{96,160},{112,17... | collective-permute-start | bytes 147464 | tf_op jit(solution)/shard_map/ppermute | solution.py:348
  79.3 5.6 %collective-permute-start.27 = (bf16[32,768]{1,0:T(8,128)(2,1)S(1)}, bf16[32,768]{1,0:T(8,128)(2,1)S(1)}, u32[]{:S(2)}, u32[]{:S(2)}) collective-permute-start(bf16[32,768]{1,0:T(8,128)(2,1)S(1)} %get-tuple-element.53), channel_id=1, source_target_pairs={{0,128},{16,144},{32,160},{48,176},{64,192},{80,208},{96,224},{112... | collective-permute-start | bytes 147464 | tf_op jit(solution)/shard_map/ppermute | solution.py:348
  81.2 5.7 %collective-permute-start.28 = (bf16[32,768]{1,0:T(8,128)(2,1)S(1)}, bf16[32,768]{1,0:T(8,128)(2,1)S(1)}, u32[]{:S(2)}, u32[]{:S(2)}) collective-permute-start(bf16[32,768]{1,0:T(8,128)(2,1)S(1)} %get-tuple-element.54), channel_id=1, source_target_pairs={{0,192},{16,208},{32,224},{48,240},{64,0},{80,16},{96,32},{112,48}... | collective-permute-start | bytes 147464 | tf_op jit(solution)/shard_map/ppermute | solution.py:348

commit v9 on v8

--- a/solution.py
+++ b/solution.py
@@ -282,8 +282,8 @@
     (b,) = after((b,), other)
     far_b = beyond(b)
     b_below, b_above = up(b), down(b)
-    far_a, a_below, a_above = after((far_a, a_below, a_above), b_below, b_above)
     a_opposite = up(a_below)
+    far_a, a_above = after((far_a, a_above), a_opposite, b_above)
     far_a_above, far_a_below = down(far_a), up(far_a)
     far_a_opposite = down(far_a_above)
     far_b, b_below = after((far_b, b_below), far_a_above, far_a_below)

time: 89.6 us -> 91.2 us (1.018)
  starting transfers between devices: 44.1 us -> 46 us
    ppermute x6, starting transfers between devices: 5.36 us -> 6.67 us  [on_device(): lax.ppermute(send, 'store', store_pairs(lambda x, z: (x, z + k)))]
    ppermute x14, starting transfers between devices: 28.5 us -> 29.6 us  [along(): return lax.ppermute(value, 'group', group_pairs(move))]
  transfers between devices with their start and end apart: 29 -> 29, of which waited for: 13 -> 12; matrix products, arithmetic and copies ran while one was open for 0% -> 0% of each run, Pallas kernels for 19% -> 18%
where the time goes in v9:
time: 91.2 us; the launch traced here: 89.7 us
  starting transfers between devices  46 us (50%)
  waiting for transfers between devices  25.5 us (28%)
  Pallas kernels  17.6 us (19%)
    ppermute x14, starting transfers between devices, along(): return lax.ppermute(value, 'group', group_pairs(move))  29.6 us
    ppermute x14, waiting for transfers between devices, along(): return lax.ppermute(value, 'group', group_pairs(move))  15.5 us
    pallas_call x2, Pallas kernels, partial_scores(): pl.pallas_call(score_kernel, out_shape=[jax.ShapeDtypeStruct((4 * ROWS, H...  10.9 us
    ppermute x8, starting transfers between devices, send(): return lax.ppermute(value, ('store', 'group'), all_pairs(move))  9.71 us
    ppermute x6, starting transfers between devices, on_device(): lax.ppermute(send, 'store', store_pairs(lambda x, z: (x, z + k)))  6.67 us
    pallas_call x2, Pallas kernels, query_grads(): pl.pallas_call(functools.partial(grad_kernel, chunk * ROWS), out_shape=ja...  5.13 us
    ppermute x6, waiting for transfers between devices, on_device(): lax.ppermute(send, 'store', store_pairs(lambda x, z: (x, z + k)))  5.04 us
    ppermute x8, waiting for transfers between devices, send(): return lax.ppermute(value, ('store', 'group'), all_pairs(move))  4.98 us
  transfers between devices with their start and end apart: 29, of which 12 were waited for; matrix products, arithmetic and copies ran while one was open for 0% of the time, Pallas kernels for 18%

profile of v9, /device:TPU:32, one launch (start us, length us, event | category | flops | bytes accessed | tf_op | source)
XLA Modules:
  0.0 89.7 jit_solution(7042788661110202147)
XLA Ops:
  0.0 2.5 %query_grads.2.refs_0_ = bf16[32,4096]{1,0:T(8,128)(2,1)S(1)} custom-call(s32[64]{0:T(128)} %lengths_hbm.3, bf16[64,1,64,256]{3,2,1,0:T(8,128)(2,1)} %acts_hbm.3, bf16[64,1,64,256]{3,2,1,0:T(8,128)(2,1)} %grads_hbm.3), custom_call_target="tpu_custom_call" | custom-call | tf_op jit(solution)/shard_map/query_grads/pallas_call | solution.py:81
  2.5 1.6 %collective-permute-start = (bf16[32,4096]{1,0:T(8,128)(2,1)S(1)}, bf16[32,4096]{1,0:T(8,128)(2,1)S(1)}, u32[]{:S(2)}, u32[]{:S(2)}) collective-permute-start(bf16[32,4096]{1,0:T(8,128)(2,1)S(1)} %query_grads.2.refs_0_), channel_id=1, source_target_pairs={{0,4},{1,5},{2,6},{3,7},{4,8},{5,9},{6,10},{7,11},{8,12},{9,13},{1... | collective-permute-start | bytes 786440 | tf_op jit(solution)/shard_map/ppermute | solution.py:247
  4.1 6.3 %collective-permute-start.1 = (bf16[32,4096]{1,0:T(8,128)(2,1)S(1)}, bf16[32,4096]{1,0:T(8,128)(2,1)S(1)}, u32[]{:S(2)}, u32[]{:S(2)}) collective-permute-start(bf16[32,4096]{1,0:T(8,128)(2,1)S(1)} %query_grads.2.refs_0_), channel_id=1, source_target_pairs={{0,2},{1,3},{2,0},{3,1},{4,6},{5,7},{6,4},{7,5},{8,10},{9,11},{10,... | collective-permute-start | bytes 786440 | tf_op jit(solution)/shard_map/ppermute | solution.py:247
  10.4 1.7 %collective-permute-start.2 = (bf16[32,4096]{1,0:T(8,128)(2,1)S(1)}, bf16[32,4096]{1,0:T(8,128)(2,1)S(1)}, u32[]{:S(2)}, u32[]{:S(2)}) collective-permute-start(bf16[32,4096]{1,0:T(8,128)(2,1)S(1)} %query_grads.2.refs_0_), channel_id=1, source_target_pairs={{0,12},{1,13},{2,14},{3,15},{4,0},{5,1},{6,2},{7,3},{8,4},{9,5},{1... | collective-permute-start | bytes 786440 | tf_op jit(solution)/shard_map/ppermute | solution.py:247
  12.1 2.6 %query_grads.3.refs_0_ = bf16[32,4096]{1,0:T(8,128)(2,1)S(1)} custom-call(s32[64]{0:T(128)} %lengths_hbm.3, bf16[64,1,64,256]{3,2,1,0:T(8,128)(2,1)} %acts_hbm.3, bf16[64,1,64,256]{3,2,1,0:T(8,128)(2,1)} %grads_hbm.3), custom_call_target="tpu_custom_call" | custom-call | tf_op jit(solution)/shard_map/query_grads/pallas_call | solution.py:81
  15.2 2.9 %collective-permute-start.5 = (bf16[32,4096]{1,0:T(8,128)(2,1)S(1)}, bf16[32,4096]{1,0:T(8,128)(2,1)S(1)}, u32[]{:S(2)}, u32[]{:S(2)}) collective-permute-start(bf16[32,4096]{1,0:T(8,128)(2,1)S(1)} %fence.5.refs_0_), channel_id=1, source_target_pairs={{0,12},{1,13},{2,14},{3,15},{4,0},{5,1},{6,2},{7,3},{8,4},{9,5},{1... | collective-permute-start | bytes 786440 | tf_op jit(solution)/shard_map/ppermute | solution.py:247
  18.1 4.8 %collective-permute-done.1.refs_0_ = bf16[32,4096]{1,0:T(8,128)(2,1)S(1)} collective-permute-done((bf16[32,4096]{1,0:T(8,128)(2,1)S(1)}, bf16[32,4096]{1,0:T(8,128)(2,1)S(1)}, u32[]{:S(2)}, u32[]{:S(2)}) %collective-permute-start.1) | collective-permute-done | bytes 262176 | tf_op jit(solution)/shard_map/ppermute | solution.py:247
  22.8 1.3 %collective-permute-done.3.refs_2_.refs_3_ = bf16[32,4096]{1,0:T(8,128)(2,1)S(1)} collective-permute-done((bf16[32,4096]{1,0:T(8,128)(2,1)S(1)}, bf16[32,4096]{1,0:T(8,128)(2,1)S(1)}, u32[]{:S(2)}, u32[]{:S(2)}) %collective-permute-start.3) | collective-permute-done | bytes 262176 | tf_op jit(solution)/shard_map/ppermute | solution.py:247
  24.2 3.1 %collective-permute-start.7 = (bf16[32,4096]{1,0:T(8,128)(2,1)S(1)}, bf16[32,4096]{1,0:T(8,128)(2,1)S(1)}, u32[]{:S(2)}, u32[]{:S(2)}) collective-permute-start(bf16[32,4096]{1,0:T(8,128)(2,1)S(1)} %get-tuple-element.30.refs_4_), channel_id=1, source_target_pairs={{0,12},{1,13},{2,14},{3,15},{4,0},{5,1},{6,2},{7,3},{8,4},{9,5},{1... | collective-permute-start | bytes 786440 | tf_op jit(solution)/shard_map/ppermute | solution.py:247
  27.3 3.8 %collective-permute-start.16 = (bf16[32,4096]{1,0:T(8,128)(2,1)S(1)}, bf16[32,4096]{1,0:T(8,128)(2,1)S(1)}, u32[]{:S(2)}, u32[]{:S(2)}) collective-permute-start(bf16[32,4096]{1,0:T(8,128)(2,1)S(1)} %fence.5.refs_0_), channel_id=1, source_target_pairs={{0,2},{1,3},{2,0},{3,1},{4,6},{5,7},{6,4},{7,5},{8,10},{9,11},{10,... | collective-permute-start | bytes 786440 | tf_op jit(solution)/shard_map/ppermute | solution.py:247
  31.1 1.0 %collective-permute-start.6 = (bf16[32,4096]{1,0:T(8,128)(2,1)S(1)}, bf16[32,4096]{1,0:T(8,128)(2,1)S(1)}, u32[]{:S(2)}, u32[]{:S(2)}) collective-permute-start(bf16[32,4096]{1,0:T(8,128)(2,1)S(1)} %get-tuple-element.30.refs_4_), channel_id=1, source_target_pairs={{0,4},{1,5},{2,6},{3,7},{4,8},{5,9},{6,10},{7,11},{8,12},{9,13},{1... | collective-permute-start | bytes 786440 | tf_op jit(solution)/shard_map/ppermute | solution.py:247
  32.1 3.5 %collective-permute-start.8 = (bf16[32,4096]{1,0:T(8,128)(2,1)S(1)}, bf16[32,4096]{1,0:T(8,128)(2,1)S(1)}, u32[]{:S(2)}, u32[]{:S(2)}) collective-permute-start(bf16[32,4096]{1,0:T(8,128)(2,1)S(1)} %collective-permute-done.7.refs_6_.refs_2_), channel_id=1, source_target_pairs={{0,12},{1,13},{2,14},{3,15},{4,0},{5,1},{6,2},{7,3},{8,4},{9,5},{1... | collective-permute-start | bytes 786440 | tf_op jit(solution)/shard_map/ppermute | solution.py:247
  35.6 8.0 %collective-permute-done.16.refs_0_ = bf16[32,4096]{1,0:T(8,128)(2,1)S(1)} collective-permute-done((bf16[32,4096]{1,0:T(8,128)(2,1)S(1)}, bf16[32,4096]{1,0:T(8,128)(2,1)S(1)}, u32[]{:S(2)}, u32[]{:S(2)}) %collective-permute-start.16) | collective-permute-done | bytes 262176 | tf_op jit(solution)/shard_map/ppermute | solution.py:247
  43.6 0.9 collective-permute-done.6.refs_5_.refs_3_
  44.7 1.8 %collective-permute-start.19 = (bf16[32,4096]{1,0:T(8,128)(2,1)S(1)}, bf16[32,4096]{1,0:T(8,128)(2,1)S(1)}, u32[]{:S(2)}, u32[]{:S(2)}) collective-permute-start(bf16[32,4096]{1,0:T(8,128)(2,1)S(1)} %get-tuple-element.40.refs_4_), channel_id=1, source_target_pairs={{0,4},{1,5},{2,6},{3,7},{4,8},{5,9},{6,10},{7,11},{8,12},{9,13},{1... | collective-permute-start | bytes 786440 | tf_op jit(solution)/shard_map/ppermute | solution.py:247
  46.6 5.5 %partial_scores.2 = (bf16[128,768]{1,0:T(8,128)(2,1)S(1)}, bf16[128,768]{1,0:T(8,128)(2,1)S(1)}, bf16[128,768]{1,0:T(8,128)(2,1)S(1)}, bf16[128,768]{1,0:T(8,128)(2,1)S(1)}) custom-call(bf16[32,4096]{1,0:T(8,128)(2,1)S(1)} %query_grads.2.refs_0_, bf16[32,4096]{1,0:T(8,128)(2,1)S(1)} %collective-permute-done.refs_1_, ...), custom_call_target="tpu_custom_call" | custom-call | flops 1 | bytes 1 | tf_op jit(solution)/shard_map/partial_scores/pallas_call | solution.py:148
  52.1 3.3 %collective-permute-start.21 = (bf16[32,4096]{1,0:T(8,128)(2,1)S(1)}, bf16[32,4096]{1,0:T(8,128)(2,1)S(1)}, u32[]{:S(2)}, u32[]{:S(2)}) collective-permute-start(bf16[32,4096]{1,0:T(8,128)(2,1)S(1)} %fence.8.refs_6_), channel_id=1, source_target_pairs={{0,12},{1,13},{2,14},{3,15},{4,0},{5,1},{6,2},{7,3},{8,4},{9,5},{1... | collective-permute-start | bytes 786440 | tf_op jit(solution)/shard_map/ppermute | solution.py:247
  55.4 2.9 %collective-permute-start.11 = (bf16[128,768]{1,0:T(8,128)(2,1)S(1)}, bf16[128,768]{1,0:T(8,128)(2,1)S(1)}, u32[]{:S(2)}, u32[]{:S(2)}) collective-permute-start(bf16[128,768]{1,0:T(8,128)(2,1)S(1)} %get-tuple-element.33), channel_id=1, source_target_pairs={{0,32},{1,16},{2,34},{3,18},{4,36},{5,20},{6,38},{7,22},{8,40},{9,... | collective-permute-start | bytes 589832 | tf_op jit(solution)/shard_map/ppermute | solution.py:317
  59.3 5.4 %partial_scores.3 = (bf16[128,768]{1,0:T(8,128)(2,1)S(1)}, bf16[128,768]{1,0:T(8,128)(2,1)S(1)}, bf16[128,768]{1,0:T(8,128)(2,1)S(1)}, bf16[128,768]{1,0:T(8,128)(2,1)S(1)}) custom-call(bf16[32,4096]{1,0:T(8,128)(2,1)S(1)} %fence.5.refs_0_, bf16[32,4096]{1,0:T(8,128)(2,1)S(1)} %get-tuple-element.39.refs_1_, ...), custom_call_target="tpu_custom_call" | custom-call | flops 1 | bytes 1 | tf_op jit(solution)/shard_map/partial_scores/pallas_call | solution.py:148
  64.7 2.0 %collective-permute-done.9.got_ref.b_ref.refs_4_ = bf16[128,768]{1,0:T(8,128)(2,1)S(1)} collective-permute-done((bf16[128,768]{1,0:T(8,128)(2,1)S(1)}, bf16[128,768]{1,0:T(8,128)(2,1)S(1)}, u32[]{:S(2)}, u32[]{:S(2)}) %collective-permute-start.9) | collective-permute-done | bytes 196640 | tf_op jit(solution)/shard_map/ppermute | solution.py:317
  66.7 0.8 collective-permute-start.22
  68.2 4.1 %collective-permute-start.23 = (bf16[128,768]{1,0:T(8,128)(2,1)S(1)}, bf16[128,768]{1,0:T(8,128)(2,1)S(1)}, u32[]{:S(2)}, u32[]{:S(2)}) collective-permute-start(bf16[128,768]{1,0:T(8,128)(2,1)S(1)} %get-tuple-element.46), channel_id=1, source_target_pairs={{0,1},{1,49},{2,3},{3,51},{4,5},{5,53},{6,7},{7,55},{8,9},{9,57},{... | collective-permute-start | bytes 589832 | tf_op jit(solution)/shard_map/ppermute | solution.py:317
  72.3 1.2 %collective-permute-done.22.got_ref.b_ref = bf16[128,768]{1,0:T(8,128)(2,1)S(1)} collective-permute-done((bf16[128,768]{1,0:T(8,128)(2,1)S(1)}, bf16[128,768]{1,0:T(8,128)(2,1)S(1)}, u32[]{:S(2)}, u32[]{:S(2)}) %collective-permute-start.22) | collective-permute-done | bytes 196640 | tf_op jit(solution)/shard_map/ppermute | solution.py:317
  74.5 1.0 %collective-permute-start.13 = (bf16[32,768]{1,0:T(8,128)(2,1)S(1)}, bf16[32,768]{1,0:T(8,128)(2,1)S(1)}, u32[]{:S(2)}, u32[]{:S(2)}) collective-permute-start(bf16[32,768]{1,0:T(8,128)(2,1)S(1)} %get-tuple-element.36), channel_id=1, source_target_pairs={{0,64},{16,80},{32,96},{48,112},{64,128},{80,144},{96,160},{112,17... | collective-permute-start | bytes 147464 | tf_op jit(solution)/shard_map/ppermute | solution.py:348
  75.5 2.1 %collective-permute-start.14 = (bf16[32,768]{1,0:T(8,128)(2,1)S(1)}, bf16[32,768]{1,0:T(8,128)(2,1)S(1)}, u32[]{:S(2)}, u32[]{:S(2)}) collective-permute-start(bf16[32,768]{1,0:T(8,128)(2,1)S(1)} %get-tuple-element.37), channel_id=1, source_target_pairs={{0,128},{16,144},{32,160},{48,176},{64,192},{80,208},{96,224},{112... | collective-permute-start | bytes 147464 | tf_op jit(solution)/shard_map/ppermute | solution.py:348
  77.8 1.8 %collective-permute-done.24.a_ref = bf16[128,768]{1,0:T(8,128)(2,1)S(1)} collective-permute-done((bf16[128,768]{1,0:T(8,128)(2,1)S(1)}, bf16[128,768]{1,0:T(8,128)(2,1)S(1)}, u32[]{:S(2)}, u32[]{:S(2)}) %collective-permute-start.24) | collective-permute-done | bytes 196640 | tf_op jit(solution)/shard_map/ppermute | solution.py:317
  79.8 1.0 %collective-permute-start.26 = (bf16[32,768]{1,0:T(8,128)(2,1)S(1)}, bf16[32,768]{1,0:T(8,128)(2,1)S(1)}, u32[]{:S(2)}, u32[]{:S(2)}) collective-permute-start(bf16[32,768]{1,0:T(8,128)(2,1)S(1)} %get-tuple-element.50), channel_id=1, source_target_pairs={{0,64},{16,80},{32,96},{48,112},{64,128},{80,144},{96,160},{112,17... | collective-permute-start | bytes 147464 | tf_op jit(solution)/shard_map/ppermute | solution.py:348
  80.7 2.1 %collective-permute-start.27 = (bf16[32,768]{1,0:T(8,128)(2,1)S(1)}, bf16[32,768]{1,0:T(8,128)(2,1)S(1)}, u32[]{:S(2)}, u32[]{:S(2)}) collective-permute-start(bf16[32,768]{1,0:T(8,128)(2,1)S(1)} %get-tuple-element.51), channel_id=1, source_target_pairs={{0,128},{16,144},{32,160},{48,176},{64,192},{80,208},{96,224},{112... | collective-permute-start | bytes 147464 | tf_op jit(solution)/shard_map/ppermute | solution.py:348
  83.5 0.7 collective-permute-done.26.refs_5_
  84.2 2.0 %collective-permute-done.27.refs_6_ = bf16[32,768]{1,0:T(8,128)(2,1)S(1)} collective-permute-done((bf16[32,768]{1,0:T(8,128)(2,1)S(1)}, bf16[32,768]{1,0:T(8,128)(2,1)S(1)}, u32[]{:S(2)}, u32[]{:S(2)}) %collective-permute-start.27) | collective-permute-done | bytes 49184 | tf_op jit(solution)/shard_map/ppermute | solution.py:348
  86.2 2.4 %collective-permute-done.28.refs_7_ = bf16[32,768]{1,0:T(8,128)(2,1)S(1)} collective-permute-done((bf16[32,768]{1,0:T(8,128)(2,1)S(1)}, bf16[32,768]{1,0:T(8,128)(2,1)S(1)}, u32[]{:S(2)}, u32[]{:S(2)}) %collective-permute-start.28) | collective-permute-done | bytes 49184 | tf_op jit(solution)/shard_map/ppermute | solution.py:348
  88.6 1.1 %final_sum.1 = f32[64,768]{1,0:T(8,128)} custom-call(f32[32,768]{1,0:T(8,128)S(1)} %get-tuple-element.35.refs_0_, bf16[32,768]{1,0:T(8,128)(2,1)S(1)} %collective-permute-done.13.refs_1_, bf16[32,768]{1,0:T(8,128)(2,1)S(1)} %collective-permute-done.14.refs_2_, bf16[32,768]{1,0:T(8,128)(2,1)S(1)} %collective-permute-done.15.refs_3_, ...), custom_call_target="tpu_custom_call" | custom-call | tf_op jit(solution)/shard_map/final_sum/pallas_call | solution.py:214
  (48 shorter events, 4.5 us)
Async XLA Ops:
  0.0 15.2 %collective-permute-start.4 = (bf16[768,4096]{1,0:T(8,128)(2,1)}, bf16[768,4096]{1,0:T(8,128)(2,1)S(1)}, u32[]{:S(2)}, u32[]{:S(2)}) collective-permute-start(bf16[768,4096]{1,0:T(8,128)(2,1)} %bitcast.1), channel_id=1, source_target_pairs={{0,1},{1,0},{2,3},{3,2},{4,5},{5,4},{6,7},{7,6},{8,9},{9,8},{10,11... | collective-permute-start | bytes 18874376 | tf_op jit(solution)/shard_map/ppermute | solution.py:332
  2.5 12.2 %collective-permute-start = (bf16[32,4096]{1,0:T(8,128)(2,1)S(1)}, bf16[32,4096]{1,0:T(8,128)(2,1)S(1)}, u32[]{:S(2)}, u32[]{:S(2)}) collective-permute-start(bf16[32,4096]{1,0:T(8,128)(2,1)S(1)} %query_grads.2.refs_0_), channel_id=1, source_target_pairs={{0,4},{1,5},{2,6},{3,7},{4,8},{5,9},{6,10},{7,11},{8,12},{9,13},{1... | collective-permute-start | bytes 786440 | tf_op jit(solution)/shard_map/ppermute | solution.py:247
  4.1 18.7 %collective-permute-start.1 = (bf16[32,4096]{1,0:T(8,128)(2,1)S(1)}, bf16[32,4096]{1,0:T(8,128)(2,1)S(1)}, u32[]{:S(2)}, u32[]{:S(2)}) collective-permute-start(bf16[32,4096]{1,0:T(8,128)(2,1)S(1)} %query_grads.2.refs_0_), channel_id=1, source_target_pairs={{0,2},{1,3},{2,0},{3,1},{4,6},{5,7},{6,4},{7,5},{8,10},{9,11},{10,... | collective-permute-start | bytes 786440 | tf_op jit(solution)/shard_map/ppermute | solution.py:247
  10.4 12.4 %collective-permute-start.2 = (bf16[32,4096]{1,0:T(8,128)(2,1)S(1)}, bf16[32,4096]{1,0:T(8,128)(2,1)S(1)}, u32[]{:S(2)}, u32[]{:S(2)}) collective-permute-start(bf16[32,4096]{1,0:T(8,128)(2,1)S(1)} %query_grads.2.refs_0_), channel_id=1, source_target_pairs={{0,12},{1,13},{2,14},{3,15},{4,0},{5,1},{6,2},{7,3},{8,4},{9,5},{1... | collective-permute-start | bytes 786440 | tf_op jit(solution)/shard_map/ppermute | solution.py:247
  12.1 34.5 %slice-start = ((s8[6291456]{0:T(1024)(128)(4,1)}), s8[4194304]{0:T(1024)(128)(4,1)S(1)}, s32[]{:S(2)}) async-start(s8[6291456]{0:T(1024)(128)(4,1)} %bitcast.2), calls=%async_computation | async-start | bytes 8388608
  14.7 31.8 %slice-start.1 = ((s8[6291456]{0:T(1024)(128)(4,1)}), s8[2097152]{0:T(1024)(128)(4,1)S(1)}, s32[]{:S(2)}) async-start(s8[6291456]{0:T(1024)(128)(4,1)} %bitcast.2), calls=%async_computation.1 | async-start | bytes 4194304
  14.7 9.4 %collective-permute-start.3 = (bf16[32,4096]{1,0:T(8,128)(2,1)S(1)}, bf16[32,4096]{1,0:T(8,128)(2,1)S(1)}, u32[]{:S(2)}, u32[]{:S(2)}) collective-permute-start(bf16[32,4096]{1,0:T(8,128)(2,1)S(1)} %collective-permute-done.refs_1_), channel_id=1, source_target_pairs={{0,4},{1,5},{2,6},{3,7},{4,8},{5,9},{6,10},{7,11},{8,12},{9,13},{1... | collective-permute-start | bytes 786440 | tf_op jit(solution)/shard_map/ppermute | solution.py:247
  15.2 9.0 %collective-permute-start.5 = (bf16[32,4096]{1,0:T(8,128)(2,1)S(1)}, bf16[32,4096]{1,0:T(8,128)(2,1)S(1)}, u32[]{:S(2)}, u32[]{:S(2)}) collective-permute-start(bf16[32,4096]{1,0:T(8,128)(2,1)S(1)} %fence.5.refs_0_), channel_id=1, source_target_pairs={{0,12},{1,13},{2,14},{3,15},{4,0},{5,1},{6,2},{7,3},{8,4},{9,5},{1... | collective-permute-start | bytes 786440 | tf_op jit(solution)/shard_map/ppermute | solution.py:247
  24.2 7.9 %collective-permute-start.7 = (bf16[32,4096]{1,0:T(8,128)(2,1)S(1)}, bf16[32,4096]{1,0:T(8,128)(2,1)S(1)}, u32[]{:S(2)}, u32[]{:S(2)}) collective-permute-start(bf16[32,4096]{1,0:T(8,128)(2,1)S(1)} %get-tuple-element.30.refs_4_), channel_id=1, source_target_pairs={{0,12},{1,13},{2,14},{3,15},{4,0},{5,1},{6,2},{7,3},{8,4},{9,5},{1... | collective-permute-start | bytes 786440 | tf_op jit(solution)/shard_map/ppermute | solution.py:247
  27.3 16.3 %collective-permute-start.16 = (bf16[32,4096]{1,0:T(8,128)(2,1)S(1)}, bf16[32,4096]{1,0:T(8,128)(2,1)S(1)}, u32[]{:S(2)}, u32[]{:S(2)}) collective-permute-start(bf16[32,4096]{1,0:T(8,128)(2,1)S(1)} %fence.5.refs_0_), channel_id=1, source_target_pairs={{0,2},{1,3},{2,0},{3,1},{4,6},{5,7},{6,4},{7,5},{8,10},{9,11},{10,... | collective-permute-start | bytes 786440 | tf_op jit(solution)/shard_map/ppermute | solution.py:247
  31.1 12.5 %collective-permute-start.17 = (bf16[32,4096]{1,0:T(8,128)(2,1)S(1)}, bf16[32,4096]{1,0:T(8,128)(2,1)S(1)}, u32[]{:S(2)}, u32[]{:S(2)}) collective-permute-start(bf16[32,4096]{1,0:T(8,128)(2,1)S(1)} %fence.5.refs_0_), channel_id=1, source_target_pairs={{0,4},{1,5},{2,6},{3,7},{4,8},{5,9},{6,10},{7,11},{8,12},{9,13},{1... | collective-permute-start | bytes 786440 | tf_op jit(solution)/shard_map/ppermute | solution.py:247
  31.1 13.4 %collective-permute-start.6 = (bf16[32,4096]{1,0:T(8,128)(2,1)S(1)}, bf16[32,4096]{1,0:T(8,128)(2,1)S(1)}, u32[]{:S(2)}, u32[]{:S(2)}) collective-permute-start(bf16[32,4096]{1,0:T(8,128)(2,1)S(1)} %get-tuple-element.30.refs_4_), channel_id=1, source_target_pairs={{0,4},{1,5},{2,6},{3,7},{4,8},{5,9},{6,10},{7,11},{8,12},{9,13},{1... | collective-permute-start | bytes 786440 | tf_op jit(solution)/shard_map/ppermute | solution.py:247
  32.1 14.4 %collective-permute-start.8 = (bf16[32,4096]{1,0:T(8,128)(2,1)S(1)}, bf16[32,4096]{1,0:T(8,128)(2,1)S(1)}, u32[]{:S(2)}, u32[]{:S(2)}) collective-permute-start(bf16[32,4096]{1,0:T(8,128)(2,1)S(1)} %collective-permute-done.7.refs_6_.refs_2_), channel_id=1, source_target_pairs={{0,12},{1,13},{2,14},{3,15},{4,0},{5,1},{6,2},{7,3},{8,4},{9,5},{1... | collective-permute-start | bytes 786440 | tf_op jit(solution)/shard_map/ppermute | solution.py:247
  44.5 7.6 %collective-permute-start.20 = (bf16[32,4096]{1,0:T(8,128)(2,1)S(1)}, bf16[32,4096]{1,0:T(8,128)(2,1)S(1)}, u32[]{:S(2)}, u32[]{:S(2)}) collective-permute-start(bf16[32,4096]{1,0:T(8,128)(2,1)S(1)} %get-tuple-element.40.refs_4_), channel_id=1, source_target_pairs={{0,12},{1,13},{2,14},{3,15},{4,0},{5,1},{6,2},{7,3},{8,4},{9,5},{1... | collective-permute-start | bytes 786440 | tf_op jit(solution)/shard_map/ppermute | solution.py:247
  44.7 13.6 %collective-permute-start.19 = (bf16[32,4096]{1,0:T(8,128)(2,1)S(1)}, bf16[32,4096]{1,0:T(8,128)(2,1)S(1)}, u32[]{:S(2)}, u32[]{:S(2)}) collective-permute-start(bf16[32,4096]{1,0:T(8,128)(2,1)S(1)} %get-tuple-element.40.refs_4_), channel_id=1, source_target_pairs={{0,4},{1,5},{2,6},{3,7},{4,8},{5,9},{6,10},{7,11},{8,12},{9,13},{1... | collective-permute-start | bytes 786440 | tf_op jit(solution)/shard_map/ppermute | solution.py:247
  46.5 12.3 %collective-permute-start.18 = (bf16[32,4096]{1,0:T(8,128)(2,1)S(1)}, bf16[32,4096]{1,0:T(8,128)(2,1)S(1)}, u32[]{:S(2)}, u32[]{:S(2)}) collective-permute-start(bf16[32,4096]{1,0:T(8,128)(2,1)S(1)} %get-tuple-element.39.refs_1_), channel_id=1, source_target_pairs={{0,4},{1,5},{2,6},{3,7},{4,8},{5,9},{6,10},{7,11},{8,12},{9,13},{1... | collective-permute-start | bytes 786440 | tf_op jit(solution)/shard_map/ppermute | solution.py:247
  52.1 7.2 %collective-permute-start.21 = (bf16[32,4096]{1,0:T(8,128)(2,1)S(1)}, bf16[32,4096]{1,0:T(8,128)(2,1)S(1)}, u32[]{:S(2)}, u32[]{:S(2)}) collective-permute-start(bf16[32,4096]{1,0:T(8,128)(2,1)S(1)} %fence.8.refs_6_), channel_id=1, source_target_pairs={{0,12},{1,13},{2,14},{3,15},{4,0},{5,1},{6,2},{7,3},{8,4},{9,5},{1... | collective-permute-start | bytes 786440 | tf_op jit(solution)/shard_map/ppermute | solution.py:247
  55.4 9.3 %collective-permute-start.10 = (bf16[128,768]{1,0:T(8,128)(2,1)S(1)}, bf16[128,768]{1,0:T(8,128)(2,1)S(1)}, u32[]{:S(2)}, u32[]{:S(2)}) collective-permute-start(bf16[128,768]{1,0:T(8,128)(2,1)S(1)} %get-tuple-element.32), channel_id=1, source_target_pairs={{0,1},{1,49},{2,3},{3,51},{4,5},{5,53},{6,7},{7,55},{8,9},{9,57},{... | collective-permute-start | bytes 589832 | tf_op jit(solution)/shard_map/ppermute | solution.py:317
  55.4 9.4 %collective-permute-start.11 = (bf16[128,768]{1,0:T(8,128)(2,1)S(1)}, bf16[128,768]{1,0:T(8,128)(2,1)S(1)}, u32[]{:S(2)}, u32[]{:S(2)}) collective-permute-start(bf16[128,768]{1,0:T(8,128)(2,1)S(1)} %get-tuple-element.33), channel_id=1, source_target_pairs={{0,32},{1,16},{2,34},{3,18},{4,36},{5,20},{6,38},{7,22},{8,40},{9,... | collective-permute-start | bytes 589832 | tf_op jit(solution)/shard_map/ppermute | solution.py:317
  58.3 8.4 %collective-permute-start.9 = (bf16[128,768]{1,0:T(8,128)(2,1)S(1)}, bf16[128,768]{1,0:T(8,128)(2,1)S(1)}, u32[]{:S(2)}, u32[]{:S(2)}) collective-permute-start(bf16[128,768]{1,0:T(8,128)(2,1)S(1)} %get-tuple-element.31), channel_id=1, source_target_pairs={{0,48},{1,17},{2,50},{3,19},{4,52},{5,21},{6,54},{7,23},{8,56},{9,... | collective-permute-start | bytes 589832 | tf_op jit(solution)/shard_map/ppermute | solution.py:317
  64.7 18.4 %copy-start = (s32[768]{0:T(1024)S(1)}, s32[768]{0:T(1024)}, u32[]{:S(2)}) copy-start(s32[768]{0:T(1024)} %param.9) | copy-start | bytes 9220
  66.7 6.9 %collective-permute-start.22 = (bf16[128,768]{1,0:T(8,128)(2,1)S(1)}, bf16[128,768]{1,0:T(8,128)(2,1)S(1)}, u32[]{:S(2)}, u32[]{:S(2)}) collective-permute-start(bf16[128,768]{1,0:T(8,128)(2,1)S(1)} %get-tuple-element.45), channel_id=1, source_target_pairs={{0,48},{1,17},{2,50},{3,19},{4,52},{5,21},{6,54},{7,23},{8,56},{9,... | collective-permute-start | bytes 589832 | tf_op jit(solution)/shard_map/ppermute | solution.py:317
  67.6 6.8 %collective-permute-start.12 = (bf16[128,768]{1,0:T(8,128)(2,1)S(1)}, bf16[128,768]{1,0:T(8,128)(2,1)S(1)}, u32[]{:S(2)}, u32[]{:S(2)}) collective-permute-start(bf16[128,768]{1,0:T(8,128)(2,1)S(1)} %join.2), channel_id=1, source_target_pairs={{1,48},{3,50},{5,52},{7,54},{9,56},{11,58},{13,60},{15,62},{16,1},... | collective-permute-start | bytes 589832 | tf_op jit(solution)/shard_map/ppermute | solution.py:317
  68.2 9.3 %collective-permute-start.23 = (bf16[128,768]{1,0:T(8,128)(2,1)S(1)}, bf16[128,768]{1,0:T(8,128)(2,1)S(1)}, u32[]{:S(2)}, u32[]{:S(2)}) collective-permute-start(bf16[128,768]{1,0:T(8,128)(2,1)S(1)} %get-tuple-element.46), channel_id=1, source_target_pairs={{0,1},{1,49},{2,3},{3,51},{4,5},{5,53},{6,7},{7,55},{8,9},{9,57},{... | collective-permute-start | bytes 589832 | tf_op jit(solution)/shard_map/ppermute | solution.py:317
  72.3 7.3 %collective-permute-start.24 = (bf16[128,768]{1,0:T(8,128)(2,1)S(1)}, bf16[128,768]{1,0:T(8,128)(2,1)S(1)}, u32[]{:S(2)}, u32[]{:S(2)}) collective-permute-start(bf16[128,768]{1,0:T(8,128)(2,1)S(1)} %get-tuple-element.47), channel_id=1, source_target_pairs={{0,32},{1,16},{2,34},{3,18},{4,36},{5,20},{6,38},{7,22},{8,40},{9,... | collective-permute-start | bytes 589832 | tf_op jit(solution)/shard_map/ppermute | solution.py:317
  73.7 6.0 %collective-permute-start.25 = (bf16[128,768]{1,0:T(8,128)(2,1)S(1)}, bf16[128,768]{1,0:T(8,128)(2,1)S(1)}, u32[]{:S(2)}, u32[]{:S(2)}) collective-permute-start(bf16[128,768]{1,0:T(8,128)(2,1)S(1)} %join.3), channel_id=1, source_target_pairs={{1,48},{3,50},{5,52},{7,54},{9,56},{11,58},{13,60},{15,62},{16,1},... | collective-permute-start | bytes 589832 | tf_op jit(solution)/shard_map/ppermute | solution.py:317
  74.5 8.4 %collective-permute-start.13 = (bf16[32,768]{1,0:T(8,128)(2,1)S(1)}, bf16[32,768]{1,0:T(8,128)(2,1)S(1)}, u32[]{:S(2)}, u32[]{:S(2)}) collective-permute-start(bf16[32,768]{1,0:T(8,128)(2,1)S(1)} %get-tuple-element.36), channel_id=1, source_target_pairs={{0,64},{16,80},{32,96},{48,112},{64,128},{80,144},{96,160},{112,17... | collective-permute-start | bytes 147464 | tf_op jit(solution)/shard_map/ppermute | solution.py:348
  75.5 8.0 %collective-permute-start.14 = (bf16[32,768]{1,0:T(8,128)(2,1)S(1)}, bf16[32,768]{1,0:T(8,128)(2,1)S(1)}, u32[]{:S(2)}, u32[]{:S(2)}) collective-permute-start(bf16[32,768]{1,0:T(8,128)(2,1)S(1)} %get-tuple-element.37), channel_id=1, source_target_pairs={{0,128},{16,144},{32,160},{48,176},{64,192},{80,208},{96,224},{112... | collective-permute-start | bytes 147464 | tf_op jit(solution)/shard_map/ppermute | solution.py:348
  77.6 5.9 %collective-permute-start.15 = (bf16[32,768]{1,0:T(8,128)(2,1)S(1)}, bf16[32,768]{1,0:T(8,128)(2,1)S(1)}, u32[]{:S(2)}, u32[]{:S(2)}) collective-permute-start(bf16[32,768]{1,0:T(8,128)(2,1)S(1)} %get-tuple-element.38), channel_id=1, source_target_pairs={{0,192},{16,208},{32,224},{48,240},{64,0},{80,16},{96,32},{112,48}... | collective-permute-start | bytes 147464 | tf_op jit(solution)/shard_map/ppermute | solution.py:348
  79.8 4.5 %collective-permute-start.26 = (bf16[32,768]{1,0:T(8,128)(2,1)S(1)}, bf16[32,768]{1,0:T(8,128)(2,1)S(1)}, u32[]{:S(2)}, u32[]{:S(2)}) collective-permute-start(bf16[32,768]{1,0:T(8,128)(2,1)S(1)} %get-tuple-element.50), channel_id=1, source_target_pairs={{0,64},{16,80},{32,96},{48,112},{64,128},{80,144},{96,160},{112,17... | collective-permute-start | bytes 147464 | tf_op jit(solution)/shard_map/ppermute | solution.py:348
  80.7 5.5 %collective-permute-start.27 = (bf16[32,768]{1,0:T(8,128)(2,1)S(1)}, bf16[32,768]{1,0:T(8,128)(2,1)S(1)}, u32[]{:S(2)}, u32[]{:S(2)}) collective-permute-start(bf16[32,768]{1,0:T(8,128)(2,1)S(1)} %get-tuple-element.51), channel_id=1, source_target_pairs={{0,128},{16,144},{32,160},{48,176},{64,192},{80,208},{96,224},{112... | collective-permute-start | bytes 147464 | tf_op jit(solution)/shard_map/ppermute | solution.py:348
  82.9 5.7 %collective-permute-start.28 = (bf16[32,768]{1,0:T(8,128)(2,1)S(1)}, bf16[32,768]{1,0:T(8,128)(2,1)S(1)}, u32[]{:S(2)}, u32[]{:S(2)}) collective-permute-start(bf16[32,768]{1,0:T(8,128)(2,1)S(1)} %get-tuple-element.52), channel_id=1, source_target_pairs={{0,192},{16,208},{32,224},{48,240},{64,0},{80,16},{96,32},{112,48}... | collective-permute-start | bytes 147464 | tf_op jit(solution)/shard_map/ppermute | solution.py:348

commit v10 on v9

--- a/solution.py
+++ b/solution.py
@@ -283,8 +283,10 @@
     far_b = beyond(b)
     b_below, b_above = up(b), down(b)
     a_opposite = up(a_below)
-    far_a, a_above = after((far_a, a_above), a_opposite, b_above)
-    far_a_above, far_a_below = down(far_a), up(far_a)
+    far_a, a_above = after((far_a, a_above), b_below, b_above)
+    far_a_above = down(far_a)
+    (far_a,) = after((far_a,), a_opposite)
+    far_a_below = up(far_a)
     far_a_opposite = down(far_a_above)
     far_b, b_below = after((far_b, b_below), far_a_above, far_a_below)
     b_opposite = up(b_below)

time: 91.2 us -> 89.9 us (0.986)
  starting transfers between devices: 46 us -> 42.4 us
  waiting for transfers between devices: 25.5 us -> 27.8 us
    ppermute x14, waiting for transfers between devices: 15.5 us -> 21.5 us  [along(): return lax.ppermute(value, 'group', group_pairs(move))]
    ppermute x14, starting transfers between devices: 29.6 us -> 23.7 us  [along(): return lax.ppermute(value, 'group', group_pairs(move))]
    ppermute x8, waiting for transfers between devices: 4.98 us -> 1.87 us  [send(): return lax.ppermute(value, ('store', 'group'), all_pairs(move))]
    ppermute x8, starting transfers between devices: 9.71 us -> 11.1 us  [send(): return lax.ppermute(value, ('store', 'group'), all_pairs(move))]
    ppermute x6, starting transfers between devices: 6.67 us -> 7.65 us  [on_device(): lax.ppermute(send, 'store', store_pairs(lambda x, z: (x, z + k)))]
  transfers between devices with their start and end apart: 29 -> 29, of which waited for: 12 -> 11; matrix products, arithmetic and copies ran while one was open for 0% -> 0% of each run, Pallas kernels for 18% -> 19%
where the time goes in v10:
time: 89.9 us; the launch traced here: 88.5 us
  starting transfers between devices  42.4 us (47%)
  waiting for transfers between devices  27.8 us (31%)
  Pallas kernels  17.6 us (20%)
    ppermute x14, starting transfers between devices, along(): return lax.ppermute(value, 'group', group_pairs(move))  23.7 us
    ppermute x14, waiting for transfers between devices, along(): return lax.ppermute(value, 'group', group_pairs(move))  21.5 us
    ppermute x8, starting transfers between devices, send(): return lax.ppermute(value, ('store', 'group'), all_pairs(move))  11.1 us
    pallas_call x2, Pallas kernels, partial_scores(): pl.pallas_call(score_kernel, out_shape=[jax.ShapeDtypeStruct((4 * ROWS, H...  10.9 us
    ppermute x6, starting transfers between devices, on_device(): lax.ppermute(send, 'store', store_pairs(lambda x, z: (x, z + k)))  7.65 us
    pallas_call x2, Pallas kernels, query_grads(): pl.pallas_call(functools.partial(grad_kernel, chunk * ROWS), out_shape=ja...  5.13 us
    ppermute x6, waiting for transfers between devices, on_device(): lax.ppermute(send, 'store', store_pairs(lambda x, z: (x, z + k)))  4.44 us
    ppermute x8, waiting for transfers between devices, send(): return lax.ppermute(value, ('store', 'group'), all_pairs(move))  1.87 us
  transfers between devices with their start and end apart: 29, of which 11 were waited for; matrix products, arithmetic and copies ran while one was open for 0% of the time, Pallas kernels for 19%

profile of v10, /device:TPU:32, one launch (start us, length us, event | category | flops | bytes accessed | tf_op | source)
XLA Modules:
  0.0 88.5 jit_solution(1095238872386606154)
XLA Ops:
  0.0 2.5 %query_grads.2.refs_0_ = bf16[32,4096]{1,0:T(8,128)(2,1)S(1)} custom-call(s32[64]{0:T(128)} %lengths_hbm.3, bf16[64,1,64,256]{3,2,1,0:T(8,128)(2,1)} %acts_hbm.3, bf16[64,1,64,256]{3,2,1,0:T(8,128)(2,1)} %grads_hbm.3), custom_call_target="tpu_custom_call" | custom-call | tf_op jit(solution)/shard_map/query_grads/pallas_call | solution.py:81
  2.5 6.3 %collective-permute-start.1 = (bf16[32,4096]{1,0:T(8,128)(2,1)S(1)}, bf16[32,4096]{1,0:T(8,128)(2,1)S(1)}, u32[]{:S(2)}, u32[]{:S(2)}) collective-permute-start(bf16[32,4096]{1,0:T(8,128)(2,1)S(1)} %query_grads.2.refs_0_), channel_id=1, source_target_pairs={{0,2},{1,3},{2,0},{3,1},{4,6},{5,7},{6,4},{7,5},{8,10},{9,11},{10,... | collective-permute-start | bytes 786440 | tf_op jit(solution)/shard_map/ppermute | solution.py:247
  8.9 3.0 %collective-permute-start.2 = (bf16[32,4096]{1,0:T(8,128)(2,1)S(1)}, bf16[32,4096]{1,0:T(8,128)(2,1)S(1)}, u32[]{:S(2)}, u32[]{:S(2)}) collective-permute-start(bf16[32,4096]{1,0:T(8,128)(2,1)S(1)} %query_grads.2.refs_0_), channel_id=1, source_target_pairs={{0,12},{1,13},{2,14},{3,15},{4,0},{5,1},{6,2},{7,3},{8,4},{9,5},{1... | collective-permute-start | bytes 786440 | tf_op jit(solution)/shard_map/ppermute | solution.py:247
  11.9 2.6 %query_grads.3.refs_0_ = bf16[32,4096]{1,0:T(8,128)(2,1)S(1)} custom-call(s32[64]{0:T(128)} %lengths_hbm.3, bf16[64,1,64,256]{3,2,1,0:T(8,128)(2,1)} %acts_hbm.3, bf16[64,1,64,256]{3,2,1,0:T(8,128)(2,1)} %grads_hbm.3), custom_call_target="tpu_custom_call" | custom-call | tf_op jit(solution)/shard_map/query_grads/pallas_call | solution.py:81
  15.2 2.7 %collective-permute-start.5 = (bf16[32,4096]{1,0:T(8,128)(2,1)S(1)}, bf16[32,4096]{1,0:T(8,128)(2,1)S(1)}, u32[]{:S(2)}, u32[]{:S(2)}) collective-permute-start(bf16[32,4096]{1,0:T(8,128)(2,1)S(1)} %fence.6.refs_0_), channel_id=1, source_target_pairs={{0,12},{1,13},{2,14},{3,15},{4,0},{5,1},{6,2},{7,3},{8,4},{9,5},{1... | collective-permute-start | bytes 786440 | tf_op jit(solution)/shard_map/ppermute | solution.py:247
  18.0 4.3 %collective-permute-done.refs_1_ = bf16[32,4096]{1,0:T(8,128)(2,1)S(1)} collective-permute-done((bf16[32,4096]{1,0:T(8,128)(2,1)S(1)}, bf16[32,4096]{1,0:T(8,128)(2,1)S(1)}, u32[]{:S(2)}, u32[]{:S(2)}) %collective-permute-start) | collective-permute-done | bytes 262176 | tf_op jit(solution)/shard_map/ppermute | solution.py:247
  22.3 5.6 %collective-permute-done.4.refs_2_.refs_1_ = bf16[32,4096]{1,0:T(8,128)(2,1)S(1)} collective-permute-done((bf16[32,4096]{1,0:T(8,128)(2,1)S(1)}, bf16[32,4096]{1,0:T(8,128)(2,1)S(1)}, u32[]{:S(2)}, u32[]{:S(2)}) %collective-permute-start.4) | collective-permute-done | bytes 262176 | tf_op jit(solution)/shard_map/ppermute | solution.py:247
  27.9 2.4 %collective-permute-start.17 = (bf16[32,4096]{1,0:T(8,128)(2,1)S(1)}, bf16[32,4096]{1,0:T(8,128)(2,1)S(1)}, u32[]{:S(2)}, u32[]{:S(2)}) collective-permute-start(bf16[32,4096]{1,0:T(8,128)(2,1)S(1)} %fence.6.refs_0_), channel_id=1, source_target_pairs={{0,2},{1,3},{2,0},{3,1},{4,6},{5,7},{6,4},{7,5},{8,10},{9,11},{10,... | collective-permute-start | bytes 786440 | tf_op jit(solution)/shard_map/ppermute | solution.py:247
  30.2 2.3 %collective-permute-done.6.refs_1_.refs_3_ = bf16[32,4096]{1,0:T(8,128)(2,1)S(1)} collective-permute-done((bf16[32,4096]{1,0:T(8,128)(2,1)S(1)}, bf16[32,4096]{1,0:T(8,128)(2,1)S(1)}, u32[]{:S(2)}, u32[]{:S(2)}) %collective-permute-start.6) | collective-permute-done | bytes 262176 | tf_op jit(solution)/shard_map/ppermute | solution.py:247
  32.5 1.8 %collective-permute-done.8.refs_6_.refs_2_ = bf16[32,4096]{1,0:T(8,128)(2,1)S(1)} collective-permute-done((bf16[32,4096]{1,0:T(8,128)(2,1)S(1)}, bf16[32,4096]{1,0:T(8,128)(2,1)S(1)}, u32[]{:S(2)}, u32[]{:S(2)}) %collective-permute-start.8) | collective-permute-done | bytes 262176 | tf_op jit(solution)/shard_map/ppermute | solution.py:247
  34.3 3.2 %collective-permute-start.9 = (bf16[32,4096]{1,0:T(8,128)(2,1)S(1)}, bf16[32,4096]{1,0:T(8,128)(2,1)S(1)}, u32[]{:S(2)}, u32[]{:S(2)}) collective-permute-start(bf16[32,4096]{1,0:T(8,128)(2,1)S(1)} %collective-permute-done.8.refs_6_.refs_2_), channel_id=1, source_target_pairs={{0,12},{1,13},{2,14},{3,15},{4,0},{5,1},{6,2},{7,3},{8,4},{9,5},{1... | collective-permute-start | bytes 786440 | tf_op jit(solution)/shard_map/ppermute | solution.py:247
  37.5 6.3 %collective-permute-done.17.refs_0_ = bf16[32,4096]{1,0:T(8,128)(2,1)S(1)} collective-permute-done((bf16[32,4096]{1,0:T(8,128)(2,1)S(1)}, bf16[32,4096]{1,0:T(8,128)(2,1)S(1)}, u32[]{:S(2)}, u32[]{:S(2)}) %collective-permute-start.17) | collective-permute-done | bytes 262176 | tf_op jit(solution)/shard_map/ppermute | solution.py:247
  43.8 2.0 %collective-permute-start.19 = (bf16[32,4096]{1,0:T(8,128)(2,1)S(1)}, bf16[32,4096]{1,0:T(8,128)(2,1)S(1)}, u32[]{:S(2)}, u32[]{:S(2)}) collective-permute-start(bf16[32,4096]{1,0:T(8,128)(2,1)S(1)} %get-tuple-element.40.refs_4_), channel_id=1, source_target_pairs={{0,4},{1,5},{2,6},{3,7},{4,8},{5,9},{6,10},{7,11},{8,12},{9,13},{1... | collective-permute-start | bytes 786440 | tf_op jit(solution)/shard_map/ppermute | solution.py:247
  45.9 1.7 %collective-permute-start.18 = (bf16[32,4096]{1,0:T(8,128)(2,1)S(1)}, bf16[32,4096]{1,0:T(8,128)(2,1)S(1)}, u32[]{:S(2)}, u32[]{:S(2)}) collective-permute-start(bf16[32,4096]{1,0:T(8,128)(2,1)S(1)} %get-tuple-element.39.refs_1_), channel_id=1, source_target_pairs={{0,4},{1,5},{2,6},{3,7},{4,8},{5,9},{6,10},{7,11},{8,12},{9,13},{1... | collective-permute-start | bytes 786440 | tf_op jit(solution)/shard_map/ppermute | solution.py:247
  47.5 5.5 %partial_scores.2 = (bf16[128,768]{1,0:T(8,128)(2,1)S(1)}, bf16[128,768]{1,0:T(8,128)(2,1)S(1)}, bf16[128,768]{1,0:T(8,128)(2,1)S(1)}, bf16[128,768]{1,0:T(8,128)(2,1)S(1)}) custom-call(bf16[32,4096]{1,0:T(8,128)(2,1)S(1)} %query_grads.2.refs_0_, bf16[32,4096]{1,0:T(8,128)(2,1)S(1)} %collective-permute-done.refs_1_, ...), custom_call_target="tpu_custom_call" | custom-call | flops 1 | bytes 1 | tf_op jit(solution)/shard_map/partial_scores/pallas_call | solution.py:148
  53.1 1.7 %collective-permute-start.21 = (bf16[32,4096]{1,0:T(8,128)(2,1)S(1)}, bf16[32,4096]{1,0:T(8,128)(2,1)S(1)}, u32[]{:S(2)}, u32[]{:S(2)}) collective-permute-start(bf16[32,4096]{1,0:T(8,128)(2,1)S(1)} %fence.10.refs_6_), channel_id=1, source_target_pairs={{0,12},{1,13},{2,14},{3,15},{4,0},{5,1},{6,2},{7,3},{8,4},{9,5},{1... | collective-permute-start | bytes 786440 | tf_op jit(solution)/shard_map/ppermute | solution.py:247
  54.7 2.7 %collective-permute-start.10 = (bf16[128,768]{1,0:T(8,128)(2,1)S(1)}, bf16[128,768]{1,0:T(8,128)(2,1)S(1)}, u32[]{:S(2)}, u32[]{:S(2)}) collective-permute-start(bf16[128,768]{1,0:T(8,128)(2,1)S(1)} %get-tuple-element.31), channel_id=1, source_target_pairs={{0,48},{1,17},{2,50},{3,19},{4,52},{5,21},{6,54},{7,23},{8,56},{9,... | collective-permute-start | bytes 589832 | tf_op jit(solution)/shard_map/ppermute | solution.py:319
  57.4 0.9 collective-permute-start.12
  58.3 1.2 %collective-permute-done.21.refs_7_ = bf16[32,4096]{1,0:T(8,128)(2,1)S(1)} collective-permute-done((bf16[32,4096]{1,0:T(8,128)(2,1)S(1)}, bf16[32,4096]{1,0:T(8,128)(2,1)S(1)}, u32[]{:S(2)}, u32[]{:S(2)}) %collective-permute-start.21) | collective-permute-done | bytes 262176 | tf_op jit(solution)/shard_map/ppermute | solution.py:247
  59.5 5.4 %partial_scores.3 = (bf16[128,768]{1,0:T(8,128)(2,1)S(1)}, bf16[128,768]{1,0:T(8,128)(2,1)S(1)}, bf16[128,768]{1,0:T(8,128)(2,1)S(1)}, bf16[128,768]{1,0:T(8,128)(2,1)S(1)}) custom-call(bf16[32,4096]{1,0:T(8,128)(2,1)S(1)} %fence.6.refs_0_, bf16[32,4096]{1,0:T(8,128)(2,1)S(1)} %get-tuple-element.39.refs_1_, ...), custom_call_target="tpu_custom_call" | custom-call | flops 1 | bytes 1 | tf_op jit(solution)/shard_map/partial_scores/pallas_call | solution.py:148
  65.6 2.2 %collective-permute-start.22 = (bf16[128,768]{1,0:T(8,128)(2,1)S(1)}, bf16[128,768]{1,0:T(8,128)(2,1)S(1)}, u32[]{:S(2)}, u32[]{:S(2)}) collective-permute-start(bf16[128,768]{1,0:T(8,128)(2,1)S(1)} %get-tuple-element.45), channel_id=1, source_target_pairs={{0,48},{1,17},{2,50},{3,19},{4,52},{5,21},{6,54},{7,23},{8,56},{9,... | collective-permute-start | bytes 589832 | tf_op jit(solution)/shard_map/ppermute | solution.py:319
  68.6 2.7 %collective-permute-start.23 = (bf16[128,768]{1,0:T(8,128)(2,1)S(1)}, bf16[128,768]{1,0:T(8,128)(2,1)S(1)}, u32[]{:S(2)}, u32[]{:S(2)}) collective-permute-start(bf16[128,768]{1,0:T(8,128)(2,1)S(1)} %get-tuple-element.46), channel_id=1, source_target_pairs={{0,1},{1,49},{2,3},{3,51},{4,5},{5,53},{6,7},{7,55},{8,9},{9,57},{... | collective-permute-start | bytes 589832 | tf_op jit(solution)/shard_map/ppermute | solution.py:319
  71.2 1.3 %collective-permute-start.24 = (bf16[128,768]{1,0:T(8,128)(2,1)S(1)}, bf16[128,768]{1,0:T(8,128)(2,1)S(1)}, u32[]{:S(2)}, u32[]{:S(2)}) collective-permute-start(bf16[128,768]{1,0:T(8,128)(2,1)S(1)} %get-tuple-element.47), channel_id=1, source_target_pairs={{0,32},{1,16},{2,34},{3,18},{4,36},{5,20},{6,38},{7,22},{8,40},{9,... | collective-permute-start | bytes 589832 | tf_op jit(solution)/shard_map/ppermute | solution.py:319
  73.5 1.0 %collective-permute-start.14 = (bf16[32,768]{1,0:T(8,128)(2,1)S(1)}, bf16[32,768]{1,0:T(8,128)(2,1)S(1)}, u32[]{:S(2)}, u32[]{:S(2)}) collective-permute-start(bf16[32,768]{1,0:T(8,128)(2,1)S(1)} %get-tuple-element.36), channel_id=1, source_target_pairs={{0,64},{16,80},{32,96},{48,112},{64,128},{80,144},{96,160},{112,17... | collective-permute-start | bytes 147464 | tf_op jit(solution)/shard_map/ppermute | solution.py:350
  74.5 2.2 %collective-permute-start.15 = (bf16[32,768]{1,0:T(8,128)(2,1)S(1)}, bf16[32,768]{1,0:T(8,128)(2,1)S(1)}, u32[]{:S(2)}, u32[]{:S(2)}) collective-permute-start(bf16[32,768]{1,0:T(8,128)(2,1)S(1)} %get-tuple-element.37), channel_id=1, source_target_pairs={{0,128},{16,144},{32,160},{48,176},{64,192},{80,208},{96,224},{112... | collective-permute-start | bytes 147464 | tf_op jit(solution)/shard_map/ppermute | solution.py:350
  76.6 1.3 %collective-permute-done.23.c_ref = bf16[128,768]{1,0:T(8,128)(2,1)S(1)} collective-permute-done((bf16[128,768]{1,0:T(8,128)(2,1)S(1)}, bf16[128,768]{1,0:T(8,128)(2,1)S(1)}, u32[]{:S(2)}, u32[]{:S(2)}) %collective-permute-start.23) | collective-permute-done | bytes 196640 | tf_op jit(solution)/shard_map/ppermute | solution.py:319
  78.7 1.4 %collective-permute-start.26 = (bf16[32,768]{1,0:T(8,128)(2,1)S(1)}, bf16[32,768]{1,0:T(8,128)(2,1)S(1)}, u32[]{:S(2)}, u32[]{:S(2)}) collective-permute-start(bf16[32,768]{1,0:T(8,128)(2,1)S(1)} %get-tuple-element.50), channel_id=1, source_target_pairs={{0,64},{16,80},{32,96},{48,112},{64,128},{80,144},{96,160},{112,17... | collective-permute-start | bytes 147464 | tf_op jit(solution)/shard_map/ppermute | solution.py:350
  80.1 1.3 %collective-permute-start.27 = (bf16[32,768]{1,0:T(8,128)(2,1)S(1)}, bf16[32,768]{1,0:T(8,128)(2,1)S(1)}, u32[]{:S(2)}, u32[]{:S(2)}) collective-permute-start(bf16[32,768]{1,0:T(8,128)(2,1)S(1)} %get-tuple-element.51), channel_id=1, source_target_pairs={{0,128},{16,144},{32,160},{48,176},{64,192},{80,208},{96,224},{112... | collective-permute-start | bytes 147464 | tf_op jit(solution)/shard_map/ppermute | solution.py:350
  81.4 1.1 %collective-permute-start.28 = (bf16[32,768]{1,0:T(8,128)(2,1)S(1)}, bf16[32,768]{1,0:T(8,128)(2,1)S(1)}, u32[]{:S(2)}, u32[]{:S(2)}) collective-permute-start(bf16[32,768]{1,0:T(8,128)(2,1)S(1)} %get-tuple-element.52), channel_id=1, source_target_pairs={{0,192},{16,208},{32,224},{48,240},{64,0},{80,16},{96,32},{112,48}... | collective-permute-start | bytes 147464 | tf_op jit(solution)/shard_map/ppermute | solution.py:350
  83.3 2.2 %collective-permute-done.27.refs_6_ = bf16[32,768]{1,0:T(8,128)(2,1)S(1)} collective-permute-done((bf16[32,768]{1,0:T(8,128)(2,1)S(1)}, bf16[32,768]{1,0:T(8,128)(2,1)S(1)}, u32[]{:S(2)}, u32[]{:S(2)}) %collective-permute-start.27) | collective-permute-done | bytes 49184 | tf_op jit(solution)/shard_map/ppermute | solution.py:350
  85.6 1.8 %collective-permute-done.28.refs_7_ = bf16[32,768]{1,0:T(8,128)(2,1)S(1)} collective-permute-done((bf16[32,768]{1,0:T(8,128)(2,1)S(1)}, bf16[32,768]{1,0:T(8,128)(2,1)S(1)}, u32[]{:S(2)}, u32[]{:S(2)}) %collective-permute-start.28) | collective-permute-done | bytes 49184 | tf_op jit(solution)/shard_map/ppermute | solution.py:350
  87.4 1.1 %final_sum.1 = f32[64,768]{1,0:T(8,128)} custom-call(f32[32,768]{1,0:T(8,128)S(1)} %get-tuple-element.35.refs_0_, bf16[32,768]{1,0:T(8,128)(2,1)S(1)} %collective-permute-done.14.refs_1_, bf16[32,768]{1,0:T(8,128)(2,1)S(1)} %collective-permute-done.15.refs_2_, bf16[32,768]{1,0:T(8,128)(2,1)S(1)} %collective-permute-done.16.refs_3_, ...), custom_call_target="tpu_custom_call" | custom-call | tf_op jit(solution)/shard_map/final_sum/pallas_call | solution.py:214
  (49 shorter events, 4.6 us)
Async XLA Ops:
  0.0 14.5 %collective-permute-start.3 = (bf16[768,4096]{1,0:T(8,128)(2,1)}, bf16[768,4096]{1,0:T(8,128)(2,1)S(1)}, u32[]{:S(2)}, u32[]{:S(2)}) collective-permute-start(bf16[768,4096]{1,0:T(8,128)(2,1)} %bitcast.1), channel_id=1, source_target_pairs={{0,1},{1,0},{2,3},{3,2},{4,5},{5,4},{6,7},{7,6},{8,9},{9,8},{10,11... | collective-permute-start | bytes 18874376 | tf_op jit(solution)/shard_map/ppermute | solution.py:334
  2.5 19.8 %collective-permute-start.1 = (bf16[32,4096]{1,0:T(8,128)(2,1)S(1)}, bf16[32,4096]{1,0:T(8,128)(2,1)S(1)}, u32[]{:S(2)}, u32[]{:S(2)}) collective-permute-start(bf16[32,4096]{1,0:T(8,128)(2,1)S(1)} %query_grads.2.refs_0_), channel_id=1, source_target_pairs={{0,2},{1,3},{2,0},{3,1},{4,6},{5,7},{6,4},{7,5},{8,10},{9,11},{10,... | collective-permute-start | bytes 786440 | tf_op jit(solution)/shard_map/ppermute | solution.py:247
  8.9 13.4 %collective-permute-start.2 = (bf16[32,4096]{1,0:T(8,128)(2,1)S(1)}, bf16[32,4096]{1,0:T(8,128)(2,1)S(1)}, u32[]{:S(2)}, u32[]{:S(2)}) collective-permute-start(bf16[32,4096]{1,0:T(8,128)(2,1)S(1)} %query_grads.2.refs_0_), channel_id=1, source_target_pairs={{0,12},{1,13},{2,14},{3,15},{4,0},{5,1},{6,2},{7,3},{8,4},{9,5},{1... | collective-permute-start | bytes 786440 | tf_op jit(solution)/shard_map/ppermute | solution.py:247
  11.9 10.4 %collective-permute-start = (bf16[32,4096]{1,0:T(8,128)(2,1)S(1)}, bf16[32,4096]{1,0:T(8,128)(2,1)S(1)}, u32[]{:S(2)}, u32[]{:S(2)}) collective-permute-start(bf16[32,4096]{1,0:T(8,128)(2,1)S(1)} %query_grads.2.refs_0_), channel_id=1, source_target_pairs={{0,4},{1,5},{2,6},{3,7},{4,8},{5,9},{6,10},{7,11},{8,12},{9,13},{1... | collective-permute-start | bytes 786440 | tf_op jit(solution)/shard_map/ppermute | solution.py:247
  11.9 35.7 %slice-start = ((s8[6291456]{0:T(1024)(128)(4,1)}), s8[4194304]{0:T(1024)(128)(4,1)S(1)}, s32[]{:S(2)}) async-start(s8[6291456]{0:T(1024)(128)(4,1)} %bitcast.2), calls=%async_computation | async-start | bytes 8388608
  14.5 33.0 %slice-start.1 = ((s8[6291456]{0:T(1024)(128)(4,1)}), s8[2097152]{0:T(1024)(128)(4,1)S(1)}, s32[]{:S(2)}) async-start(s8[6291456]{0:T(1024)(128)(4,1)} %bitcast.2), calls=%async_computation.1 | async-start | bytes 4194304
  14.6 13.3 %collective-permute-start.4 = (bf16[32,4096]{1,0:T(8,128)(2,1)S(1)}, bf16[32,4096]{1,0:T(8,128)(2,1)S(1)}, u32[]{:S(2)}, u32[]{:S(2)}) collective-permute-start(bf16[32,4096]{1,0:T(8,128)(2,1)S(1)} %fence.6.refs_0_), channel_id=1, source_target_pairs={{0,4},{1,5},{2,6},{3,7},{4,8},{5,9},{6,10},{7,11},{8,12},{9,13},{1... | collective-permute-start | bytes 786440 | tf_op jit(solution)/shard_map/ppermute | solution.py:247
  15.2 12.7 %collective-permute-start.5 = (bf16[32,4096]{1,0:T(8,128)(2,1)S(1)}, bf16[32,4096]{1,0:T(8,128)(2,1)S(1)}, u32[]{:S(2)}, u32[]{:S(2)}) collective-permute-start(bf16[32,4096]{1,0:T(8,128)(2,1)S(1)} %fence.6.refs_0_), channel_id=1, source_target_pairs={{0,12},{1,13},{2,14},{3,15},{4,0},{5,1},{6,2},{7,3},{8,4},{9,5},{1... | collective-permute-start | bytes 786440 | tf_op jit(solution)/shard_map/ppermute | solution.py:247
  22.3 10.2 %collective-permute-start.6 = (bf16[32,4096]{1,0:T(8,128)(2,1)S(1)}, bf16[32,4096]{1,0:T(8,128)(2,1)S(1)}, u32[]{:S(2)}, u32[]{:S(2)}) collective-permute-start(bf16[32,4096]{1,0:T(8,128)(2,1)S(1)} %collective-permute-done.refs_1_), channel_id=1, source_target_pairs={{0,4},{1,5},{2,6},{3,7},{4,8},{5,9},{6,10},{7,11},{8,12},{9,13},{1... | collective-permute-start | bytes 786440 | tf_op jit(solution)/shard_map/ppermute | solution.py:247
  27.9 6.4 %collective-permute-start.8 = (bf16[32,4096]{1,0:T(8,128)(2,1)S(1)}, bf16[32,4096]{1,0:T(8,128)(2,1)S(1)}, u32[]{:S(2)}, u32[]{:S(2)}) collective-permute-start(bf16[32,4096]{1,0:T(8,128)(2,1)S(1)} %get-tuple-element.30.refs_0_), channel_id=1, source_target_pairs={{0,12},{1,13},{2,14},{3,15},{4,0},{5,1},{6,2},{7,3},{8,4},{9,5},{1... | collective-permute-start | bytes 786440 | tf_op jit(solution)/shard_map/ppermute | solution.py:247
  27.9 15.9 %collective-permute-start.17 = (bf16[32,4096]{1,0:T(8,128)(2,1)S(1)}, bf16[32,4096]{1,0:T(8,128)(2,1)S(1)}, u32[]{:S(2)}, u32[]{:S(2)}) collective-permute-start(bf16[32,4096]{1,0:T(8,128)(2,1)S(1)} %fence.6.refs_0_), channel_id=1, source_target_pairs={{0,2},{1,3},{2,0},{3,1},{4,6},{5,7},{6,4},{7,5},{8,10},{9,11},{10,... | collective-permute-start | bytes 786440 | tf_op jit(solution)/shard_map/ppermute | solution.py:247
  34.3 9.6 %collective-permute-start.7 = (bf16[32,4096]{1,0:T(8,128)(2,1)S(1)}, bf16[32,4096]{1,0:T(8,128)(2,1)S(1)}, u32[]{:S(2)}, u32[]{:S(2)}) collective-permute-start(bf16[32,4096]{1,0:T(8,128)(2,1)S(1)} %fence.8.refs_4_), channel_id=1, source_target_pairs={{0,4},{1,5},{2,6},{3,7},{4,8},{5,9},{6,10},{7,11},{8,12},{9,13},{1... | collective-permute-start | bytes 786440 | tf_op jit(solution)/shard_map/ppermute | solution.py:247
  34.3 13.3 %collective-permute-start.9 = (bf16[32,4096]{1,0:T(8,128)(2,1)S(1)}, bf16[32,4096]{1,0:T(8,128)(2,1)S(1)}, u32[]{:S(2)}, u32[]{:S(2)}) collective-permute-start(bf16[32,4096]{1,0:T(8,128)(2,1)S(1)} %collective-permute-done.8.refs_6_.refs_2_), channel_id=1, source_target_pairs={{0,12},{1,13},{2,14},{3,15},{4,0},{5,1},{6,2},{7,3},{8,4},{9,5},{1... | collective-permute-start | bytes 786440 | tf_op jit(solution)/shard_map/ppermute | solution.py:247
  43.8 9.2 %collective-permute-start.20 = (bf16[32,4096]{1,0:T(8,128)(2,1)S(1)}, bf16[32,4096]{1,0:T(8,128)(2,1)S(1)}, u32[]{:S(2)}, u32[]{:S(2)}) collective-permute-start(bf16[32,4096]{1,0:T(8,128)(2,1)S(1)} %get-tuple-element.40.refs_4_), channel_id=1, source_target_pairs={{0,12},{1,13},{2,14},{3,15},{4,0},{5,1},{6,2},{7,3},{8,4},{9,5},{1... | collective-permute-start | bytes 786440 | tf_op jit(solution)/shard_map/ppermute | solution.py:247
  43.8 13.6 %collective-permute-start.19 = (bf16[32,4096]{1,0:T(8,128)(2,1)S(1)}, bf16[32,4096]{1,0:T(8,128)(2,1)S(1)}, u32[]{:S(2)}, u32[]{:S(2)}) collective-permute-start(bf16[32,4096]{1,0:T(8,128)(2,1)S(1)} %get-tuple-element.40.refs_4_), channel_id=1, source_target_pairs={{0,4},{1,5},{2,6},{3,7},{4,8},{5,9},{6,10},{7,11},{8,12},{9,13},{1... | collective-permute-start | bytes 786440 | tf_op jit(solution)/shard_map/ppermute | solution.py:247
  45.9 12.4 %collective-permute-start.18 = (bf16[32,4096]{1,0:T(8,128)(2,1)S(1)}, bf16[32,4096]{1,0:T(8,128)(2,1)S(1)}, u32[]{:S(2)}, u32[]{:S(2)}) collective-permute-start(bf16[32,4096]{1,0:T(8,128)(2,1)S(1)} %get-tuple-element.39.refs_1_), channel_id=1, source_target_pairs={{0,4},{1,5},{2,6},{3,7},{4,8},{5,9},{6,10},{7,11},{8,12},{9,13},{1... | collective-permute-start | bytes 786440 | tf_op jit(solution)/shard_map/ppermute | solution.py:247
  53.1 6.4 %collective-permute-start.21 = (bf16[32,4096]{1,0:T(8,128)(2,1)S(1)}, bf16[32,4096]{1,0:T(8,128)(2,1)S(1)}, u32[]{:S(2)}, u32[]{:S(2)}) collective-permute-start(bf16[32,4096]{1,0:T(8,128)(2,1)S(1)} %fence.10.refs_6_), channel_id=1, source_target_pairs={{0,12},{1,13},{2,14},{3,15},{4,0},{5,1},{6,2},{7,3},{8,4},{9,5},{1... | collective-permute-start | bytes 786440 | tf_op jit(solution)/shard_map/ppermute | solution.py:247
  54.7 10.3 %collective-permute-start.10 = (bf16[128,768]{1,0:T(8,128)(2,1)S(1)}, bf16[128,768]{1,0:T(8,128)(2,1)S(1)}, u32[]{:S(2)}, u32[]{:S(2)}) collective-permute-start(bf16[128,768]{1,0:T(8,128)(2,1)S(1)} %get-tuple-element.31), channel_id=1, source_target_pairs={{0,48},{1,17},{2,50},{3,19},{4,52},{5,21},{6,54},{7,23},{8,56},{9,... | collective-permute-start | bytes 589832 | tf_op jit(solution)/shard_map/ppermute | solution.py:319
  57.4 7.6 %collective-permute-start.11 = (bf16[128,768]{1,0:T(8,128)(2,1)S(1)}, bf16[128,768]{1,0:T(8,128)(2,1)S(1)}, u32[]{:S(2)}, u32[]{:S(2)}) collective-permute-start(bf16[128,768]{1,0:T(8,128)(2,1)S(1)} %get-tuple-element.32), channel_id=1, source_target_pairs={{0,1},{1,49},{2,3},{3,51},{4,5},{5,53},{6,7},{7,55},{8,9},{9,57},{... | collective-permute-start | bytes 589832 | tf_op jit(solution)/shard_map/ppermute | solution.py:319
  57.4 8.2 %collective-permute-start.12 = (bf16[128,768]{1,0:T(8,128)(2,1)S(1)}, bf16[128,768]{1,0:T(8,128)(2,1)S(1)}, u32[]{:S(2)}, u32[]{:S(2)}) collective-permute-start(bf16[128,768]{1,0:T(8,128)(2,1)S(1)} %get-tuple-element.33), channel_id=1, source_target_pairs={{0,32},{1,16},{2,34},{3,18},{4,36},{5,20},{6,38},{7,22},{8,40},{9,... | collective-permute-start | bytes 589832 | tf_op jit(solution)/shard_map/ppermute | solution.py:319
  65.0 17.6 %copy-start = (s32[768]{0:T(1024)S(1)}, s32[768]{0:T(1024)}, u32[]{:S(2)}) copy-start(s32[768]{0:T(1024)} %param.9) | copy-start | bytes 9220
  65.6 6.9 %collective-permute-start.22 = (bf16[128,768]{1,0:T(8,128)(2,1)S(1)}, bf16[128,768]{1,0:T(8,128)(2,1)S(1)}, u32[]{:S(2)}, u32[]{:S(2)}) collective-permute-start(bf16[128,768]{1,0:T(8,128)(2,1)S(1)} %get-tuple-element.45), channel_id=1, source_target_pairs={{0,48},{1,17},{2,50},{3,19},{4,52},{5,21},{6,54},{7,23},{8,56},{9,... | collective-permute-start | bytes 589832 | tf_op jit(solution)/shard_map/ppermute | solution.py:319
  67.9 5.4 %collective-permute-start.13 = (bf16[128,768]{1,0:T(8,128)(2,1)S(1)}, bf16[128,768]{1,0:T(8,128)(2,1)S(1)}, u32[]{:S(2)}, u32[]{:S(2)}) collective-permute-start(bf16[128,768]{1,0:T(8,128)(2,1)S(1)} %join.2), channel_id=1, source_target_pairs={{1,48},{3,50},{5,52},{7,54},{9,56},{11,58},{13,60},{15,62},{16,1},... | collective-permute-start | bytes 589832 | tf_op jit(solution)/shard_map/ppermute | solution.py:319
  68.6 9.3 %collective-permute-start.23 = (bf16[128,768]{1,0:T(8,128)(2,1)S(1)}, bf16[128,768]{1,0:T(8,128)(2,1)S(1)}, u32[]{:S(2)}, u32[]{:S(2)}) collective-permute-start(bf16[128,768]{1,0:T(8,128)(2,1)S(1)} %get-tuple-element.46), channel_id=1, source_target_pairs={{0,1},{1,49},{2,3},{3,51},{4,5},{5,53},{6,7},{7,55},{8,9},{9,57},{... | collective-permute-start | bytes 589832 | tf_op jit(solution)/shard_map/ppermute | solution.py:319
  71.2 7.4 %collective-permute-start.24 = (bf16[128,768]{1,0:T(8,128)(2,1)S(1)}, bf16[128,768]{1,0:T(8,128)(2,1)S(1)}, u32[]{:S(2)}, u32[]{:S(2)}) collective-permute-start(bf16[128,768]{1,0:T(8,128)(2,1)S(1)} %get-tuple-element.47), channel_id=1, source_target_pairs={{0,32},{1,16},{2,34},{3,18},{4,36},{5,20},{6,38},{7,22},{8,40},{9,... | collective-permute-start | bytes 589832 | tf_op jit(solution)/shard_map/ppermute | solution.py:319
  72.6 6.0 %collective-permute-start.25 = (bf16[128,768]{1,0:T(8,128)(2,1)S(1)}, bf16[128,768]{1,0:T(8,128)(2,1)S(1)}, u32[]{:S(2)}, u32[]{:S(2)}) collective-permute-start(bf16[128,768]{1,0:T(8,128)(2,1)S(1)} %join.3), channel_id=1, source_target_pairs={{1,48},{3,50},{5,52},{7,54},{9,56},{11,58},{13,60},{15,62},{16,1},... | collective-permute-start | bytes 589832 | tf_op jit(solution)/shard_map/ppermute | solution.py:319
  73.5 8.0 %collective-permute-start.14 = (bf16[32,768]{1,0:T(8,128)(2,1)S(1)}, bf16[32,768]{1,0:T(8,128)(2,1)S(1)}, u32[]{:S(2)}, u32[]{:S(2)}) collective-permute-start(bf16[32,768]{1,0:T(8,128)(2,1)S(1)} %get-tuple-element.36), channel_id=1, source_target_pairs={{0,64},{16,80},{32,96},{48,112},{64,128},{80,144},{96,160},{112,17... | collective-permute-start | bytes 147464 | tf_op jit(solution)/shard_map/ppermute | solution.py:350
  74.5 8.5 %collective-permute-start.15 = (bf16[32,768]{1,0:T(8,128)(2,1)S(1)}, bf16[32,768]{1,0:T(8,128)(2,1)S(1)}, u32[]{:S(2)}, u32[]{:S(2)}) collective-permute-start(bf16[32,768]{1,0:T(8,128)(2,1)S(1)} %get-tuple-element.37), channel_id=1, source_target_pairs={{0,128},{16,144},{32,160},{48,176},{64,192},{80,208},{96,224},{112... | collective-permute-start | bytes 147464 | tf_op jit(solution)/shard_map/ppermute | solution.py:350
  77.9 5.1 %collective-permute-start.16 = (bf16[32,768]{1,0:T(8,128)(2,1)S(1)}, bf16[32,768]{1,0:T(8,128)(2,1)S(1)}, u32[]{:S(2)}, u32[]{:S(2)}) collective-permute-start(bf16[32,768]{1,0:T(8,128)(2,1)S(1)} %get-tuple-element.38), channel_id=1, source_target_pairs={{0,192},{16,208},{32,224},{48,240},{64,0},{80,16},{96,32},{112,48}... | collective-permute-start | bytes 147464 | tf_op jit(solution)/shard_map/ppermute | solution.py:350
  78.7 4.6 %collective-permute-start.26 = (bf16[32,768]{1,0:T(8,128)(2,1)S(1)}, bf16[32,768]{1,0:T(8,128)(2,1)S(1)}, u32[]{:S(2)}, u32[]{:S(2)}) collective-permute-start(bf16[32,768]{1,0:T(8,128)(2,1)S(1)} %get-tuple-element.50), channel_id=1, source_target_pairs={{0,64},{16,80},{32,96},{48,112},{64,128},{80,144},{96,160},{112,17... | collective-permute-start | bytes 147464 | tf_op jit(solution)/shard_map/ppermute | solution.py:350
  80.1 5.4 %collective-permute-start.27 = (bf16[32,768]{1,0:T(8,128)(2,1)S(1)}, bf16[32,768]{1,0:T(8,128)(2,1)S(1)}, u32[]{:S(2)}, u32[]{:S(2)}) collective-permute-start(bf16[32,768]{1,0:T(8,128)(2,1)S(1)} %get-tuple-element.51), channel_id=1, source_target_pairs={{0,128},{16,144},{32,160},{48,176},{64,192},{80,208},{96,224},{112... | collective-permute-start | bytes 147464 | tf_op jit(solution)/shard_map/ppermute | solution.py:350
  81.4 6.0 %collective-permute-start.28 = (bf16[32,768]{1,0:T(8,128)(2,1)S(1)}, bf16[32,768]{1,0:T(8,128)(2,1)S(1)}, u32[]{:S(2)}, u32[]{:S(2)}) collective-permute-start(bf16[32,768]{1,0:T(8,128)(2,1)S(1)} %get-tuple-element.52), channel_id=1, source_target_pairs={{0,192},{16,208},{32,224},{48,240},{64,0},{80,16},{96,32},{112,48}... | collective-permute-start | bytes 147464 | tf_op jit(solution)/shard_map/ppermute | solution.py:350

commit v11 on v8

--- a/solution.py
+++ b/solution.py
@@ -286,7 +286,7 @@
     a_opposite = up(a_below)
     far_a_above, far_a_below = down(far_a), up(far_a)
     far_a_opposite = down(far_a_above)
-    far_b, b_below = after((far_b, b_below), far_a_above, far_a_below)
+    far_b, b_below = after((far_b, b_below), far_a_above, a_opposite)
     b_opposite = up(b_below)
     far_b_above, far_b_below = down(far_b), up(far_b)
     a_blocks = [a, a_below, a_above, a_opposite, far_a, far_a_below, far_a_above, far_a_opposite]

time: 89.6 us -> 89.6 us (level)
  no operation moved by 1% of the time
where the time goes in v11:
time: 89.6 us; the launch traced here: 88 us
  starting transfers between devices  44.1 us (49%)
  waiting for transfers between devices  25.7 us (29%)
  Pallas kernels  17.6 us (20%)
    ppermute x14, starting transfers between devices, along(): return lax.ppermute(value, 'group', group_pairs(move))  28.5 us
    ppermute x14, waiting for transfers between devices, along(): return lax.ppermute(value, 'group', group_pairs(move))  15.4 us
    pallas_call x2, Pallas kernels, partial_scores(): pl.pallas_call(score_kernel, out_shape=[jax.ShapeDtypeStruct((4 * ROWS, H...  10.9 us
    ppermute x8, starting transfers between devices, send(): return lax.ppermute(value, ('store', 'group'), all_pairs(move))  10.2 us
    ppermute x6, starting transfers between devices, on_device(): lax.ppermute(send, 'store', store_pairs(lambda x, z: (x, z + k)))  5.36 us
    ppermute x6, waiting for transfers between devices, on_device(): lax.ppermute(send, 'store', store_pairs(lambda x, z: (x, z + k)))  5.26 us
    pallas_call x2, Pallas kernels, query_grads(): pl.pallas_call(functools.partial(grad_kernel, chunk * ROWS), out_shape=ja...  5.12 us
    ppermute x8, waiting for transfers between devices, send(): return lax.ppermute(value, ('store', 'group'), all_pairs(move))  5.06 us
  transfers between devices with their start and end apart: 29, of which 13 were waited for; matrix products, arithmetic and copies ran while one was open for 0% of the time, Pallas kernels for 19%

profile of v11, /device:TPU:32, one launch (start us, length us, event | category | flops | bytes accessed | tf_op | source)
XLA Modules:
  0.0 88.0 jit_solution(8881336815143385710)
XLA Ops:
  0.0 2.5 %query_grads.2.refs_0_ = bf16[32,4096]{1,0:T(8,128)(2,1)S(1)} custom-call(s32[64]{0:T(128)} %lengths_hbm.3, bf16[64,1,64,256]{3,2,1,0:T(8,128)(2,1)} %acts_hbm.3, bf16[64,1,64,256]{3,2,1,0:T(8,128)(2,1)} %grads_hbm.3), custom_call_target="tpu_custom_call" | custom-call | tf_op jit(solution)/shard_map/query_grads/pallas_call | solution.py:81
  2.5 6.3 %collective-permute-start = (bf16[32,4096]{1,0:T(8,128)(2,1)S(1)}, bf16[32,4096]{1,0:T(8,128)(2,1)S(1)}, u32[]{:S(2)}, u32[]{:S(2)}) collective-permute-start(bf16[32,4096]{1,0:T(8,128)(2,1)S(1)} %query_grads.2.refs_0_), channel_id=1, source_target_pairs={{0,2},{1,3},{2,0},{3,1},{4,6},{5,7},{6,4},{7,5},{8,10},{9,11},{10,... | collective-permute-start | bytes 786440 | tf_op jit(solution)/shard_map/ppermute | solution.py:247
  8.9 1.6 %collective-permute-start.1 = (bf16[32,4096]{1,0:T(8,128)(2,1)S(1)}, bf16[32,4096]{1,0:T(8,128)(2,1)S(1)}, u32[]{:S(2)}, u32[]{:S(2)}) collective-permute-start(bf16[32,4096]{1,0:T(8,128)(2,1)S(1)} %query_grads.2.refs_0_), channel_id=1, source_target_pairs={{0,4},{1,5},{2,6},{3,7},{4,8},{5,9},{6,10},{7,11},{8,12},{9,13},{1... | collective-permute-start | bytes 786440 | tf_op jit(solution)/shard_map/ppermute | solution.py:247
  10.4 1.7 %collective-permute-start.2 = (bf16[32,4096]{1,0:T(8,128)(2,1)S(1)}, bf16[32,4096]{1,0:T(8,128)(2,1)S(1)}, u32[]{:S(2)}, u32[]{:S(2)}) collective-permute-start(bf16[32,4096]{1,0:T(8,128)(2,1)S(1)} %query_grads.2.refs_0_), channel_id=1, source_target_pairs={{0,12},{1,13},{2,14},{3,15},{4,0},{5,1},{6,2},{7,3},{8,4},{9,5},{1... | collective-permute-start | bytes 786440 | tf_op jit(solution)/shard_map/ppermute | solution.py:247
  12.1 2.6 %query_grads.3.refs_0_ = bf16[32,4096]{1,0:T(8,128)(2,1)S(1)} custom-call(s32[64]{0:T(128)} %lengths_hbm.3, bf16[64,1,64,256]{3,2,1,0:T(8,128)(2,1)} %acts_hbm.3, bf16[64,1,64,256]{3,2,1,0:T(8,128)(2,1)} %grads_hbm.3), custom_call_target="tpu_custom_call" | custom-call | tf_op jit(solution)/shard_map/query_grads/pallas_call | solution.py:81
  15.2 2.9 %collective-permute-start.5 = (bf16[32,4096]{1,0:T(8,128)(2,1)S(1)}, bf16[32,4096]{1,0:T(8,128)(2,1)S(1)}, u32[]{:S(2)}, u32[]{:S(2)}) collective-permute-start(bf16[32,4096]{1,0:T(8,128)(2,1)S(1)} %fence.5.refs_0_), channel_id=1, source_target_pairs={{0,12},{1,13},{2,14},{3,15},{4,0},{5,1},{6,2},{7,3},{8,4},{9,5},{1... | collective-permute-start | bytes 786440 | tf_op jit(solution)/shard_map/ppermute | solution.py:247
  18.1 3.5 %collective-permute-done.refs_0_ = bf16[32,4096]{1,0:T(8,128)(2,1)S(1)} collective-permute-done((bf16[32,4096]{1,0:T(8,128)(2,1)S(1)}, bf16[32,4096]{1,0:T(8,128)(2,1)S(1)}, u32[]{:S(2)}, u32[]{:S(2)}) %collective-permute-start) | collective-permute-done | bytes 262176 | tf_op jit(solution)/shard_map/ppermute | solution.py:247
  21.6 2.6 %collective-permute-done.4.refs_3_.refs_1_ = bf16[32,4096]{1,0:T(8,128)(2,1)S(1)} collective-permute-done((bf16[32,4096]{1,0:T(8,128)(2,1)S(1)}, bf16[32,4096]{1,0:T(8,128)(2,1)S(1)}, u32[]{:S(2)}, u32[]{:S(2)}) %collective-permute-start.4) | collective-permute-done | bytes 262176 | tf_op jit(solution)/shard_map/ppermute | solution.py:247
  24.2 2.9 %collective-permute-start.8 = (bf16[32,4096]{1,0:T(8,128)(2,1)S(1)}, bf16[32,4096]{1,0:T(8,128)(2,1)S(1)}, u32[]{:S(2)}, u32[]{:S(2)}) collective-permute-start(bf16[32,4096]{1,0:T(8,128)(2,1)S(1)} %get-tuple-element.32.refs_4_), channel_id=1, source_target_pairs={{0,12},{1,13},{2,14},{3,15},{4,0},{5,1},{6,2},{7,3},{8,4},{9,5},{1... | collective-permute-start | bytes 786440 | tf_op jit(solution)/shard_map/ppermute | solution.py:247
  27.2 3.1 %collective-permute-start.17 = (bf16[32,4096]{1,0:T(8,128)(2,1)S(1)}, bf16[32,4096]{1,0:T(8,128)(2,1)S(1)}, u32[]{:S(2)}, u32[]{:S(2)}) collective-permute-start(bf16[32,4096]{1,0:T(8,128)(2,1)S(1)} %fence.5.refs_0_), channel_id=1, source_target_pairs={{0,2},{1,3},{2,0},{3,1},{4,6},{5,7},{6,4},{7,5},{8,10},{9,11},{10,... | collective-permute-start | bytes 786440 | tf_op jit(solution)/shard_map/ppermute | solution.py:247
  31.6 3.7 %collective-permute-start.9 = (bf16[32,4096]{1,0:T(8,128)(2,1)S(1)}, bf16[32,4096]{1,0:T(8,128)(2,1)S(1)}, u32[]{:S(2)}, u32[]{:S(2)}) collective-permute-start(bf16[32,4096]{1,0:T(8,128)(2,1)S(1)} %collective-permute-done.8.refs_6_.refs_2_), channel_id=1, source_target_pairs={{0,12},{1,13},{2,14},{3,15},{4,0},{5,1},{6,2},{7,3},{8,4},{9,5},{1... | collective-permute-start | bytes 786440 | tf_op jit(solution)/shard_map/ppermute | solution.py:247
  35.3 8.0 %collective-permute-done.17.refs_0_ = bf16[32,4096]{1,0:T(8,128)(2,1)S(1)} collective-permute-done((bf16[32,4096]{1,0:T(8,128)(2,1)S(1)}, bf16[32,4096]{1,0:T(8,128)(2,1)S(1)}, u32[]{:S(2)}, u32[]{:S(2)}) %collective-permute-start.17) | collective-permute-done | bytes 262176 | tf_op jit(solution)/shard_map/ppermute | solution.py:247
  43.4 0.9 %collective-permute-start.20 = (bf16[32,4096]{1,0:T(8,128)(2,1)S(1)}, bf16[32,4096]{1,0:T(8,128)(2,1)S(1)}, u32[]{:S(2)}, u32[]{:S(2)}) collective-permute-start(bf16[32,4096]{1,0:T(8,128)(2,1)S(1)} %get-tuple-element.42.refs_4_), channel_id=1, source_target_pairs={{0,12},{1,13},{2,14},{3,15},{4,0},{5,1},{6,2},{7,3},{8,4},{9,5},{1... | collective-permute-start | bytes 786440 | tf_op jit(solution)/shard_map/ppermute | solution.py:247
  44.3 1.1 %collective-permute-start.19 = (bf16[32,4096]{1,0:T(8,128)(2,1)S(1)}, bf16[32,4096]{1,0:T(8,128)(2,1)S(1)}, u32[]{:S(2)}, u32[]{:S(2)}) collective-permute-start(bf16[32,4096]{1,0:T(8,128)(2,1)S(1)} %get-tuple-element.42.refs_4_), channel_id=1, source_target_pairs={{0,4},{1,5},{2,6},{3,7},{4,8},{5,9},{6,10},{7,11},{8,12},{9,13},{1... | collective-permute-start | bytes 786440 | tf_op jit(solution)/shard_map/ppermute | solution.py:247
  45.5 5.5 %partial_scores.2 = (bf16[128,768]{1,0:T(8,128)(2,1)S(1)}, bf16[128,768]{1,0:T(8,128)(2,1)S(1)}, bf16[128,768]{1,0:T(8,128)(2,1)S(1)}, bf16[128,768]{1,0:T(8,128)(2,1)S(1)}) custom-call(bf16[32,4096]{1,0:T(8,128)(2,1)S(1)} %query_grads.2.refs_0_, bf16[32,4096]{1,0:T(8,128)(2,1)S(1)} %get-tuple-element.30.refs_1_, ...), custom_call_target="tpu_custom_call" | custom-call | flops 1 | bytes 1 | tf_op jit(solution)/shard_map/partial_scores/pallas_call | solution.py:148
  51.0 3.3 %collective-permute-start.21 = (bf16[32,4096]{1,0:T(8,128)(2,1)S(1)}, bf16[32,4096]{1,0:T(8,128)(2,1)S(1)}, u32[]{:S(2)}, u32[]{:S(2)}) collective-permute-start(bf16[32,4096]{1,0:T(8,128)(2,1)S(1)} %fence.8.refs_6_), channel_id=1, source_target_pairs={{0,12},{1,13},{2,14},{3,15},{4,0},{5,1},{6,2},{7,3},{8,4},{9,5},{1... | collective-permute-start | bytes 786440 | tf_op jit(solution)/shard_map/ppermute | solution.py:247
  54.3 2.7 %collective-permute-start.10 = (bf16[128,768]{1,0:T(8,128)(2,1)S(1)}, bf16[128,768]{1,0:T(8,128)(2,1)S(1)}, u32[]{:S(2)}, u32[]{:S(2)}) collective-permute-start(bf16[128,768]{1,0:T(8,128)(2,1)S(1)} %get-tuple-element.33), channel_id=1, source_target_pairs={{0,48},{1,17},{2,50},{3,19},{4,52},{5,21},{6,54},{7,23},{8,56},{9,... | collective-permute-start | bytes 589832 | tf_op jit(solution)/shard_map/ppermute | solution.py:317
  57.0 0.8 collective-permute-start.12
  58.2 5.4 %partial_scores.3 = (bf16[128,768]{1,0:T(8,128)(2,1)S(1)}, bf16[128,768]{1,0:T(8,128)(2,1)S(1)}, bf16[128,768]{1,0:T(8,128)(2,1)S(1)}, bf16[128,768]{1,0:T(8,128)(2,1)S(1)}) custom-call(bf16[32,4096]{1,0:T(8,128)(2,1)S(1)} %fence.5.refs_0_, bf16[32,4096]{1,0:T(8,128)(2,1)S(1)} %get-tuple-element.41.refs_1_, ...), custom_call_target="tpu_custom_call" | custom-call | flops 1 | bytes 1 | tf_op jit(solution)/shard_map/partial_scores/pallas_call | solution.py:148
  63.7 1.4 %collective-permute-done.12.a_ref.refs_6_ = bf16[128,768]{1,0:T(8,128)(2,1)S(1)} collective-permute-done((bf16[128,768]{1,0:T(8,128)(2,1)S(1)}, bf16[128,768]{1,0:T(8,128)(2,1)S(1)}, u32[]{:S(2)}, u32[]{:S(2)}) %collective-permute-start.12) | collective-permute-done | bytes 196640 | tf_op jit(solution)/shard_map/ppermute | solution.py:317
  65.1 1.3 %collective-permute-start.22 = (bf16[128,768]{1,0:T(8,128)(2,1)S(1)}, bf16[128,768]{1,0:T(8,128)(2,1)S(1)}, u32[]{:S(2)}, u32[]{:S(2)}) collective-permute-start(bf16[128,768]{1,0:T(8,128)(2,1)S(1)} %get-tuple-element.47), channel_id=1, source_target_pairs={{0,48},{1,17},{2,50},{3,19},{4,52},{5,21},{6,54},{7,23},{8,56},{9,... | collective-permute-start | bytes 589832 | tf_op jit(solution)/shard_map/ppermute | solution.py:317
  67.2 3.6 %collective-permute-start.23 = (bf16[128,768]{1,0:T(8,128)(2,1)S(1)}, bf16[128,768]{1,0:T(8,128)(2,1)S(1)}, u32[]{:S(2)}, u32[]{:S(2)}) collective-permute-start(bf16[128,768]{1,0:T(8,128)(2,1)S(1)} %get-tuple-element.48), channel_id=1, source_target_pairs={{0,1},{1,49},{2,3},{3,51},{4,5},{5,53},{6,7},{7,55},{8,9},{9,57},{... | collective-permute-start | bytes 589832 | tf_op jit(solution)/shard_map/ppermute | solution.py:317
  73.0 1.0 %collective-permute-start.14 = (bf16[32,768]{1,0:T(8,128)(2,1)S(1)}, bf16[32,768]{1,0:T(8,128)(2,1)S(1)}, u32[]{:S(2)}, u32[]{:S(2)}) collective-permute-start(bf16[32,768]{1,0:T(8,128)(2,1)S(1)} %get-tuple-element.38), channel_id=1, source_target_pairs={{0,64},{16,80},{32,96},{48,112},{64,128},{80,144},{96,160},{112,17... | collective-permute-start | bytes 147464 | tf_op jit(solution)/shard_map/ppermute | solution.py:348
  74.0 0.9 collective-permute-start.15
  74.9 1.5 %collective-permute-done.23.c_ref = bf16[128,768]{1,0:T(8,128)(2,1)S(1)} collective-permute-done((bf16[128,768]{1,0:T(8,128)(2,1)S(1)}, bf16[128,768]{1,0:T(8,128)(2,1)S(1)}, u32[]{:S(2)}, u32[]{:S(2)}) %collective-permute-start.23) | collective-permute-done | bytes 196640 | tf_op jit(solution)/shard_map/ppermute | solution.py:317
  76.9 1.2 %collective-permute-done.24.a_ref = bf16[128,768]{1,0:T(8,128)(2,1)S(1)} collective-permute-done((bf16[128,768]{1,0:T(8,128)(2,1)S(1)}, bf16[128,768]{1,0:T(8,128)(2,1)S(1)}, u32[]{:S(2)}, u32[]{:S(2)}) %collective-permute-start.24) | collective-permute-done | bytes 196640 | tf_op jit(solution)/shard_map/ppermute | solution.py:317
  78.2 1.0 %collective-permute-start.26 = (bf16[32,768]{1,0:T(8,128)(2,1)S(1)}, bf16[32,768]{1,0:T(8,128)(2,1)S(1)}, u32[]{:S(2)}, u32[]{:S(2)}) collective-permute-start(bf16[32,768]{1,0:T(8,128)(2,1)S(1)} %get-tuple-element.52), channel_id=1, source_target_pairs={{0,64},{16,80},{32,96},{48,112},{64,128},{80,144},{96,160},{112,17... | collective-permute-start | bytes 147464 | tf_op jit(solution)/shard_map/ppermute | solution.py:348
  79.3 2.0 %collective-permute-start.27 = (bf16[32,768]{1,0:T(8,128)(2,1)S(1)}, bf16[32,768]{1,0:T(8,128)(2,1)S(1)}, u32[]{:S(2)}, u32[]{:S(2)}) collective-permute-start(bf16[32,768]{1,0:T(8,128)(2,1)S(1)} %get-tuple-element.53), channel_id=1, source_target_pairs={{0,128},{16,144},{32,160},{48,176},{64,192},{80,208},{96,224},{112... | collective-permute-start | bytes 147464 | tf_op jit(solution)/shard_map/ppermute | solution.py:348
  81.7 1.1 %collective-permute-done.26.refs_5_ = bf16[32,768]{1,0:T(8,128)(2,1)S(1)} collective-permute-done((bf16[32,768]{1,0:T(8,128)(2,1)S(1)}, bf16[32,768]{1,0:T(8,128)(2,1)S(1)}, u32[]{:S(2)}, u32[]{:S(2)}) %collective-permute-start.26) | collective-permute-done | bytes 49184 | tf_op jit(solution)/shard_map/ppermute | solution.py:348
  82.8 2.0 %collective-permute-done.27.refs_6_ = bf16[32,768]{1,0:T(8,128)(2,1)S(1)} collective-permute-done((bf16[32,768]{1,0:T(8,128)(2,1)S(1)}, bf16[32,768]{1,0:T(8,128)(2,1)S(1)}, u32[]{:S(2)}, u32[]{:S(2)}) %collective-permute-start.27) | collective-permute-done | bytes 49184 | tf_op jit(solution)/shard_map/ppermute | solution.py:348
  84.9 2.1 %collective-permute-done.28.refs_7_ = bf16[32,768]{1,0:T(8,128)(2,1)S(1)} collective-permute-done((bf16[32,768]{1,0:T(8,128)(2,1)S(1)}, bf16[32,768]{1,0:T(8,128)(2,1)S(1)}, u32[]{:S(2)}, u32[]{:S(2)}) %collective-permute-start.28) | collective-permute-done | bytes 49184 | tf_op jit(solution)/shard_map/ppermute | solution.py:348
  86.9 1.1 %final_sum.1 = f32[64,768]{1,0:T(8,128)} custom-call(f32[32,768]{1,0:T(8,128)S(1)} %get-tuple-element.37.refs_0_, bf16[32,768]{1,0:T(8,128)(2,1)S(1)} %collective-permute-done.14.refs_1_, bf16[32,768]{1,0:T(8,128)(2,1)S(1)} %collective-permute-done.15.refs_2_, bf16[32,768]{1,0:T(8,128)(2,1)S(1)} %collective-permute-done.16.refs_3_, ...), custom_call_target="tpu_custom_call" | custom-call | tf_op jit(solution)/shard_map/final_sum/pallas_call | solution.py:214
  (48 shorter events, 6.2 us)
Async XLA Ops:
  0.0 14.8 %collective-permute-start.3 = (bf16[768,4096]{1,0:T(8,128)(2,1)}, bf16[768,4096]{1,0:T(8,128)(2,1)S(1)}, u32[]{:S(2)}, u32[]{:S(2)}) collective-permute-start(bf16[768,4096]{1,0:T(8,128)(2,1)} %bitcast.1), channel_id=1, source_target_pairs={{0,1},{1,0},{2,3},{3,2},{4,5},{5,4},{6,7},{7,6},{8,9},{9,8},{10,11... | collective-permute-start | bytes 18874376 | tf_op jit(solution)/shard_map/ppermute | solution.py:332
  2.5 19.1 %collective-permute-start = (bf16[32,4096]{1,0:T(8,128)(2,1)S(1)}, bf16[32,4096]{1,0:T(8,128)(2,1)S(1)}, u32[]{:S(2)}, u32[]{:S(2)}) collective-permute-start(bf16[32,4096]{1,0:T(8,128)(2,1)S(1)} %query_grads.2.refs_0_), channel_id=1, source_target_pairs={{0,2},{1,3},{2,0},{3,1},{4,6},{5,7},{6,4},{7,5},{8,10},{9,11},{10,... | collective-permute-start | bytes 786440 | tf_op jit(solution)/shard_map/ppermute | solution.py:247
  8.9 12.7 %collective-permute-start.1 = (bf16[32,4096]{1,0:T(8,128)(2,1)S(1)}, bf16[32,4096]{1,0:T(8,128)(2,1)S(1)}, u32[]{:S(2)}, u32[]{:S(2)}) collective-permute-start(bf16[32,4096]{1,0:T(8,128)(2,1)S(1)} %query_grads.2.refs_0_), channel_id=1, source_target_pairs={{0,4},{1,5},{2,6},{3,7},{4,8},{5,9},{6,10},{7,11},{8,12},{9,13},{1... | collective-permute-start | bytes 786440 | tf_op jit(solution)/shard_map/ppermute | solution.py:247
  10.4 11.1 %collective-permute-start.2 = (bf16[32,4096]{1,0:T(8,128)(2,1)S(1)}, bf16[32,4096]{1,0:T(8,128)(2,1)S(1)}, u32[]{:S(2)}, u32[]{:S(2)}) collective-permute-start(bf16[32,4096]{1,0:T(8,128)(2,1)S(1)} %query_grads.2.refs_0_), channel_id=1, source_target_pairs={{0,12},{1,13},{2,14},{3,15},{4,0},{5,1},{6,2},{7,3},{8,4},{9,5},{1... | collective-permute-start | bytes 786440 | tf_op jit(solution)/shard_map/ppermute | solution.py:247
  12.1 33.4 %slice-start = ((s8[6291456]{0:T(1024)(128)(4,1)}), s8[4194304]{0:T(1024)(128)(4,1)S(1)}, s32[]{:S(2)}) async-start(s8[6291456]{0:T(1024)(128)(4,1)} %bitcast.2), calls=%async_computation | async-start | bytes 8388608
  14.7 30.7 %slice-start.1 = ((s8[6291456]{0:T(1024)(128)(4,1)}), s8[2097152]{0:T(1024)(128)(4,1)S(1)}, s32[]{:S(2)}) async-start(s8[6291456]{0:T(1024)(128)(4,1)} %bitcast.2), calls=%async_computation.1 | async-start | bytes 4194304
  14.8 9.4 %collective-permute-start.4 = (bf16[32,4096]{1,0:T(8,128)(2,1)S(1)}, bf16[32,4096]{1,0:T(8,128)(2,1)S(1)}, u32[]{:S(2)}, u32[]{:S(2)}) collective-permute-start(bf16[32,4096]{1,0:T(8,128)(2,1)S(1)} %fence.5.refs_0_), channel_id=1, source_target_pairs={{0,4},{1,5},{2,6},{3,7},{4,8},{5,9},{6,10},{7,11},{8,12},{9,13},{1... | collective-permute-start | bytes 786440 | tf_op jit(solution)/shard_map/ppermute | solution.py:247
  15.2 9.0 %collective-permute-start.5 = (bf16[32,4096]{1,0:T(8,128)(2,1)S(1)}, bf16[32,4096]{1,0:T(8,128)(2,1)S(1)}, u32[]{:S(2)}, u32[]{:S(2)}) collective-permute-start(bf16[32,4096]{1,0:T(8,128)(2,1)S(1)} %fence.5.refs_0_), channel_id=1, source_target_pairs={{0,12},{1,13},{2,14},{3,15},{4,0},{5,1},{6,2},{7,3},{8,4},{9,5},{1... | collective-permute-start | bytes 786440 | tf_op jit(solution)/shard_map/ppermute | solution.py:247
  24.2 7.4 %collective-permute-start.8 = (bf16[32,4096]{1,0:T(8,128)(2,1)S(1)}, bf16[32,4096]{1,0:T(8,128)(2,1)S(1)}, u32[]{:S(2)}, u32[]{:S(2)}) collective-permute-start(bf16[32,4096]{1,0:T(8,128)(2,1)S(1)} %get-tuple-element.32.refs_4_), channel_id=1, source_target_pairs={{0,12},{1,13},{2,14},{3,15},{4,0},{5,1},{6,2},{7,3},{8,4},{9,5},{1... | collective-permute-start | bytes 786440 | tf_op jit(solution)/shard_map/ppermute | solution.py:247
  27.2 16.2 %collective-permute-start.17 = (bf16[32,4096]{1,0:T(8,128)(2,1)S(1)}, bf16[32,4096]{1,0:T(8,128)(2,1)S(1)}, u32[]{:S(2)}, u32[]{:S(2)}) collective-permute-start(bf16[32,4096]{1,0:T(8,128)(2,1)S(1)} %fence.5.refs_0_), channel_id=1, source_target_pairs={{0,2},{1,3},{2,0},{3,1},{4,6},{5,7},{6,4},{7,5},{8,10},{9,11},{10,... | collective-permute-start | bytes 786440 | tf_op jit(solution)/shard_map/ppermute | solution.py:247
  30.3 13.1 %collective-permute-start.6 = (bf16[32,4096]{1,0:T(8,128)(2,1)S(1)}, bf16[32,4096]{1,0:T(8,128)(2,1)S(1)}, u32[]{:S(2)}, u32[]{:S(2)}) collective-permute-start(bf16[32,4096]{1,0:T(8,128)(2,1)S(1)} %get-tuple-element.30.refs_1_), channel_id=1, source_target_pairs={{0,4},{1,5},{2,6},{3,7},{4,8},{5,9},{6,10},{7,11},{8,12},{9,13},{1... | collective-permute-start | bytes 786440 | tf_op jit(solution)/shard_map/ppermute | solution.py:247
  30.3 15.2 %collective-permute-start.7 = (bf16[32,4096]{1,0:T(8,128)(2,1)S(1)}, bf16[32,4096]{1,0:T(8,128)(2,1)S(1)}, u32[]{:S(2)}, u32[]{:S(2)}) collective-permute-start(bf16[32,4096]{1,0:T(8,128)(2,1)S(1)} %get-tuple-element.32.refs_4_), channel_id=1, source_target_pairs={{0,4},{1,5},{2,6},{3,7},{4,8},{5,9},{6,10},{7,11},{8,12},{9,13},{1... | collective-permute-start | bytes 786440 | tf_op jit(solution)/shard_map/ppermute | solution.py:247
  31.6 13.8 %collective-permute-start.9 = (bf16[32,4096]{1,0:T(8,128)(2,1)S(1)}, bf16[32,4096]{1,0:T(8,128)(2,1)S(1)}, u32[]{:S(2)}, u32[]{:S(2)}) collective-permute-start(bf16[32,4096]{1,0:T(8,128)(2,1)S(1)} %collective-permute-done.8.refs_6_.refs_2_), channel_id=1, source_target_pairs={{0,12},{1,13},{2,14},{3,15},{4,0},{5,1},{6,2},{7,3},{8,4},{9,5},{1... | collective-permute-start | bytes 786440 | tf_op jit(solution)/shard_map/ppermute | solution.py:247
  43.4 7.6 %collective-permute-start.20 = (bf16[32,4096]{1,0:T(8,128)(2,1)S(1)}, bf16[32,4096]{1,0:T(8,128)(2,1)S(1)}, u32[]{:S(2)}, u32[]{:S(2)}) collective-permute-start(bf16[32,4096]{1,0:T(8,128)(2,1)S(1)} %get-tuple-element.42.refs_4_), channel_id=1, source_target_pairs={{0,12},{1,13},{2,14},{3,15},{4,0},{5,1},{6,2},{7,3},{8,4},{9,5},{1... | collective-permute-start | bytes 786440 | tf_op jit(solution)/shard_map/ppermute | solution.py:247
  44.3 12.7 %collective-permute-start.19 = (bf16[32,4096]{1,0:T(8,128)(2,1)S(1)}, bf16[32,4096]{1,0:T(8,128)(2,1)S(1)}, u32[]{:S(2)}, u32[]{:S(2)}) collective-permute-start(bf16[32,4096]{1,0:T(8,128)(2,1)S(1)} %get-tuple-element.42.refs_4_), channel_id=1, source_target_pairs={{0,4},{1,5},{2,6},{3,7},{4,8},{5,9},{6,10},{7,11},{8,12},{9,13},{1... | collective-permute-start | bytes 786440 | tf_op jit(solution)/shard_map/ppermute | solution.py:247
  45.4 12.7 %collective-permute-start.18 = (bf16[32,4096]{1,0:T(8,128)(2,1)S(1)}, bf16[32,4096]{1,0:T(8,128)(2,1)S(1)}, u32[]{:S(2)}, u32[]{:S(2)}) collective-permute-start(bf16[32,4096]{1,0:T(8,128)(2,1)S(1)} %get-tuple-element.41.refs_1_), channel_id=1, source_target_pairs={{0,4},{1,5},{2,6},{3,7},{4,8},{5,9},{6,10},{7,11},{8,12},{9,13},{1... | collective-permute-start | bytes 786440 | tf_op jit(solution)/shard_map/ppermute | solution.py:247
  51.0 7.2 %collective-permute-start.21 = (bf16[32,4096]{1,0:T(8,128)(2,1)S(1)}, bf16[32,4096]{1,0:T(8,128)(2,1)S(1)}, u32[]{:S(2)}, u32[]{:S(2)}) collective-permute-start(bf16[32,4096]{1,0:T(8,128)(2,1)S(1)} %fence.8.refs_6_), channel_id=1, source_target_pairs={{0,12},{1,13},{2,14},{3,15},{4,0},{5,1},{6,2},{7,3},{8,4},{9,5},{1... | collective-permute-start | bytes 786440 | tf_op jit(solution)/shard_map/ppermute | solution.py:247
  54.3 9.4 %collective-permute-start.10 = (bf16[128,768]{1,0:T(8,128)(2,1)S(1)}, bf16[128,768]{1,0:T(8,128)(2,1)S(1)}, u32[]{:S(2)}, u32[]{:S(2)}) collective-permute-start(bf16[128,768]{1,0:T(8,128)(2,1)S(1)} %get-tuple-element.33), channel_id=1, source_target_pairs={{0,48},{1,17},{2,50},{3,19},{4,52},{5,21},{6,54},{7,23},{8,56},{9,... | collective-permute-start | bytes 589832 | tf_op jit(solution)/shard_map/ppermute | solution.py:317
  57.0 6.7 %collective-permute-start.11 = (bf16[128,768]{1,0:T(8,128)(2,1)S(1)}, bf16[128,768]{1,0:T(8,128)(2,1)S(1)}, u32[]{:S(2)}, u32[]{:S(2)}) collective-permute-start(bf16[128,768]{1,0:T(8,128)(2,1)S(1)} %get-tuple-element.34), channel_id=1, source_target_pairs={{0,1},{1,49},{2,3},{3,51},{4,5},{5,53},{6,7},{7,55},{8,9},{9,57},{... | collective-permute-start | bytes 589832 | tf_op jit(solution)/shard_map/ppermute | solution.py:317
  57.0 8.2 %collective-permute-start.12 = (bf16[128,768]{1,0:T(8,128)(2,1)S(1)}, bf16[128,768]{1,0:T(8,128)(2,1)S(1)}, u32[]{:S(2)}, u32[]{:S(2)}) collective-permute-start(bf16[128,768]{1,0:T(8,128)(2,1)S(1)} %get-tuple-element.35), channel_id=1, source_target_pairs={{0,32},{1,16},{2,34},{3,18},{4,36},{5,20},{6,38},{7,22},{8,40},{9,... | collective-permute-start | bytes 589832 | tf_op jit(solution)/shard_map/ppermute | solution.py:317
  63.7 17.6 %copy-start = (s32[768]{0:T(1024)S(1)}, s32[768]{0:T(1024)}, u32[]{:S(2)}) copy-start(s32[768]{0:T(1024)} %param.9) | copy-start | bytes 9220
  65.1 6.9 %collective-permute-start.22 = (bf16[128,768]{1,0:T(8,128)(2,1)S(1)}, bf16[128,768]{1,0:T(8,128)(2,1)S(1)}, u32[]{:S(2)}, u32[]{:S(2)}) collective-permute-start(bf16[128,768]{1,0:T(8,128)(2,1)S(1)} %get-tuple-element.47), channel_id=1, source_target_pairs={{0,48},{1,17},{2,50},{3,19},{4,52},{5,21},{6,54},{7,23},{8,56},{9,... | collective-permute-start | bytes 589832 | tf_op jit(solution)/shard_map/ppermute | solution.py:317
  66.6 6.2 %collective-permute-start.13 = (bf16[128,768]{1,0:T(8,128)(2,1)S(1)}, bf16[128,768]{1,0:T(8,128)(2,1)S(1)}, u32[]{:S(2)}, u32[]{:S(2)}) collective-permute-start(bf16[128,768]{1,0:T(8,128)(2,1)S(1)} %join.2), channel_id=1, source_target_pairs={{1,48},{3,50},{5,52},{7,54},{9,56},{11,58},{13,60},{15,62},{16,1},... | collective-permute-start | bytes 589832 | tf_op jit(solution)/shard_map/ppermute | solution.py:317
  67.2 9.2 %collective-permute-start.23 = (bf16[128,768]{1,0:T(8,128)(2,1)S(1)}, bf16[128,768]{1,0:T(8,128)(2,1)S(1)}, u32[]{:S(2)}, u32[]{:S(2)}) collective-permute-start(bf16[128,768]{1,0:T(8,128)(2,1)S(1)} %get-tuple-element.48), channel_id=1, source_target_pairs={{0,1},{1,49},{2,3},{3,51},{4,5},{5,53},{6,7},{7,55},{8,9},{9,57},{... | collective-permute-start | bytes 589832 | tf_op jit(solution)/shard_map/ppermute | solution.py:317
  70.8 7.3 %collective-permute-start.24 = (bf16[128,768]{1,0:T(8,128)(2,1)S(1)}, bf16[128,768]{1,0:T(8,128)(2,1)S(1)}, u32[]{:S(2)}, u32[]{:S(2)}) collective-permute-start(bf16[128,768]{1,0:T(8,128)(2,1)S(1)} %get-tuple-element.49), channel_id=1, source_target_pairs={{0,32},{1,16},{2,34},{3,18},{4,36},{5,20},{6,38},{7,22},{8,40},{9,... | collective-permute-start | bytes 589832 | tf_op jit(solution)/shard_map/ppermute | solution.py:317
  72.1 6.0 %collective-permute-start.25 = (bf16[128,768]{1,0:T(8,128)(2,1)S(1)}, bf16[128,768]{1,0:T(8,128)(2,1)S(1)}, u32[]{:S(2)}, u32[]{:S(2)}) collective-permute-start(bf16[128,768]{1,0:T(8,128)(2,1)S(1)} %join.3), channel_id=1, source_target_pairs={{1,48},{3,50},{5,52},{7,54},{9,56},{11,58},{13,60},{15,62},{16,1},... | collective-permute-start | bytes 589832 | tf_op jit(solution)/shard_map/ppermute | solution.py:317
  73.0 8.3 %collective-permute-start.14 = (bf16[32,768]{1,0:T(8,128)(2,1)S(1)}, bf16[32,768]{1,0:T(8,128)(2,1)S(1)}, u32[]{:S(2)}, u32[]{:S(2)}) collective-permute-start(bf16[32,768]{1,0:T(8,128)(2,1)S(1)} %get-tuple-element.38), channel_id=1, source_target_pairs={{0,64},{16,80},{32,96},{48,112},{64,128},{80,144},{96,160},{112,17... | collective-permute-start | bytes 147464 | tf_op jit(solution)/shard_map/ppermute | solution.py:348
  74.0 7.7 %collective-permute-start.15 = (bf16[32,768]{1,0:T(8,128)(2,1)S(1)}, bf16[32,768]{1,0:T(8,128)(2,1)S(1)}, u32[]{:S(2)}, u32[]{:S(2)}) collective-permute-start(bf16[32,768]{1,0:T(8,128)(2,1)S(1)} %get-tuple-element.39), channel_id=1, source_target_pairs={{0,128},{16,144},{32,160},{48,176},{64,192},{80,208},{96,224},{112... | collective-permute-start | bytes 147464 | tf_op jit(solution)/shard_map/ppermute | solution.py:348
  76.4 5.3 %collective-permute-start.16 = (bf16[32,768]{1,0:T(8,128)(2,1)S(1)}, bf16[32,768]{1,0:T(8,128)(2,1)S(1)}, u32[]{:S(2)}, u32[]{:S(2)}) collective-permute-start(bf16[32,768]{1,0:T(8,128)(2,1)S(1)} %get-tuple-element.40), channel_id=1, source_target_pairs={{0,192},{16,208},{32,224},{48,240},{64,0},{80,16},{96,32},{112,48}... | collective-permute-start | bytes 147464 | tf_op jit(solution)/shard_map/ppermute | solution.py:348
  78.2 4.6 %collective-permute-start.26 = (bf16[32,768]{1,0:T(8,128)(2,1)S(1)}, bf16[32,768]{1,0:T(8,128)(2,1)S(1)}, u32[]{:S(2)}, u32[]{:S(2)}) collective-permute-start(bf16[32,768]{1,0:T(8,128)(2,1)S(1)} %get-tuple-element.52), channel_id=1, source_target_pairs={{0,64},{16,80},{32,96},{48,112},{64,128},{80,144},{96,160},{112,17... | collective-permute-start | bytes 147464 | tf_op jit(solution)/shard_map/ppermute | solution.py:348
  79.3 5.6 %collective-permute-start.27 = (bf16[32,768]{1,0:T(8,128)(2,1)S(1)}, bf16[32,768]{1,0:T(8,128)(2,1)S(1)}, u32[]{:S(2)}, u32[]{:S(2)}) collective-permute-start(bf16[32,768]{1,0:T(8,128)(2,1)S(1)} %get-tuple-element.53), channel_id=1, source_target_pairs={{0,128},{16,144},{32,160},{48,176},{64,192},{80,208},{96,224},{112... | collective-permute-start | bytes 147464 | tf_op jit(solution)/shard_map/ppermute | solution.py:348
  81.2 5.7 %collective-permute-start.28 = (bf16[32,768]{1,0:T(8,128)(2,1)S(1)}, bf16[32,768]{1,0:T(8,128)(2,1)S(1)}, u32[]{:S(2)}, u32[]{:S(2)}) collective-permute-start(bf16[32,768]{1,0:T(8,128)(2,1)S(1)} %get-tuple-element.54), channel_id=1, source_target_pairs={{0,192},{16,208},{32,224},{48,240},{64,0},{80,16},{96,32},{112,48}... | collective-permute-start | bytes 147464 | tf_op jit(solution)/shard_map/ppermute | solution.py:348
